TPU v7x, 32 devices: a whole 2x2x4 slice. The times are simulated.
32 devices in a mesh: gx: 2 (over x), gy: 4 (over y, core), gz: 4 (over z).
Axes of the slice: x: 2, y: 2, z: 4, core: 2. Of those that a mesh axis runs over, the one named last changes fastest.
Arguments:
- inputs: bfloat16 [384, 6144], P(('gx', 'gz'), 'gy'), may hold values from -6 to 6
- cotangent: bfloat16 [384, 6144], P(('gx', 'gz'), 'gy'), may hold values from -1.1953125 to 1.1953125
- up_weight: bfloat16 [6144, 24576], P('gy', ('gz', 'gx')), may hold values from -0.078125 to 0.078125
- down_weight: bfloat16 [24576, 6144], P(('gz', 'gx'), 'gy'), may hold values from -0.0390625 to 0.0390625
Outputs:
- grad_inputs: bfloat16 [384, 6144], P(('gx', 'gz'), 'gy')
- grad_up: float32 [6144, 24576], P('gy', ('gz', 'gx'))
- grad_down: float32 [24576, 6144], P(('gz', 'gx'), 'gy')
All inputs are finite; a program needn't handle non-finite values.
Results may differ from a plain program's by a relative error of at most 0.0049.
Values may be sent and summed in bfloat16 or wider, within the bound.
No kernel may reach another device: no remote copies, remote signals or barrier semaphores. Data moves between devices by JAX's collectives and lax.ppermute only.
A program may use at most 192 MiB of HBM per device.

v0:
```python
import jax
import jax.numpy as jnp
from jax import lax
from jax.sharding import PartitionSpec as P


def gelu_exact(value):
    return jax.nn.gelu(value, approximate=False)


def activate(preact, grad_hidden):
    activated, pullback = jax.vjp(gelu_exact, preact)
    grad_preact = pullback(grad_hidden)[0]
    return (activated.astype(jnp.bfloat16), grad_preact.astype(jnp.bfloat16))


def contract(left, right, left_dim, right_dim):
    return lax.dot_general(
        left, right, (((left_dim,), (right_dim,)), ((), ())), preferred_element_type=jnp.float32
    )


def body(inputs, cotangent, up_weight, down_weight):
    block_inputs, block_cotan = (
        lax.all_gather(inputs, "gz", axis=0, tiled=True),
        lax.all_gather(cotangent, "gz", axis=0, tiled=True),
    )
    up_block, down_block = (
        lax.all_gather(up_weight, "gx", axis=1, tiled=True),
        lax.all_gather(down_weight, "gx", axis=0, tiled=True),
    )
    preact_part = contract(block_inputs, up_block, 1, 0)
    grad_hidden_part = contract(block_cotan, down_block, 1, 1)
    preact_share, grad_share = (
        lax.psum_scatter(preact_part, "gy", scatter_dimension=1, tiled=True),
        lax.psum_scatter(grad_hidden_part, "gy", scatter_dimension=1, tiled=True),
    )
    hidden_share, grad_pre_share = activate(preact_share, grad_share)
    hidden, grad_preact = (
        lax.all_gather(hidden_share, "gy", axis=1, tiled=True),
        lax.all_gather(grad_pre_share, "gy", axis=1, tiled=True),
    )
    hidden_cols, grad_cols = (
        lax.all_to_all(hidden, "gx", split_axis=1, concat_axis=0, tiled=True),
        lax.all_to_all(grad_preact, "gx", split_axis=1, concat_axis=0, tiled=True),
    )
    all_inputs, all_cotan = (
        lax.all_gather(block_inputs, "gx", axis=0, tiled=True),
        lax.all_gather(block_cotan, "gx", axis=0, tiled=True),
    )
    grad_down = contract(hidden_cols, all_cotan, 0, 0)
    grad_up = contract(all_inputs, grad_cols, 0, 0)
    grad_inputs = lax.psum_scatter(
        contract(grad_preact, up_block, 1, 1), "gz", scatter_dimension=0, tiled=True
    ).astype(jnp.bfloat16)
    return (grad_inputs, grad_up, grad_down)


def solution(mesh):
    placed = (
        P(("gx", "gz"), "gy"),
        P(("gx", "gz"), "gy"),
        P("gy", ("gz", "gx")),
        P(("gz", "gx"), "gy"),
    )
    return jax.shard_map(
        body,
        mesh=mesh,
        in_specs=placed,
        out_specs=(P(("gx", "gz"), "gy"), P("gy", ("gz", "gx")), P(("gz", "gx"), "gy")),
        check_vma=False,
    )
```

profile of v0, /device:TPU:0, one launch (start us, length us, event | category | flops | bytes accessed | tf_op | source)
XLA Modules:
  0.0 718.6 jit_solution(11002080842374575167)
XLA Ops:
  7.2 0.0 all-gather.7.cloned.1.call-start
  7.2 0.7 all-gather.7.cloned.1.call-update
  7.9 0.0 copy-start.3
  7.9 0.0 all-gather.9.cloned.1.call-start
  8.0 0.7 all-gather.9.cloned.1.call-update
  8.7 0.0 reduce-scatter.4.cloned.1.call-start
  8.7 0.1 copy-done.3
  8.8 18.2 %all_gather.24 = bf16[192,1536]{1,0:T(8,128)(2,1)S(1)} all-gather(bf16[48,1536]{1,0:T(8,128)(2,1)S(1)} %copy-done.3), channel_id=1, replica_groups=mesh['gx'=2,'gy'=4,'gz'=4] {'gz'}, dimensions={0}, use_global_device_ids=true | all-gather | bytes 737280 | tf_op jit(solution)/shard_map/all_gather | solution.py:25
  27.0 0.0 copy-start
  27.0 209.6 %all-gather.7.cloned.1.call-done = bf16[1536,6144]{1,0:T(8,128)(2,1)} async-done(((bf16[1536,3072]{1,0:T(8,128)(2,1)}), bf16[1536,6144]{1,0:T(8,128)(2,1)}) %all-gather.7.cloned.1.call-update) | async-done | bytes 18874384 | tf_op jit(solution)/shard_map/all_gather | solution.py:29
  236.6 13.6 %fusion.7 = f32[192,6144]{1,0:T(8,128)} fusion(bf16[192,1536]{1,0:T(8,128)(2,1)S(1)} %all_gather.24, bf16[1536,6144]{1,0:T(8,128)(2,1)} %all-gather.7.cloned.1.call-done), kind=kOutput, calls=%fused_computation.20 | convolution fusion | flops 3623878656 | bytes 24182784 | tf_op jit(solution)/shard_map/dot_general | solution.py:18
  250.2 0.0 copy-done
  250.2 0.0 copy-start.4
  250.2 0.0 reduce-scatter.4.cloned.1.call-update
  250.2 0.0 reduce-scatter.6.cloned.1.call-start
  250.3 0.9 copy-done.4
  251.2 16.7 %all_gather.26 = bf16[192,1536]{1,0:T(8,128)(2,1)S(1)} all-gather(bf16[48,1536]{1,0:T(8,128)(2,1)S(1)} %copy-done.4), channel_id=1, replica_groups=mesh['gx'=2,'gy'=4,'gz'=4] {'gz'}, dimensions={0}, use_global_device_ids=true | all-gather | bytes 737280 | tf_op jit(solution)/shard_map/all_gather | solution.py:26
  267.9 0.0 copy-start.2
  267.9 194.7 %all-gather.9.cloned.1.call-done = bf16[6144,1536]{1,0:T(8,128)(2,1)} async-done(((bf16[3072,1536]{1,0:T(8,128)(2,1)}), bf16[6144,1536]{1,0:T(8,128)(2,1)}) %all-gather.9.cloned.1.call-update) | async-done | bytes 18874384 | tf_op jit(solution)/shard_map/all_gather | solution.py:30
  462.6 14.8 %fusion.8 = f32[192,6144]{1,0:T(8,128)} fusion(bf16[192,1536]{1,0:T(8,128)(2,1)S(1)} %all_gather.26, bf16[6144,1536]{1,0:T(8,128)(2,1)} %all-gather.9.cloned.1.call-done), kind=kOutput, calls=%fused_computation.21 | convolution fusion | flops 3623878656 | bytes 24182784 | tf_op jit(solution)/shard_map/dot_general | solution.py:18
  477.3 0.0 copy-done.2
  477.3 0.0 reduce-scatter.6.cloned.1.call-update
  477.4 0.0 all-gather.11.cloned.1.call-start
  477.4 36.1 %reduce-scatter.4.cloned.1.call-done = f32[192,1536]{1,0:T(8,128)} async-done(((f32[192,6144]{1,0:T(8,128)}), f32[192,1536]{1,0:T(8,128)}) %reduce-scatter.4.cloned.1.call-update) | async-done | bytes 1179664 | tf_op jit(solution)/shard_map/reduce_scatter | solution.py:35
  513.6 0.0 copy-start.1
  513.6 4.4 multiply_convert_fusion
  518.0 46.6 %reduce-scatter.6.cloned.1.call-done = f32[192,1536]{1,0:T(8,128)} async-done(((f32[192,6144]{1,0:T(8,128)}), f32[192,1536]{1,0:T(8,128)}) %reduce-scatter.6.cloned.1.call-update) | async-done | bytes 1179664 | tf_op jit(solution)/shard_map/reduce_scatter | solution.py:36
  564.6 0.0 copy-done.1
  564.6 2.6 add_convert_fusion
  567.1 0.0 all-gather.11.cloned.1.call-update
  567.2 0.0 all-gather.15.cloned.1.call-start
  567.2 0.5 all-gather.15.cloned.1.call-update
  567.7 0.0 all-gather.13.cloned.1.call-start
  567.8 0.7 all-gather.13.cloned.1.call-update
  568.5 0.0 all-gather.17.cloned.1.call-start
  568.5 0.7 all-gather.17.cloned.1.call-update
  569.2 22.1 %all-gather.11.cloned.1.call-done = bf16[192,6144]{1,0:T(8,128)(2,1)} async-done(((bf16[192,1536]{1,0:T(8,128)(2,1)}), bf16[192,6144]{1,0:T(8,128)(2,1)}) %all-gather.11.cloned.1.call-update) | async-done | bytes 2359312 | tf_op jit(solution)/shard_map/all_gather | solution.py:41
  591.4 3.2 copy.16
  594.6 3.8 all-to-all-start
  598.4 0.2 reduce-scatter.8.cloned.1.call-start
  598.7 18.8 %all-gather.15.cloned.1.call-done = bf16[192,6144]{1,0:T(8,128)(2,1)} async-done(((bf16[192,1536]{1,0:T(8,128)(2,1)}), bf16[192,6144]{1,0:T(8,128)(2,1)}) %all-gather.15.cloned.1.call-update) | async-done | bytes 2359312 | tf_op jit(solution)/shard_map/all_gather | solution.py:40
  617.5 3.2 copy.15
  620.7 15.1 %fusion.9 = f32[192,1536]{1,0:T(8,128)} fusion(bf16[192,6144]{1,0:T(8,128)(2,1)} %all-gather.11.cloned.1.call-done, bf16[1536,6144]{1,0:T(8,128)(2,1)} %all-gather.7.cloned.1.call-done), kind=kOutput, calls=%fused_computation.22 | convolution fusion | flops 3623878656 | bytes 22413312 | tf_op jit(solution)/shard_map/dot_general | solution.py:18
  635.8 0.0 reduce-scatter.8.cloned.1.call-update
  635.8 0.0 all-to-all-done
  635.8 4.9 all-to-all-start.1
  640.8 1.1 all-gather.13.cloned.1.call-done
  641.8 10.8 %convolution_bitcast_fusion = f32[1536,3072]{0,1:T(8,128)} fusion(bf16[384,3072]{1,0:T(8,128)(2,1)S(1)} %bitcast.26, bf16[384,1536]{1,0:T(8,128)(2,1)} %all-gather.13.cloned.1.call-done), kind=kOutput, calls=%fused_computation | convolution fusion | flops 3623878656 | bytes 22413312 | tf_op jit(solution)/shard_map/dot_general | solution.py:18
  652.6 18.6 %copy.10 = f32[1536,3072]{1,0:T(8,128)} copy(f32[1536,3072]{0,1:T(8,128)} %convolution_bitcast_fusion) | data formatting | bytes 37748736
  671.2 7.7 %all-gather.17.cloned.1.call-done = bf16[384,1536]{1,0:T(8,128)(2,1)} async-done(((bf16[192,1536]{1,0:T(8,128)(2,1)}), bf16[384,1536]{1,0:T(8,128)(2,1)}) %all-gather.17.cloned.1.call-update) | async-done | bytes 1179664 | tf_op jit(solution)/shard_map/all_gather | solution.py:49
  678.9 2.9 all-to-all-done.1
  681.8 11.1 %fusion.10 = f32[3072,1536]{1,0:T(8,128)} fusion(bf16[384,3072]{1,0:T(8,128)(2,1)} %bitcast.4, bf16[384,1536]{1,0:T(8,128)(2,1)} %all-gather.17.cloned.1.call-done), kind=kOutput, calls=%fused_computation.23 | convolution fusion | flops 3623878656 | bytes 22413312 | tf_op jit(solution)/shard_map/dot_general | solution.py:18
  692.9 17.5 %reduce-scatter.8.cloned.1.call-done = f32[48,1536]{1,0:T(8,128)} async-done(((f32[192,1536]{1,0:T(8,128)}), f32[48,1536]{1,0:T(8,128)}) %reduce-scatter.8.cloned.1.call-update) | async-done | bytes 294928 | tf_op jit(solution)/shard_map/reduce_scatter | solution.py:53
  710.5 1.6 convert_element_type.10
Async XLA Ops:
  7.2 229.4 %all-gather.7.cloned.1.call-start = ((), (), s32[]{:S(2)}) async-start(), calls=%async_computation.5 | async-start | bytes 28311552 | tf_op jit(solution)/shard_map/all_gather | solution.py:29
  7.9 0.9 copy-start.3
  7.9 454.7 %all-gather.9.cloned.1.call-start = ((), (), s32[]{:S(2)}) async-start(), calls=%async_computation.7 | async-start | bytes 28311552 | tf_op jit(solution)/shard_map/all_gather | solution.py:30
  8.7 504.9 %reduce-scatter.4.cloned.1.call-start = ((), (), s32[]{:S(2)}) async-start(), calls=%async_computation.6 | async-start | bytes 5898240 | tf_op jit(solution)/shard_map/reduce_scatter | solution.py:35
  27.0 223.2 %copy-start = (bf16[192,1536]{1,0:T(8,128)(2,1)}, bf16[192,1536]{1,0:T(8,128)(2,1)S(1)}, u32[]{:S(2)}) copy-start(bf16[192,1536]{1,0:T(8,128)(2,1)S(1)} %all_gather.24) | copy-start | bytes 1769476
  250.2 1.0 copy-start.4
  250.2 314.3 %reduce-scatter.6.cloned.1.call-start = ((), (), s32[]{:S(2)}) async-start(), calls=%async_computation.8 | async-start | bytes 5898240 | tf_op jit(solution)/shard_map/reduce_scatter | solution.py:36
  267.9 209.4 %copy-start.2 = (bf16[192,1536]{1,0:T(8,128)(2,1)}, bf16[192,1536]{1,0:T(8,128)(2,1)S(1)}, u32[]{:S(2)}) copy-start(bf16[192,1536]{1,0:T(8,128)(2,1)S(1)} %all_gather.26) | copy-start | bytes 1769476
  477.4 114.0 %all-gather.11.cloned.1.call-start = ((), (), s32[]{:S(2)}) async-start(), calls=%async_computation.9 | async-start | bytes 2949120 | tf_op jit(solution)/shard_map/all_gather | solution.py:41
  513.6 51.0 %copy-start.1 = (f32[192,1536]{1,0:T(8,128)S(1)}, f32[192,1536]{1,0:T(8,128)}, u32[]{:S(2)}) copy-start(f32[192,1536]{1,0:T(8,128)} %reduce-scatter.4.cloned.1.call-done) | copy-start | bytes 3538948
  567.2 50.3 %all-gather.15.cloned.1.call-start = ((), (), s32[]{:S(2)}) async-start(), calls=%async_computation.12 | async-start | bytes 2949120 | tf_op jit(solution)/shard_map/all_gather | solution.py:40
  567.7 74.1 %all-gather.13.cloned.1.call-start = ((), (), s32[]{:S(2)}) async-start(), calls=%async_computation.11 | async-start | bytes 1769472 | tf_op jit(solution)/shard_map/all_gather | solution.py:48
  568.5 110.5 %all-gather.17.cloned.1.call-start = ((), (), s32[]{:S(2)}) async-start(), calls=%async_computation.13 | async-start | bytes 1769472 | tf_op jit(solution)/shard_map/all_gather | solution.py:49
  594.6 41.2 %all-to-all-start = ((bf16[192,2,3072]{2,0,1:T(8,128)(2,1)}), bf16[192,2,3072]{2,0,1:T(8,128)(2,1)S(1)}, u32[]{:S(2)}, u32[]{:S(2)}) async-start(bf16[192,2,3072]{2,0,1:T(8,128)(2,1)} %bitcast.28), calls=%async_computation.3 | async-start | bytes 4718592 | tf_op jit(solution)/shard_map/all_to_all | solution.py:45
  598.4 112.0 %reduce-scatter.8.cloned.1.call-start = ((), (), s32[]{:S(2)}) async-start(), calls=%async_computation.10 | async-start | bytes 1474560 | tf_op jit(solution)/shard_map/reduce_scatter | solution.py:53
  635.8 46.0 %all-to-all-start.1 = ((bf16[192,2,3072]{2,0,1:T(8,128)(2,1)}), bf16[192,2,3072]{2,0,1:T(8,128)(2,1)}, u32[]{:S(2)}, u32[]{:S(2)}) async-start(bf16[192,2,3072]{2,0,1:T(8,128)(2,1)} %bitcast.27), calls=%async_computation.4 | async-start | bytes 4718592 | tf_op jit(solution)/shard_map/all_to_all | solution.py:44
Sparse Core Ops, SparseCore 0:
  9.6 227.0 all-gather.6
  238.2 224.3 all-gather.8
  465.7 47.8 reduce-scatter.3
  516.7 47.8 reduce-scatter.5
  567.3 24.0 all-gather.10
  593.4 24.0 all-gather.14
  619.0 22.7 all-gather.12
  643.4 35.5 all-gather.16
  681.3 29.1 reduce-scatter.7
where the time goes:
time: 719 us
  waiting for transfers between devices  561 us (78%)
  matrix products  65.3 us (9%)
  blocking collectives  34.9 us (5%)
  local copies, waits for them, and re-layouts  26.1 us (4%)
  between operations  13.9 us (2%)
  starting transfers between devices  9.29 us (1%)
  other arithmetic  8.6 us (1%)
    all_gather x1, waiting for transfers between devices, body(): lax.all_gather(up_weight, 'gx', axis=1, tiled=True)  210 us
    all_gather x1, waiting for transfers between devices, body(): lax.all_gather(down_weight, 'gx', axis=0, tiled=True)  195 us
    dot_general x5, matrix products, contract(): lax.dot_general(left, right, (((left_dim,), (right_dim,)), ((), ())), pre...  65.3 us
    reduce_scatter x1, waiting for transfers between devices, body(): lax.psum_scatter(grad_hidden_part, 'gy', scatter_dimension=1, tiled=True)  46.6 us
    reduce_scatter x1, waiting for transfers between devices, body(): lax.psum_scatter(preact_part, 'gy', scatter_dimension=1, tiled=True)  36.1 us
    all_gather x1, waiting for transfers between devices, body(): lax.all_gather(grad_pre_share, 'gy', axis=1, tiled=True)  22.1 us
    unnamed x11, local copies, waits for them, and re-layouts  19.7 us
    all_gather x1, waiting for transfers between devices, body(): lax.all_gather(hidden_share, 'gy', axis=1, tiled=True)  18.8 us
  transfers between devices with their start and end apart: 11, of which 10 were waited for; matrix products, arithmetic and copies ran while one was open for 13% of the time, Pallas kernels for 0%

commit v1 on v0

v1 whole, which is shorter than its diff:
```python
import functools

import jax
import jax.numpy as jnp
from jax import lax
from jax.experimental import pallas as pl
from jax.experimental.pallas import tpu as pltpu
from jax.sharding import PartitionSpec as P

F32 = jnp.float32
BF16 = jnp.bfloat16
VMEM_LIMIT = 40 * 1024 * 1024


def gelu_exact(value):
    return jax.nn.gelu(value, approximate=False)


def activate(preact, grad_hidden):
    activated, pullback = jax.vjp(gelu_exact, preact)
    grad_preact = pullback(grad_hidden)[0]
    return (activated.astype(BF16), grad_preact.astype(BF16))


def contract(left, right, left_dim, right_dim):
    return lax.dot_general(
        left, right, (((left_dim,), (right_dim,)), ((), ())), preferred_element_type=F32
    )


def general_body(inputs, cotangent, up_weight, down_weight):
    all_inputs = lax.all_gather(inputs, ("gx", "gz"), axis=0, tiled=True)
    all_cotan = lax.all_gather(cotangent, ("gx", "gz"), axis=0, tiled=True)
    preact = lax.psum_scatter(
        contract(all_inputs, up_weight, 1, 0), "gy", scatter_dimension=0, tiled=True
    )
    grad_hidden = lax.psum_scatter(
        contract(all_cotan, down_weight, 1, 1), "gy", scatter_dimension=0, tiled=True
    )
    hidden, grad_preact = activate(preact, grad_hidden)
    hidden = lax.all_gather(hidden, "gy", axis=0, tiled=True)
    grad_preact = lax.all_gather(grad_preact, "gy", axis=0, tiled=True)
    grad_down = contract(hidden, all_cotan, 0, 0)
    grad_up = contract(all_inputs, grad_preact, 0, 0)
    grad_inputs = lax.psum_scatter(
        contract(grad_preact, up_weight, 1, 1), ("gx", "gz"), scatter_dimension=0, tiled=True
    ).astype(BF16)
    return (grad_inputs, grad_up, grad_down)


def params():
    return pltpu.CompilerParams(vmem_limit_bytes=VMEM_LIMIT)


def tile_of(width, most):
    tile = most
    while width % tile:
        tile //= 2
    return tile


def partial_kernel(core_ref, own_ref, other_ref, up_ref, down_ref, keep_ref, send_ref):
    first = core_ref[0] == 0
    rows = own_ref.shape[1]
    for which in range(2):
        own, other = own_ref[which], other_ref[which]
        acts = jnp.concatenate(
            [jnp.where(first, own, other), jnp.where(first, other, own)], axis=0
        )
        if which == 0:
            part = contract(acts, up_ref[...], 1, 0)
        else:
            part = contract(acts, down_ref[...], 1, 1)
        keep_ref[which] = part[:rows]
        send_ref[which] = part[rows:].astype(BF16)


def partial_sums(core, own, other, up, down, start, width):
    _, rows, depth = own.shape
    tile = tile_of(width, 512)
    first = start // tile
    block = pl.BlockSpec((2, rows, depth), lambda i, c: (0, 0, 0))
    return pl.pallas_call(
        partial_kernel,
        grid_spec=pltpu.PrefetchScalarGridSpec(
            num_scalar_prefetch=1,
            grid=(width // tile,),
            in_specs=[
                block,
                block,
                pl.BlockSpec((depth, tile), lambda i, c: (0, first + i)),
                pl.BlockSpec((tile, depth), lambda i, c: (first + i, 0)),
            ],
            out_specs=[
                pl.BlockSpec((2, rows, tile), lambda i, c: (0, 0, i)),
                pl.BlockSpec((2, rows, tile), lambda i, c: (0, 0, i)),
            ],
        ),
        out_shape=[
            jax.ShapeDtypeStruct((2, rows, width), F32),
            jax.ShapeDtypeStruct((2, rows, width), BF16),
        ],
        compiler_params=params(),
        cost_estimate=pl.CostEstimate(
            flops=8 * rows * depth * width,
            bytes_accessed=4 * depth * width + 12 * rows * width,
            transcendentals=0,
        ),
        name="partial_sums",
    )(core, own, other, up, down)


def back_kernel(core_ref, mine_ref, theirs_ref, up_ref, stay_ref, go_ref):
    first = core_ref[0] == 0
    rows = mine_ref.shape[1]
    grads = jnp.concatenate([mine_ref[1], theirs_ref[1]], axis=0)
    part = contract(grads, up_ref[...], 1, 1)
    stay_ref[...] = jnp.where(first, part[:rows], part[rows:])
    go_ref[...] = jnp.where(first, part[rows:], part[:rows]).astype(BF16)


def back(core, mine, theirs, up):
    _, rows, width = mine.shape
    depth = up.shape[0]
    tile = tile_of(depth, 256)
    block = pl.BlockSpec((2, rows, width), lambda i, c: (0, 0, 0))
    out = pl.BlockSpec((rows, tile), lambda i, c: (0, i))
    return pl.pallas_call(
        back_kernel,
        grid_spec=pltpu.PrefetchScalarGridSpec(
            num_scalar_prefetch=1,
            grid=(depth // tile,),
            in_specs=[block, block, pl.BlockSpec((tile, width), lambda i, c: (i, 0))],
            out_specs=[out, out],
        ),
        out_shape=[
            jax.ShapeDtypeStruct((rows, depth), F32),
            jax.ShapeDtypeStruct((rows, depth), BF16),
        ],
        compiler_params=params(),
        cost_estimate=pl.CostEstimate(
            flops=4 * rows * depth * width,
            bytes_accessed=2 * depth * width + 6 * rows * depth,
            transcendentals=0,
        ),
        name="back",
    )(core, mine, theirs, up)


def grads_kernel(groups, core_ref, *refs):
    blocks = refs[: 2 * groups]
    acts = refs[2 * groups : 4 * groups]
    up_out, down_out, inputs_t, cotan = refs[4 * groups :]
    first = core_ref[0] == 0

    @pl.when(pl.program_id(0) == 0)
    def _():
        stacked = [[], []]
        for group in range(groups):
            own, other = blocks[2 * group], blocks[2 * group + 1]
            for which in range(2):
                stacked[which].append(jnp.where(first, own[which], other[which]))
                stacked[which].append(jnp.where(first, other[which], own[which]))
        inputs_t[...] = jnp.concatenate(stacked[0], axis=0).T
        cotan[...] = jnp.concatenate(stacked[1], axis=0)

    hidden = jnp.concatenate([ref[0] for ref in acts], axis=0)
    grad = jnp.concatenate([ref[1] for ref in acts], axis=0)
    up_out[...] = contract(inputs_t[...], grad, 1, 0)
    down_out[...] = contract(hidden, cotan[...], 0, 0)


def weight_grads(core, blocks, acts):
    groups = len(blocks) // 2
    _, rows, depth = blocks[0].shape
    width = acts[0].shape[2]
    tokens = rows * len(blocks)
    tile = tile_of(width, 256)
    block = pl.BlockSpec((2, rows, depth), lambda i, c: (0, 0, 0))
    act = pl.BlockSpec((2, rows, tile), lambda i, c: (0, 0, i))
    return pl.pallas_call(
        functools.partial(grads_kernel, groups),
        grid_spec=pltpu.PrefetchScalarGridSpec(
            num_scalar_prefetch=1,
            grid=(width // tile,),
            in_specs=[block] * len(blocks) + [act] * len(acts),
            out_specs=[
                pl.BlockSpec((depth, tile), lambda i, c: (0, i)),
                pl.BlockSpec((tile, depth), lambda i, c: (i, 0)),
            ],
            scratch_shapes=[pltpu.VMEM((depth, tokens), BF16), pltpu.VMEM((tokens, depth), BF16)],
        ),
        out_shape=[
            jax.ShapeDtypeStruct((depth, width), F32),
            jax.ShapeDtypeStruct((width, depth), F32),
        ],
        compiler_params=params(),
        cost_estimate=pl.CostEstimate(
            flops=4 * tokens * depth * width,
            bytes_accessed=8 * depth * width + 4 * tokens * (depth + width),
            transcendentals=0,
        ),
        name="weight_grads",
    )(core, *blocks, *acts)


def swap(value, axis, size, bits):
    return lax.ppermute(value, axis, [(i, i ^ bits) for i in range(size)])


def cube_body(gz, inputs, cotangent, up_weight, down_weight):
    width = up_weight.shape[1]
    core = (lax.axis_index("gy") % 2).astype(jnp.int32).reshape(1)
    mine = jnp.stack([inputs, cotangent])
    blocks = []
    for d in range(gz):
        own = mine if d == 0 else swap(mine, "gz", gz, d)
        blocks += [own, swap(own, "gx", 2, 1)]

    acts = []
    total = None
    for d in range(gz):
        own, other = blocks[2 * d : 2 * d + 2]
        keep, send = partial_sums(core, own, other, up_weight, down_weight, 0, width)
        near = swap(send, "gy", 4, 1)
        chip = (keep + near.astype(F32)).astype(BF16)
        far = swap(chip, "gy", 4, 2)
        summed = (keep + near.astype(F32)) + far.astype(F32)
        act = jnp.stack(activate(summed[0], summed[1]))
        act_near = swap(act, "gy", 4, 1)
        acts += [act, act_near]
        stay, go = back(core, act, act_near, up_weight)
        stay = stay + swap(go, "gx", 2, 1).astype(F32)
        if d:
            stay = swap(stay.astype(BF16), "gz", gz, d).astype(F32)
        total = stay if total is None else total + stay

    grad_up, grad_down = weight_grads(core, blocks, acts)
    return (total.astype(BF16), grad_up, grad_down)


def solution(mesh):
    placed = (
        P(("gx", "gz"), "gy"),
        P(("gx", "gz"), "gy"),
        P("gy", ("gz", "gx")),
        P(("gz", "gx"), "gy"),
    )
    gx, gy, gz = (mesh.shape[axis] for axis in ("gx", "gy", "gz"))
    if gx == 2 and gy == 4 and gz & (gz - 1) == 0:
        body = functools.partial(cube_body, gz)
    else:
        body = general_body
    return jax.shard_map(
        body,
        mesh=mesh,
        in_specs=placed,
        out_specs=(P(("gx", "gz"), "gy"), P("gy", ("gz", "gx")), P(("gz", "gx"), "gy")),
        check_vma=False,
    )
```

time: 719 us -> 176 us (0.24)
  waiting for transfers between devices: 561 us -> 59.3 us
  Pallas kernels: 0 us -> 69.4 us
  matrix products: 65.3 us -> 0 us
  blocking collectives: 34.9 us -> 0 us
  local copies, waits for them, and re-layouts: 26.1 us -> 5.38 us
  starting transfers between devices: 9.29 us -> 26.5 us
  between operations: 13.9 us -> 0.94 us
    all_gather x6 -> x0, waiting for transfers between devices: 454 us -> none  [the longest x1 210 us: body(): lax.all_gather(up_weight, 'gx', axis=1, tiled=True)]
    reduce_scatter x3 -> x0, waiting for transfers between devices: 100 us -> none  [the longest x1 46.6 us: body(): lax.psum_scatter(grad_hidden_part, 'gy', scatter_dimension=1, tiled=True)]
    pallas_call x0 -> x9, Pallas kernels: none -> 69.4 us  [the longest x4 36.2 us: partial_sums(): pl.pallas_call(partial_kernel, grid_spec=pltpu.PrefetchScalarGridSpec(num...]
    dot_general x5 -> x0, matrix products: 65.3 us -> none  [contract(): lax.dot_general(left, right, (((left_dim,), (right_dim,)), ((), ())), pre...]
    ppermute x0 -> x26, waiting for transfers between devices: none -> 59.3 us  [swap(): return lax.ppermute(value, axis, [(i, i ^ bits) for i in range(size)])]
    all_gather x2 -> x0, blocking collectives: 34.9 us -> none  [the longest x1 18.2 us: body(): lax.all_gather(inputs, 'gz', axis=0, tiled=True)]
    ppermute x0 -> x26, starting transfers between devices: none -> 26.5 us  [swap(): return lax.ppermute(value, axis, [(i, i ^ bits) for i in range(size)])]
    unnamed x11 -> x14, local copies, waits for them, and re-layouts: 19.7 us -> 5.38 us
  transfers between devices with their start and end apart: 11 -> 26, of which waited for: 10 -> 7; matrix products, arithmetic and copies ran while one was open for 13% -> 7% of each run, Pallas kernels for 0% -> 40%
where the time goes in v1:
time: 176 us; the launch traced here: 175 us
  Pallas kernels  69.4 us (39%)
  waiting for transfers between devices  59.3 us (34%)
  starting transfers between devices  26.5 us (15%)
  other arithmetic  13.5 us (8%)
  local copies, waits for them, and re-layouts  5.38 us (3%)
    ppermute x26, waiting for transfers between devices, swap(): return lax.ppermute(value, axis, [(i, i ^ bits) for i in range(size)])  59.3 us
    pallas_call x4, Pallas kernels, partial_sums(): pl.pallas_call(partial_kernel, grid_spec=pltpu.PrefetchScalarGridSpec(num...  36.2 us
    ppermute x26, starting transfers between devices, swap(): return lax.ppermute(value, axis, [(i, i ^ bits) for i in range(size)])  26.5 us
    pallas_call x1, Pallas kernels, weight_grads(): pl.pallas_call(functools.partial(grads_kernel, groups), grid_spec=pltpu.P...  17.7 us
    pallas_call x4, Pallas kernels, back(): pl.pallas_call(back_kernel, grid_spec=pltpu.PrefetchScalarGridSpec(num_sc...  15.4 us
    convert_element_type x8, other arithmetic, activate(): return (activated.astype(BF16), grad_preact.astype(BF16))  6.01 us
    unnamed x14, local copies, waits for them, and re-layouts  5.38 us
  transfers between devices with their start and end apart: 26, of which 7 were waited for; matrix products, arithmetic and copies ran while one was open for 7% of the time, Pallas kernels for 40%

profile of v1, /device:TPU:0, one launch (start us, length us, event | category | flops | bytes accessed | tf_op | source)
XLA Modules:
  0.0 174.9 jit_solution(3073593225036563271)
XLA Ops:
  0.6 1.0 pad_maximum_fusion.4.own_ref.refs_0_
  1.6 3.1 %collective-permute-start.5 = (bf16[2,48,1536]{2,1,0:T(8,128)(2,1)S(1)}, bf16[2,48,1536]{2,1,0:T(8,128)(2,1)S(1)}, u32[]{:S(2)}, u32[]{:S(2)}) collective-permute-start(bf16[2,48,1536]{2,1,0:T(8,128)(2,1)S(1)} %pad_maximum_fusion.4.own_ref.refs_0_), channel_id=1, source_target_pairs={{0,1},{1,0},{2,3},{3,2},{4,5},{5,4},{6,7},{7,6},{8,9},{9,8},{10,11... | collective-permute-start | bytes 884744 | tf_op jit(solution)/shard_map/ppermute | solution.py:208
  4.7 2.6 %collective-permute-start.12 = (bf16[2,48,1536]{2,1,0:T(8,128)(2,1)S(1)}, bf16[2,48,1536]{2,1,0:T(8,128)(2,1)S(1)}, u32[]{:S(2)}, u32[]{:S(2)}) collective-permute-start(bf16[2,48,1536]{2,1,0:T(8,128)(2,1)S(1)} %pad_maximum_fusion.4.own_ref.refs_0_), channel_id=1, source_target_pairs={{0,2},{1,3},{2,0},{3,1},{4,6},{5,7},{6,4},{7,5},{8,10},{9,11},{10,... | collective-permute-start | bytes 884744 | tf_op jit(solution)/shard_map/ppermute | solution.py:208
  7.3 1.5 collective-permute-start
  8.8 0.2 collective-permute-start.19
  9.0 8.3 %collective-permute-done.5.own_ref.refs_2_ = bf16[2,48,1536]{2,1,0:T(8,128)(2,1)S(1)} collective-permute-done((bf16[2,48,1536]{2,1,0:T(8,128)(2,1)S(1)}, bf16[2,48,1536]{2,1,0:T(8,128)(2,1)S(1)}, u32[]{:S(2)}, u32[]{:S(2)}) %collective-permute-start.5) | collective-permute-done | bytes 294944 | tf_op jit(solution)/shard_map/ppermute | solution.py:208
  17.3 1.7 collective-permute-start.6
  18.9 9.3 %collective-permute-done.12.own_ref.refs_4_ = bf16[2,48,1536]{2,1,0:T(8,128)(2,1)S(1)} collective-permute-done((bf16[2,48,1536]{2,1,0:T(8,128)(2,1)S(1)}, bf16[2,48,1536]{2,1,0:T(8,128)(2,1)S(1)}, u32[]{:S(2)}, u32[]{:S(2)}) %collective-permute-start.12) | collective-permute-done | bytes 294944 | tf_op jit(solution)/shard_map/ppermute | solution.py:208
  28.2 1.5 collective-permute-start.13
  29.7 3.7 %copy-done = bf16[1536,3072]{1,0:T(8,128)(2,1)S(1)} copy-done((bf16[1536,3072]{1,0:T(8,128)(2,1)S(1)}, bf16[1536,3072]{1,0:T(8,128)(2,1)}, u32[]{:S(2)}) %copy-start) | copy-done | bytes 9437208
  33.4 9.0 %partial_sums.4 = (f32[2,48,3072]{2,1,0:T(8,128)S(1)}, bf16[2,48,3072]{2,1,0:T(8,128)(2,1)}) custom-call(s32[1]{0:T(128)} %bitcast.core_ref, bf16[2,48,1536]{2,1,0:T(8,128)(2,1)S(1)} %pad_maximum_fusion.4.own_ref.refs_0_, bf16[2,48,1536]{2,1,0:T(8,128)(2,1)S(1)} %collective-permute-done.other_ref.refs_1_, bf16[1536,3072]{1,0:T(8,128)(2,1)S(1)} %copy-done, ...), custom_call_target="tpu_custom_call" | custom-call | flops 1811939328 | bytes 20643840 | tf_op jit(solution)/shard_map/partial_sums/pallas_call | solution.py:83
  42.4 0.6 collective-permute-start.20
  43.0 0.7 copy-done.1
  43.7 1.0 copy-done.2
  44.7 9.8 %partial_sums.5 = (f32[2,48,3072]{2,1,0:T(8,128)S(1)}, bf16[2,48,3072]{2,1,0:T(8,128)(2,1)}) custom-call(s32[1]{0:T(128)} %bitcast.core_ref, bf16[2,48,1536]{2,1,0:T(8,128)(2,1)S(1)} %collective-permute-done.5.own_ref.refs_2_, bf16[2,48,1536]{2,1,0:T(8,128)(2,1)S(1)} %copy-done.2, bf16[1536,3072]{1,0:T(8,128)(2,1)S(1)} %copy-done, bf16[3072,1536]{1,0:T(8,128)(2,1)} %down_ref.7), custom_call_target="tpu_custom_call" | custom-call | flops 1811939328 | bytes 20643840 | tf_op jit(solution)/shard_map/partial_sums/pallas_call | solution.py:83
  54.5 0.2 collective-permute-start.7
  54.7 9.0 %partial_sums.6 = (f32[2,48,3072]{2,1,0:T(8,128)S(1)}, bf16[2,48,3072]{2,1,0:T(8,128)(2,1)}) custom-call(s32[1]{0:T(128)} %bitcast.core_ref, bf16[2,48,1536]{2,1,0:T(8,128)(2,1)S(1)} %collective-permute-done.12.own_ref.refs_4_, bf16[2,48,1536]{2,1,0:T(8,128)(2,1)S(1)} %collective-permute-done.13.other_ref.refs_5_, bf16[1536,3072]{1,0:T(8,128)(2,1)S(1)} %copy-done, ...), custom_call_target="tpu_custom_call" | custom-call | flops 1811939328 | bytes 20643840 | tf_op jit(solution)/shard_map/partial_sums/pallas_call | solution.py:83
  63.7 0.3 collective-permute-start.14
  64.0 8.4 %partial_sums.7 = (f32[2,48,3072]{2,1,0:T(8,128)S(1)}, bf16[2,48,3072]{2,1,0:T(8,128)(2,1)S(1)}) custom-call(s32[1]{0:T(128)} %bitcast.core_ref, bf16[2,48,1536]{2,1,0:T(8,128)(2,1)S(1)} %collective-permute-done.19.own_ref.refs_6_, bf16[2,48,1536]{2,1,0:T(8,128)(2,1)S(1)} %collective-permute-done.20.other_ref.refs_7_, bf16[1536,3072]{1,0:T(8,128)(2,1)S(1)} %bitcast.4, ...), custom_call_target="tpu_custom_call" | custom-call | flops 1811939328 | bytes 20643840 | tf_op jit(solution)/shard_map/partial_sums/pallas_call | solution.py:83
  72.4 0.3 collective-permute-start.21
  72.7 1.2 fusion
  73.9 1.6 collective-permute-start.2
  75.5 1.2 fusion.1
  76.7 0.6 collective-permute-start.8
  77.3 0.1 fusion.2
  77.4 1.6 collective-permute-start.15
  79.0 0.1 fusion.3
  79.1 0.6 collective-permute-start.22
  79.7 10.4 %collective-permute-done.2 = bf16[2,48,3072]{2,1,0:T(8,128)(2,1)S(1)} collective-permute-done((bf16[2,48,3072]{2,1,0:T(8,128)(2,1)S(1)}, bf16[2,48,3072]{2,1,0:T(8,128)(2,1)S(1)}, u32[]{:S(2)}, u32[]{:S(2)}) %collective-permute-start.2) | collective-permute-done | bytes 589856 | tf_op jit(solution)/shard_map/ppermute | solution.py:208
  90.1 1.3 convert_add_fusion.6
  91.4 1.3 multiply_convert_fusion.3
  92.6 0.2 add_convert_fusion.3
  92.9 0.1 pad_maximum_fusion.mine_ref.refs_8_
  93.0 0.1 collective-permute-start.3
  93.0 9.7 %collective-permute-done.8 = bf16[2,48,3072]{2,1,0:T(8,128)(2,1)S(1)} collective-permute-done((bf16[2,48,3072]{2,1,0:T(8,128)(2,1)S(1)}, bf16[2,48,3072]{2,1,0:T(8,128)(2,1)S(1)}, u32[]{:S(2)}, u32[]{:S(2)}) %collective-permute-start.8) | collective-permute-done | bytes 589856 | tf_op jit(solution)/shard_map/ppermute | solution.py:208
  102.8 1.3 convert_add_fusion.4
  104.0 1.3 multiply_convert_fusion.2
  105.3 0.2 add_convert_fusion.2
  105.6 0.1 collective-permute-start.9
  105.7 9.7 %collective-permute-done.15 = bf16[2,48,3072]{2,1,0:T(8,128)(2,1)S(1)} collective-permute-done((bf16[2,48,3072]{2,1,0:T(8,128)(2,1)S(1)}, bf16[2,48,3072]{2,1,0:T(8,128)(2,1)S(1)}, u32[]{:S(2)}, u32[]{:S(2)}) %collective-permute-start.15) | collective-permute-done | bytes 589856 | tf_op jit(solution)/shard_map/ppermute | solution.py:208
  115.4 0.2 convert_add_fusion.2
  115.6 1.3 multiply_convert_fusion.1
  116.8 0.2 add_convert_fusion.1
  117.2 0.1 collective-permute-start.16
  117.2 10.2 %collective-permute-done.22 = bf16[2,48,3072]{2,1,0:T(8,128)(2,1)S(1)} collective-permute-done((bf16[2,48,3072]{2,1,0:T(8,128)(2,1)S(1)}, bf16[2,48,3072]{2,1,0:T(8,128)(2,1)S(1)}, u32[]{:S(2)}, u32[]{:S(2)}) %collective-permute-start.22) | collective-permute-done | bytes 589856 | tf_op jit(solution)/shard_map/ppermute | solution.py:208
  127.4 0.2 convert_add_fusion
  127.6 1.3 multiply_convert_fusion
  128.9 0.2 add_convert_fusion
  129.1 0.1 pad_maximum_fusion.3.mine_ref.refs_14_
  129.2 0.1 collective-permute-start.23
  129.3 3.9 %back.4 = (f32[48,1536]{1,0:T(8,128)S(1)}, bf16[48,1536]{1,0:T(8,128)(2,1)S(1)}) custom-call(s32[1]{0:T(128)} %bitcast.core_ref, bf16[2,48,3072]{2,1,0:T(8,128)(2,1)S(1)} %pad_maximum_fusion.mine_ref.refs_8_, bf16[2,48,3072]{2,1,0:T(8,128)(2,1)S(1)} %collective-permute-done.3.theirs_ref.refs_9_, bf16[1536,3072]{1,0:T(8,128)(2,1)S(1)} %bitcast.4), custom_call_target="tpu_custom_call" | custom-call | flops 905969664 | bytes 9879552 | tf_op jit(solution)/shard_map/back/pallas_call | solution.py:128
  133.2 1.5 collective-permute-start.4
  134.7 3.8 %back.5 = (f32[48,1536]{1,0:T(8,128)S(1)}, bf16[48,1536]{1,0:T(8,128)(2,1)S(1)}) custom-call(s32[1]{0:T(128)} %bitcast.core_ref, bf16[2,48,3072]{2,1,0:T(8,128)(2,1)S(1)} %pad_maximum_fusion.1.mine_ref.refs_10_, bf16[2,48,3072]{2,1,0:T(8,128)(2,1)S(1)} %collective-permute-done.9.theirs_ref.refs_11_, bf16[1536,3072]{1,0:T(8,128)(2,1)S(1)} %bitcast.4), custom_call_target="tpu_custom_call" | custom-call | flops 905969664 | bytes 9879552 | tf_op jit(solution)/shard_map/back/pallas_call | solution.py:128
  138.6 0.6 collective-permute-start.10
  139.2 3.8 %back.6 = (f32[48,1536]{1,0:T(8,128)S(1)}, bf16[48,1536]{1,0:T(8,128)(2,1)S(1)}) custom-call(s32[1]{0:T(128)} %bitcast.core_ref, bf16[2,48,3072]{2,1,0:T(8,128)(2,1)S(1)} %pad_maximum_fusion.2.mine_ref.refs_12_, bf16[2,48,3072]{2,1,0:T(8,128)(2,1)S(1)} %collective-permute-done.16.theirs_ref.refs_13_, bf16[1536,3072]{1,0:T(8,128)(2,1)S(1)} %bitcast.4), custom_call_target="tpu_custom_call" | custom-call | flops 905969664 | bytes 9879552 | tf_op jit(solution)/shard_map/back/pallas_call | solution.py:128
  143.0 1.5 collective-permute-start.17
  144.6 3.8 %back.7 = (f32[48,1536]{1,0:T(8,128)S(1)}, bf16[48,1536]{1,0:T(8,128)(2,1)S(1)}) custom-call(s32[1]{0:T(128)} %bitcast.core_ref, bf16[2,48,3072]{2,1,0:T(8,128)(2,1)S(1)} %pad_maximum_fusion.3.mine_ref.refs_14_, bf16[2,48,3072]{2,1,0:T(8,128)(2,1)S(1)} %collective-permute-done.23.theirs_ref.refs_15_, bf16[1536,3072]{1,0:T(8,128)(2,1)S(1)} %bitcast.4), custom_call_target="tpu_custom_call" | custom-call | flops 905969664 | bytes 9879552 | tf_op jit(solution)/shard_map/back/pallas_call | solution.py:128
  148.4 0.6 collective-permute-start.24
  149.1 0.1 collective-permute-start.11
  149.2 3.1 %collective-permute-start.18 = (bf16[48,1536]{1,0:T(8,128)(2,1)S(1)}, bf16[48,1536]{1,0:T(8,128)(2,1)S(1)}, u32[]{:S(2)}, u32[]{:S(2)}) collective-permute-start(bf16[48,1536]{1,0:T(8,128)(2,1)S(1)} %add_convert_fusion.6), channel_id=1, source_target_pairs={{0,2},{1,3},{2,0},{3,1},{4,6},{5,7},{6,4},{7,5},{8,10},{9,11},{10,... | collective-permute-start | bytes 442376 | tf_op jit(solution)/shard_map/ppermute | solution.py:208
  152.3 1.6 collective-permute-done.24
  153.9 2.5 %collective-permute-start.25 = (bf16[48,1536]{1,0:T(8,128)(2,1)S(1)}, bf16[48,1536]{1,0:T(8,128)(2,1)S(1)}, u32[]{:S(2)}, u32[]{:S(2)}) collective-permute-start(bf16[48,1536]{1,0:T(8,128)(2,1)S(1)} %add_convert_fusion.5), channel_id=1, source_target_pairs={{0,3},{1,2},{2,1},{3,0},{4,7},{5,6},{6,5},{7,4},{8,11},{9,10},{10,... | collective-permute-start | bytes 442376 | tf_op jit(solution)/shard_map/ppermute | solution.py:208
  156.5 17.7 %weight_grads.1 = (f32[1536,3072]{1,0:T(8,128)}, f32[3072,1536]{1,0:T(8,128)}) custom-call(s32[1]{0:T(128)} %bitcast.core_ref, bf16[2,48,1536]{2,1,0:T(8,128)(2,1)S(1)} %pad_maximum_fusion.4.own_ref.refs_0_, bf16[2,48,1536]{2,1,0:T(8,128)(2,1)S(1)} %collective-permute-done.other_ref.refs_1_, bf16[2,48,1536]{2,1,0:T(8,128)(2,1)S(1)} %collective-permute-done.5.own_ref.refs_2_, ...), custom_call_target="tpu_custom_call" | custom-call | flops 7247757312 | bytes 44826624 | tf_op jit(solution)/shard_map/weight_grads/pallas_call | solution.py:181
  174.2 0.7 add_convert_fusion.4
  (37 shorter events, 0.3 us)
Async XLA Ops:
  1.6 15.6 %collective-permute-start.5 = (bf16[2,48,1536]{2,1,0:T(8,128)(2,1)S(1)}, bf16[2,48,1536]{2,1,0:T(8,128)(2,1)S(1)}, u32[]{:S(2)}, u32[]{:S(2)}) collective-permute-start(bf16[2,48,1536]{2,1,0:T(8,128)(2,1)S(1)} %pad_maximum_fusion.4.own_ref.refs_0_), channel_id=1, source_target_pairs={{0,1},{1,0},{2,3},{3,2},{4,5},{5,4},{6,7},{7,6},{8,9},{9,8},{10,11... | collective-permute-start | bytes 884744 | tf_op jit(solution)/shard_map/ppermute | solution.py:208
  4.7 23.5 %collective-permute-start.12 = (bf16[2,48,1536]{2,1,0:T(8,128)(2,1)S(1)}, bf16[2,48,1536]{2,1,0:T(8,128)(2,1)S(1)}, u32[]{:S(2)}, u32[]{:S(2)}) collective-permute-start(bf16[2,48,1536]{2,1,0:T(8,128)(2,1)S(1)} %pad_maximum_fusion.4.own_ref.refs_0_), channel_id=1, source_target_pairs={{0,2},{1,3},{2,0},{3,1},{4,6},{5,7},{6,4},{7,5},{8,10},{9,11},{10,... | collective-permute-start | bytes 884744 | tf_op jit(solution)/shard_map/ppermute | solution.py:208
  7.3 22.4 %collective-permute-start = (bf16[2,48,1536]{2,1,0:T(8,128)(2,1)S(1)}, bf16[2,48,1536]{2,1,0:T(8,128)(2,1)S(1)}, u32[]{:S(2)}, u32[]{:S(2)}) collective-permute-start(bf16[2,48,1536]{2,1,0:T(8,128)(2,1)S(1)} %pad_maximum_fusion.4.own_ref.refs_0_), channel_id=1, source_target_pairs={{0,16},{16,0},{1,17},{17,1},{2,18},{18,2},{3,19},{19,3},{4,20},{20... | collective-permute-start | bytes 884744 | tf_op jit(solution)/shard_map/ppermute | solution.py:208
  8.8 33.6 %collective-permute-start.19 = (bf16[2,48,1536]{2,1,0:T(8,128)(2,1)S(1)}, bf16[2,48,1536]{2,1,0:T(8,128)(2,1)S(1)}, u32[]{:S(2)}, u32[]{:S(2)}) collective-permute-start(bf16[2,48,1536]{2,1,0:T(8,128)(2,1)S(1)} %pad_maximum_fusion.4.own_ref.refs_0_), channel_id=1, source_target_pairs={{0,3},{1,2},{2,1},{3,0},{4,7},{5,6},{6,5},{7,4},{8,11},{9,10},{10,... | collective-permute-start | bytes 884744 | tf_op jit(solution)/shard_map/ppermute | solution.py:208
  17.3 25.7 %collective-permute-start.6 = (bf16[2,48,1536]{2,1,0:T(8,128)(2,1)S(1)}, bf16[2,48,1536]{2,1,0:T(8,128)(2,1)S(1)}, u32[]{:S(2)}, u32[]{:S(2)}) collective-permute-start(bf16[2,48,1536]{2,1,0:T(8,128)(2,1)S(1)} %collective-permute-done.5.own_ref.refs_2_), channel_id=1, source_target_pairs={{0,16},{16,0},{1,17},{17,1},{2,18},{18,2},{3,19},{19,3},{4,20},{20... | collective-permute-start | bytes 884744 | tf_op jit(solution)/shard_map/ppermute | solution.py:208
  28.2 26.5 %collective-permute-start.13 = (bf16[2,48,1536]{2,1,0:T(8,128)(2,1)S(1)}, bf16[2,48,1536]{2,1,0:T(8,128)(2,1)S(1)}, u32[]{:S(2)}, u32[]{:S(2)}) collective-permute-start(bf16[2,48,1536]{2,1,0:T(8,128)(2,1)S(1)} %collective-permute-done.12.own_ref.refs_4_), channel_id=1, source_target_pairs={{0,16},{16,0},{1,17},{17,1},{2,18},{18,2},{3,19},{19,3},{4,20},{20... | collective-permute-start | bytes 884744 | tf_op jit(solution)/shard_map/ppermute | solution.py:208
  29.7 3.7 %copy-start = (bf16[1536,3072]{1,0:T(8,128)(2,1)S(1)}, bf16[1536,3072]{1,0:T(8,128)(2,1)}, u32[]{:S(2)}) copy-start(bf16[1536,3072]{1,0:T(8,128)(2,1)} %up_ref.15) | copy-start | bytes 28311556
  42.4 30.3 %collective-permute-start.1 = (bf16[2,48,3072]{2,1,0:T(8,128)(2,1)}, bf16[2,48,3072]{2,1,0:T(8,128)(2,1)}, u32[]{:S(2)}, u32[]{:S(2)}) collective-permute-start(bf16[2,48,3072]{2,1,0:T(8,128)(2,1)} %get-tuple-element.22), channel_id=1, source_target_pairs={{0,4},{4,0},{8,12},{12,8},{1,5},{5,1},{9,13},{13,9},{2,6},{6,2},{1... | collective-permute-start | bytes 1769480 | tf_op jit(solution)/shard_map/ppermute | solution.py:208
  42.4 21.6 %collective-permute-start.20 = (bf16[2,48,1536]{2,1,0:T(8,128)(2,1)S(1)}, bf16[2,48,1536]{2,1,0:T(8,128)(2,1)S(1)}, u32[]{:S(2)}, u32[]{:S(2)}) collective-permute-start(bf16[2,48,1536]{2,1,0:T(8,128)(2,1)S(1)} %collective-permute-done.19.own_ref.refs_6_), channel_id=1, source_target_pairs={{0,16},{16,0},{1,17},{17,1},{2,18},{18,2},{3,19},{19,3},{4,20},{20... | collective-permute-start | bytes 884744 | tf_op jit(solution)/shard_map/ppermute | solution.py:208
  43.0 0.7 copy-start.1
  43.7 1.0 copy-start.2
  44.7 19.3 %slice-start = ((s8[9437184]{0:T(1024)(128)(4,1)}), s8[4194304]{0:T(1024)(128)(4,1)S(1)}, s32[]{:S(2)}) async-start(s8[9437184]{0:T(1024)(128)(4,1)} %bitcast.3), calls=%async_computation | async-start | bytes 8388608
  44.7 19.3 %slice-start.1 = ((s8[9437184]{0:T(1024)(128)(4,1)}), s8[4194304]{0:T(1024)(128)(4,1)S(1)}, s32[]{:S(2)}) async-start(s8[9437184]{0:T(1024)(128)(4,1)} %bitcast.3), calls=%async_computation.1 | async-start | bytes 8388608
  54.5 9.5 %slice-start.2 = ((s8[9437184]{0:T(1024)(128)(4,1)}), s8[1048576]{0:T(1024)(128)(4,1)S(1)}, s32[]{:S(2)}) async-start(s8[9437184]{0:T(1024)(128)(4,1)} %bitcast.3), calls=%async_computation.2 | async-start | bytes 2097152
  54.5 21.0 %collective-permute-start.7 = (bf16[2,48,3072]{2,1,0:T(8,128)(2,1)}, bf16[2,48,3072]{2,1,0:T(8,128)(2,1)}, u32[]{:S(2)}, u32[]{:S(2)}) collective-permute-start(bf16[2,48,3072]{2,1,0:T(8,128)(2,1)} %get-tuple-element.26), channel_id=1, source_target_pairs={{0,4},{4,0},{8,12},{12,8},{1,5},{5,1},{9,13},{13,9},{2,6},{6,2},{1... | collective-permute-start | bytes 1769480 | tf_op jit(solution)/shard_map/ppermute | solution.py:208
  63.7 13.6 %collective-permute-start.14 = (bf16[2,48,3072]{2,1,0:T(8,128)(2,1)}, bf16[2,48,3072]{2,1,0:T(8,128)(2,1)S(1)}, u32[]{:S(2)}, u32[]{:S(2)}) collective-permute-start(bf16[2,48,3072]{2,1,0:T(8,128)(2,1)} %get-tuple-element.30), channel_id=1, source_target_pairs={{0,4},{4,0},{8,12},{12,8},{1,5},{5,1},{9,13},{13,9},{2,6},{6,2},{1... | collective-permute-start | bytes 1769480 | tf_op jit(solution)/shard_map/ppermute | solution.py:208
  72.4 6.6 %collective-permute-start.21 = (bf16[2,48,3072]{2,1,0:T(8,128)(2,1)S(1)}, bf16[2,48,3072]{2,1,0:T(8,128)(2,1)S(1)}, u32[]{:S(2)}, u32[]{:S(2)}) collective-permute-start(bf16[2,48,3072]{2,1,0:T(8,128)(2,1)S(1)} %get-tuple-element.34), channel_id=1, source_target_pairs={{0,4},{4,0},{8,12},{12,8},{1,5},{5,1},{9,13},{13,9},{2,6},{6,2},{1... | collective-permute-start | bytes 1769480 | tf_op jit(solution)/shard_map/ppermute | solution.py:208
  73.9 16.2 %collective-permute-start.2 = (bf16[2,48,3072]{2,1,0:T(8,128)(2,1)S(1)}, bf16[2,48,3072]{2,1,0:T(8,128)(2,1)S(1)}, u32[]{:S(2)}, u32[]{:S(2)}) collective-permute-start(bf16[2,48,3072]{2,1,0:T(8,128)(2,1)S(1)} %fusion), channel_id=1, source_target_pairs={{0,8},{4,12},{8,0},{12,4},{1,9},{5,13},{9,1},{13,5},{2,10},{6,14},... | collective-permute-start | bytes 1769480 | tf_op jit(solution)/shard_map/ppermute | solution.py:208
  76.7 26.1 %collective-permute-start.8 = (bf16[2,48,3072]{2,1,0:T(8,128)(2,1)S(1)}, bf16[2,48,3072]{2,1,0:T(8,128)(2,1)S(1)}, u32[]{:S(2)}, u32[]{:S(2)}) collective-permute-start(bf16[2,48,3072]{2,1,0:T(8,128)(2,1)S(1)} %fusion.1), channel_id=1, source_target_pairs={{0,8},{4,12},{8,0},{12,4},{1,9},{5,13},{9,1},{13,5},{2,10},{6,14},... | collective-permute-start | bytes 1769480 | tf_op jit(solution)/shard_map/ppermute | solution.py:208
  77.4 38.0 %collective-permute-start.15 = (bf16[2,48,3072]{2,1,0:T(8,128)(2,1)S(1)}, bf16[2,48,3072]{2,1,0:T(8,128)(2,1)S(1)}, u32[]{:S(2)}, u32[]{:S(2)}) collective-permute-start(bf16[2,48,3072]{2,1,0:T(8,128)(2,1)S(1)} %fusion.2), channel_id=1, source_target_pairs={{0,8},{4,12},{8,0},{12,4},{1,9},{5,13},{9,1},{13,5},{2,10},{6,14},... | collective-permute-start | bytes 1769480 | tf_op jit(solution)/shard_map/ppermute | solution.py:208
  79.1 48.3 %collective-permute-start.22 = (bf16[2,48,3072]{2,1,0:T(8,128)(2,1)S(1)}, bf16[2,48,3072]{2,1,0:T(8,128)(2,1)S(1)}, u32[]{:S(2)}, u32[]{:S(2)}) collective-permute-start(bf16[2,48,3072]{2,1,0:T(8,128)(2,1)S(1)} %fusion.3), channel_id=1, source_target_pairs={{0,8},{4,12},{8,0},{12,4},{1,9},{5,13},{9,1},{13,5},{2,10},{6,14},... | collective-permute-start | bytes 1769480 | tf_op jit(solution)/shard_map/ppermute | solution.py:208
  93.0 36.3 %collective-permute-start.3 = (bf16[2,48,3072]{2,1,0:T(8,128)(2,1)S(1)}, bf16[2,48,3072]{2,1,0:T(8,128)(2,1)S(1)}, u32[]{:S(2)}, u32[]{:S(2)}) collective-permute-start(bf16[2,48,3072]{2,1,0:T(8,128)(2,1)S(1)} %pad_maximum_fusion.mine_ref.refs_8_), channel_id=1, source_target_pairs={{0,4},{4,0},{8,12},{12,8},{1,5},{5,1},{9,13},{13,9},{2,6},{6,2},{1... | collective-permute-start | bytes 1769480 | tf_op jit(solution)/shard_map/ppermute | solution.py:208
  105.6 29.1 %collective-permute-start.9 = (bf16[2,48,3072]{2,1,0:T(8,128)(2,1)S(1)}, bf16[2,48,3072]{2,1,0:T(8,128)(2,1)S(1)}, u32[]{:S(2)}, u32[]{:S(2)}) collective-permute-start(bf16[2,48,3072]{2,1,0:T(8,128)(2,1)S(1)} %pad_maximum_fusion.1.mine_ref.refs_10_), channel_id=1, source_target_pairs={{0,4},{4,0},{8,12},{12,8},{1,5},{5,1},{9,13},{13,9},{2,6},{6,2},{1... | collective-permute-start | bytes 1769480 | tf_op jit(solution)/shard_map/ppermute | solution.py:208
  117.2 22.0 %collective-permute-start.16 = (bf16[2,48,3072]{2,1,0:T(8,128)(2,1)S(1)}, bf16[2,48,3072]{2,1,0:T(8,128)(2,1)S(1)}, u32[]{:S(2)}, u32[]{:S(2)}) collective-permute-start(bf16[2,48,3072]{2,1,0:T(8,128)(2,1)S(1)} %pad_maximum_fusion.2.mine_ref.refs_12_), channel_id=1, source_target_pairs={{0,4},{4,0},{8,12},{12,8},{1,5},{5,1},{9,13},{13,9},{2,6},{6,2},{1... | collective-permute-start | bytes 1769480 | tf_op jit(solution)/shard_map/ppermute | solution.py:208
  129.2 15.4 %collective-permute-start.23 = (bf16[2,48,3072]{2,1,0:T(8,128)(2,1)S(1)}, bf16[2,48,3072]{2,1,0:T(8,128)(2,1)S(1)}, u32[]{:S(2)}, u32[]{:S(2)}) collective-permute-start(bf16[2,48,3072]{2,1,0:T(8,128)(2,1)S(1)} %pad_maximum_fusion.3.mine_ref.refs_14_), channel_id=1, source_target_pairs={{0,4},{4,0},{8,12},{12,8},{1,5},{5,1},{9,13},{13,9},{2,6},{6,2},{1... | collective-permute-start | bytes 1769480 | tf_op jit(solution)/shard_map/ppermute | solution.py:208
  133.2 41.0 %collective-permute-start.4 = (bf16[48,1536]{1,0:T(8,128)(2,1)S(1)}, bf16[48,1536]{1,0:T(8,128)(2,1)S(1)}, u32[]{:S(2)}, u32[]{:S(2)}) collective-permute-start(bf16[48,1536]{1,0:T(8,128)(2,1)S(1)} %get-tuple-element.24), channel_id=1, source_target_pairs={{0,16},{16,0},{1,17},{17,1},{2,18},{18,2},{3,19},{19,3},{4,20},{20... | collective-permute-start | bytes 442376 | tf_op jit(solution)/shard_map/ppermute | solution.py:208
  138.6 10.5 %collective-permute-start.10 = (bf16[48,1536]{1,0:T(8,128)(2,1)S(1)}, bf16[48,1536]{1,0:T(8,128)(2,1)S(1)}, u32[]{:S(2)}, u32[]{:S(2)}) collective-permute-start(bf16[48,1536]{1,0:T(8,128)(2,1)S(1)} %get-tuple-element.28), channel_id=1, source_target_pairs={{0,16},{16,0},{1,17},{17,1},{2,18},{18,2},{3,19},{19,3},{4,20},{20... | collective-permute-start | bytes 442376 | tf_op jit(solution)/shard_map/ppermute | solution.py:208
  143.0 6.1 %collective-permute-start.17 = (bf16[48,1536]{1,0:T(8,128)(2,1)S(1)}, bf16[48,1536]{1,0:T(8,128)(2,1)S(1)}, u32[]{:S(2)}, u32[]{:S(2)}) collective-permute-start(bf16[48,1536]{1,0:T(8,128)(2,1)S(1)} %get-tuple-element.32), channel_id=1, source_target_pairs={{0,16},{16,0},{1,17},{17,1},{2,18},{18,2},{3,19},{19,3},{4,20},{20... | collective-permute-start | bytes 442376 | tf_op jit(solution)/shard_map/ppermute | solution.py:208
  148.4 8.0 %copy-start.3 = (bf16[2,48,1536]{2,1,0:T(8,128)(2,1)S(1)}, bf16[2,48,1536]{2,1,0:T(8,128)(2,1)}, u32[]{:S(2)}) copy-start(bf16[2,48,1536]{2,1,0:T(8,128)(2,1)} %copy-done.1) | copy-start | bytes 884740
  148.4 5.4 %collective-permute-start.24 = (bf16[48,1536]{1,0:T(8,128)(2,1)S(1)}, bf16[48,1536]{1,0:T(8,128)(2,1)S(1)}, u32[]{:S(2)}, u32[]{:S(2)}) collective-permute-start(bf16[48,1536]{1,0:T(8,128)(2,1)S(1)} %get-tuple-element.36), channel_id=1, source_target_pairs={{0,16},{16,0},{1,17},{17,1},{2,18},{18,2},{3,19},{19,3},{4,20},{20... | collective-permute-start | bytes 442376 | tf_op jit(solution)/shard_map/ppermute | solution.py:208
  149.1 25.1 %collective-permute-start.11 = (bf16[48,1536]{1,0:T(8,128)(2,1)S(1)}, bf16[48,1536]{1,0:T(8,128)(2,1)S(1)}, u32[]{:S(2)}, u32[]{:S(2)}) collective-permute-start(bf16[48,1536]{1,0:T(8,128)(2,1)S(1)} %add_convert_fusion.7), channel_id=1, source_target_pairs={{0,1},{1,0},{2,3},{3,2},{4,5},{5,4},{6,7},{7,6},{8,9},{9,8},{10,11... | collective-permute-start | bytes 442376 | tf_op jit(solution)/shard_map/ppermute | solution.py:208
  149.2 24.9 %collective-permute-start.18 = (bf16[48,1536]{1,0:T(8,128)(2,1)S(1)}, bf16[48,1536]{1,0:T(8,128)(2,1)S(1)}, u32[]{:S(2)}, u32[]{:S(2)}) collective-permute-start(bf16[48,1536]{1,0:T(8,128)(2,1)S(1)} %add_convert_fusion.6), channel_id=1, source_target_pairs={{0,2},{1,3},{2,0},{3,1},{4,6},{5,7},{6,4},{7,5},{8,10},{9,11},{10,... | collective-permute-start | bytes 442376 | tf_op jit(solution)/shard_map/ppermute | solution.py:208
  153.9 20.3 %collective-permute-start.25 = (bf16[48,1536]{1,0:T(8,128)(2,1)S(1)}, bf16[48,1536]{1,0:T(8,128)(2,1)S(1)}, u32[]{:S(2)}, u32[]{:S(2)}) collective-permute-start(bf16[48,1536]{1,0:T(8,128)(2,1)S(1)} %add_convert_fusion.5), channel_id=1, source_target_pairs={{0,3},{1,2},{2,1},{3,0},{4,7},{5,6},{6,5},{7,4},{8,11},{9,10},{10,... | collective-permute-start | bytes 442376 | tf_op jit(solution)/shard_map/ppermute | solution.py:208

commit v2 on v0

v2 whole, which is shorter than its diff:
```python
import math

import jax
import jax.numpy as jnp
from jax import lax
from jax.experimental import pallas as pl
from jax.experimental.pallas import tpu as pltpu
from jax.sharding import PartitionSpec as P

F32 = jnp.float32
BF16 = jnp.bfloat16
VMEM_LIMIT = 24 * 1024 * 1024
COST_PART = 16


def gelu_exact(value):
    return jax.nn.gelu(value, approximate=False)


def activate(preact, grad_hidden):
    activated, pullback = jax.vjp(gelu_exact, preact)
    grad_preact = pullback(grad_hidden)[0]
    return (activated.astype(BF16), grad_preact.astype(BF16))


def contract(left, right, left_dim, right_dim):
    return lax.dot_general(
        left, right, (((left_dim,), (right_dim,)), ((), ())), preferred_element_type=F32
    )


def general_body(inputs, cotangent, up_weight, down_weight):
    all_inputs = lax.all_gather(inputs, ("gx", "gz"), axis=0, tiled=True)
    all_cotan = lax.all_gather(cotangent, ("gx", "gz"), axis=0, tiled=True)
    preact = lax.psum_scatter(
        contract(all_inputs, up_weight, 1, 0), "gy", scatter_dimension=0, tiled=True
    )
    grad_hidden = lax.psum_scatter(
        contract(all_cotan, down_weight, 1, 1), "gy", scatter_dimension=0, tiled=True
    )
    hidden, grad_preact = activate(preact, grad_hidden)
    hidden = lax.all_gather(hidden, "gy", axis=0, tiled=True)
    grad_preact = lax.all_gather(grad_preact, "gy", axis=0, tiled=True)
    grad_down = contract(hidden, all_cotan, 0, 0)
    grad_up = contract(all_inputs, grad_preact, 0, 0)
    grad_inputs = lax.psum_scatter(
        contract(grad_preact, up_weight, 1, 1), ("gx", "gz"), scatter_dimension=0, tiled=True
    ).astype(BF16)
    return (grad_inputs, grad_up, grad_down)


def tile_of(width, most):
    tile = most
    while width % tile:
        tile //= 2
    return tile


def call(body, core, operands, in_specs, outs, out_specs, grid, cost, name, after=(), scratch=(), aliases=None):
    after = list(after)
    inner = len(operands) + 1

    def kernel(*refs):
        body(*refs[:inner], *refs[inner + len(after) :])

    flops, moved = cost
    return pl.pallas_call(
        kernel,
        grid_spec=pltpu.PrefetchScalarGridSpec(
            num_scalar_prefetch=1,
            grid=grid,
            in_specs=list(in_specs) + [pl.BlockSpec(memory_space=pl.ANY)] * len(after),
            out_specs=out_specs,
            scratch_shapes=list(scratch),
        ),
        out_shape=outs,
        input_output_aliases=aliases or {},
        compiler_params=pltpu.CompilerParams(vmem_limit_bytes=VMEM_LIMIT),
        cost_estimate=pl.CostEstimate(
            flops=flops // COST_PART, bytes_accessed=moved // COST_PART, transcendentals=0
        ),
        name=name,
    )(core, *operands, *after)


def whole(shape):
    return pl.BlockSpec(shape, lambda i, c: (0,) * len(shape))


def side_of(core_ref, side):
    return core_ref[0] if side == 0 else 1 - core_ref[0]


def partial_sums(core, units, up, down, side, start, width, dtype, after=()):
    _, rows, depth = units[0].shape
    tokens = rows * len(units)
    half = up.shape[1] // 2
    tile = tile_of(width, 256)

    def body(core_ref, *refs):
        *unit_refs, up_ref, down_ref, out_ref, acts = refs

        @pl.when(pl.program_id(0) == 0)
        def _():
            for n, ref in enumerate(unit_refs):
                acts[:, n * rows : (n + 1) * rows, :] = ref[...]

        out_ref[0] = contract(acts[0], up_ref[...], 1, 0).astype(dtype)
        out_ref[1] = contract(acts[1], down_ref[...], 1, 1).astype(dtype)

    def place(i, c):
        return side_of(c, side) * (half // tile) + start // tile + i

    return call(
        body,
        core,
        [*units, up, down],
        [whole(units[0].shape)] * len(units)
        + [
            pl.BlockSpec((depth, tile), lambda i, c: (0, place(i, c))),
            pl.BlockSpec((tile, depth), lambda i, c: (place(i, c), 0)),
        ],
        jax.ShapeDtypeStruct((2, tokens, width), dtype),
        pl.BlockSpec((2, tokens, tile), lambda i, c: (0, 0, i)),
        (width // tile,),
        (4 * tokens * depth * width, 4 * depth * width),
        "sums_send" if side else "sums_keep",
        after,
        [pltpu.VMEM((2, tokens, depth), BF16)],
    )


def activations(core, keep, near, far, after=()):
    _, tokens, width = keep.shape
    tile = tile_of(width, 256)
    block = pl.BlockSpec((2, tokens, tile), lambda i, c: (0, 0, i))

    def body(core_ref, keep_ref, near_ref, far_ref, act_ref):
        def total(which):
            return keep_ref[which] + near_ref[which].astype(F32) + far_ref[which].astype(F32)

        preact = total(0)
        cdf = 0.5 + 0.5 * lax.erf(preact * (0.5**0.5))
        pdf = jnp.exp(-0.5 * preact * preact) * ((0.5 / math.pi) ** 0.5)
        act_ref[0] = (preact * cdf).astype(BF16)
        act_ref[1] = (total(1) * (cdf + preact * pdf)).astype(BF16)

    return call(
        body,
        core,
        [keep, near, far],
        [block] * 3,
        jax.ShapeDtypeStruct(keep.shape, BF16),
        block,
        (width // tile,),
        (60 * tokens * width, 20 * tokens * width),
        "activations",
        after,
    )


def back(core, keep, near, up, start, before, leave, after=()):
    _, tokens, width = keep.shape
    depth, half = up.shape[0], up.shape[1] // 2
    tile = tile_of(depth, 512)
    act = pl.BlockSpec((1, tokens, width), lambda i, c: (1, 0, 0))

    def body(core_ref, keep_ref, near_ref, up_keep, up_near, *refs):
        part = contract(keep_ref[0], up_keep[...], 1, 1) + contract(near_ref[0], up_near[...], 1, 1)
        if before is not None:
            part = part + refs[0][...]
        outs = refs[(before is not None) :]
        if leave is None:
            outs[0][...] = part
        else:
            outs[0][...] = part[:leave]
            if leave < tokens:
                outs[1][...] = part[leave:].astype(BF16)

    def weights(side):
        return pl.BlockSpec(
            (tile, width), lambda i, c: (i, side_of(c, side) * (half // width) + start // width)
        )

    kinds = [(tokens if leave is None else leave, F32)]
    if leave is not None and leave < tokens:
        kinds.append((tokens - leave, BF16))
    return call(
        body,
        core,
        [keep, near, up, up] + ([] if before is None else [before]),
        [act, act, weights(0), weights(1)]
        + ([] if before is None else [pl.BlockSpec((tokens, tile), lambda i, c: (0, i))]),
        [jax.ShapeDtypeStruct((rows, depth), dtype) for rows, dtype in kinds],
        [pl.BlockSpec((rows, tile), lambda i, c: (0, i)) for rows, _ in kinds],
        (depth // tile,),
        (4 * tokens * depth * width, 4 * depth * width + 4 * tokens * depth),
        "back",
        after,
    )


def arrange(core, units, after=()):
    _, rows, depth = units[0].shape
    tokens = rows * len(units)

    def body(core_ref, *refs):
        *unit_refs, inputs_t, cotan = refs
        inputs_t[...] = jnp.concatenate([ref[0] for ref in unit_refs], axis=0).T
        cotan[...] = jnp.concatenate([ref[1] for ref in unit_refs], axis=0)

    return call(
        body,
        core,
        units,
        [whole(units[0].shape)] * len(units),
        [jax.ShapeDtypeStruct((depth, tokens), BF16), jax.ShapeDtypeStruct((tokens, depth), BF16)],
        [whole((depth, tokens)), whole((tokens, depth))],
        (1,),
        (0, 8 * tokens * depth),
        "arrange",
        after,
    )


def weight_grads(core, inputs_t, cotan, sides, acts, start, width, shape, outputs, after=()):
    depth, full = shape
    tokens = cotan.shape[0]
    half = full // 2
    tile = tile_of(width, 256)
    steps = width // tile
    groups = len(acts[0])

    def act_spec(order, array, offset):
        def index(i, c):
            return (0, 0, offset // tile + jnp.clip(i - order * steps, 0, steps - 1))

        return pl.BlockSpec((2, array.shape[1], tile), index)

    def body(core_ref, inputs_ref, cotan_ref, *refs):
        up_out, down_out, done = refs[-3:]
        done[...] = jnp.zeros_like(done)
        for order in range(len(sides)):
            mine = refs[order * groups : (order + 1) * groups]

            @pl.when(pl.program_id(0) // steps == order)
            def _(mine=mine):
                hidden = jnp.concatenate([ref[0] for ref in mine], axis=0)
                grad = jnp.concatenate([ref[1] for ref in mine], axis=0)
                up_out[...] = contract(inputs_ref[...], grad, 1, 0)
                down_out[...] = contract(hidden, cotan_ref[...], 0, 0)

    def place(i, c):
        which = side_of(c, sides[0])
        if len(sides) > 1:
            which = jnp.where(i // steps == 0, which, 1 - which)
        return which * (half // tile) + start // tile + i % steps

    operands = [inputs_t, cotan]
    specs = [whole(inputs_t.shape), whole(cotan.shape)]
    for order in range(len(sides)):
        for array, offset in acts[order]:
            operands.append(array)
            specs.append(act_spec(order, array, offset))
    aliases = None
    if outputs is not None:
        aliases = {len(operands) + 1: 0, len(operands) + 2: 1}
        operands += list(outputs)
        specs += [pl.BlockSpec(memory_space=pl.ANY)] * 2
    many = width * len(sides)
    return call(
        body,
        core,
        operands,
        specs,
        [
            jax.ShapeDtypeStruct((depth, full), F32),
            jax.ShapeDtypeStruct((full, depth), F32),
            jax.ShapeDtypeStruct((8, 128), F32),
        ],
        [
            pl.BlockSpec((depth, tile), lambda i, c: (0, place(i, c))),
            pl.BlockSpec((tile, depth), lambda i, c: (place(i, c), 0)),
            whole((8, 128)),
        ],
        (steps * len(sides),),
        (4 * tokens * depth * many, 8 * depth * many),
        "weight_grads",
        after,
        aliases=aliases,
    )


def swap(value, axis, size, bits):
    return lax.ppermute(value, axis, [(i, i ^ bits) for i in range(size)])


def cube_body(inputs, cotangent, up, down):
    rows = inputs.shape[0]
    half = up.shape[1] // 2
    width = half // 3 if half % 384 == 0 else half
    chunks = half // width
    core = (lax.axis_index("gy") % 2).astype(jnp.int32).reshape(1)

    unit = {(0, 0): jnp.stack([inputs, cotangent])}
    unit[0, 1] = swap(unit[0, 0], "gx", 2, 1)
    for d in (1, 2, 3):
        unit[d, 0] = swap(unit[0, 0], "gz", 4, d)
        unit[d, 1] = swap(unit[d, 0], "gx", 2, 1)
    groups = [
        [unit[0, 0]],
        [unit[1, 0], unit[0, 1], unit[1, 1]],
        [unit[2, 0], unit[3, 0], unit[2, 1], unit[3, 1]],
    ]

    def sums(piece, side, after):
        group, start, size = piece
        dtype = F32 if side == 0 else BF16
        weights = (up, down)
        if group == 0:
            weights = [pltpu.with_memory_space_constraint(array, pltpu.HBM) for array in weights]
        return partial_sums(core, groups[group], *weights, side, start, size, dtype, after)

    def over_cores(keep, near):
        return (keep + near.astype(F32)).astype(BF16)

    pieces = [(0, 0, half)] + [(g, j * width, width) for g in (1, 2) for j in range(chunks)]
    near, keep, chip, far, act, act_near = {}, {}, {}, {}, {}, {}

    def send(n, after):
        out = sums(pieces[n], 1, after)
        near[n] = swap(out, "gy", 4, 1)
        return out

    def hold(n, after):
        keep[n] = sums(pieces[n], 0, after)
        chip[n] = over_cores(keep[n], near[n])
        far[n] = swap(chip[n], "gy", 4, 2)
        return chip[n]

    def ready(n, after):
        act[n] = activations(core, keep[n], near[n], far[n], after)
        act_near[n] = swap(act[n], "gy", 4, 1)
        return act[n]

    one, two = 1, 1 + chunks
    last = send(0, ())
    last = hold(0, [last])
    last = ready(0, [last])
    last = send(one, [last])
    for j in range(chunks):
        if j + 1 < chunks:
            last = send(one + j + 1, [last])
        last = hold(one + j, [last])
    stay0, = back(core, act[0], act_near[0], up, 0, None, rows, [last])
    last = send(two, [stay0])
    for j in range(chunks):
        if j + 1 < chunks:
            last = send(two + j + 1, [last])
        last = hold(two + j, [last])
    inputs_t, cotan = arrange(core, groups[0] + groups[1] + groups[2], [last])
    last = ready(one, [inputs_t])
    part = None
    for j in range(chunks):
        n = one + j
        if j + 1 < chunks:
            last = ready(n + 1, [last])
        out = back(
            core, act[n], act_near[n], up, j * width, part, rows if j + 1 == chunks else None, [last]
        )
        last = part = out[0]
    stay1, go1 = out
    near1 = swap(go1, "gx", 2, 1).astype(F32)
    total = stay0 + near1[:rows]
    far1 = swap((stay1 + near1[rows:]).astype(BF16), "gz", 4, 1)

    outputs, part, last = None, None, [stay1]
    shape = up.shape

    def gradients(j, sides, after):
        acts = [
            [(array[0], j * width), (array[one + j], 0), (array[two + j], 0)]
            for array in (act, act_near)
        ]
        acts = [acts[side] for side in sides]
        return weight_grads(
            core, inputs_t, cotan, sides, acts, j * width, width, shape, outputs, after
        )

    for j in range(chunks):
        n = two + j
        last = [ready(n, last)]
        final = j + 1 == chunks
        if final:
            *outputs, done = gradients(j, (0,), last)
            last = [done]
        out = back(
            core, act[n], act_near[n], up, j * width, part, 2 * rows if final else None, last
        )
        part = out[0]
        *outputs, done = gradients(j, (1,) if final else (0, 1), [part])
        last = [done]
    stay2, go2 = out
    stay2 = (stay2 + swap(go2, "gx", 2, 1).astype(F32)).astype(BF16)
    far2 = swap(stay2[:rows], "gz", 4, 2)
    far3 = swap(stay2[rows:], "gz", 4, 3)
    total = total + far1.astype(F32) + far2.astype(F32) + far3.astype(F32)
    return (total.astype(BF16), *outputs)


def solution(mesh):
    placed = (
        P(("gx", "gz"), "gy"),
        P(("gx", "gz"), "gy"),
        P("gy", ("gz", "gx")),
        P(("gz", "gx"), "gy"),
    )
    cube = tuple(mesh.shape[axis] for axis in ("gx", "gy", "gz")) == (2, 4, 4)
    return jax.shard_map(
        cube_body if cube else general_body,
        mesh=mesh,
        in_specs=placed,
        out_specs=(P(("gx", "gz"), "gy"), P("gy", ("gz", "gx")), P(("gz", "gx"), "gy")),
        check_vma=False,
    )
```

time: 719 us -> 175 us (0.24)
  waiting for transfers between devices: 561 us -> 74 us
  Pallas kernels: 0 us -> 71.4 us
  matrix products: 65.3 us -> 0 us
  blocking collectives: 34.9 us -> 0 us
  local copies, waits for them, and re-layouts: 26.1 us -> 0.06 us
  starting transfers between devices: 9.29 us -> 25.4 us
  between operations: 13.9 us -> 1.19 us
    all_gather x6 -> x0, waiting for transfers between devices: 454 us -> none  [the longest x1 210 us: body(): lax.all_gather(up_weight, 'gx', axis=1, tiled=True)]
    reduce_scatter x3 -> x0, waiting for transfers between devices: 100 us -> none  [the longest x1 46.6 us: body(): lax.psum_scatter(grad_hidden_part, 'gy', scatter_dimension=1, tiled=True)]
    ppermute x0 -> x33, waiting for transfers between devices: none -> 74 us  [swap(): return lax.ppermute(value, axis, [(i, i ^ bits) for i in range(size)])]
    pallas_call x0 -> x33, Pallas kernels: none -> 71.4 us  [call(): pl.pallas_call(kernel, grid_spec=pltpu.PrefetchScalarGridSpec(num_scalar_...]
    dot_general x5 -> x0, matrix products: 65.3 us -> none  [contract(): lax.dot_general(left, right, (((left_dim,), (right_dim,)), ((), ())), pre...]
    all_gather x2 -> x0, blocking collectives: 34.9 us -> none  [the longest x1 18.2 us: body(): lax.all_gather(inputs, 'gz', axis=0, tiled=True)]
    ppermute x0 -> x33, starting transfers between devices: none -> 25.4 us  [swap(): return lax.ppermute(value, axis, [(i, i ^ bits) for i in range(size)])]
    unnamed x11 -> x12, local copies, waits for them, and re-layouts: 19.7 us -> 0.04 us
  transfers between devices with their start and end apart: 11 -> 33, of which waited for: 10 -> 17; matrix products, arithmetic and copies ran while one was open for 13% -> 0% of each run, Pallas kernels for 0% -> 33%
where the time goes in v2:
time: 175 us
  waiting for transfers between devices  74 us (42%)
  Pallas kernels  71.4 us (41%)
  starting transfers between devices  25.4 us (15%)
  other arithmetic  2.62 us (1%)
    ppermute x33, waiting for transfers between devices, swap(): return lax.ppermute(value, axis, [(i, i ^ bits) for i in range(size)])  74 us
    pallas_call x33, Pallas kernels, call(): pl.pallas_call(kernel, grid_spec=pltpu.PrefetchScalarGridSpec(num_scalar_...  71.4 us
    ppermute x33, starting transfers between devices, swap(): return lax.ppermute(value, axis, [(i, i ^ bits) for i in range(size)])  25.4 us
  transfers between devices with their start and end apart: 33, of which 17 were waited for; matrix products, arithmetic and copies ran while one was open for 0% of the time, Pallas kernels for 33%

profile of v2, /device:TPU:0, one launch (start us, length us, event | category | flops | bytes accessed | tf_op | source)
XLA Modules:
  0.0 174.8 jit_solution(6031063732814699146)
XLA Ops:
  0.6 1.0 pad_maximum_fusion.refs_1_
  1.7 8.0 %sums_send.7.refs_4_ = bf16[2,48,1536]{2,1,0:T(8,128)(2,1)S(1)} custom-call(s32[1]{0:T(128)} %bitcast.refs_0_, bf16[2,48,1536]{2,1,0:T(8,128)(2,1)S(1)} %pad_maximum_fusion.refs_1_, bf16[1536,3072]{1,0:T(8,128)(2,1)} %refs_4_.25, bf16[3072,1536]{1,0:T(8,128)(2,1)} %refs_6_.11), custom_call_target="tpu_custom_call" | custom-call | flops 28311552 | bytes 589824 | tf_op jit(solution)/shard_map/sums_send/pallas_call | solution.py:67
  9.8 0.5 collective-permute-start
  10.3 2.6 %collective-permute-start.3 = (bf16[2,48,1536]{2,1,0:T(8,128)(2,1)S(1)}, bf16[2,48,1536]{2,1,0:T(8,128)(2,1)S(1)}, u32[]{:S(2)}, u32[]{:S(2)}) collective-permute-start(bf16[2,48,1536]{2,1,0:T(8,128)(2,1)S(1)} %pad_maximum_fusion.refs_1_), channel_id=1, source_target_pairs={{0,1},{1,0},{2,3},{3,2},{4,5},{5,4},{6,7},{7,6},{8,9},{9,8},{10,11... | collective-permute-start | bytes 884744 | tf_op jit(solution)/shard_map/ppermute | solution.py:295
  13.0 6.5 %sums_keep.7.refs_1_ = f32[2,48,1536]{2,1,0:T(8,128)S(1)} custom-call(s32[1]{0:T(128)} %bitcast.refs_0_, bf16[2,48,1536]{2,1,0:T(8,128)(2,1)S(1)} %pad_maximum_fusion.refs_1_, bf16[1536,3072]{1,0:T(8,128)(2,1)} %refs_4_.25, bf16[3072,1536]{1,0:T(8,128)(2,1)} %refs_6_.11, bf16[2,48,1536]{2,1,0:T(8,128)(2,1)S(1)} %sums_send.7.refs_4_), custom_call_target="tpu_custom_call" | custom-call | flops 28311552 | bytes 589824 | tf_op jit(solution)/shard_map/sums_keep/pallas_call | solution.py:67
  19.5 1.6 collective-permute-start.1
  21.1 1.5 collective-permute-start.4
  22.6 0.5 collective-permute-start.5
  23.1 5.5 %collective-permute-done.1.refs_3_ = bf16[2,48,1536]{2,1,0:T(8,128)(2,1)S(1)} collective-permute-done((bf16[2,48,1536]{2,1,0:T(8,128)(2,1)S(1)}, bf16[2,48,1536]{2,1,0:T(8,128)(2,1)S(1)}, u32[]{:S(2)}, u32[]{:S(2)}) %collective-permute-start.1) | collective-permute-done | bytes 294944 | tf_op jit(solution)/shard_map/ppermute | solution.py:295
  29.2 1.8 %collective-permute-done.4.refs_2_.refs_3_ = bf16[2,48,1536]{2,1,0:T(8,128)(2,1)S(1)} collective-permute-done((bf16[2,48,1536]{2,1,0:T(8,128)(2,1)S(1)}, bf16[2,48,1536]{2,1,0:T(8,128)(2,1)S(1)}, u32[]{:S(2)}, u32[]{:S(2)}) %collective-permute-start.4) | collective-permute-done | bytes 294944 | tf_op jit(solution)/shard_map/ppermute | solution.py:295
  31.0 5.2 %collective-permute-done.5.refs_3_.refs_4_ = bf16[2,48,1536]{2,1,0:T(8,128)(2,1)S(1)} collective-permute-done((bf16[2,48,1536]{2,1,0:T(8,128)(2,1)S(1)}, bf16[2,48,1536]{2,1,0:T(8,128)(2,1)S(1)}, u32[]{:S(2)}, u32[]{:S(2)}) %collective-permute-start.5) | collective-permute-done | bytes 294944 | tf_op jit(solution)/shard_map/ppermute | solution.py:295
  36.3 1.4 sums_send.8.refs_6_
  37.7 2.7 %collective-permute-start.11 = (bf16[2,48,1536]{2,1,0:T(8,128)(2,1)S(1)}, bf16[2,48,1536]{2,1,0:T(8,128)(2,1)S(1)}, u32[]{:S(2)}, u32[]{:S(2)}) collective-permute-start(bf16[2,48,1536]{2,1,0:T(8,128)(2,1)S(1)} %pad_maximum_fusion.refs_1_), channel_id=1, source_target_pairs={{0,2},{1,3},{2,0},{3,1},{4,6},{5,7},{6,4},{7,5},{8,10},{9,11},{10,... | collective-permute-start | bytes 884744 | tf_op jit(solution)/shard_map/ppermute | solution.py:295
  40.6 1.4 sums_send.9.refs_6_
  42.1 1.4 sums_keep.8.refs_1_
  43.6 1.4 sums_send.10.refs_6_
  45.0 0.5 collective-permute-start.8
  45.5 15.1 %collective-permute-done.11.refs_1_.refs_5_ = bf16[2,48,1536]{2,1,0:T(8,128)(2,1)S(1)} collective-permute-done((bf16[2,48,1536]{2,1,0:T(8,128)(2,1)S(1)}, bf16[2,48,1536]{2,1,0:T(8,128)(2,1)S(1)}, u32[]{:S(2)}, u32[]{:S(2)}) %collective-permute-start.11) | collective-permute-done | bytes 294944 | tf_op jit(solution)/shard_map/ppermute | solution.py:295
  60.6 1.5 collective-permute-start.13
  62.1 0.5 collective-permute-start.14
  62.7 1.4 sums_keep.9.refs_1_
  64.2 1.4 sums_keep.10.refs_1_
  65.7 3.9 %back.7.refs_7_ = f32[48,1536]{1,0:T(8,128)S(1)} custom-call(s32[1]{0:T(128)} %bitcast.refs_0_, bf16[2,48,1536]{2,1,0:T(8,128)(2,1)S(1)} %activations.7.refs_6_.refs_1_.refs_3_, bf16[2,48,1536]{2,1,0:T(8,128)(2,1)S(1)} %collective-permute-done.2.refs_2_.refs_6_.refs_3_, bf16[1536,3072]{1,0:T(8,128)(2,1)S(1)} %bitcast.4, bf16[1536,3072]{1,0:T(8,128)(2,1)S(1)} %bitcast.4, ...), custom_call_target="tpu_custom_call" | custom-call | flops 28311552 | bytes 608256 | tf_op jit(solution)/shard_map/back/pallas_call | solution.py:67
  69.5 1.0 collective-permute-done.13.refs_3_.refs_7_
  70.5 5.4 %collective-permute-done.14.refs_4_.refs_8_ = bf16[2,48,1536]{2,1,0:T(8,128)(2,1)S(1)} collective-permute-done((bf16[2,48,1536]{2,1,0:T(8,128)(2,1)S(1)}, bf16[2,48,1536]{2,1,0:T(8,128)(2,1)S(1)}, u32[]{:S(2)}, u32[]{:S(2)}) %collective-permute-start.14) | collective-permute-done | bytes 294944 | tf_op jit(solution)/shard_map/ppermute | solution.py:295
  75.9 1.5 sums_send.11.refs_7_
  77.4 1.5 sums_send.12.refs_7_
  78.9 0.5 collective-permute-start.16
  79.5 1.5 sums_keep.11.refs_1_
  81.1 1.5 sums_send.13.refs_7_
  83.2 1.6 collective-permute-start.19
  84.7 1.5 sums_keep.12.refs_1_
  86.4 1.5 sums_keep.13.refs_1_
  88.4 4.1 %collective-permute-done.10.refs_3_ = bf16[2,144,512]{2,1,0:T(8,128)(2,1)S(1)} collective-permute-done((bf16[2,144,512]{2,1,0:T(8,128)(2,1)S(1)}, bf16[2,144,512]{2,1,0:T(8,128)(2,1)S(1)}, u32[]{:S(2)}, u32[]{:S(2)}) %collective-permute-start.10) | collective-permute-done | bytes 294944 | tf_op jit(solution)/shard_map/ppermute | solution.py:295
  93.0 0.5 collective-permute-start.9
  93.5 1.6 collective-permute-start.26
  95.1 3.8 %collective-permute-done.19.refs_3_ = bf16[2,144,512]{2,1,0:T(8,128)(2,1)S(1)} collective-permute-done((bf16[2,144,512]{2,1,0:T(8,128)(2,1)S(1)}, bf16[2,144,512]{2,1,0:T(8,128)(2,1)S(1)}, u32[]{:S(2)}, u32[]{:S(2)}) %collective-permute-start.19) | collective-permute-done | bytes 294944 | tf_op jit(solution)/shard_map/ppermute | solution.py:295
  99.3 1.8 %back.8.refs_4_.refs_5_ = f32[144,1536]{1,0:T(8,128)S(1)} custom-call(s32[1]{0:T(128)} %bitcast.refs_0_, bf16[2,144,512]{2,1,0:T(8,128)(2,1)S(1)} %activations.8.refs_4_.refs_1_, bf16[2,144,512]{2,1,0:T(8,128)(2,1)S(1)} %collective-permute-done.18.refs_2_.refs_7_, bf16[1536,3072]{1,0:T(8,128)(2,1)S(1)} %bitcast.4, bf16[1536,3072]{1,0:T(8,128)(2,1)S(1)} %bitcast.4, ...), custom_call_target="tpu_custom_call" | custom-call | flops 28311552 | bytes 251904 | tf_op jit(solution)/shard_map/back/pallas_call | solution.py:67
  101.1 4.0 %collective-permute-done.9.refs_3_ = bf16[2,144,512]{2,1,0:T(8,128)(2,1)S(1)} collective-permute-done((bf16[2,144,512]{2,1,0:T(8,128)(2,1)S(1)}, bf16[2,144,512]{2,1,0:T(8,128)(2,1)S(1)}, u32[]{:S(2)}, u32[]{:S(2)}) %collective-permute-start.9) | collective-permute-done | bytes 294944 | tf_op jit(solution)/shard_map/ppermute | solution.py:295
  105.2 0.6 activations.10.refs_6_.refs_1_.refs_4_
  105.8 1.9 %back.9.refs_5_.refs_6_ = f32[144,1536]{1,0:T(8,128)S(1)} custom-call(s32[1]{0:T(128)} %bitcast.refs_0_, bf16[2,144,512]{2,1,0:T(8,128)(2,1)S(1)} %activations.9.refs_5_.refs_1_.refs_4_, bf16[2,144,512]{2,1,0:T(8,128)(2,1)S(1)} %collective-permute-done.21.refs_2_.refs_7_, bf16[1536,3072]{1,0:T(8,128)(2,1)S(1)} %bitcast.4, bf16[1536,3072]{1,0:T(8,128)(2,1)S(1)} %bitcast.4, ...), custom_call_target="tpu_custom_call" | custom-call | flops 28311552 | bytes 251904 | tf_op jit(solution)/shard_map/back/pallas_call | solution.py:67
  107.7 1.9 %back.10 = (f32[48,1536]{1,0:T(8,128)S(1)}, bf16[96,1536]{1,0:T(8,128)(2,1)S(1)}) custom-call(s32[1]{0:T(128)} %bitcast.refs_0_, bf16[2,144,512]{2,1,0:T(8,128)(2,1)S(1)} %activations.10.refs_6_.refs_1_.refs_4_, bf16[2,144,512]{2,1,0:T(8,128)(2,1)S(1)} %collective-permute-done.20.refs_2_.refs_4_, bf16[1536,3072]{1,0:T(8,128)(2,1)S(1)} %bitcast.4, ...), custom_call_target="tpu_custom_call" | custom-call | flops 28311552 | bytes 251904 | tf_op jit(solution)/shard_map/back/pallas_call | solution.py:67
  109.6 3.5 %collective-permute-done.26.refs_3_ = bf16[2,192,512]{2,1,0:T(8,128)(2,1)S(1)} collective-permute-done((bf16[2,192,512]{2,1,0:T(8,128)(2,1)S(1)}, bf16[2,192,512]{2,1,0:T(8,128)(2,1)S(1)}, u32[]{:S(2)}, u32[]{:S(2)}) %collective-permute-start.26) | collective-permute-done | bytes 393248 | tf_op jit(solution)/shard_map/ppermute | solution.py:295
  113.7 0.5 collective-permute-start.25
  114.2 1.2 collective-permute-done.27.refs_2_.refs_8_
  115.4 1.8 %back.11.refs_9_.refs_5_ = f32[192,1536]{1,0:T(8,128)S(1)} custom-call(s32[1]{0:T(128)} %bitcast.refs_0_, bf16[2,192,512]{2,1,0:T(8,128)(2,1)S(1)} %activations.11.refs_1_.refs_5_, bf16[2,192,512]{2,1,0:T(8,128)(2,1)S(1)} %collective-permute-done.27.refs_2_.refs_8_, bf16[1536,3072]{1,0:T(8,128)(2,1)S(1)} %bitcast.4, bf16[1536,3072]{1,0:T(8,128)(2,1)S(1)} %bitcast.4, ...), custom_call_target="tpu_custom_call" | custom-call | flops 37748736 | bytes 270336 | tf_op jit(solution)/shard_map/back/pallas_call | solution.py:67
  117.3 6.6 %weight_grads.4 = (f32[1536,3072]{1,0:T(8,128)}, f32[3072,1536]{1,0:T(8,128)}, f32[8,128]{1,0:T(8,128)S(1)}) custom-call(s32[1]{0:T(128)} %bitcast.refs_0_, bf16[1536,384]{1,0:T(8,128)(2,1)S(1)} %get-tuple-element.20.refs_4_.refs_1_, bf16[384,1536]{1,0:T(8,128)(2,1)S(1)} %get-tuple-element.23.refs_2_, ...), custom_call_target="tpu_custom_call" | custom-call | flops 150994944 | bytes 786432 | tf_op jit(solution)/shard_map/weight_grads/pallas_call | solution.py:67
  123.9 1.3 collective-permute-done.25.refs_3_
  126.3 1.2 collective-permute-done.28.refs_2_.refs_8_
  127.5 1.9 %back.12.refs_11_.refs_5_ = f32[192,1536]{1,0:T(8,128)S(1)} custom-call(s32[1]{0:T(128)} %bitcast.refs_0_, bf16[2,192,512]{2,1,0:T(8,128)(2,1)S(1)} %activations.12.refs_1_.refs_6_.refs_5_, bf16[2,192,512]{2,1,0:T(8,128)(2,1)S(1)} %collective-permute-done.28.refs_2_.refs_8_, bf16[1536,3072]{1,0:T(8,128)(2,1)S(1)} %bitcast.4, bf16[1536,3072]{1,0:T(8,128)(2,1)S(1)} %bitcast.4, ...), custom_call_target="tpu_custom_call" | custom-call | flops 37748736 | bytes 270336 | tf_op jit(solution)/shard_map/back/pallas_call | solution.py:67
  129.4 6.7 %weight_grads.5 = (f32[1536,3072]{1,0:T(8,128)}, f32[3072,1536]{1,0:T(8,128)}, f32[8,128]{1,0:T(8,128)S(1)}) custom-call(s32[1]{0:T(128)} %bitcast.refs_0_, bf16[1536,384]{1,0:T(8,128)(2,1)S(1)} %get-tuple-element.20.refs_4_.refs_1_, bf16[384,1536]{1,0:T(8,128)(2,1)S(1)} %get-tuple-element.23.refs_2_, ...), custom_call_target="tpu_custom_call", output_to_operand_aliasing={{0}: (9, {}), {1}: (10, {})} | custom-call | flops 150994944 | bytes 786432 | tf_op jit(solution)/shard_map/weight_grads/pallas_call | solution.py:67
  136.1 1.2 collective-permute-done.24.refs_3_
  137.9 1.6 collective-permute-start.22
  139.4 7.9 %collective-permute-done.22 = bf16[96,1536]{1,0:T(8,128)(2,1)S(1)} collective-permute-done((bf16[96,1536]{1,0:T(8,128)(2,1)S(1)}, bf16[96,1536]{1,0:T(8,128)(2,1)S(1)}, u32[]{:S(2)}, u32[]{:S(2)}) %collective-permute-start.22) | collective-permute-done | bytes 294944 | tf_op jit(solution)/shard_map/ppermute | solution.py:295
  147.4 3.9 %weight_grads.6 = (f32[1536,3072]{1,0:T(8,128)}, f32[3072,1536]{1,0:T(8,128)}, f32[8,128]{1,0:T(8,128)S(1)}) custom-call(s32[1]{0:T(128)} %bitcast.refs_0_, bf16[1536,384]{1,0:T(8,128)(2,1)S(1)} %get-tuple-element.20.refs_4_.refs_1_, bf16[384,1536]{1,0:T(8,128)(2,1)S(1)} %get-tuple-element.23.refs_2_, ...), custom_call_target="tpu_custom_call", output_to_operand_aliasing={{0}: (6, {}), {1}: (7, {})} | custom-call | flops 75497472 | bytes 393216 | tf_op jit(solution)/shard_map/weight_grads/pallas_call | solution.py:67
  151.2 1.9 %back.13 = (f32[96,1536]{1,0:T(8,128)S(1)}, bf16[96,1536]{1,0:T(8,128)(2,1)S(1)}) custom-call(s32[1]{0:T(128)} %bitcast.refs_0_, bf16[2,192,512]{2,1,0:T(8,128)(2,1)S(1)} %activations.13.refs_5_.refs_8_.refs_1_, bf16[2,192,512]{2,1,0:T(8,128)(2,1)S(1)} %collective-permute-done.29.refs_2_.refs_5_, bf16[1536,3072]{1,0:T(8,128)(2,1)S(1)} %bitcast.4, ...), custom_call_target="tpu_custom_call" | custom-call | flops 37748736 | bytes 270336 | tf_op jit(solution)/shard_map/back/pallas_call | solution.py:67
  153.2 1.6 collective-permute-start.30
  154.8 0.6 collective-permute-start.23
  155.4 6.4 %collective-permute-done.30 = bf16[96,1536]{1,0:T(8,128)(2,1)S(1)} collective-permute-done((bf16[96,1536]{1,0:T(8,128)(2,1)S(1)}, bf16[96,1536]{1,0:T(8,128)(2,1)S(1)}, u32[]{:S(2)}, u32[]{:S(2)}) %collective-permute-start.30) | collective-permute-done | bytes 294944 | tf_op jit(solution)/shard_map/ppermute | solution.py:295
  161.9 1.3 collective-permute-start.31
  163.2 1.6 collective-permute-start.32
  164.9 3.8 %weight_grads.7 = (f32[1536,3072]{1,0:T(8,128)}, f32[3072,1536]{1,0:T(8,128)}, f32[8,128]{1,0:T(8,128)}) custom-call(s32[1]{0:T(128)} %bitcast.refs_0_, bf16[1536,384]{1,0:T(8,128)(2,1)S(1)} %get-tuple-element.20.refs_4_.refs_1_, bf16[384,1536]{1,0:T(8,128)(2,1)S(1)} %get-tuple-element.23.refs_2_, ...), custom_call_target="tpu_custom_call", output_to_operand_aliasing={{0}: (6, {}), {1}: (7, {})} | custom-call | flops 75497472 | bytes 393216 | tf_op jit(solution)/shard_map/weight_grads/pallas_call | solution.py:67
  168.7 5.3 %collective-permute-done.31 = bf16[48,1536]{1,0:T(8,128)(2,1)S(1)} collective-permute-done((bf16[48,1536]{1,0:T(8,128)(2,1)S(1)}, bf16[48,1536]{1,0:T(8,128)(2,1)S(1)}, u32[]{:S(2)}, u32[]{:S(2)}) %collective-permute-start.31) | collective-permute-done | bytes 147488 | tf_op jit(solution)/shard_map/ppermute | solution.py:295
  174.0 0.8 fusion.4
  (62 shorter events, 6.0 us)
Async XLA Ops:
  1.7 34.6 %slice-start = ((s8[9437184]{0:T(1024)(128)(4,1)}), s8[4194304]{0:T(1024)(128)(4,1)S(1)}, s32[]{:S(2)}) async-start(s8[9437184]{0:T(1024)(128)(4,1)} %bitcast.3), calls=%async_computation | async-start | bytes 8388608
  1.7 34.5 %slice-start.1 = ((s8[9437184]{0:T(1024)(128)(4,1)}), s8[4194304]{0:T(1024)(128)(4,1)S(1)}, s32[]{:S(2)}) async-start(s8[9437184]{0:T(1024)(128)(4,1)} %bitcast.3), calls=%async_computation.1 | async-start | bytes 8388608
  1.7 34.5 %slice-start.3 = ((s8[9437184]{0:T(1024)(128)(4,1)}), s8[4194304]{0:T(1024)(128)(4,1)S(1)}, s32[]{:S(2)}) async-start(s8[9437184]{0:T(1024)(128)(4,1)} %bitcast.5), calls=%async_computation.3 | async-start | bytes 8388608
  1.7 34.5 %slice-start.4 = ((s8[9437184]{0:T(1024)(128)(4,1)}), s8[4194304]{0:T(1024)(128)(4,1)S(1)}, s32[]{:S(2)}) async-start(s8[9437184]{0:T(1024)(128)(4,1)} %bitcast.5), calls=%async_computation.4 | async-start | bytes 8388608
  9.8 26.5 %slice-start.2 = ((s8[9437184]{0:T(1024)(128)(4,1)}), s8[1048576]{0:T(1024)(128)(4,1)S(1)}, s32[]{:S(2)}) async-start(s8[9437184]{0:T(1024)(128)(4,1)} %bitcast.3), calls=%async_computation.2 | async-start | bytes 2097152
  9.8 26.5 %slice-start.5 = ((s8[9437184]{0:T(1024)(128)(4,1)}), s8[1048576]{0:T(1024)(128)(4,1)S(1)}, s32[]{:S(2)}) async-start(s8[9437184]{0:T(1024)(128)(4,1)} %bitcast.5), calls=%async_computation.5 | async-start | bytes 2097152
  9.8 9.6 %collective-permute-start = (bf16[2,48,1536]{2,1,0:T(8,128)(2,1)S(1)}, bf16[2,48,1536]{2,1,0:T(8,128)(2,1)S(1)}, u32[]{:S(2)}, u32[]{:S(2)}) collective-permute-start(bf16[2,48,1536]{2,1,0:T(8,128)(2,1)S(1)} %sums_send.7.refs_4_), channel_id=1, source_target_pairs={{0,4},{4,0},{8,12},{12,8},{1,5},{5,1},{9,13},{13,9},{2,6},{6,2},{1... | collective-permute-start | bytes 884744 | tf_op jit(solution)/shard_map/ppermute | solution.py:295
  10.3 12.3 %collective-permute-start.3 = (bf16[2,48,1536]{2,1,0:T(8,128)(2,1)S(1)}, bf16[2,48,1536]{2,1,0:T(8,128)(2,1)S(1)}, u32[]{:S(2)}, u32[]{:S(2)}) collective-permute-start(bf16[2,48,1536]{2,1,0:T(8,128)(2,1)S(1)} %pad_maximum_fusion.refs_1_), channel_id=1, source_target_pairs={{0,1},{1,0},{2,3},{3,2},{4,5},{5,4},{6,7},{7,6},{8,9},{9,8},{10,11... | collective-permute-start | bytes 884744 | tf_op jit(solution)/shard_map/ppermute | solution.py:295
  19.5 9.1 %collective-permute-start.1 = (bf16[2,48,1536]{2,1,0:T(8,128)(2,1)S(1)}, bf16[2,48,1536]{2,1,0:T(8,128)(2,1)S(1)}, u32[]{:S(2)}, u32[]{:S(2)}) collective-permute-start(bf16[2,48,1536]{2,1,0:T(8,128)(2,1)S(1)} %add_convert_fusion.7.refs_4_), channel_id=1, source_target_pairs={{0,8},{4,12},{8,0},{12,4},{1,9},{5,13},{9,1},{13,5},{2,10},{6,14},... | collective-permute-start | bytes 884744 | tf_op jit(solution)/shard_map/ppermute | solution.py:295
  21.1 9.9 %collective-permute-start.4 = (bf16[2,48,1536]{2,1,0:T(8,128)(2,1)S(1)}, bf16[2,48,1536]{2,1,0:T(8,128)(2,1)S(1)}, u32[]{:S(2)}, u32[]{:S(2)}) collective-permute-start(bf16[2,48,1536]{2,1,0:T(8,128)(2,1)S(1)} %pad_maximum_fusion.refs_1_), channel_id=1, source_target_pairs={{0,16},{16,0},{1,17},{17,1},{2,18},{18,2},{3,19},{19,3},{4,20},{20... | collective-permute-start | bytes 884744 | tf_op jit(solution)/shard_map/ppermute | solution.py:295
  22.6 13.6 %collective-permute-start.5 = (bf16[2,48,1536]{2,1,0:T(8,128)(2,1)S(1)}, bf16[2,48,1536]{2,1,0:T(8,128)(2,1)S(1)}, u32[]{:S(2)}, u32[]{:S(2)}) collective-permute-start(bf16[2,48,1536]{2,1,0:T(8,128)(2,1)S(1)} %collective-permute-done.3.refs_1_.refs_2_), channel_id=1, source_target_pairs={{0,16},{16,0},{1,17},{17,1},{2,18},{18,2},{3,19},{19,3},{4,20},{20... | collective-permute-start | bytes 884744 | tf_op jit(solution)/shard_map/ppermute | solution.py:295
  37.7 5.8 %collective-permute-start.6 = (bf16[2,144,512]{2,1,0:T(8,128)(2,1)S(1)}, bf16[2,144,512]{2,1,0:T(8,128)(2,1)S(1)}, u32[]{:S(2)}, u32[]{:S(2)}) collective-permute-start(bf16[2,144,512]{2,1,0:T(8,128)(2,1)S(1)} %sums_send.8.refs_6_), channel_id=1, source_target_pairs={{0,4},{4,0},{8,12},{12,8},{1,5},{5,1},{9,13},{13,9},{2,6},{6,2},{1... | collective-permute-start | bytes 884744 | tf_op jit(solution)/shard_map/ppermute | solution.py:295
  37.7 22.9 %collective-permute-start.11 = (bf16[2,48,1536]{2,1,0:T(8,128)(2,1)S(1)}, bf16[2,48,1536]{2,1,0:T(8,128)(2,1)S(1)}, u32[]{:S(2)}, u32[]{:S(2)}) collective-permute-start(bf16[2,48,1536]{2,1,0:T(8,128)(2,1)S(1)} %pad_maximum_fusion.refs_1_), channel_id=1, source_target_pairs={{0,2},{1,3},{2,0},{3,1},{4,6},{5,7},{6,4},{7,5},{8,10},{9,11},{10,... | collective-permute-start | bytes 884744 | tf_op jit(solution)/shard_map/ppermute | solution.py:295
  40.4 21.7 %collective-permute-start.12 = (bf16[2,48,1536]{2,1,0:T(8,128)(2,1)S(1)}, bf16[2,48,1536]{2,1,0:T(8,128)(2,1)S(1)}, u32[]{:S(2)}, u32[]{:S(2)}) collective-permute-start(bf16[2,48,1536]{2,1,0:T(8,128)(2,1)S(1)} %pad_maximum_fusion.refs_1_), channel_id=1, source_target_pairs={{0,3},{1,2},{2,1},{3,0},{4,7},{5,6},{6,5},{7,4},{8,11},{9,10},{10,... | collective-permute-start | bytes 884744 | tf_op jit(solution)/shard_map/ppermute | solution.py:295
  42.0 22.1 %collective-permute-start.7 = (bf16[2,144,512]{2,1,0:T(8,128)(2,1)S(1)}, bf16[2,144,512]{2,1,0:T(8,128)(2,1)S(1)}, u32[]{:S(2)}, u32[]{:S(2)}) collective-permute-start(bf16[2,144,512]{2,1,0:T(8,128)(2,1)S(1)} %sums_send.9.refs_6_), channel_id=1, source_target_pairs={{0,4},{4,0},{8,12},{12,8},{1,5},{5,1},{9,13},{13,9},{2,6},{6,2},{1... | collective-permute-start | bytes 884744 | tf_op jit(solution)/shard_map/ppermute | solution.py:295
  45.0 20.6 %collective-permute-start.8 = (bf16[2,144,512]{2,1,0:T(8,128)(2,1)S(1)}, bf16[2,144,512]{2,1,0:T(8,128)(2,1)S(1)}, u32[]{:S(2)}, u32[]{:S(2)}) collective-permute-start(bf16[2,144,512]{2,1,0:T(8,128)(2,1)S(1)} %sums_send.10.refs_6_), channel_id=1, source_target_pairs={{0,4},{4,0},{8,12},{12,8},{1,5},{5,1},{9,13},{13,9},{2,6},{6,2},{1... | collective-permute-start | bytes 884744 | tf_op jit(solution)/shard_map/ppermute | solution.py:295
  60.6 9.9 %collective-permute-start.13 = (bf16[2,48,1536]{2,1,0:T(8,128)(2,1)S(1)}, bf16[2,48,1536]{2,1,0:T(8,128)(2,1)S(1)}, u32[]{:S(2)}, u32[]{:S(2)}) collective-permute-start(bf16[2,48,1536]{2,1,0:T(8,128)(2,1)S(1)} %collective-permute-done.11.refs_1_.refs_5_), channel_id=1, source_target_pairs={{0,16},{16,0},{1,17},{17,1},{2,18},{18,2},{3,19},{19,3},{4,20},{20... | collective-permute-start | bytes 884744 | tf_op jit(solution)/shard_map/ppermute | solution.py:295
  62.1 13.8 %collective-permute-start.14 = (bf16[2,48,1536]{2,1,0:T(8,128)(2,1)S(1)}, bf16[2,48,1536]{2,1,0:T(8,128)(2,1)S(1)}, u32[]{:S(2)}, u32[]{:S(2)}) collective-permute-start(bf16[2,48,1536]{2,1,0:T(8,128)(2,1)S(1)} %collective-permute-done.12.refs_2_.refs_6_), channel_id=1, source_target_pairs={{0,16},{16,0},{1,17},{17,1},{2,18},{18,2},{3,19},{19,3},{4,20},{20... | collective-permute-start | bytes 884744 | tf_op jit(solution)/shard_map/ppermute | solution.py:295
  62.7 3.0 %collective-permute-start.2 = (bf16[2,48,1536]{2,1,0:T(8,128)(2,1)S(1)}, bf16[2,48,1536]{2,1,0:T(8,128)(2,1)S(1)}, u32[]{:S(2)}, u32[]{:S(2)}) collective-permute-start(bf16[2,48,1536]{2,1,0:T(8,128)(2,1)S(1)} %activations.7.refs_6_.refs_1_.refs_3_), channel_id=1, source_target_pairs={{0,4},{4,0},{8,12},{12,8},{1,5},{5,1},{9,13},{13,9},{2,6},{6,2},{1... | collective-permute-start | bytes 884744 | tf_op jit(solution)/shard_map/ppermute | solution.py:295
  77.4 3.6 %collective-permute-start.15 = (bf16[2,192,512]{2,1,0:T(8,128)(2,1)S(1)}, bf16[2,192,512]{2,1,0:T(8,128)(2,1)S(1)}, u32[]{:S(2)}, u32[]{:S(2)}) collective-permute-start(bf16[2,192,512]{2,1,0:T(8,128)(2,1)S(1)} %sums_send.11.refs_7_), channel_id=1, source_target_pairs={{0,4},{4,0},{8,12},{12,8},{1,5},{5,1},{9,13},{13,9},{2,6},{6,2},{1... | collective-permute-start | bytes 1179656 | tf_op jit(solution)/shard_map/ppermute | solution.py:295
  78.9 7.3 %collective-permute-start.16 = (bf16[2,192,512]{2,1,0:T(8,128)(2,1)S(1)}, bf16[2,192,512]{2,1,0:T(8,128)(2,1)S(1)}, u32[]{:S(2)}, u32[]{:S(2)}) collective-permute-start(bf16[2,192,512]{2,1,0:T(8,128)(2,1)S(1)} %sums_send.12.refs_7_), channel_id=1, source_target_pairs={{0,4},{4,0},{8,12},{12,8},{1,5},{5,1},{9,13},{13,9},{2,6},{6,2},{1... | collective-permute-start | bytes 1179656 | tf_op jit(solution)/shard_map/ppermute | solution.py:295
  82.6 5.3 %collective-permute-start.17 = (bf16[2,192,512]{2,1,0:T(8,128)(2,1)S(1)}, bf16[2,192,512]{2,1,0:T(8,128)(2,1)S(1)}, u32[]{:S(2)}, u32[]{:S(2)}) collective-permute-start(bf16[2,192,512]{2,1,0:T(8,128)(2,1)S(1)} %sums_send.13.refs_7_), channel_id=1, source_target_pairs={{0,4},{4,0},{8,12},{12,8},{1,5},{5,1},{9,13},{13,9},{2,6},{6,2},{1... | collective-permute-start | bytes 1179656 | tf_op jit(solution)/shard_map/ppermute | solution.py:295
  82.7 9.8 %collective-permute-start.10 = (bf16[2,144,512]{2,1,0:T(8,128)(2,1)S(1)}, bf16[2,144,512]{2,1,0:T(8,128)(2,1)S(1)}, u32[]{:S(2)}, u32[]{:S(2)}) collective-permute-start(bf16[2,144,512]{2,1,0:T(8,128)(2,1)S(1)} %add_convert_fusion.6.refs_6_), channel_id=1, source_target_pairs={{0,8},{4,12},{8,0},{12,4},{1,9},{5,13},{9,1},{13,5},{2,10},{6,14},... | collective-permute-start | bytes 884744 | tf_op jit(solution)/shard_map/ppermute | solution.py:295
  83.2 15.7 %collective-permute-start.19 = (bf16[2,144,512]{2,1,0:T(8,128)(2,1)S(1)}, bf16[2,144,512]{2,1,0:T(8,128)(2,1)S(1)}, u32[]{:S(2)}, u32[]{:S(2)}) collective-permute-start(bf16[2,144,512]{2,1,0:T(8,128)(2,1)S(1)} %add_convert_fusion.5.refs_6_), channel_id=1, source_target_pairs={{0,8},{4,12},{8,0},{12,4},{1,9},{5,13},{9,1},{13,5},{2,10},{6,14},... | collective-permute-start | bytes 884744 | tf_op jit(solution)/shard_map/ppermute | solution.py:295
  92.9 6.4 %collective-permute-start.18 = (bf16[2,144,512]{2,1,0:T(8,128)(2,1)S(1)}, bf16[2,144,512]{2,1,0:T(8,128)(2,1)S(1)}, u32[]{:S(2)}, u32[]{:S(2)}) collective-permute-start(bf16[2,144,512]{2,1,0:T(8,128)(2,1)S(1)} %activations.8.refs_4_.refs_1_), channel_id=1, source_target_pairs={{0,4},{4,0},{8,12},{12,8},{1,5},{5,1},{9,13},{13,9},{2,6},{6,2},{1... | collective-permute-start | bytes 884744 | tf_op jit(solution)/shard_map/ppermute | solution.py:295
  93.0 12.2 %collective-permute-start.9 = (bf16[2,144,512]{2,1,0:T(8,128)(2,1)S(1)}, bf16[2,144,512]{2,1,0:T(8,128)(2,1)S(1)}, u32[]{:S(2)}, u32[]{:S(2)}) collective-permute-start(bf16[2,144,512]{2,1,0:T(8,128)(2,1)S(1)} %add_convert_fusion.4.refs_5_), channel_id=1, source_target_pairs={{0,8},{4,12},{8,0},{12,4},{1,9},{5,13},{9,1},{13,5},{2,10},{6,14},... | collective-permute-start | bytes 884744 | tf_op jit(solution)/shard_map/ppermute | solution.py:295
  93.5 19.7 %collective-permute-start.26 = (bf16[2,192,512]{2,1,0:T(8,128)(2,1)S(1)}, bf16[2,192,512]{2,1,0:T(8,128)(2,1)S(1)}, u32[]{:S(2)}, u32[]{:S(2)}) collective-permute-start(bf16[2,192,512]{2,1,0:T(8,128)(2,1)S(1)} %add_convert_fusion.2.refs_7_), channel_id=1, source_target_pairs={{0,8},{4,12},{8,0},{12,4},{1,9},{5,13},{9,1},{13,5},{2,10},{6,14},... | collective-permute-start | bytes 1179656 | tf_op jit(solution)/shard_map/ppermute | solution.py:295
  99.2 6.6 %collective-permute-start.21 = (bf16[2,144,512]{2,1,0:T(8,128)(2,1)S(1)}, bf16[2,144,512]{2,1,0:T(8,128)(2,1)S(1)}, u32[]{:S(2)}, u32[]{:S(2)}) collective-permute-start(bf16[2,144,512]{2,1,0:T(8,128)(2,1)S(1)} %activations.9.refs_5_.refs_1_.refs_4_), channel_id=1, source_target_pairs={{0,4},{4,0},{8,12},{12,8},{1,5},{5,1},{9,13},{13,9},{2,6},{6,2},{1... | collective-permute-start | bytes 884744 | tf_op jit(solution)/shard_map/ppermute | solution.py:295
  105.7 2.0 %collective-permute-start.20 = (bf16[2,144,512]{2,1,0:T(8,128)(2,1)S(1)}, bf16[2,144,512]{2,1,0:T(8,128)(2,1)S(1)}, u32[]{:S(2)}, u32[]{:S(2)}) collective-permute-start(bf16[2,144,512]{2,1,0:T(8,128)(2,1)S(1)} %activations.10.refs_6_.refs_1_.refs_4_), channel_id=1, source_target_pairs={{0,4},{4,0},{8,12},{12,8},{1,5},{5,1},{9,13},{13,9},{2,6},{6,2},{1... | collective-permute-start | bytes 884744 | tf_op jit(solution)/shard_map/ppermute | solution.py:295
  113.6 1.8 %collective-permute-start.27 = (bf16[2,192,512]{2,1,0:T(8,128)(2,1)S(1)}, bf16[2,192,512]{2,1,0:T(8,128)(2,1)S(1)}, u32[]{:S(2)}, u32[]{:S(2)}) collective-permute-start(bf16[2,192,512]{2,1,0:T(8,128)(2,1)S(1)} %activations.11.refs_1_.refs_5_), channel_id=1, source_target_pairs={{0,4},{4,0},{8,12},{12,8},{1,5},{5,1},{9,13},{13,9},{2,6},{6,2},{1... | collective-permute-start | bytes 1179656 | tf_op jit(solution)/shard_map/ppermute | solution.py:295
  113.7 11.5 %collective-permute-start.25 = (bf16[2,192,512]{2,1,0:T(8,128)(2,1)S(1)}, bf16[2,192,512]{2,1,0:T(8,128)(2,1)S(1)}, u32[]{:S(2)}, u32[]{:S(2)}) collective-permute-start(bf16[2,192,512]{2,1,0:T(8,128)(2,1)S(1)} %add_convert_fusion.1.refs_7_), channel_id=1, source_target_pairs={{0,8},{4,12},{8,0},{12,4},{1,9},{5,13},{9,1},{13,5},{2,10},{6,14},... | collective-permute-start | bytes 1179656 | tf_op jit(solution)/shard_map/ppermute | solution.py:295
  125.7 1.8 %collective-permute-start.28 = (bf16[2,192,512]{2,1,0:T(8,128)(2,1)S(1)}, bf16[2,192,512]{2,1,0:T(8,128)(2,1)S(1)}, u32[]{:S(2)}, u32[]{:S(2)}) collective-permute-start(bf16[2,192,512]{2,1,0:T(8,128)(2,1)S(1)} %activations.12.refs_1_.refs_6_.refs_5_), channel_id=1, source_target_pairs={{0,4},{4,0},{8,12},{12,8},{1,5},{5,1},{9,13},{13,9},{2,6},{6,2},{1... | collective-permute-start | bytes 1179656 | tf_op jit(solution)/shard_map/ppermute | solution.py:295
  125.8 11.5 %collective-permute-start.24 = (bf16[2,192,512]{2,1,0:T(8,128)(2,1)S(1)}, bf16[2,192,512]{2,1,0:T(8,128)(2,1)S(1)}, u32[]{:S(2)}, u32[]{:S(2)}) collective-permute-start(bf16[2,192,512]{2,1,0:T(8,128)(2,1)S(1)} %add_convert_fusion.refs_9_), channel_id=1, source_target_pairs={{0,8},{4,12},{8,0},{12,4},{1,9},{5,13},{9,1},{13,5},{2,10},{6,14},... | collective-permute-start | bytes 1179656 | tf_op jit(solution)/shard_map/ppermute | solution.py:295
  137.8 13.4 %collective-permute-start.29 = (bf16[2,192,512]{2,1,0:T(8,128)(2,1)S(1)}, bf16[2,192,512]{2,1,0:T(8,128)(2,1)S(1)}, u32[]{:S(2)}, u32[]{:S(2)}) collective-permute-start(bf16[2,192,512]{2,1,0:T(8,128)(2,1)S(1)} %activations.13.refs_5_.refs_8_.refs_1_), channel_id=1, source_target_pairs={{0,4},{4,0},{8,12},{12,8},{1,5},{5,1},{9,13},{13,9},{2,6},{6,2},{1... | collective-permute-start | bytes 1179656 | tf_op jit(solution)/shard_map/ppermute | solution.py:295
  137.9 9.4 %collective-permute-start.22 = (bf16[96,1536]{1,0:T(8,128)(2,1)S(1)}, bf16[96,1536]{1,0:T(8,128)(2,1)S(1)}, u32[]{:S(2)}, u32[]{:S(2)}) collective-permute-start(bf16[96,1536]{1,0:T(8,128)(2,1)S(1)} %get-tuple-element.21), channel_id=1, source_target_pairs={{0,16},{16,0},{1,17},{17,1},{2,18},{18,2},{3,19},{19,3},{4,20},{20... | collective-permute-start | bytes 884744 | tf_op jit(solution)/shard_map/ppermute | solution.py:295
  153.2 8.6 %collective-permute-start.30 = (bf16[96,1536]{1,0:T(8,128)(2,1)S(1)}, bf16[96,1536]{1,0:T(8,128)(2,1)S(1)}, u32[]{:S(2)}, u32[]{:S(2)}) collective-permute-start(bf16[96,1536]{1,0:T(8,128)(2,1)S(1)} %get-tuple-element.32), channel_id=1, source_target_pairs={{0,16},{16,0},{1,17},{17,1},{2,18},{18,2},{3,19},{19,3},{4,20},{20... | collective-permute-start | bytes 884744 | tf_op jit(solution)/shard_map/ppermute | solution.py:295
  154.8 13.9 %collective-permute-start.23 = (bf16[48,1536]{1,0:T(8,128)(2,1)S(1)}, bf16[48,1536]{1,0:T(8,128)(2,1)S(1)}, u32[]{:S(2)}, u32[]{:S(2)}) collective-permute-start(bf16[48,1536]{1,0:T(8,128)(2,1)S(1)} %fusion), channel_id=1, source_target_pairs={{0,1},{1,0},{2,3},{3,2},{4,5},{5,4},{6,7},{7,6},{8,9},{9,8},{10,11... | collective-permute-start | bytes 442376 | tf_op jit(solution)/shard_map/ppermute | solution.py:295
  161.9 12.1 %collective-permute-start.31 = (bf16[48,1536]{1,0:T(8,128)(2,1)S(1)}, bf16[48,1536]{1,0:T(8,128)(2,1)S(1)}, u32[]{:S(2)}, u32[]{:S(2)}) collective-permute-start(bf16[48,1536]{1,0:T(8,128)(2,1)S(1)} %get-tuple-element.37), channel_id=1, source_target_pairs={{0,2},{1,3},{2,0},{3,1},{4,6},{5,7},{6,4},{7,5},{8,10},{9,11},{10,... | collective-permute-start | bytes 442376 | tf_op jit(solution)/shard_map/ppermute | solution.py:295
  163.2 10.8 %collective-permute-start.32 = (bf16[48,1536]{1,0:T(8,128)(2,1)S(1)}, bf16[48,1536]{1,0:T(8,128)(2,1)S(1)}, u32[]{:S(2)}, u32[]{:S(2)}) collective-permute-start(bf16[48,1536]{1,0:T(8,128)(2,1)S(1)} %get-tuple-element.38), channel_id=1, source_target_pairs={{0,3},{1,2},{2,1},{3,0},{4,7},{5,6},{6,5},{7,4},{8,11},{9,10},{10,... | collective-permute-start | bytes 442376 | tf_op jit(solution)/shard_map/ppermute | solution.py:295

commit v3 on v2

--- a/solution.py
+++ b/solution.py
@@ -10,7 +10,7 @@
 F32 = jnp.float32
 BF16 = jnp.bfloat16
 VMEM_LIMIT = 24 * 1024 * 1024
-COST_PART = 16
+COST_PART = 1
 
 
 def gelu_exact(value):
@@ -91,25 +91,40 @@
     return core_ref[0] if side == 0 else 1 - core_ref[0]
 
 
-def partial_sums(core, units, up, down, side, start, width, dtype, after=()):
+def partial_sums(core, units, up, down, side, start, width, apart, after=()):
     _, rows, depth = units[0].shape
     tokens = rows * len(units)
     half = up.shape[1] // 2
     tile = tile_of(width, 256)
+    dtype = BF16 if side else F32
 
     def body(core_ref, *refs):
-        *unit_refs, up_ref, down_ref, out_ref, acts = refs
+        *unit_refs, up_ref, down_ref = refs[: len(units) + 2]
+        *out_refs, acts = refs[len(units) + 2 :]
 
         @pl.when(pl.program_id(0) == 0)
         def _():
             for n, ref in enumerate(unit_refs):
                 acts[:, n * rows : (n + 1) * rows, :] = ref[...]
 
-        out_ref[0] = contract(acts[0], up_ref[...], 1, 0).astype(dtype)
-        out_ref[1] = contract(acts[1], down_ref[...], 1, 1).astype(dtype)
+        preact = contract(acts[0], up_ref[...], 1, 0)
+        grad_hidden = contract(acts[1], down_ref[...], 1, 1)
+        if apart:
+            out_refs[0][...] = preact.astype(dtype)
+            out_refs[1][...] = grad_hidden.astype(dtype)
+        else:
+            out_refs[0][0] = preact.astype(dtype)
+            out_refs[0][1] = grad_hidden.astype(dtype)
 
     def place(i, c):
         return side_of(c, side) * (half // tile) + start // tile + i
+
+    if apart:
+        outs = [jax.ShapeDtypeStruct((tokens, width), dtype)] * 2
+        specs = [pl.BlockSpec((tokens, tile), lambda i, c: (0, i))] * 2
+    else:
+        outs = [jax.ShapeDtypeStruct((2, tokens, width), dtype)]
+        specs = [pl.BlockSpec((2, tokens, tile), lambda i, c: (0, 0, i))]
 
     return call(
         body,
@@ -120,8 +135,8 @@
             pl.BlockSpec((depth, tile), lambda i, c: (0, place(i, c))),
             pl.BlockSpec((tile, depth), lambda i, c: (place(i, c), 0)),
         ],
-        jax.ShapeDtypeStruct((2, tokens, width), dtype),
-        pl.BlockSpec((2, tokens, tile), lambda i, c: (0, 0, i)),
+        outs,
+        specs,
         (width // tile,),
         (4 * tokens * depth * width, 4 * depth * width),
         "sums_send" if side else "sums_keep",
@@ -130,14 +145,44 @@
     )
 
 
-def activations(core, keep, near, far, after=()):
+def combine(core, keep, near, after):
     _, tokens, width = keep.shape
+    tile = tile_of(width, 512)
+    both = pl.BlockSpec((2, tokens, tile), lambda i, c: (0, 0, i))
+    one = pl.BlockSpec((tokens, tile), lambda i, c: (0, i))
+
+    def body(core_ref, keep_ref, preact_ref, grad_ref, chip_ref):
+        chip_ref[0] = (keep_ref[0] + preact_ref[...].astype(F32)).astype(BF16)
+        chip_ref[1] = (keep_ref[1] + grad_ref[...].astype(F32)).astype(BF16)
+
+    return call(
+        body,
+        core,
+        [keep, *near],
+        [both, one, one],
+        jax.ShapeDtypeStruct(keep.shape, BF16),
+        both,
+        (width // tile,),
+        (4 * tokens * width, 16 * tokens * width),
+        "combine",
+        after,
+    )
+
+
+def activations(core, keep, near, far, start, after=()):
+    _, tokens, width = far.shape
     tile = tile_of(width, 256)
-    block = pl.BlockSpec((2, tokens, tile), lambda i, c: (0, 0, i))
-
-    def body(core_ref, keep_ref, near_ref, far_ref, act_ref):
+    first = start // tile
+    both = pl.BlockSpec((2, tokens, tile), lambda i, c: (0, 0, first + i))
+    both_here = pl.BlockSpec((2, tokens, tile), lambda i, c: (0, 0, i))
+    one = pl.BlockSpec((tokens, tile), lambda i, c: (0, first + i))
+
+    def body(core_ref, keep_ref, *refs):
+        *near_refs, far_ref, act_ref = refs
+
         def total(which):
-            return keep_ref[which] + near_ref[which].astype(F32) + far_ref[which].astype(F32)
+            part = near_refs[which][...] if len(near) > 1 else near_refs[0][which]
+            return keep_ref[which] + part.astype(F32) + far_ref[which].astype(F32)
 
         preact = total(0)
         cdf = 0.5 + 0.5 * lax.erf(preact * (0.5**0.5))
@@ -148,10 +193,10 @@
     return call(
         body,
         core,
-        [keep, near, far],
-        [block] * 3,
-        jax.ShapeDtypeStruct(keep.shape, BF16),
-        block,
+        [keep, *near, far],
+        [both] + [one if len(near) > 1 else both] * len(near) + [both_here],
+        jax.ShapeDtypeStruct(far.shape, BF16),
+        both_here,
         (width // tile,),
         (60 * tokens * width, 20 * tokens * width),
         "activations",
@@ -223,51 +268,37 @@
     )
 
 
-def weight_grads(core, inputs_t, cotan, sides, acts, start, width, shape, outputs, after=()):
+def weight_grads(core, inputs_t, cotan, side, acts, start, width, shape, outputs, after=()):
     depth, full = shape
     tokens = cotan.shape[0]
     half = full // 2
     tile = tile_of(width, 256)
-    steps = width // tile
-    groups = len(acts[0])
-
-    def act_spec(order, array, offset):
-        def index(i, c):
-            return (0, 0, offset // tile + jnp.clip(i - order * steps, 0, steps - 1))
-
-        return pl.BlockSpec((2, array.shape[1], tile), index)
+    groups = len(acts)
 
     def body(core_ref, inputs_ref, cotan_ref, *refs):
         up_out, down_out, done = refs[-3:]
         done[...] = jnp.zeros_like(done)
-        for order in range(len(sides)):
-            mine = refs[order * groups : (order + 1) * groups]
-
-            @pl.when(pl.program_id(0) // steps == order)
-            def _(mine=mine):
-                hidden = jnp.concatenate([ref[0] for ref in mine], axis=0)
-                grad = jnp.concatenate([ref[1] for ref in mine], axis=0)
-                up_out[...] = contract(inputs_ref[...], grad, 1, 0)
-                down_out[...] = contract(hidden, cotan_ref[...], 0, 0)
+        hidden = jnp.concatenate([ref[0] for ref in refs[:groups]], axis=0)
+        grad = jnp.concatenate([ref[1] for ref in refs[:groups]], axis=0)
+        up_out[...] = contract(inputs_ref[...], grad, 1, 0)
+        down_out[...] = contract(hidden, cotan_ref[...], 0, 0)
 
     def place(i, c):
-        which = side_of(c, sides[0])
-        if len(sides) > 1:
-            which = jnp.where(i // steps == 0, which, 1 - which)
-        return which * (half // tile) + start // tile + i % steps
+        return side_of(c, side) * (half // tile) + start // tile + i
 
     operands = [inputs_t, cotan]
     specs = [whole(inputs_t.shape), whole(cotan.shape)]
-    for order in range(len(sides)):
-        for array, offset in acts[order]:
-            operands.append(array)
-            specs.append(act_spec(order, array, offset))
+    for array, offset in acts:
+        first = offset // tile
+        operands.append(array)
+        specs.append(
+            pl.BlockSpec((2, array.shape[1], tile), lambda i, c, first=first: (0, 0, first + i))
+        )
     aliases = None
     if outputs is not None:
         aliases = {len(operands) + 1: 0, len(operands) + 2: 1}
         operands += list(outputs)
         specs += [pl.BlockSpec(memory_space=pl.ANY)] * 2
-    many = width * len(sides)
     return call(
         body,
         core,
@@ -283,8 +314,8 @@
             pl.BlockSpec((tile, depth), lambda i, c: (place(i, c), 0)),
             whole((8, 128)),
         ],
-        (steps * len(sides),),
-        (4 * tokens * depth * many, 8 * depth * many),
+        (width // tile,),
+        (4 * tokens * depth * width, 8 * depth * width),
         "weight_grads",
         after,
         aliases=aliases,
@@ -309,101 +340,101 @@
         unit[d, 1] = swap(unit[d, 0], "gx", 2, 1)
     groups = [
         [unit[0, 0]],
-        [unit[1, 0], unit[0, 1], unit[1, 1]],
-        [unit[2, 0], unit[3, 0], unit[2, 1], unit[3, 1]],
+        [unit[1, 0], unit[0, 1]],
+        [unit[2, 0], unit[1, 1]],
+        [unit[3, 0], unit[2, 1], unit[3, 1]],
     ]
 
-    def sums(piece, side, after):
-        group, start, size = piece
-        dtype = F32 if side == 0 else BF16
+    pieces = [(g, 0, half) for g in range(3)] + [(3, j * width, width) for j in range(chunks)]
+    near, keep, far, act, act_near = {}, {}, {}, {}, {}
+
+    def sums(group, side, after):
         weights = (up, down)
         if group == 0:
             weights = [pltpu.with_memory_space_constraint(array, pltpu.HBM) for array in weights]
-        return partial_sums(core, groups[group], *weights, side, start, size, dtype, after)
-
-    def over_cores(keep, near):
-        return (keep + near.astype(F32)).astype(BF16)
-
-    pieces = [(0, 0, half)] + [(g, j * width, width) for g in (1, 2) for j in range(chunks)]
-    near, keep, chip, far, act, act_near = {}, {}, {}, {}, {}, {}
-
-    def send(n, after):
-        out = sums(pieces[n], 1, after)
-        near[n] = swap(out, "gy", 4, 1)
-        return out
-
-    def hold(n, after):
-        keep[n] = sums(pieces[n], 0, after)
-        chip[n] = over_cores(keep[n], near[n])
-        far[n] = swap(chip[n], "gy", 4, 2)
-        return chip[n]
+        apart = side == 1 and group != 2
+        return partial_sums(core, groups[group], *weights, side, 0, half, apart, after)
+
+    def product(group, after, between=()):
+        out = sums(group, 1, after)
+        near[group] = [swap(array, "gy", 4, 1) for array in out]
+        keep[group], = sums(group, 0, [out[0], *between])
+        return [keep[group]]
+
+    def cross(n, after=()):
+        group, start, size = pieces[n]
+        span = slice(start, start + size)
+        parts = near[group] if len(near[group]) > 1 else near[group][0]
+        if after:
+            chip = combine(core, keep[group], parts, after)
+        else:
+            chip = jnp.stack([
+                (keep[group][which, :, span] + parts[which][:, span].astype(F32)).astype(BF16)
+                for which in range(2)
+            ])
+        far[n] = swap(chip, "gy", 4, 2)
+        return [chip]
 
     def ready(n, after):
-        act[n] = activations(core, keep[n], near[n], far[n], after)
+        group, start, _ = pieces[n]
+        act[n] = activations(core, keep[group], near[group], far[n], start, after)
         act_near[n] = swap(act[n], "gy", 4, 1)
-        return act[n]
-
-    one, two = 1, 1 + chunks
-    last = send(0, ())
-    last = hold(0, [last])
-    last = ready(0, [last])
-    last = send(one, [last])
+        return [act[n]]
+
+    def inward(n, part, leave, after):
+        group, start, _ = pieces[n]
+        return back(core, act[n], act_near[n], up, start, part, leave, after)
+
+    outputs = None
+
+    def gradients(j, side, after):
+        array = act_near if side else act
+        acts = [(array[n], j * width) for n in range(3)] + [(array[3 + j], 0)]
+        return weight_grads(
+            core, inputs_t, cotan, side, acts, j * width, width, up.shape, outputs, after
+        )
+
+    def exchange(value):
+        return swap(value, "gx", 2, 1).astype(F32)
+
+    last = product(0, (), [unit[1, 0], unit[0, 1]])
+    last = cross(0)
+    last = product(1, last, [unit[2, 0]])
+    last = ready(0, last)
+    last = cross(1, last)
+    last = product(2, last)
+    total, = last = inward(0, None, rows, last)
+    last = ready(1, [*last, unit[2, 1], unit[3, 1]])
+    last = cross(2) + last
+    last = product(3, last)
+    stay1, go1 = inward(1, None, rows, last)
+    last = ready(2, [stay1])
     for j in range(chunks):
+        last = cross(3 + j) + last
+    inputs_t, cotan = arrange(core, [u for group in groups for u in group], last)
+    stay2, go2 = inward(2, None, rows, [inputs_t])
+    total = total + exchange(go1)
+    back1 = (stay1 + exchange(go2)).astype(BF16)
+    far1 = swap(back1, "gz", 4, 1)
+
+    part, last = None, [stay2]
+    for j in range(chunks):
+        n = 3 + j
+        last = ready(n, last)
         if j + 1 < chunks:
-            last = send(one + j + 1, [last])
-        last = hold(one + j, [last])
-    stay0, = back(core, act[0], act_near[0], up, 0, None, rows, [last])
-    last = send(two, [stay0])
-    for j in range(chunks):
-        if j + 1 < chunks:
-            last = send(two + j + 1, [last])
-        last = hold(two + j, [last])
-    inputs_t, cotan = arrange(core, groups[0] + groups[1] + groups[2], [last])
-    last = ready(one, [inputs_t])
-    part = None
-    for j in range(chunks):
-        n = one + j
-        if j + 1 < chunks:
-            last = ready(n + 1, [last])
-        out = back(
-            core, act[n], act_near[n], up, j * width, part, rows if j + 1 == chunks else None, [last]
-        )
-        last = part = out[0]
-    stay1, go1 = out
-    near1 = swap(go1, "gx", 2, 1).astype(F32)
-    total = stay0 + near1[:rows]
-    far1 = swap((stay1 + near1[rows:]).astype(BF16), "gz", 4, 1)
-
-    outputs, part, last = None, None, [stay1]
-    shape = up.shape
-
-    def gradients(j, sides, after):
-        acts = [
-            [(array[0], j * width), (array[one + j], 0), (array[two + j], 0)]
-            for array in (act, act_near)
-        ]
-        acts = [acts[side] for side in sides]
-        return weight_grads(
-            core, inputs_t, cotan, sides, acts, j * width, width, shape, outputs, after
-        )
-
-    for j in range(chunks):
-        n = two + j
-        last = [ready(n, last)]
-        final = j + 1 == chunks
-        if final:
-            *outputs, done = gradients(j, (0,), last)
+            *outputs, done = gradients(j, 0, last)
+            part, = inward(n, part, None, [done])
+            *outputs, done = gradients(j, 1, [part] if j else [part, back1])
             last = [done]
-        out = back(
-            core, act[n], act_near[n], up, j * width, part, 2 * rows if final else None, last
-        )
-        part = out[0]
-        *outputs, done = gradients(j, (1,) if final else (0, 1), [part])
-        last = [done]
-    stay2, go2 = out
-    stay2 = (stay2 + swap(go2, "gx", 2, 1).astype(F32)).astype(BF16)
-    far2 = swap(stay2[:rows], "gz", 4, 2)
-    far3 = swap(stay2[rows:], "gz", 4, 3)
+        else:
+            stay3, go3 = inward(n, part, rows, last)
+            near3 = exchange(go3)
+            *outputs, done = gradients(j, 0, [stay3])
+            back2 = (stay2 + near3[:rows]).astype(BF16)
+            back3 = (stay3 + near3[rows:]).astype(BF16)
+            far2 = swap(back2, "gz", 4, 2)
+            far3 = swap(back3, "gz", 4, 3)
+            *outputs, done = gradients(j, 1, [done, back2, back3])
     total = total + far1.astype(F32) + far2.astype(F32) + far3.astype(F32)
     return (total.astype(BF16), *outputs)
 

time: 175 us -> 135 us (0.77)
  waiting for transfers between devices: 74 us -> 22.4 us
  Pallas kernels: 71.4 us -> 82.3 us
    ppermute x33 -> x32, waiting for transfers between devices: 74 us -> 22.4 us  [swap(): return lax.ppermute(value, axis, [(i, i ^ bits) for i in range(size)])]
    pallas_call x33 -> x28, Pallas kernels: 71.4 us -> 82.3 us  [call(): pl.pallas_call(kernel, grid_spec=pltpu.PrefetchScalarGridSpec(num_scalar_...]
    ppermute x33 -> x32, starting transfers between devices: 25.4 us -> 25.7 us  [swap(): return lax.ppermute(value, axis, [(i, i ^ bits) for i in range(size)])]
  transfers between devices with their start and end apart: 33 -> 32, of which waited for: 17 -> 8; matrix products, arithmetic and copies ran while one was open for 0% -> 1% of each run, Pallas kernels for 33% -> 59%
where the time goes in v3:
time: 135 us; the launch traced here: 134 us
  Pallas kernels  82.3 us (61%)
  starting transfers between devices  25.7 us (19%)
  waiting for transfers between devices  22.4 us (17%)
  other arithmetic  2.58 us (2%)
    pallas_call x28, Pallas kernels, call(): pl.pallas_call(kernel, grid_spec=pltpu.PrefetchScalarGridSpec(num_scalar_...  82.3 us
    ppermute x32, starting transfers between devices, swap(): return lax.ppermute(value, axis, [(i, i ^ bits) for i in range(size)])  25.7 us
    ppermute x32, waiting for transfers between devices, swap(): return lax.ppermute(value, axis, [(i, i ^ bits) for i in range(size)])  22.4 us
  transfers between devices with their start and end apart: 32, of which 8 were waited for; matrix products, arithmetic and copies ran while one was open for 1% of the time, Pallas kernels for 59%

profile of v3, /device:TPU:0, one launch (start us, length us, event | category | flops | bytes accessed | tf_op | source)
XLA Modules:
  0.0 134.2 jit_solution(6546778446461942775)
XLA Ops:
  0.6 1.0 pad_maximum_fusion.1.refs_1_
  1.6 3.1 %collective-permute-start = (bf16[2,48,1536]{2,1,0:T(8,128)(2,1)S(1)}, bf16[2,48,1536]{2,1,0:T(8,128)(2,1)S(1)}, u32[]{:S(2)}, u32[]{:S(2)}) collective-permute-start(bf16[2,48,1536]{2,1,0:T(8,128)(2,1)S(1)} %pad_maximum_fusion.1.refs_1_), channel_id=1, source_target_pairs={{0,1},{1,0},{2,3},{3,2},{4,5},{5,4},{6,7},{7,6},{8,9},{9,8},{10,11... | collective-permute-start | bytes 884744 | tf_op jit(solution)/shard_map/ppermute | solution.py:326
  4.7 1.5 %collective-permute-start.1 = (bf16[2,48,1536]{2,1,0:T(8,128)(2,1)S(1)}, bf16[2,48,1536]{2,1,0:T(8,128)(2,1)S(1)}, u32[]{:S(2)}, u32[]{:S(2)}) collective-permute-start(bf16[2,48,1536]{2,1,0:T(8,128)(2,1)S(1)} %pad_maximum_fusion.1.refs_1_), channel_id=1, source_target_pairs={{0,16},{16,0},{1,17},{17,1},{2,18},{18,2},{3,19},{19,3},{4,20},{20... | collective-permute-start | bytes 884744 | tf_op jit(solution)/shard_map/ppermute | solution.py:326
  6.2 8.1 %sums_send.4 = (bf16[48,1536]{1,0:T(8,128)(2,1)S(1)}, bf16[48,1536]{1,0:T(8,128)(2,1)S(1)}) custom-call(s32[1]{0:T(128)} %bitcast.refs_0_, bf16[2,48,1536]{2,1,0:T(8,128)(2,1)S(1)} %pad_maximum_fusion.1.refs_1_, bf16[1536,3072]{1,0:T(8,128)(2,1)} %refs_4_.23, bf16[3072,1536]{1,0:T(8,128)(2,1)} %refs_5_.3), custom_call_target="tpu_custom_call" | custom-call | flops 452984832 | bytes 9437184 | tf_op jit(solution)/shard_map/sums_send/pallas_call | solution.py:67
  14.4 0.5 collective-permute-start.3
  14.9 2.6 %collective-permute-start.5 = (bf16[2,48,1536]{2,1,0:T(8,128)(2,1)S(1)}, bf16[2,48,1536]{2,1,0:T(8,128)(2,1)S(1)}, u32[]{:S(2)}, u32[]{:S(2)}) collective-permute-start(bf16[2,48,1536]{2,1,0:T(8,128)(2,1)S(1)} %pad_maximum_fusion.1.refs_1_), channel_id=1, source_target_pairs={{0,2},{1,3},{2,0},{3,1},{4,6},{5,7},{6,4},{7,5},{8,10},{9,11},{10,... | collective-permute-start | bytes 884744 | tf_op jit(solution)/shard_map/ppermute | solution.py:326
  17.5 6.5 %sums_keep.4.refs_1_ = f32[2,48,1536]{2,1,0:T(8,128)S(1)} custom-call(s32[1]{0:T(128)} %bitcast.refs_0_, bf16[2,48,1536]{2,1,0:T(8,128)(2,1)S(1)} %pad_maximum_fusion.1.refs_1_, bf16[1536,3072]{1,0:T(8,128)(2,1)} %refs_4_.23, bf16[3072,1536]{1,0:T(8,128)(2,1)} %refs_5_.3, bf16[48,1536]{1,0:T(8,128)(2,1)S(1)} %get-tuple-element.34.refs_4_, ...), custom_call_target="tpu_custom_call" | custom-call | flops 452984832 | bytes 9437184 | tf_op jit(solution)/shard_map/sums_keep/pallas_call | solution.py:67
  24.1 1.6 %collective-permute-start.4 = (bf16[2,48,1536]{2,1,0:T(8,128)(2,1)S(1)}, bf16[2,48,1536]{2,1,0:T(8,128)(2,1)S(1)}, u32[]{:S(2)}, u32[]{:S(2)}) collective-permute-start(bf16[2,48,1536]{2,1,0:T(8,128)(2,1)S(1)} %pad_maximum_fusion.2.refs_5_), channel_id=1, source_target_pairs={{0,8},{4,12},{8,0},{12,4},{1,9},{5,13},{9,1},{13,5},{2,10},{6,14},... | collective-permute-start | bytes 884744 | tf_op jit(solution)/shard_map/ppermute | solution.py:326
  25.7 3.9 %sums_send.5 = (bf16[96,1536]{1,0:T(8,128)(2,1)S(1)}, bf16[96,1536]{1,0:T(8,128)(2,1)S(1)}) custom-call(s32[1]{0:T(128)} %bitcast.refs_0_, bf16[2,48,1536]{2,1,0:T(8,128)(2,1)S(1)} %collective-permute-done.refs_5_.refs_1_.refs_2_, bf16[2,48,1536]{2,1,0:T(8,128)(2,1)S(1)} %collective-permute-done.1.refs_6_.refs_2_.refs_3_, bf16[1536,3072]{1,0:T(8,128)(2,1)S(1)} %bitcast.84, ...), custom_call_target="tpu_custom_call" | custom-call | flops 905969664 | bytes 9437184 | tf_op jit(solution)/shard_map/sums_send/pallas_call | solution.py:67
  29.7 0.5 collective-permute-start.9
  30.2 0.5 collective-permute-start.7
  30.8 0.2 collective-permute-done.5.refs_6_.refs_1_.refs_4_
  31.0 2.6 %collective-permute-start.12 = (bf16[2,48,1536]{2,1,0:T(8,128)(2,1)S(1)}, bf16[2,48,1536]{2,1,0:T(8,128)(2,1)S(1)}, u32[]{:S(2)}, u32[]{:S(2)}) collective-permute-start(bf16[2,48,1536]{2,1,0:T(8,128)(2,1)S(1)} %pad_maximum_fusion.1.refs_1_), channel_id=1, source_target_pairs={{0,3},{1,2},{2,1},{3,0},{4,7},{5,6},{6,5},{7,4},{8,11},{9,10},{10,... | collective-permute-start | bytes 884744 | tf_op jit(solution)/shard_map/ppermute | solution.py:326
  33.6 3.9 %sums_keep.5.refs_5_.refs_1_ = f32[2,96,1536]{2,1,0:T(8,128)S(1)} custom-call(s32[1]{0:T(128)} %bitcast.refs_0_, bf16[2,48,1536]{2,1,0:T(8,128)(2,1)S(1)} %collective-permute-done.refs_5_.refs_1_.refs_2_, bf16[2,48,1536]{2,1,0:T(8,128)(2,1)S(1)} %collective-permute-done.1.refs_6_.refs_2_.refs_3_, bf16[1536,3072]{1,0:T(8,128)(2,1)S(1)} %bitcast.84, ...), custom_call_target="tpu_custom_call" | custom-call | flops 905969664 | bytes 9437184 | tf_op jit(solution)/shard_map/sums_keep/pallas_call | solution.py:67
  37.5 0.5 activations.6.refs_4_.refs_1_.refs_3_
  38.1 0.4 combine.1.refs_5_
  38.5 1.6 %collective-permute-start.10 = (bf16[2,96,1536]{2,1,0:T(8,128)(2,1)S(1)}, bf16[2,96,1536]{2,1,0:T(8,128)(2,1)S(1)}, u32[]{:S(2)}, u32[]{:S(2)}) collective-permute-start(bf16[2,96,1536]{2,1,0:T(8,128)(2,1)S(1)} %combine.1.refs_5_), channel_id=1, source_target_pairs={{0,8},{4,12},{8,0},{12,4},{1,9},{5,13},{9,1},{13,5},{2,10},{6,14},... | collective-permute-start | bytes 1769480 | tf_op jit(solution)/shard_map/ppermute | solution.py:326
  40.1 3.9 %sums_send.6.refs_5_ = bf16[2,96,1536]{2,1,0:T(8,128)(2,1)S(1)} custom-call(s32[1]{0:T(128)} %bitcast.refs_0_, bf16[2,48,1536]{2,1,0:T(8,128)(2,1)S(1)} %collective-permute-done.5.refs_6_.refs_1_.refs_4_, bf16[2,48,1536]{2,1,0:T(8,128)(2,1)S(1)} %collective-permute-done.7.refs_2_.refs_5_, bf16[1536,3072]{1,0:T(8,128)(2,1)S(1)} %bitcast.84, ...), custom_call_target="tpu_custom_call" | custom-call | flops 905969664 | bytes 9437184 | tf_op jit(solution)/shard_map/sums_send/pallas_call | solution.py:67
  44.1 0.5 collective-permute-start.6
  44.6 0.5 collective-permute-start.11
  45.1 1.5 %collective-permute-start.13 = (bf16[2,48,1536]{2,1,0:T(8,128)(2,1)S(1)}, bf16[2,48,1536]{2,1,0:T(8,128)(2,1)S(1)}, u32[]{:S(2)}, u32[]{:S(2)}) collective-permute-start(bf16[2,48,1536]{2,1,0:T(8,128)(2,1)S(1)} %collective-permute-done.12.refs_1_.refs_6_), channel_id=1, source_target_pairs={{0,16},{16,0},{1,17},{17,1},{2,18},{18,2},{3,19},{19,3},{4,20},{20... | collective-permute-start | bytes 884744 | tf_op jit(solution)/shard_map/ppermute | solution.py:326
  46.6 3.9 %sums_keep.6.refs_5_.refs_1_ = f32[2,96,1536]{2,1,0:T(8,128)S(1)} custom-call(s32[1]{0:T(128)} %bitcast.refs_0_, bf16[2,48,1536]{2,1,0:T(8,128)(2,1)S(1)} %collective-permute-done.5.refs_6_.refs_1_.refs_4_, bf16[2,48,1536]{2,1,0:T(8,128)(2,1)S(1)} %collective-permute-done.7.refs_2_.refs_5_, bf16[1536,3072]{1,0:T(8,128)(2,1)S(1)} %bitcast.84, ...), custom_call_target="tpu_custom_call" | custom-call | flops 905969664 | bytes 9437184 | tf_op jit(solution)/shard_map/sums_keep/pallas_call | solution.py:67
  50.6 3.9 %back.6.refs_5_ = f32[48,1536]{1,0:T(8,128)S(1)} custom-call(s32[1]{0:T(128)} %bitcast.refs_0_, bf16[2,48,1536]{2,1,0:T(8,128)(2,1)S(1)} %activations.6.refs_4_.refs_1_.refs_3_, bf16[2,48,1536]{2,1,0:T(8,128)(2,1)S(1)} %collective-permute-done.6.refs_2_.refs_3_, bf16[1536,3072]{1,0:T(8,128)(2,1)S(1)} %bitcast.84, bf16[1536,3072]{1,0:T(8,128)(2,1)S(1)} %bitcast.84, ...), custom_call_target="tpu_custom_call" | custom-call | flops 452984832 | bytes 9732096 | tf_op jit(solution)/shard_map/back/pallas_call | solution.py:67
  54.4 5.4 %collective-permute-done.13.refs_7_.refs_3_.refs_8_ = bf16[2,48,1536]{2,1,0:T(8,128)(2,1)S(1)} collective-permute-done((bf16[2,48,1536]{2,1,0:T(8,128)(2,1)S(1)}, bf16[2,48,1536]{2,1,0:T(8,128)(2,1)S(1)}, u32[]{:S(2)}, u32[]{:S(2)}) %collective-permute-start.13) | collective-permute-done | bytes 294944 | tf_op jit(solution)/shard_map/ppermute | solution.py:326
  59.9 0.8 activations.7.refs_7_.refs_1_.refs_4_
  60.8 0.1 fusion.1
  61.0 0.6 collective-permute-start.17
  61.5 3.9 %sums_send.7 = (bf16[144,1536]{1,0:T(8,128)(2,1)S(1)}, bf16[144,1536]{1,0:T(8,128)(2,1)S(1)}) custom-call(s32[1]{0:T(128)} %bitcast.refs_0_, bf16[2,48,1536]{2,1,0:T(8,128)(2,1)S(1)} %collective-permute-done.12.refs_1_.refs_6_, bf16[2,48,1536]{2,1,0:T(8,128)(2,1)S(1)} %collective-permute-done.11.refs_6_.refs_2_.refs_7_, ...), custom_call_target="tpu_custom_call" | custom-call | flops 1358954496 | bytes 9437184 | tf_op jit(solution)/shard_map/sums_send/pallas_call | solution.py:67
  65.5 0.3 collective-permute-start.19
  65.8 0.3 collective-permute-start.20
  66.1 4.0 %sums_keep.7.refs_5_.refs_1_ = f32[2,144,1536]{2,1,0:T(8,128)S(1)} custom-call(s32[1]{0:T(128)} %bitcast.refs_0_, bf16[2,48,1536]{2,1,0:T(8,128)(2,1)S(1)} %collective-permute-done.12.refs_1_.refs_6_, bf16[2,48,1536]{2,1,0:T(8,128)(2,1)S(1)} %collective-permute-done.11.refs_6_.refs_2_.refs_7_, ...), custom_call_target="tpu_custom_call" | custom-call | flops 1358954496 | bytes 9437184 | tf_op jit(solution)/shard_map/sums_keep/pallas_call | solution.py:67
  70.0 4.0 %back.7 = (f32[48,1536]{1,0:T(8,128)S(1)}, bf16[48,1536]{1,0:T(8,128)(2,1)S(1)}) custom-call(s32[1]{0:T(128)} %bitcast.refs_0_, bf16[2,96,1536]{2,1,0:T(8,128)(2,1)S(1)} %activations.7.refs_7_.refs_1_.refs_4_, bf16[2,96,1536]{2,1,0:T(8,128)(2,1)S(1)} %collective-permute-done.14.refs_2_.refs_4_, bf16[1536,3072]{1,0:T(8,128)(2,1)S(1)} %bitcast.84, ...), custom_call_target="tpu_custom_call" | custom-call | flops 905969664 | bytes 10027008 | tf_op jit(solution)/shard_map/back/pallas_call | solution.py:67
  74.1 2.7 %collective-permute-done.17.refs_3_ = bf16[2,96,1536]{2,1,0:T(8,128)(2,1)S(1)} collective-permute-done((bf16[2,96,1536]{2,1,0:T(8,128)(2,1)S(1)}, bf16[2,96,1536]{2,1,0:T(8,128)(2,1)S(1)}, u32[]{:S(2)}, u32[]{:S(2)}) %collective-permute-start.17) | collective-permute-done | bytes 589856 | tf_op jit(solution)/shard_map/ppermute | solution.py:326
  76.8 0.8 activations.8.refs_12_.refs_1_.refs_5_
  77.6 0.3 fusion.26
  78.0 0.6 collective-permute-start.25
  78.6 0.4 arrange.1
  79.1 0.6 collective-permute-done.18.refs_2_.refs_5_
  79.6 4.0 %back.8 = (f32[48,1536]{1,0:T(8,128)S(1)}, bf16[48,1536]{1,0:T(8,128)(2,1)S(1)}) custom-call(s32[1]{0:T(128)} %bitcast.refs_0_, bf16[2,96,1536]{2,1,0:T(8,128)(2,1)S(1)} %activations.8.refs_12_.refs_1_.refs_5_, bf16[2,96,1536]{2,1,0:T(8,128)(2,1)S(1)} %collective-permute-done.18.refs_2_.refs_5_, bf16[1536,3072]{1,0:T(8,128)(2,1)S(1)} %bitcast.84, ...), custom_call_target="tpu_custom_call" | custom-call | flops 905969664 | bytes 10027008 | tf_op jit(solution)/shard_map/back/pallas_call | solution.py:67
  83.6 0.6 collective-permute-start.21
  84.2 1.0 collective-permute-start.24
  85.2 2.7 %collective-permute-done.25.refs_4_ = bf16[2,144,512]{2,1,0:T(8,128)(2,1)S(1)} collective-permute-done((bf16[2,144,512]{2,1,0:T(8,128)(2,1)S(1)}, bf16[2,144,512]{2,1,0:T(8,128)(2,1)S(1)}, u32[]{:S(2)}, u32[]{:S(2)}) %collective-permute-start.25) | collective-permute-done | bytes 294944 | tf_op jit(solution)/shard_map/ppermute | solution.py:326
  87.9 0.4 activations.9.refs_6_.refs_7_.refs_1_
  88.3 3.8 %weight_grads.6 = (f32[1536,3072]{1,0:T(8,128)}, f32[3072,1536]{1,0:T(8,128)}, f32[8,128]{1,0:T(8,128)S(1)}) custom-call(s32[1]{0:T(128)} %bitcast.refs_0_, bf16[1536,384]{1,0:T(8,128)(2,1)S(1)} %get-tuple-element.42.refs_5_.refs_1_, bf16[384,1536]{1,0:T(8,128)(2,1)S(1)} %get-tuple-element.45.refs_2_, ...), custom_call_target="tpu_custom_call" | custom-call | flops 1207959552 | bytes 6291456 | tf_op jit(solution)/shard_map/weight_grads/pallas_call | solution.py:67
  92.2 1.8 %back.9.refs_9_.refs_5_ = f32[144,1536]{1,0:T(8,128)S(1)} custom-call(s32[1]{0:T(128)} %bitcast.refs_0_, bf16[2,144,512]{2,1,0:T(8,128)(2,1)S(1)} %activations.9.refs_6_.refs_7_.refs_1_, bf16[2,144,512]{2,1,0:T(8,128)(2,1)S(1)} %collective-permute-done.26.refs_2_.refs_6_, bf16[1536,3072]{1,0:T(8,128)(2,1)S(1)} %bitcast.84, bf16[1536,3072]{1,0:T(8,128)(2,1)S(1)} %bitcast.84, ...), custom_call_target="tpu_custom_call" | custom-call | flops 452984832 | bytes 4030464 | tf_op jit(solution)/shard_map/back/pallas_call | solution.py:67
  94.0 3.8 %weight_grads.7 = (f32[1536,3072]{1,0:T(8,128)}, f32[3072,1536]{1,0:T(8,128)}, f32[8,128]{1,0:T(8,128)S(1)}) custom-call(s32[1]{0:T(128)} %bitcast.refs_0_, bf16[1536,384]{1,0:T(8,128)(2,1)S(1)} %get-tuple-element.42.refs_5_.refs_1_, bf16[384,1536]{1,0:T(8,128)(2,1)S(1)} %get-tuple-element.45.refs_2_, ...), custom_call_target="tpu_custom_call", output_to_operand_aliasing={{0}: (7, {}), {1}: (8, {})} | custom-call | flops 1207959552 | bytes 6291456 | tf_op jit(solution)/shard_map/weight_grads/pallas_call | solution.py:67
  97.8 0.4 activations.10.refs_6_.refs_9_.refs_1_
  98.2 0.5 collective-permute-start.27
  98.8 0.3 collective-permute-start.23
  99.0 3.8 %weight_grads.8 = (f32[1536,3072]{1,0:T(8,128)}, f32[3072,1536]{1,0:T(8,128)}, f32[8,128]{1,0:T(8,128)S(1)}) custom-call(s32[1]{0:T(128)} %bitcast.refs_0_, bf16[1536,384]{1,0:T(8,128)(2,1)S(1)} %get-tuple-element.42.refs_5_.refs_1_, bf16[384,1536]{1,0:T(8,128)(2,1)S(1)} %get-tuple-element.45.refs_2_, ...), custom_call_target="tpu_custom_call", output_to_operand_aliasing={{0}: (7, {}), {1}: (8, {})} | custom-call | flops 1207959552 | bytes 6291456 | tf_op jit(solution)/shard_map/weight_grads/pallas_call | solution.py:67
  102.8 1.9 %back.10.refs_9_.refs_5_ = f32[144,1536]{1,0:T(8,128)S(1)} custom-call(s32[1]{0:T(128)} %bitcast.refs_0_, bf16[2,144,512]{2,1,0:T(8,128)(2,1)S(1)} %activations.10.refs_6_.refs_9_.refs_1_, bf16[2,144,512]{2,1,0:T(8,128)(2,1)S(1)} %collective-permute-done.27.refs_2_.refs_6_, bf16[1536,3072]{1,0:T(8,128)(2,1)S(1)} %bitcast.84, ...), custom_call_target="tpu_custom_call" | custom-call | flops 452984832 | bytes 4030464 | tf_op jit(solution)/shard_map/back/pallas_call | solution.py:67
  104.7 3.8 %weight_grads.9 = (f32[1536,3072]{1,0:T(8,128)}, f32[3072,1536]{1,0:T(8,128)}, f32[8,128]{1,0:T(8,128)S(1)}) custom-call(s32[1]{0:T(128)} %bitcast.refs_0_, bf16[1536,384]{1,0:T(8,128)(2,1)S(1)} %get-tuple-element.42.refs_5_.refs_1_, bf16[384,1536]{1,0:T(8,128)(2,1)S(1)} %get-tuple-element.45.refs_2_, ...), custom_call_target="tpu_custom_call", output_to_operand_aliasing={{0}: (7, {}), {1}: (8, {})} | custom-call | flops 1207959552 | bytes 6291456 | tf_op jit(solution)/shard_map/weight_grads/pallas_call | solution.py:67
  108.5 0.4 activations.11.refs_1_.refs_6_
  108.9 0.1 collective-permute-start.28
  109.0 1.6 %collective-permute-done.28.refs_2_.refs_6_ = bf16[2,144,512]{2,1,0:T(8,128)(2,1)S(1)} collective-permute-done((bf16[2,144,512]{2,1,0:T(8,128)(2,1)S(1)}, bf16[2,144,512]{2,1,0:T(8,128)(2,1)S(1)}, u32[]{:S(2)}, u32[]{:S(2)}) %collective-permute-start.28) | collective-permute-done | bytes 294944 | tf_op jit(solution)/shard_map/ppermute | solution.py:326
  110.5 1.9 %back.11 = (f32[48,1536]{1,0:T(8,128)S(1)}, bf16[96,1536]{1,0:T(8,128)(2,1)S(1)}) custom-call(s32[1]{0:T(128)} %bitcast.refs_0_, bf16[2,144,512]{2,1,0:T(8,128)(2,1)S(1)} %activations.11.refs_1_.refs_6_, bf16[2,144,512]{2,1,0:T(8,128)(2,1)S(1)} %collective-permute-done.28.refs_2_.refs_6_, bf16[1536,3072]{1,0:T(8,128)(2,1)S(1)} %bitcast.84, ...), custom_call_target="tpu_custom_call" | custom-call | flops 452984832 | bytes 4030464 | tf_op jit(solution)/shard_map/back/pallas_call | solution.py:67
  112.4 0.4 collective-permute-start.29
  112.8 1.7 %collective-permute-start.16 = (bf16[48,1536]{1,0:T(8,128)(2,1)S(1)}, bf16[48,1536]{1,0:T(8,128)(2,1)S(1)}, u32[]{:S(2)}, u32[]{:S(2)}) collective-permute-start(bf16[48,1536]{1,0:T(8,128)(2,1)S(1)} %get-tuple-element.39), channel_id=1, source_target_pairs={{0,16},{16,0},{1,17},{17,1},{2,18},{18,2},{3,19},{19,3},{4,20},{20... | collective-permute-start | bytes 442376 | tf_op jit(solution)/shard_map/ppermute | solution.py:326
  114.5 7.8 %collective-permute-done.29 = bf16[96,1536]{1,0:T(8,128)(2,1)S(1)} collective-permute-done((bf16[96,1536]{1,0:T(8,128)(2,1)S(1)}, bf16[96,1536]{1,0:T(8,128)(2,1)S(1)}, u32[]{:S(2)}, u32[]{:S(2)}) %collective-permute-start.29) | collective-permute-done | bytes 294944 | tf_op jit(solution)/shard_map/ppermute | solution.py:326
  122.5 2.0 %collective-permute-start.31 = (bf16[48,1536]{1,0:T(8,128)(2,1)S(1)}, bf16[48,1536]{1,0:T(8,128)(2,1)S(1)}, u32[]{:S(2)}, u32[]{:S(2)}) collective-permute-start(bf16[48,1536]{1,0:T(8,128)(2,1)S(1)} %get-tuple-element.77.refs_11_), channel_id=1, source_target_pairs={{0,3},{1,2},{2,1},{3,0},{4,7},{5,6},{6,5},{7,4},{8,11},{9,10},{10,... | collective-permute-start | bytes 442376 | tf_op jit(solution)/shard_map/ppermute | solution.py:326
  124.5 3.8 %weight_grads.10 = (f32[1536,3072]{1,0:T(8,128)}, f32[3072,1536]{1,0:T(8,128)}, f32[8,128]{1,0:T(8,128)S(1)}) custom-call(s32[1]{0:T(128)} %bitcast.refs_0_, bf16[1536,384]{1,0:T(8,128)(2,1)S(1)} %get-tuple-element.42.refs_5_.refs_1_, bf16[384,1536]{1,0:T(8,128)(2,1)S(1)} %get-tuple-element.45.refs_2_, ...), custom_call_target="tpu_custom_call", output_to_operand_aliasing={{0}: (7, {}), {1}: (8, {})} | custom-call | flops 1207959552 | bytes 6291456 | tf_op jit(solution)/shard_map/weight_grads/pallas_call | solution.py:67
  128.3 3.8 %weight_grads.11 = (f32[1536,3072]{1,0:T(8,128)}, f32[3072,1536]{1,0:T(8,128)}, f32[8,128]{1,0:T(8,128)}) custom-call(s32[1]{0:T(128)} %bitcast.refs_0_, bf16[1536,384]{1,0:T(8,128)(2,1)S(1)} %get-tuple-element.42.refs_5_.refs_1_, bf16[384,1536]{1,0:T(8,128)(2,1)S(1)} %get-tuple-element.45.refs_2_, ...), custom_call_target="tpu_custom_call", output_to_operand_aliasing={{0}: (7, {}), {1}: (8, {})} | custom-call | flops 1207959552 | bytes 6291456 | tf_op jit(solution)/shard_map/weight_grads/pallas_call | solution.py:67
  132.1 1.3 collective-permute-done.30
  133.4 0.8 add_convert_fusion
  (55 shorter events, 1.0 us)
Async XLA Ops:
  1.6 15.8 %collective-permute-start = (bf16[2,48,1536]{2,1,0:T(8,128)(2,1)S(1)}, bf16[2,48,1536]{2,1,0:T(8,128)(2,1)S(1)}, u32[]{:S(2)}, u32[]{:S(2)}) collective-permute-start(bf16[2,48,1536]{2,1,0:T(8,128)(2,1)S(1)} %pad_maximum_fusion.1.refs_1_), channel_id=1, source_target_pairs={{0,1},{1,0},{2,3},{3,2},{4,5},{5,4},{6,7},{7,6},{8,9},{9,8},{10,11... | collective-permute-start | bytes 884744 | tf_op jit(solution)/shard_map/ppermute | solution.py:326
  4.7 12.7 %collective-permute-start.1 = (bf16[2,48,1536]{2,1,0:T(8,128)(2,1)S(1)}, bf16[2,48,1536]{2,1,0:T(8,128)(2,1)S(1)}, u32[]{:S(2)}, u32[]{:S(2)}) collective-permute-start(bf16[2,48,1536]{2,1,0:T(8,128)(2,1)S(1)} %pad_maximum_fusion.1.refs_1_), channel_id=1, source_target_pairs={{0,16},{16,0},{1,17},{17,1},{2,18},{18,2},{3,19},{19,3},{4,20},{20... | collective-permute-start | bytes 884744 | tf_op jit(solution)/shard_map/ppermute | solution.py:326
  6.2 19.4 %slice-start = ((s8[9437184]{0:T(1024)(128)(4,1)}), s8[4194304]{0:T(1024)(128)(4,1)S(1)}, s32[]{:S(2)}) async-start(s8[9437184]{0:T(1024)(128)(4,1)} %bitcast.83), calls=%async_computation | async-start | bytes 8388608
  6.2 19.4 %slice-start.1 = ((s8[9437184]{0:T(1024)(128)(4,1)}), s8[4194304]{0:T(1024)(128)(4,1)S(1)}, s32[]{:S(2)}) async-start(s8[9437184]{0:T(1024)(128)(4,1)} %bitcast.83), calls=%async_computation.1 | async-start | bytes 8388608
  6.2 19.4 %slice-start.3 = ((s8[9437184]{0:T(1024)(128)(4,1)}), s8[4194304]{0:T(1024)(128)(4,1)S(1)}, s32[]{:S(2)}) async-start(s8[9437184]{0:T(1024)(128)(4,1)} %bitcast.85), calls=%async_computation.3 | async-start | bytes 8388608
  6.2 19.4 %slice-start.4 = ((s8[9437184]{0:T(1024)(128)(4,1)}), s8[4194304]{0:T(1024)(128)(4,1)S(1)}, s32[]{:S(2)}) async-start(s8[9437184]{0:T(1024)(128)(4,1)} %bitcast.85), calls=%async_computation.4 | async-start | bytes 8388608
  14.3 9.7 %collective-permute-start.2 = (bf16[48,1536]{1,0:T(8,128)(2,1)S(1)}, bf16[48,1536]{1,0:T(8,128)(2,1)S(1)}, u32[]{:S(2)}, u32[]{:S(2)}) collective-permute-start(bf16[48,1536]{1,0:T(8,128)(2,1)S(1)} %get-tuple-element.34.refs_4_), channel_id=1, source_target_pairs={{0,4},{4,0},{8,12},{12,8},{1,5},{5,1},{9,13},{13,9},{2,6},{6,2},{1... | collective-permute-start | bytes 442376 | tf_op jit(solution)/shard_map/ppermute | solution.py:326
  14.4 11.3 %slice-start.2 = ((s8[9437184]{0:T(1024)(128)(4,1)}), s8[1048576]{0:T(1024)(128)(4,1)S(1)}, s32[]{:S(2)}) async-start(s8[9437184]{0:T(1024)(128)(4,1)} %bitcast.83), calls=%async_computation.2 | async-start | bytes 2097152
  14.4 11.3 %slice-start.5 = ((s8[9437184]{0:T(1024)(128)(4,1)}), s8[1048576]{0:T(1024)(128)(4,1)S(1)}, s32[]{:S(2)}) async-start(s8[9437184]{0:T(1024)(128)(4,1)} %bitcast.85), calls=%async_computation.5 | async-start | bytes 2097152
  14.4 9.6 %collective-permute-start.3 = (bf16[48,1536]{1,0:T(8,128)(2,1)S(1)}, bf16[48,1536]{1,0:T(8,128)(2,1)S(1)}, u32[]{:S(2)}, u32[]{:S(2)}) collective-permute-start(bf16[48,1536]{1,0:T(8,128)(2,1)S(1)} %get-tuple-element.35), channel_id=1, source_target_pairs={{0,4},{4,0},{8,12},{12,8},{1,5},{5,1},{9,13},{13,9},{2,6},{6,2},{1... | collective-permute-start | bytes 442376 | tf_op jit(solution)/shard_map/ppermute | solution.py:326
  14.9 16.1 %collective-permute-start.5 = (bf16[2,48,1536]{2,1,0:T(8,128)(2,1)S(1)}, bf16[2,48,1536]{2,1,0:T(8,128)(2,1)S(1)}, u32[]{:S(2)}, u32[]{:S(2)}) collective-permute-start(bf16[2,48,1536]{2,1,0:T(8,128)(2,1)S(1)} %pad_maximum_fusion.1.refs_1_), channel_id=1, source_target_pairs={{0,2},{1,3},{2,0},{3,1},{4,6},{5,7},{6,4},{7,5},{8,10},{9,11},{10,... | collective-permute-start | bytes 884744 | tf_op jit(solution)/shard_map/ppermute | solution.py:326
  24.1 13.5 %collective-permute-start.4 = (bf16[2,48,1536]{2,1,0:T(8,128)(2,1)S(1)}, bf16[2,48,1536]{2,1,0:T(8,128)(2,1)S(1)}, u32[]{:S(2)}, u32[]{:S(2)}) collective-permute-start(bf16[2,48,1536]{2,1,0:T(8,128)(2,1)S(1)} %pad_maximum_fusion.2.refs_5_), channel_id=1, source_target_pairs={{0,8},{4,12},{8,0},{12,4},{1,9},{5,13},{9,1},{13,5},{2,10},{6,14},... | collective-permute-start | bytes 884744 | tf_op jit(solution)/shard_map/ppermute | solution.py:326
  29.7 8.4 %collective-permute-start.8 = (bf16[96,1536]{1,0:T(8,128)(2,1)S(1)}, bf16[96,1536]{1,0:T(8,128)(2,1)S(1)}, u32[]{:S(2)}, u32[]{:S(2)}) collective-permute-start(bf16[96,1536]{1,0:T(8,128)(2,1)S(1)} %get-tuple-element.36.refs_5_), channel_id=1, source_target_pairs={{0,4},{4,0},{8,12},{12,8},{1,5},{5,1},{9,13},{13,9},{2,6},{6,2},{1... | collective-permute-start | bytes 884744 | tf_op jit(solution)/shard_map/ppermute | solution.py:326
  29.7 8.3 %collective-permute-start.9 = (bf16[96,1536]{1,0:T(8,128)(2,1)S(1)}, bf16[96,1536]{1,0:T(8,128)(2,1)S(1)}, u32[]{:S(2)}, u32[]{:S(2)}) collective-permute-start(bf16[96,1536]{1,0:T(8,128)(2,1)S(1)} %get-tuple-element.37), channel_id=1, source_target_pairs={{0,4},{4,0},{8,12},{12,8},{1,5},{5,1},{9,13},{13,9},{2,6},{6,2},{1... | collective-permute-start | bytes 884744 | tf_op jit(solution)/shard_map/ppermute | solution.py:326
  30.2 9.8 %collective-permute-start.7 = (bf16[2,48,1536]{2,1,0:T(8,128)(2,1)S(1)}, bf16[2,48,1536]{2,1,0:T(8,128)(2,1)S(1)}, u32[]{:S(2)}, u32[]{:S(2)}) collective-permute-start(bf16[2,48,1536]{2,1,0:T(8,128)(2,1)S(1)} %collective-permute-done.refs_5_.refs_1_.refs_2_), channel_id=1, source_target_pairs={{0,16},{16,0},{1,17},{17,1},{2,18},{18,2},{3,19},{19,3},{4,20},{20... | collective-permute-start | bytes 884744 | tf_op jit(solution)/shard_map/ppermute | solution.py:326
  31.0 14.1 %collective-permute-start.12 = (bf16[2,48,1536]{2,1,0:T(8,128)(2,1)S(1)}, bf16[2,48,1536]{2,1,0:T(8,128)(2,1)S(1)}, u32[]{:S(2)}, u32[]{:S(2)}) collective-permute-start(bf16[2,48,1536]{2,1,0:T(8,128)(2,1)S(1)} %pad_maximum_fusion.1.refs_1_), channel_id=1, source_target_pairs={{0,3},{1,2},{2,1},{3,0},{4,7},{5,6},{6,5},{7,4},{8,11},{9,10},{10,... | collective-permute-start | bytes 884744 | tf_op jit(solution)/shard_map/ppermute | solution.py:326
  38.5 21.4 %collective-permute-start.10 = (bf16[2,96,1536]{2,1,0:T(8,128)(2,1)S(1)}, bf16[2,96,1536]{2,1,0:T(8,128)(2,1)S(1)}, u32[]{:S(2)}, u32[]{:S(2)}) collective-permute-start(bf16[2,96,1536]{2,1,0:T(8,128)(2,1)S(1)} %combine.1.refs_5_), channel_id=1, source_target_pairs={{0,8},{4,12},{8,0},{12,4},{1,9},{5,13},{9,1},{13,5},{2,10},{6,14},... | collective-permute-start | bytes 1769480 | tf_op jit(solution)/shard_map/ppermute | solution.py:326
  44.0 16.8 %collective-permute-start.15 = (bf16[2,96,1536]{2,1,0:T(8,128)(2,1)S(1)}, bf16[2,96,1536]{2,1,0:T(8,128)(2,1)S(1)}, u32[]{:S(2)}, u32[]{:S(2)}) collective-permute-start(bf16[2,96,1536]{2,1,0:T(8,128)(2,1)S(1)} %sums_send.6.refs_5_), channel_id=1, source_target_pairs={{0,4},{4,0},{8,12},{12,8},{1,5},{5,1},{9,13},{13,9},{2,6},{6,2},{1... | collective-permute-start | bytes 1769480 | tf_op jit(solution)/shard_map/ppermute | solution.py:326
  44.1 6.5 %collective-permute-start.6 = (bf16[2,48,1536]{2,1,0:T(8,128)(2,1)S(1)}, bf16[2,48,1536]{2,1,0:T(8,128)(2,1)S(1)}, u32[]{:S(2)}, u32[]{:S(2)}) collective-permute-start(bf16[2,48,1536]{2,1,0:T(8,128)(2,1)S(1)} %activations.6.refs_4_.refs_1_.refs_3_), channel_id=1, source_target_pairs={{0,4},{4,0},{8,12},{12,8},{1,5},{5,1},{9,13},{13,9},{2,6},{6,2},{1... | collective-permute-start | bytes 884744 | tf_op jit(solution)/shard_map/ppermute | solution.py:326
  44.6 9.9 %collective-permute-start.11 = (bf16[2,48,1536]{2,1,0:T(8,128)(2,1)S(1)}, bf16[2,48,1536]{2,1,0:T(8,128)(2,1)S(1)}, u32[]{:S(2)}, u32[]{:S(2)}) collective-permute-start(bf16[2,48,1536]{2,1,0:T(8,128)(2,1)S(1)} %collective-permute-done.5.refs_6_.refs_1_.refs_4_), channel_id=1, source_target_pairs={{0,16},{16,0},{1,17},{17,1},{2,18},{18,2},{3,19},{19,3},{4,20},{20... | collective-permute-start | bytes 884744 | tf_op jit(solution)/shard_map/ppermute | solution.py:326
  45.1 14.8 %collective-permute-start.13 = (bf16[2,48,1536]{2,1,0:T(8,128)(2,1)S(1)}, bf16[2,48,1536]{2,1,0:T(8,128)(2,1)S(1)}, u32[]{:S(2)}, u32[]{:S(2)}) collective-permute-start(bf16[2,48,1536]{2,1,0:T(8,128)(2,1)S(1)} %collective-permute-done.12.refs_1_.refs_6_), channel_id=1, source_target_pairs={{0,16},{16,0},{1,17},{17,1},{2,18},{18,2},{3,19},{19,3},{4,20},{20... | collective-permute-start | bytes 884744 | tf_op jit(solution)/shard_map/ppermute | solution.py:326
  60.7 9.3 %collective-permute-start.14 = (bf16[2,96,1536]{2,1,0:T(8,128)(2,1)S(1)}, bf16[2,96,1536]{2,1,0:T(8,128)(2,1)S(1)}, u32[]{:S(2)}, u32[]{:S(2)}) collective-permute-start(bf16[2,96,1536]{2,1,0:T(8,128)(2,1)S(1)} %activations.7.refs_7_.refs_1_.refs_4_), channel_id=1, source_target_pairs={{0,4},{4,0},{8,12},{12,8},{1,5},{5,1},{9,13},{13,9},{2,6},{6,2},{1... | collective-permute-start | bytes 1769480 | tf_op jit(solution)/shard_map/ppermute | solution.py:326
  61.0 15.8 %collective-permute-start.17 = (bf16[2,96,1536]{2,1,0:T(8,128)(2,1)S(1)}, bf16[2,96,1536]{2,1,0:T(8,128)(2,1)S(1)}, u32[]{:S(2)}, u32[]{:S(2)}) collective-permute-start(bf16[2,96,1536]{2,1,0:T(8,128)(2,1)S(1)} %pad_maximum_fusion.refs_6_), channel_id=1, source_target_pairs={{0,8},{4,12},{8,0},{12,4},{1,9},{5,13},{9,1},{13,5},{2,10},{6,14},... | collective-permute-start | bytes 1769480 | tf_op jit(solution)/shard_map/ppermute | solution.py:326
  65.5 12.1 %collective-permute-start.19 = (bf16[144,1536]{1,0:T(8,128)(2,1)S(1)}, bf16[144,1536]{1,0:T(8,128)(2,1)S(1)}, u32[]{:S(2)}, u32[]{:S(2)}) collective-permute-start(bf16[144,1536]{1,0:T(8,128)(2,1)S(1)} %get-tuple-element.38.refs_6_), channel_id=1, source_target_pairs={{0,4},{4,0},{8,12},{12,8},{1,5},{5,1},{9,13},{13,9},{2,6},{6,2},{1... | collective-permute-start | bytes 1327112 | tf_op jit(solution)/shard_map/ppermute | solution.py:326
  65.8 11.9 %collective-permute-start.20 = (bf16[144,1536]{1,0:T(8,128)(2,1)S(1)}, bf16[144,1536]{1,0:T(8,128)(2,1)S(1)}, u32[]{:S(2)}, u32[]{:S(2)}) collective-permute-start(bf16[144,1536]{1,0:T(8,128)(2,1)S(1)} %get-tuple-element.41), channel_id=1, source_target_pairs={{0,4},{4,0},{8,12},{12,8},{1,5},{5,1},{9,13},{13,9},{2,6},{6,2},{1... | collective-permute-start | bytes 1327112 | tf_op jit(solution)/shard_map/ppermute | solution.py:326
  77.5 2.1 %collective-permute-start.18 = (bf16[2,96,1536]{2,1,0:T(8,128)(2,1)S(1)}, bf16[2,96,1536]{2,1,0:T(8,128)(2,1)S(1)}, u32[]{:S(2)}, u32[]{:S(2)}) collective-permute-start(bf16[2,96,1536]{2,1,0:T(8,128)(2,1)S(1)} %activations.8.refs_12_.refs_1_.refs_5_), channel_id=1, source_target_pairs={{0,4},{4,0},{8,12},{12,8},{1,5},{5,1},{9,13},{13,9},{2,6},{6,2},{1... | collective-permute-start | bytes 1769480 | tf_op jit(solution)/shard_map/ppermute | solution.py:326
  78.0 9.9 %collective-permute-start.25 = (bf16[2,144,512]{2,1,0:T(8,128)(2,1)S(1)}, bf16[2,144,512]{2,1,0:T(8,128)(2,1)S(1)}, u32[]{:S(2)}, u32[]{:S(2)}) collective-permute-start(bf16[2,144,512]{2,1,0:T(8,128)(2,1)S(1)} %pad_maximum_fusion.5.refs_11_), channel_id=1, source_target_pairs={{0,8},{4,12},{8,0},{12,4},{1,9},{5,13},{9,1},{13,5},{2,10},{6,14},... | collective-permute-start | bytes 884744 | tf_op jit(solution)/shard_map/ppermute | solution.py:326
  83.6 8.6 %collective-permute-start.21 = (bf16[48,1536]{1,0:T(8,128)(2,1)S(1)}, bf16[48,1536]{1,0:T(8,128)(2,1)S(1)}, u32[]{:S(2)}, u32[]{:S(2)}) collective-permute-start(bf16[48,1536]{1,0:T(8,128)(2,1)S(1)} %get-tuple-element.43), channel_id=1, source_target_pairs={{0,16},{16,0},{1,17},{17,1},{2,18},{18,2},{3,19},{19,3},{4,20},{20... | collective-permute-start | bytes 442376 | tf_op jit(solution)/shard_map/ppermute | solution.py:326
  84.2 13.6 %collective-permute-start.24 = (bf16[2,144,512]{2,1,0:T(8,128)(2,1)S(1)}, bf16[2,144,512]{2,1,0:T(8,128)(2,1)S(1)}, u32[]{:S(2)}, u32[]{:S(2)}) collective-permute-start(bf16[2,144,512]{2,1,0:T(8,128)(2,1)S(1)} %pad_maximum_fusion.4.refs_10_), channel_id=1, source_target_pairs={{0,8},{4,12},{8,0},{12,4},{1,9},{5,13},{9,1},{13,5},{2,10},{6,14},... | collective-permute-start | bytes 884744 | tf_op jit(solution)/shard_map/ppermute | solution.py:326
  88.3 3.9 %collective-permute-start.26 = (bf16[2,144,512]{2,1,0:T(8,128)(2,1)S(1)}, bf16[2,144,512]{2,1,0:T(8,128)(2,1)S(1)}, u32[]{:S(2)}, u32[]{:S(2)}) collective-permute-start(bf16[2,144,512]{2,1,0:T(8,128)(2,1)S(1)} %activations.9.refs_6_.refs_7_.refs_1_), channel_id=1, source_target_pairs={{0,4},{4,0},{8,12},{12,8},{1,5},{5,1},{9,13},{13,9},{2,6},{6,2},{1... | collective-permute-start | bytes 884744 | tf_op jit(solution)/shard_map/ppermute | solution.py:326
  98.2 4.6 %collective-permute-start.27 = (bf16[2,144,512]{2,1,0:T(8,128)(2,1)S(1)}, bf16[2,144,512]{2,1,0:T(8,128)(2,1)S(1)}, u32[]{:S(2)}, u32[]{:S(2)}) collective-permute-start(bf16[2,144,512]{2,1,0:T(8,128)(2,1)S(1)} %activations.10.refs_6_.refs_9_.refs_1_), channel_id=1, source_target_pairs={{0,4},{4,0},{8,12},{12,8},{1,5},{5,1},{9,13},{13,9},{2,6},{6,2},{1... | collective-permute-start | bytes 884744 | tf_op jit(solution)/shard_map/ppermute | solution.py:326
  98.8 9.8 %collective-permute-start.23 = (bf16[2,144,512]{2,1,0:T(8,128)(2,1)S(1)}, bf16[2,144,512]{2,1,0:T(8,128)(2,1)S(1)}, u32[]{:S(2)}, u32[]{:S(2)}) collective-permute-start(bf16[2,144,512]{2,1,0:T(8,128)(2,1)S(1)} %pad_maximum_fusion.3.refs_9_), channel_id=1, source_target_pairs={{0,8},{4,12},{8,0},{12,4},{1,9},{5,13},{9,1},{13,5},{2,10},{6,14},... | collective-permute-start | bytes 884744 | tf_op jit(solution)/shard_map/ppermute | solution.py:326
  108.9 1.6 %collective-permute-start.28 = (bf16[2,144,512]{2,1,0:T(8,128)(2,1)S(1)}, bf16[2,144,512]{2,1,0:T(8,128)(2,1)S(1)}, u32[]{:S(2)}, u32[]{:S(2)}) collective-permute-start(bf16[2,144,512]{2,1,0:T(8,128)(2,1)S(1)} %activations.11.refs_1_.refs_6_), channel_id=1, source_target_pairs={{0,4},{4,0},{8,12},{12,8},{1,5},{5,1},{9,13},{13,9},{2,6},{6,2},{1... | collective-permute-start | bytes 884744 | tf_op jit(solution)/shard_map/ppermute | solution.py:326
  112.4 9.9 %collective-permute-start.29 = (bf16[96,1536]{1,0:T(8,128)(2,1)S(1)}, bf16[96,1536]{1,0:T(8,128)(2,1)S(1)}, u32[]{:S(2)}, u32[]{:S(2)}) collective-permute-start(bf16[96,1536]{1,0:T(8,128)(2,1)S(1)} %get-tuple-element.56), channel_id=1, source_target_pairs={{0,16},{16,0},{1,17},{17,1},{2,18},{18,2},{3,19},{19,3},{4,20},{20... | collective-permute-start | bytes 884744 | tf_op jit(solution)/shard_map/ppermute | solution.py:326
  112.8 19.3 %collective-permute-start.16 = (bf16[48,1536]{1,0:T(8,128)(2,1)S(1)}, bf16[48,1536]{1,0:T(8,128)(2,1)S(1)}, u32[]{:S(2)}, u32[]{:S(2)}) collective-permute-start(bf16[48,1536]{1,0:T(8,128)(2,1)S(1)} %get-tuple-element.39), channel_id=1, source_target_pairs={{0,16},{16,0},{1,17},{17,1},{2,18},{18,2},{3,19},{19,3},{4,20},{20... | collective-permute-start | bytes 442376 | tf_op jit(solution)/shard_map/ppermute | solution.py:326
  114.5 17.6 %collective-permute-start.22 = (bf16[48,1536]{1,0:T(8,128)(2,1)S(1)}, bf16[48,1536]{1,0:T(8,128)(2,1)S(1)}, u32[]{:S(2)}, u32[]{:S(2)}) collective-permute-start(bf16[48,1536]{1,0:T(8,128)(2,1)S(1)} %add_convert_fusion.1.refs_10_), channel_id=1, source_target_pairs={{0,1},{1,0},{2,3},{3,2},{4,5},{5,4},{6,7},{7,6},{8,9},{9,8},{10,11... | collective-permute-start | bytes 442376 | tf_op jit(solution)/shard_map/ppermute | solution.py:326
  122.5 10.9 %collective-permute-start.30 = (bf16[48,1536]{1,0:T(8,128)(2,1)S(1)}, bf16[48,1536]{1,0:T(8,128)(2,1)S(1)}, u32[]{:S(2)}, u32[]{:S(2)}) collective-permute-start(bf16[48,1536]{1,0:T(8,128)(2,1)S(1)} %get-tuple-element.76.refs_10_), channel_id=1, source_target_pairs={{0,2},{1,3},{2,0},{3,1},{4,6},{5,7},{6,4},{7,5},{8,10},{9,11},{10,... | collective-permute-start | bytes 442376 | tf_op jit(solution)/shard_map/ppermute | solution.py:326
  122.5 10.9 %collective-permute-start.31 = (bf16[48,1536]{1,0:T(8,128)(2,1)S(1)}, bf16[48,1536]{1,0:T(8,128)(2,1)S(1)}, u32[]{:S(2)}, u32[]{:S(2)}) collective-permute-start(bf16[48,1536]{1,0:T(8,128)(2,1)S(1)} %get-tuple-element.77.refs_11_), channel_id=1, source_target_pairs={{0,3},{1,2},{2,1},{3,0},{4,7},{5,6},{6,5},{7,4},{8,11},{9,10},{10,... | collective-permute-start | bytes 442376 | tf_op jit(solution)/shard_map/ppermute | solution.py:326

commit v4 on v3

--- a/solution.py
+++ b/solution.py
@@ -91,10 +91,10 @@
     return core_ref[0] if side == 0 else 1 - core_ref[0]
 
 
-def partial_sums(core, units, up, down, side, start, width, apart, after=()):
+def partial_sums(core, units, up, down, side, apart, load, after=()):
     _, rows, depth = units[0].shape
     tokens = rows * len(units)
-    half = up.shape[1] // 2
+    width = up.shape[1] // 2 if load else up.shape[1]
     tile = tile_of(width, 256)
     dtype = BF16 if side else F32
 
@@ -107,6 +107,9 @@
             for n, ref in enumerate(unit_refs):
                 acts[:, n * rows : (n + 1) * rows, :] = ref[...]
 
+        if load:
+            out_refs[-2][...] = up_ref[...]
+            out_refs[-1][...] = down_ref[...]
         preact = contract(acts[0], up_ref[...], 1, 0)
         grad_hidden = contract(acts[1], down_ref[...], 1, 1)
         if apart:
@@ -117,7 +120,7 @@
             out_refs[0][1] = grad_hidden.astype(dtype)
 
     def place(i, c):
-        return side_of(c, side) * (half // tile) + start // tile + i
+        return side_of(c, side) * (width // tile) + i if load else i
 
     if apart:
         outs = [jax.ShapeDtypeStruct((tokens, width), dtype)] * 2
@@ -125,6 +128,13 @@
     else:
         outs = [jax.ShapeDtypeStruct((2, tokens, width), dtype)]
         specs = [pl.BlockSpec((2, tokens, tile), lambda i, c: (0, 0, i))]
+    if load:
+        outs += [jax.ShapeDtypeStruct((depth, width), BF16), jax.ShapeDtypeStruct((width, depth), BF16)]
+        specs += [
+            pl.BlockSpec((depth, tile), lambda i, c: (0, i)),
+            pl.BlockSpec((tile, depth), lambda i, c: (i, 0)),
+        ]
+        up, down = (pltpu.with_memory_space_constraint(array, pltpu.HBM) for array in (up, down))
 
     return call(
         body,
@@ -204,43 +214,69 @@
     )
 
 
-def back(core, keep, near, up, start, before, leave, after=()):
-    _, tokens, width = keep.shape
-    depth, half = up.shape[0], up.shape[1] // 2
+def back(core, acts, ups, start, before, order, leave, after=()):
+    width = acts[0][0].shape[2]
+    tokens = sum(keep.shape[1] for keep, _ in acts)
+    depth = ups[0].shape[0]
     tile = tile_of(depth, 512)
-    act = pl.BlockSpec((1, tokens, width), lambda i, c: (1, 0, 0))
-
-    def body(core_ref, keep_ref, near_ref, up_keep, up_near, *refs):
-        part = contract(keep_ref[0], up_keep[...], 1, 1) + contract(near_ref[0], up_near[...], 1, 1)
+    groups = len(acts)
+
+    def body(core_ref, *refs):
+        part = None
+        for side in range(2):
+            mine = [ref[0] for ref in refs[side * groups : (side + 1) * groups]]
+            mine = mine[0] if groups == 1 else jnp.concatenate(mine, axis=0)
+            term = contract(mine, refs[2 * groups + side][...], 1, 1)
+            part = term if part is None else part + term
+        refs = refs[2 * groups + 2 :]
         if before is not None:
             part = part + refs[0][...]
         outs = refs[(before is not None) :]
         if leave is None:
             outs[0][...] = part
         else:
-            outs[0][...] = part[:leave]
-            if leave < tokens:
-                outs[1][...] = part[leave:].astype(BF16)
-
-    def weights(side):
-        return pl.BlockSpec(
-            (tile, width), lambda i, c: (i, side_of(c, side) * (half // width) + start // width)
-        )
-
-    kinds = [(tokens if leave is None else leave, F32)]
-    if leave is not None and leave < tokens:
-        kinds.append((tokens - leave, BF16))
-    return call(
-        body,
-        core,
-        [keep, near, up, up] + ([] if before is None else [before]),
-        [act, act, weights(0), weights(1)]
+            rows = tokens // len(order)
+            part = [part[n * rows : (n + 1) * rows] for n in order]
+            outs[0][...] = jnp.concatenate(part[:leave], axis=0) if leave > 1 else part[0]
+            outs[1][...] = jnp.concatenate(part[leave:], axis=0).astype(BF16)
+
+    kinds = [(tokens, F32)]
+    if leave is not None:
+        rows = tokens // len(order)
+        kinds = [(leave * rows, F32), (tokens - leave * rows, BF16)]
+    operands = [which[side] for side in range(2) for which in acts]
+    return call(
+        body,
+        core,
+        [*operands, *ups] + ([] if before is None else [before]),
+        [pl.BlockSpec((1, array.shape[1], width), lambda i, c: (1, 0, 0)) for array in operands]
+        + [pl.BlockSpec((tile, width), lambda i, c: (i, start // width))] * 2
         + ([] if before is None else [pl.BlockSpec((tokens, tile), lambda i, c: (0, i))]),
         [jax.ShapeDtypeStruct((rows, depth), dtype) for rows, dtype in kinds],
         [pl.BlockSpec((rows, tile), lambda i, c: (0, i)) for rows, _ in kinds],
         (depth // tile,),
         (4 * tokens * depth * width, 4 * depth * width + 4 * tokens * depth),
         "back",
+        after,
+    )
+
+
+def fold(core, stay, near, after=()):
+    rows, depth = stay.shape
+
+    def body(core_ref, stay_ref, near_ref, out_ref):
+        out_ref[...] = (stay_ref[...] + near_ref[...].astype(F32)).astype(BF16)
+
+    return call(
+        body,
+        core,
+        [stay, near],
+        [whole(stay.shape)] * 2,
+        jax.ShapeDtypeStruct(stay.shape, BF16),
+        whole(stay.shape),
+        (1,),
+        (rows * depth, 8 * rows * depth),
+        "fold",
         after,
     )
 
@@ -268,37 +304,49 @@
     )
 
 
-def weight_grads(core, inputs_t, cotan, side, acts, start, width, shape, outputs, after=()):
+def weight_grads(core, inputs_t, cotan, sides, acts, start, width, shape, outputs, after=()):
     depth, full = shape
     tokens = cotan.shape[0]
     half = full // 2
     tile = tile_of(width, 256)
-    groups = len(acts)
+    steps = width // tile
+    groups = len(acts[0])
 
     def body(core_ref, inputs_ref, cotan_ref, *refs):
         up_out, down_out, done = refs[-3:]
         done[...] = jnp.zeros_like(done)
-        hidden = jnp.concatenate([ref[0] for ref in refs[:groups]], axis=0)
-        grad = jnp.concatenate([ref[1] for ref in refs[:groups]], axis=0)
-        up_out[...] = contract(inputs_ref[...], grad, 1, 0)
-        down_out[...] = contract(hidden, cotan_ref[...], 0, 0)
+        for order in range(len(sides)):
+            mine = refs[order * groups : (order + 1) * groups]
+
+            @pl.when(pl.program_id(0) // steps == order)
+            def _(mine=mine):
+                hidden = jnp.concatenate([ref[0] for ref in mine], axis=0)
+                grad = jnp.concatenate([ref[1] for ref in mine], axis=0)
+                up_out[...] = contract(inputs_ref[...], grad, 1, 0)
+                down_out[...] = contract(hidden, cotan_ref[...], 0, 0)
 
     def place(i, c):
-        return side_of(c, side) * (half // tile) + start // tile + i
+        which = side_of(c, sides[0])
+        if len(sides) > 1:
+            which = jnp.where(i // steps == 0, which, 1 - which)
+        return which * (half // tile) + start // tile + i % steps
 
     operands = [inputs_t, cotan]
     specs = [whole(inputs_t.shape), whole(cotan.shape)]
-    for array, offset in acts:
-        first = offset // tile
-        operands.append(array)
-        specs.append(
-            pl.BlockSpec((2, array.shape[1], tile), lambda i, c, first=first: (0, 0, first + i))
-        )
+    for order in range(len(sides)):
+        for array, offset in acts[order]:
+
+            def index(i, c, order=order, first=offset // tile):
+                return (0, 0, first + jnp.clip(i - order * steps, 0, steps - 1))
+
+            operands.append(array)
+            specs.append(pl.BlockSpec((2, array.shape[1], tile), index))
     aliases = None
     if outputs is not None:
         aliases = {len(operands) + 1: 0, len(operands) + 2: 1}
         operands += list(outputs)
         specs += [pl.BlockSpec(memory_space=pl.ANY)] * 2
+    many = width * len(sides)
     return call(
         body,
         core,
@@ -314,8 +362,8 @@
             pl.BlockSpec((tile, depth), lambda i, c: (place(i, c), 0)),
             whole((8, 128)),
         ],
-        (width // tile,),
-        (4 * tokens * depth * width, 8 * depth * width),
+        (steps * len(sides),),
+        (4 * tokens * depth * many, 8 * depth * many),
         "weight_grads",
         after,
         aliases=aliases,
@@ -335,25 +383,36 @@
 
     unit = {(0, 0): jnp.stack([inputs, cotangent])}
     unit[0, 1] = swap(unit[0, 0], "gx", 2, 1)
+    unit[1, 0] = swap(unit[0, 0], "gz", 4, 1)
+    z = lax.axis_index("gz")
+    middle = (z == 1) | (z == 2)
+    across, outward = [(1, 2), (2, 1)], [(1, 0), (2, 3)]
+    first = lax.ppermute(unit[0, 0], "gz", across)
+    second = lax.ppermute(unit[1, 0], "gz", across)
+    first_on = lax.ppermute(first, "gz", outward)
+    second_on = lax.ppermute(second, "gz", outward)
+    unit[2, 0] = jnp.where(middle, second, first_on)
+    unit[3, 0] = jnp.where(middle, first, second_on)
     for d in (1, 2, 3):
-        unit[d, 0] = swap(unit[0, 0], "gz", 4, d)
         unit[d, 1] = swap(unit[d, 0], "gx", 2, 1)
     groups = [
-        [unit[0, 0]],
-        [unit[1, 0], unit[0, 1]],
-        [unit[2, 0], unit[1, 1]],
-        [unit[3, 0], unit[2, 1], unit[3, 1]],
+        [unit[0, 0], unit[0, 1]],
+        [unit[1, 0], unit[1, 1]],
+        [unit[2, 0], unit[3, 0], unit[2, 1], unit[3, 1]],
     ]
 
-    pieces = [(g, 0, half) for g in range(3)] + [(3, j * width, width) for j in range(chunks)]
-    near, keep, far, act, act_near = {}, {}, {}, {}, {}
+    pieces = [(0, 0, half), (1, 0, half)] + [(2, j * width, width) for j in range(chunks)]
+    near, keep, far, act, act_near, ups, downs = {}, {}, {}, {}, {}, {}, {}
 
     def sums(group, side, after):
-        weights = (up, down)
-        if group == 0:
-            weights = [pltpu.with_memory_space_constraint(array, pltpu.HBM) for array in weights]
-        apart = side == 1 and group != 2
-        return partial_sums(core, groups[group], *weights, side, 0, half, apart, after)
+        if group:
+            return partial_sums(
+                core, groups[group], ups[side], downs[side], side, side == 1, False, after
+            )
+        *out, ups[side], downs[side] = partial_sums(
+            core, groups[group], up, down, side, side == 1, True, after
+        )
+        return out
 
     def product(group, after, between=()):
         out = sums(group, 1, after)
@@ -364,12 +423,11 @@
     def cross(n, after=()):
         group, start, size = pieces[n]
         span = slice(start, start + size)
-        parts = near[group] if len(near[group]) > 1 else near[group][0]
         if after:
-            chip = combine(core, keep[group], parts, after)
+            chip = combine(core, keep[group], near[group], after)
         else:
             chip = jnp.stack([
-                (keep[group][which, :, span] + parts[which][:, span].astype(F32)).astype(BF16)
+                (keep[group][which, :, span] + near[group][which][:, span].astype(F32)).astype(BF16)
                 for which in range(2)
             ])
         far[n] = swap(chip, "gy", 4, 2)
@@ -381,60 +439,56 @@
         act_near[n] = swap(act[n], "gy", 4, 1)
         return [act[n]]
 
-    def inward(n, part, leave, after):
-        group, start, _ = pieces[n]
-        return back(core, act[n], act_near[n], up, start, part, leave, after)
+    def inward(many, start, part, order, leave, after):
+        which = [(act[n], act_near[n]) for n in many]
+        return back(core, which, (ups[0], ups[1]), start, part, order, leave, after)
 
     outputs = None
 
-    def gradients(j, side, after):
-        array = act_near if side else act
-        acts = [(array[n], j * width) for n in range(3)] + [(array[3 + j], 0)]
+    def gradients(j, sides, after):
+        acts = [
+            [(array[n], j * width) for n in range(2)] + [(array[2 + j], 0)]
+            for array in (act, act_near)
+        ]
+        acts = [acts[side] for side in sides]
         return weight_grads(
-            core, inputs_t, cotan, side, acts, j * width, width, up.shape, outputs, after
+            core, inputs_t, cotan, sides, acts, j * width, width, up.shape, outputs, after
         )
 
-    def exchange(value):
-        return swap(value, "gx", 2, 1).astype(F32)
-
-    last = product(0, (), [unit[1, 0], unit[0, 1]])
-    last = cross(0)
-    last = product(1, last, [unit[2, 0]])
-    last = ready(0, last)
-    last = cross(1, last)
+    last = product(0, (), [unit[1, 0], first])
+    last = cross(0, [unit[1, 1], first_on, second])
+    last = product(1, last, [second_on])
+    last = ready(0, last + [unit[2, 1]])
+    last = cross(1, last + [])
     last = product(2, last)
-    total, = last = inward(0, None, rows, last)
-    last = ready(1, [*last, unit[2, 1], unit[3, 1]])
-    last = cross(2) + last
-    last = product(3, last)
-    stay1, go1 = inward(1, None, rows, last)
-    last = ready(2, [stay1])
+    last = ready(1, last)
     for j in range(chunks):
-        last = cross(3 + j) + last
+        last = cross(2 + j) + last
     inputs_t, cotan = arrange(core, [u for group in groups for u in group], last)
-    stay2, go2 = inward(2, None, rows, [inputs_t])
-    total = total + exchange(go1)
-    back1 = (stay1 + exchange(go2)).astype(BF16)
-    far1 = swap(back1, "gz", 4, 1)
-
-    part, last = None, [stay2]
+    stay1, go1 = inward((0, 1), 0, None, (0, 2, 1, 3), 2, [inputs_t])
+    near1 = swap(go1, "gx", 2, 1)
+
+    part, last = None, [stay1]
     for j in range(chunks):
-        n = 3 + j
+        n = 2 + j
         last = ready(n, last)
+        if j == 0:
+            total = stay1[:rows] + near1[:rows].astype(F32)
+            back1 = fold(core, stay1[rows:], near1[rows:], last)
+            far1 = swap(back1, "gz", 4, 1)
+            last = [back1]
         if j + 1 < chunks:
-            *outputs, done = gradients(j, 0, last)
-            part, = inward(n, part, None, [done])
-            *outputs, done = gradients(j, 1, [part] if j else [part, back1])
+            last = part, = inward((n,), j * width, part, None, None, last)
+            *outputs, done = gradients(j, (0, 1), last)
             last = [done]
         else:
-            stay3, go3 = inward(n, part, rows, last)
-            near3 = exchange(go3)
-            *outputs, done = gradients(j, 0, [stay3])
-            back2 = (stay2 + near3[:rows]).astype(BF16)
-            back3 = (stay3 + near3[rows:]).astype(BF16)
-            far2 = swap(back2, "gz", 4, 2)
-            far3 = swap(back3, "gz", 4, 3)
-            *outputs, done = gradients(j, 1, [done, back2, back3])
+            stay2, go2 = inward((n,), j * width, part, (0, 1, 2, 3), 2, last)
+            near2 = swap(go2, "gx", 2, 1)
+            *outputs, done = gradients(j, (0,), [stay2])
+            back2 = fold(core, stay2, near2, [done])
+            far2 = swap(back2[:rows], "gz", 4, 2)
+            far3 = swap(back2[rows:], "gz", 4, 3)
+            *outputs, done = gradients(j, (1,), [back2])
     total = total + far1.astype(F32) + far2.astype(F32) + far3.astype(F32)
     return (total.astype(BF16), *outputs)
 

time: 135 us -> 137 us (1.015)
  Pallas kernels: 82.3 us -> 63.6 us
  waiting for transfers between devices: 22.4 us -> 34.7 us
  starting transfers between devices: 25.7 us -> 34.7 us
    pallas_call x28 -> x24, Pallas kernels: 82.3 us -> 63.6 us  [call(): pl.pallas_call(kernel, grid_spec=pltpu.PrefetchScalarGridSpec(num_scalar_...]
    ppermute x32 -> x26, waiting for transfers between devices: 22.4 us -> 30.1 us  [swap(): return lax.ppermute(value, axis, [(i, i ^ bits) for i in range(size)])]
    ppermute x32 -> x26, starting transfers between devices: 25.7 us -> 30.8 us  [swap(): return lax.ppermute(value, axis, [(i, i ^ bits) for i in range(size)])]
    ppermute x0 -> x4, waiting for transfers between devices: none -> 4.59 us  [the longest x1 4.58 us: cube_body(): second_on = lax.ppermute(second, 'gz', outward)]
    ppermute x0 -> x4, starting transfers between devices: none -> 3.92 us  [the longest x1 1.29 us: cube_body(): first_on = lax.ppermute(first, 'gz', outward)]
  transfers between devices with their start and end apart: 32 -> 30, of which waited for: 8 -> 12; matrix products, arithmetic and copies ran while one was open for 1% -> 0% of each run, Pallas kernels for 59% -> 44%
where the time goes in v4:
time: 137 us; the launch traced here: 136 us
  Pallas kernels  63.6 us (46%)
  starting transfers between devices  34.7 us (25%)
  waiting for transfers between devices  34.7 us (25%)
  other arithmetic  2.39 us (2%)
    pallas_call x24, Pallas kernels, call(): pl.pallas_call(kernel, grid_spec=pltpu.PrefetchScalarGridSpec(num_scalar_...  63.6 us
    ppermute x26, starting transfers between devices, swap(): return lax.ppermute(value, axis, [(i, i ^ bits) for i in range(size)])  30.8 us
    ppermute x26, waiting for transfers between devices, swap(): return lax.ppermute(value, axis, [(i, i ^ bits) for i in range(size)])  30.1 us
    ppermute x1, waiting for transfers between devices, cube_body(): second_on = lax.ppermute(second, 'gz', outward)  4.58 us
  transfers between devices with their start and end apart: 30, of which 12 were waited for; matrix products, arithmetic and copies ran while one was open for 0% of the time, Pallas kernels for 44%

profile of v4, /device:TPU:0, one launch (start us, length us, event | category | flops | bytes accessed | tf_op | source)
XLA Modules:
  0.0 136.5 jit_solution(6941427459677461230)
XLA Ops:
  0.6 1.0 pad_maximum_fusion.3.refs_1_
  1.6 3.1 %collective-permute-start.1 = (bf16[2,48,1536]{2,1,0:T(8,128)(2,1)S(1)}, bf16[2,48,1536]{2,1,0:T(8,128)(2,1)S(1)}, u32[]{:S(2)}, u32[]{:S(2)}) collective-permute-start(bf16[2,48,1536]{2,1,0:T(8,128)(2,1)S(1)} %pad_maximum_fusion.3.refs_1_), channel_id=1, source_target_pairs={{0,1},{1,0},{2,3},{3,2},{4,5},{5,4},{6,7},{7,6},{8,9},{9,8},{10,11... | collective-permute-start | bytes 884744 | tf_op jit(solution)/shard_map/ppermute | solution.py:374
  4.7 0.7 collective-permute-start.2
  5.4 1.6 %collective-permute-start = (bf16[2,48,1536]{2,1,0:T(8,128)(2,1)S(1)}, bf16[2,48,1536]{2,1,0:T(8,128)(2,1)S(1)}, u32[]{:S(2)}, u32[]{:S(2)}) collective-permute-start(bf16[2,48,1536]{2,1,0:T(8,128)(2,1)S(1)} %pad_maximum_fusion.3.refs_1_), channel_id=1, source_target_pairs={{0,16},{16,0},{1,17},{17,1},{2,18},{18,2},{3,19},{19,3},{4,20},{20... | collective-permute-start | bytes 884744 | tf_op jit(solution)/shard_map/ppermute | solution.py:374
  7.0 4.8 %collective-permute-done.1.refs_6_.refs_1_.refs_3_ = bf16[2,48,1536]{2,1,0:T(8,128)(2,1)S(1)} collective-permute-done((bf16[2,48,1536]{2,1,0:T(8,128)(2,1)S(1)}, bf16[2,48,1536]{2,1,0:T(8,128)(2,1)S(1)}, u32[]{:S(2)}, u32[]{:S(2)}) %collective-permute-start.1) | collective-permute-done | bytes 294944 | tf_op jit(solution)/shard_map/ppermute | solution.py:374
  11.7 0.7 collective-permute-start.7
  12.4 1.3 collective-permute-start.6
  13.7 0.2 collective-permute-done.refs_2_
  13.9 7.1 %sums_send.3 = (bf16[96,1536]{1,0:T(8,128)(2,1)S(1)}, bf16[96,1536]{1,0:T(8,128)(2,1)S(1)}, bf16[1536,1536]{1,0:T(8,128)(2,1)S(1)}, bf16[1536,1536]{1,0:T(8,128)(2,1)S(1)}) custom-call(s32[1]{0:T(128)} %bitcast.refs_0_, bf16[2,48,1536]{2,1,0:T(8,128)(2,1)S(1)} %pad_maximum_fusion.3.refs_1_, bf16[2,48,1536]{2,1,0:T(8,128)(2,1)S(1)} %collective-permute-done.refs_2_, ...), custom_call_target="tpu_custom_call" | custom-call | flops 905969664 | bytes 9437184 | tf_op jit(solution)/shard_map/sums_send/pallas_call | solution.py:67
  21.1 0.5 collective-permute-start.3
  21.6 1.5 %collective-permute-start.5 = (bf16[2,48,1536]{2,1,0:T(8,128)(2,1)S(1)}, bf16[2,48,1536]{2,1,0:T(8,128)(2,1)S(1)}, u32[]{:S(2)}, u32[]{:S(2)}) collective-permute-start(bf16[2,48,1536]{2,1,0:T(8,128)(2,1)S(1)} %collective-permute-done.1.refs_6_.refs_1_.refs_3_), channel_id=1, source_target_pairs={{0,16},{16,0},{1,17},{17,1},{2,18},{18,2},{3,19},{19,3},{4,20},{20... | collective-permute-start | bytes 884744 | tf_op jit(solution)/shard_map/ppermute | solution.py:374
  23.1 7.1 %sums_keep.3 = (f32[2,96,1536]{2,1,0:T(8,128)S(1)}, bf16[1536,1536]{1,0:T(8,128)(2,1)S(1)}, bf16[1536,1536]{1,0:T(8,128)(2,1)S(1)}) custom-call(s32[1]{0:T(128)} %bitcast.refs_0_, bf16[2,48,1536]{2,1,0:T(8,128)(2,1)S(1)} %pad_maximum_fusion.3.refs_1_, bf16[2,48,1536]{2,1,0:T(8,128)(2,1)S(1)} %collective-permute-done.refs_2_, bf16[1536,3072]{1,0:T(8,128)(2,1)} %refs_3_.3, ...), custom_call_target="tpu_custom_call" | custom-call | flops 905969664 | bytes 9437184 | tf_op jit(solution)/shard_map/sums_keep/pallas_call | solution.py:67
  30.3 1.3 collective-permute-start.9
  31.6 0.6 collective-permute-start.10
  32.2 0.4 combine.2.refs_5_
  32.6 1.6 %collective-permute-start.8 = (bf16[2,96,1536]{2,1,0:T(8,128)(2,1)S(1)}, bf16[2,96,1536]{2,1,0:T(8,128)(2,1)S(1)}, u32[]{:S(2)}, u32[]{:S(2)}) collective-permute-start(bf16[2,96,1536]{2,1,0:T(8,128)(2,1)S(1)} %combine.2.refs_5_), channel_id=1, source_target_pairs={{0,8},{4,12},{8,0},{12,4},{1,9},{5,13},{9,1},{13,5},{2,10},{6,14},... | collective-permute-start | bytes 1769480 | tf_op jit(solution)/shard_map/ppermute | solution.py:374
  34.2 3.6 %sums_send.4 = (bf16[96,1536]{1,0:T(8,128)(2,1)S(1)}, bf16[96,1536]{1,0:T(8,128)(2,1)S(1)}) custom-call(s32[1]{0:T(128)} %bitcast.refs_0_, bf16[2,48,1536]{2,1,0:T(8,128)(2,1)S(1)} %collective-permute-done.1.refs_6_.refs_1_.refs_3_, bf16[2,48,1536]{2,1,0:T(8,128)(2,1)S(1)} %collective-permute-done.5.refs_4_.refs_2_, ...), custom_call_target="tpu_custom_call" | custom-call | flops 905969664 | bytes 9437184 | tf_op jit(solution)/shard_map/sums_send/pallas_call | solution.py:67
  37.7 0.1 collective-permute-start.12
  37.8 0.5 collective-permute-start.11
  38.3 4.6 %collective-permute-done.9.refs_6_ = bf16[2,48,1536]{2,1,0:T(8,128)(2,1)S(1)} collective-permute-done((bf16[2,48,1536]{2,1,0:T(8,128)(2,1)S(1)}, bf16[2,48,1536]{2,1,0:T(8,128)(2,1)S(1)}, u32[]{:S(2)}, u32[]{:S(2)}) %collective-permute-start.9) | collective-permute-done | bytes 294944 | tf_op jit(solution)/shard_map/ppermute | solution.py:393
  42.9 0.6 collective-permute-start.14
  43.5 3.6 %sums_keep.4.refs_5_.refs_1_ = f32[2,96,1536]{2,1,0:T(8,128)S(1)} custom-call(s32[1]{0:T(128)} %bitcast.refs_0_, bf16[2,48,1536]{2,1,0:T(8,128)(2,1)S(1)} %collective-permute-done.1.refs_6_.refs_1_.refs_3_, bf16[2,48,1536]{2,1,0:T(8,128)(2,1)S(1)} %collective-permute-done.5.refs_4_.refs_2_, bf16[1536,1536]{1,0:T(8,128)(2,1)S(1)} %get-tuple-element.34.refs_3_.refs_5_, ...), custom_call_target="tpu_custom_call" | custom-call | flops 905969664 | bytes 9437184 | tf_op jit(solution)/shard_map/sums_keep/pallas_call | solution.py:67
  47.1 0.3 collective-permute-done.8.refs_4_
  47.4 0.8 activations.5.refs_4_.refs_1_.refs_3_
  48.2 0.4 combine.3.refs_7_
  48.6 1.6 %collective-permute-start.13 = (bf16[2,96,1536]{2,1,0:T(8,128)(2,1)S(1)}, bf16[2,96,1536]{2,1,0:T(8,128)(2,1)S(1)}, u32[]{:S(2)}, u32[]{:S(2)}) collective-permute-start(bf16[2,96,1536]{2,1,0:T(8,128)(2,1)S(1)} %combine.3.refs_7_), channel_id=1, source_target_pairs={{0,8},{4,12},{8,0},{12,4},{1,9},{5,13},{9,1},{13,5},{2,10},{6,14},... | collective-permute-start | bytes 1769480 | tf_op jit(solution)/shard_map/ppermute | solution.py:374
  50.2 1.0 collective-permute-done.14.refs_4_.refs_8_
  51.2 3.8 %sums_send.5 = (bf16[192,1536]{1,0:T(8,128)(2,1)S(1)}, bf16[192,1536]{1,0:T(8,128)(2,1)S(1)}) custom-call(s32[1]{0:T(128)} %bitcast.refs_0_, bf16[2,48,1536]{2,1,0:T(8,128)(2,1)S(1)} %broadcast_select_fusion.1.refs_1_.refs_5_, bf16[2,48,1536]{2,1,0:T(8,128)(2,1)S(1)} %broadcast_select_fusion.refs_2_.refs_6_, ...), custom_call_target="tpu_custom_call" | custom-call | flops 1811939328 | bytes 9437184 | tf_op jit(solution)/shard_map/sums_send/pallas_call | solution.py:67
  55.1 0.5 collective-permute-start.17
  55.6 0.1 collective-permute-start.15
  55.7 3.9 %sums_keep.5.refs_5_.refs_1_ = f32[2,192,1536]{2,1,0:T(8,128)S(1)} custom-call(s32[1]{0:T(128)} %bitcast.refs_0_, bf16[2,48,1536]{2,1,0:T(8,128)(2,1)S(1)} %broadcast_select_fusion.1.refs_1_.refs_5_, bf16[2,48,1536]{2,1,0:T(8,128)(2,1)S(1)} %broadcast_select_fusion.refs_2_.refs_6_, bf16[2,48,1536]{2,1,0:T(8,128)(2,1)S(1)} %collective-permute-done.10.refs_6_.refs_3_.refs_7_, ...), custom_call_target="tpu_custom_call" | custom-call | flops 1811939328 | bytes 9437184 | tf_op jit(solution)/shard_map/sums_keep/pallas_call | solution.py:67
  59.5 3.1 %collective-permute-done.13.refs_4_ = bf16[2,96,1536]{2,1,0:T(8,128)(2,1)S(1)} collective-permute-done((bf16[2,96,1536]{2,1,0:T(8,128)(2,1)S(1)}, bf16[2,96,1536]{2,1,0:T(8,128)(2,1)S(1)}, u32[]{:S(2)}, u32[]{:S(2)}) %collective-permute-start.13) | collective-permute-done | bytes 589856 | tf_op jit(solution)/shard_map/ppermute | solution.py:374
  62.6 0.8 activations.6.refs_12_.refs_2_.refs_4_
  63.4 0.1 collective-permute-start.16
  63.5 0.4 fusion.16
  64.0 1.6 %collective-permute-start.20 = (bf16[2,192,512]{2,1,0:T(8,128)(2,1)S(1)}, bf16[2,192,512]{2,1,0:T(8,128)(2,1)S(1)}, u32[]{:S(2)}, u32[]{:S(2)}) collective-permute-start(bf16[2,192,512]{2,1,0:T(8,128)(2,1)S(1)} %pad_maximum_fusion.2.refs_11_), channel_id=1, source_target_pairs={{0,8},{4,12},{8,0},{12,4},{1,9},{5,13},{9,1},{13,5},{2,10},{6,14},... | collective-permute-start | bytes 1179656 | tf_op jit(solution)/shard_map/ppermute | solution.py:374
  65.7 0.4 arrange.1
  66.1 3.6 %back.4 = (f32[96,1536]{1,0:T(8,128)S(1)}, bf16[96,1536]{1,0:T(8,128)(2,1)S(1)}) custom-call(s32[1]{0:T(128)} %bitcast.refs_0_, bf16[2,96,1536]{2,1,0:T(8,128)(2,1)S(1)} %activations.5.refs_4_.refs_1_.refs_3_, bf16[2,96,1536]{2,1,0:T(8,128)(2,1)S(1)} %activations.6.refs_12_.refs_2_.refs_4_, bf16[2,96,1536]{2,1,0:T(8,128)(2,1)S(1)} %collective-permute-done.15.refs_3_.refs_6_, ...), custom_call_target="tpu_custom_call" | custom-call | flops 1811939328 | bytes 10616832 | tf_op jit(solution)/shard_map/back/pallas_call | solution.py:67
  69.7 5.8 %collective-permute-done.20.refs_4_ = bf16[2,192,512]{2,1,0:T(8,128)(2,1)S(1)} collective-permute-done((bf16[2,192,512]{2,1,0:T(8,128)(2,1)S(1)}, bf16[2,192,512]{2,1,0:T(8,128)(2,1)S(1)}, u32[]{:S(2)}, u32[]{:S(2)}) %collective-permute-start.20) | collective-permute-done | bytes 393248 | tf_op jit(solution)/shard_map/ppermute | solution.py:374
  75.6 0.5 activations.7.refs_3_.refs_1_.refs_5_
  76.1 0.1 collective-permute-start.24
  76.1 1.6 %collective-permute-start.19 = (bf16[96,1536]{1,0:T(8,128)(2,1)S(1)}, bf16[96,1536]{1,0:T(8,128)(2,1)S(1)}, u32[]{:S(2)}, u32[]{:S(2)}) collective-permute-start(bf16[96,1536]{1,0:T(8,128)(2,1)S(1)} %get-tuple-element.44), channel_id=1, source_target_pairs={{0,16},{16,0},{1,17},{17,1},{2,18},{18,2},{3,19},{19,3},{4,20},{20... | collective-permute-start | bytes 884744 | tf_op jit(solution)/shard_map/ppermute | solution.py:374
  77.7 1.5 %collective-permute-start.23 = (bf16[2,192,512]{2,1,0:T(8,128)(2,1)S(1)}, bf16[2,192,512]{2,1,0:T(8,128)(2,1)S(1)}, u32[]{:S(2)}, u32[]{:S(2)}) collective-permute-start(bf16[2,192,512]{2,1,0:T(8,128)(2,1)S(1)} %pad_maximum_fusion.1.refs_10_), channel_id=1, source_target_pairs={{0,8},{4,12},{8,0},{12,4},{1,9},{5,13},{9,1},{13,5},{2,10},{6,14},... | collective-permute-start | bytes 1179656 | tf_op jit(solution)/shard_map/ppermute | solution.py:374
  79.2 6.3 %collective-permute-done.19 = bf16[96,1536]{1,0:T(8,128)(2,1)S(1)} collective-permute-done((bf16[96,1536]{1,0:T(8,128)(2,1)S(1)}, bf16[96,1536]{1,0:T(8,128)(2,1)S(1)}, u32[]{:S(2)}, u32[]{:S(2)}) %collective-permute-start.19) | collective-permute-done | bytes 294944 | tf_op jit(solution)/shard_map/ppermute | solution.py:374
  85.6 1.8 %back.5.refs_9_.refs_5_ = f32[192,1536]{1,0:T(8,128)S(1)} custom-call(s32[1]{0:T(128)} %bitcast.refs_0_, bf16[2,192,512]{2,1,0:T(8,128)(2,1)S(1)} %activations.7.refs_3_.refs_1_.refs_5_, bf16[2,192,512]{2,1,0:T(8,128)(2,1)S(1)} %collective-permute-done.24.refs_2_.refs_8_, bf16[1536,1536]{1,0:T(8,128)(2,1)S(1)} %get-tuple-element.34.refs_3_.refs_5_, ...), custom_call_target="tpu_custom_call" | custom-call | flops 603979776 | bytes 4325376 | tf_op jit(solution)/shard_map/back/pallas_call | solution.py:67
  87.5 6.6 %weight_grads.4 = (f32[1536,3072]{1,0:T(8,128)}, f32[3072,1536]{1,0:T(8,128)}, f32[8,128]{1,0:T(8,128)S(1)}) custom-call(s32[1]{0:T(128)} %bitcast.refs_0_, bf16[1536,384]{1,0:T(8,128)(2,1)S(1)} %get-tuple-element.42.refs_7_.refs_1_, bf16[384,1536]{1,0:T(8,128)(2,1)S(1)} %get-tuple-element.45.refs_2_, ...), custom_call_target="tpu_custom_call" | custom-call | flops 2415919104 | bytes 12582912 | tf_op jit(solution)/shard_map/weight_grads/pallas_call | solution.py:67
  94.1 0.5 activations.8.refs_1_.refs_6_.refs_5_
  94.7 1.6 %collective-permute-start.22 = (bf16[2,192,512]{2,1,0:T(8,128)(2,1)S(1)}, bf16[2,192,512]{2,1,0:T(8,128)(2,1)S(1)}, u32[]{:S(2)}, u32[]{:S(2)}) collective-permute-start(bf16[2,192,512]{2,1,0:T(8,128)(2,1)S(1)} %pad_maximum_fusion.refs_9_), channel_id=1, source_target_pairs={{0,8},{4,12},{8,0},{12,4},{1,9},{5,13},{9,1},{13,5},{2,10},{6,14},... | collective-permute-start | bytes 1179656 | tf_op jit(solution)/shard_map/ppermute | solution.py:374
  96.3 0.1 collective-permute-done.25.refs_2_.refs_8_
  96.4 1.9 %back.6.refs_11_.refs_5_ = f32[192,1536]{1,0:T(8,128)S(1)} custom-call(s32[1]{0:T(128)} %bitcast.refs_0_, bf16[2,192,512]{2,1,0:T(8,128)(2,1)S(1)} %activations.8.refs_1_.refs_6_.refs_5_, bf16[2,192,512]{2,1,0:T(8,128)(2,1)S(1)} %collective-permute-done.25.refs_2_.refs_8_, bf16[1536,1536]{1,0:T(8,128)(2,1)S(1)} %get-tuple-element.34.refs_3_.refs_5_, ...), custom_call_target="tpu_custom_call" | custom-call | flops 603979776 | bytes 4325376 | tf_op jit(solution)/shard_map/back/pallas_call | solution.py:67
  98.3 6.7 %weight_grads.5 = (f32[1536,3072]{1,0:T(8,128)}, f32[3072,1536]{1,0:T(8,128)}, f32[8,128]{1,0:T(8,128)S(1)}) custom-call(s32[1]{0:T(128)} %bitcast.refs_0_, bf16[1536,384]{1,0:T(8,128)(2,1)S(1)} %get-tuple-element.42.refs_7_.refs_1_, bf16[384,1536]{1,0:T(8,128)(2,1)S(1)} %get-tuple-element.45.refs_2_, ...), custom_call_target="tpu_custom_call", output_to_operand_aliasing={{0}: (9, {}), {1}: (10, {})} | custom-call | flops 2415919104 | bytes 12582912 | tf_op jit(solution)/shard_map/weight_grads/pallas_call | solution.py:67
  105.0 1.2 collective-permute-done.22.refs_4_
  106.2 0.5 activations.9.refs_1_.refs_6_.refs_5_
  106.8 1.7 %collective-permute-done.26.refs_2_.refs_5_ = bf16[2,192,512]{2,1,0:T(8,128)(2,1)S(1)} collective-permute-done((bf16[2,192,512]{2,1,0:T(8,128)(2,1)S(1)}, bf16[2,192,512]{2,1,0:T(8,128)(2,1)S(1)}, u32[]{:S(2)}, u32[]{:S(2)}) %collective-permute-start.26) | collective-permute-done | bytes 393248 | tf_op jit(solution)/shard_map/ppermute | solution.py:374
  108.5 1.9 %back.7 = (f32[96,1536]{1,0:T(8,128)S(1)}, bf16[96,1536]{1,0:T(8,128)(2,1)S(1)}) custom-call(s32[1]{0:T(128)} %bitcast.refs_0_, bf16[2,192,512]{2,1,0:T(8,128)(2,1)S(1)} %activations.9.refs_1_.refs_6_.refs_5_, bf16[2,192,512]{2,1,0:T(8,128)(2,1)S(1)} %collective-permute-done.26.refs_2_.refs_5_, bf16[1536,1536]{1,0:T(8,128)(2,1)S(1)} %get-tuple-element.34.refs_3_.refs_5_, ...), custom_call_target="tpu_custom_call" | custom-call | flops 603979776 | bytes 4325376 | tf_op jit(solution)/shard_map/back/pallas_call | solution.py:67
  110.4 1.6 %collective-permute-start.27 = (bf16[96,1536]{1,0:T(8,128)(2,1)S(1)}, bf16[96,1536]{1,0:T(8,128)(2,1)S(1)}, u32[]{:S(2)}, u32[]{:S(2)}) collective-permute-start(bf16[96,1536]{1,0:T(8,128)(2,1)S(1)} %get-tuple-element.51), channel_id=1, source_target_pairs={{0,16},{16,0},{1,17},{17,1},{2,18},{18,2},{3,19},{19,3},{4,20},{20... | collective-permute-start | bytes 884744 | tf_op jit(solution)/shard_map/ppermute | solution.py:374
  111.9 4.3 %collective-permute-start.21 = (bf16[48,1536]{1,0:T(8,128)(2,1)S(1)}, bf16[48,1536]{1,0:T(8,128)(2,1)S(1)}, u32[]{:S(2)}, u32[]{:S(2)}) collective-permute-start(bf16[48,1536]{1,0:T(8,128)(2,1)S(1)} %fold.2.refs_5_), channel_id=1, source_target_pairs={{0,1},{1,0},{2,3},{3,2},{4,5},{5,4},{6,7},{7,6},{8,9},{9,8},{10,11... | collective-permute-start | bytes 442376 | tf_op jit(solution)/shard_map/ppermute | solution.py:374
  116.2 3.8 %weight_grads.6 = (f32[1536,3072]{1,0:T(8,128)}, f32[3072,1536]{1,0:T(8,128)}, f32[8,128]{1,0:T(8,128)S(1)}) custom-call(s32[1]{0:T(128)} %bitcast.refs_0_, bf16[1536,384]{1,0:T(8,128)(2,1)S(1)} %get-tuple-element.42.refs_7_.refs_1_, bf16[384,1536]{1,0:T(8,128)(2,1)S(1)} %get-tuple-element.45.refs_2_, ...), custom_call_target="tpu_custom_call", output_to_operand_aliasing={{0}: (6, {}), {1}: (7, {})} | custom-call | flops 1207959552 | bytes 6291456 | tf_op jit(solution)/shard_map/weight_grads/pallas_call | solution.py:67
  120.1 0.1 fold.3.refs_8_
  120.2 4.5 %collective-permute-start.28 = (bf16[48,1536]{1,0:T(8,128)(2,1)S(1)}, bf16[48,1536]{1,0:T(8,128)(2,1)S(1)}, u32[]{:S(2)}, u32[]{:S(2)}) collective-permute-start(bf16[48,1536]{1,0:T(8,128)(2,1)S(1)} %get-tuple-element.68), channel_id=1, source_target_pairs={{0,2},{1,3},{2,0},{3,1},{4,6},{5,7},{6,4},{7,5},{8,10},{9,11},{10,... | collective-permute-start | bytes 442376 | tf_op jit(solution)/shard_map/ppermute | solution.py:374
  124.6 1.7 %collective-permute-start.29 = (bf16[48,1536]{1,0:T(8,128)(2,1)S(1)}, bf16[48,1536]{1,0:T(8,128)(2,1)S(1)}, u32[]{:S(2)}, u32[]{:S(2)}) collective-permute-start(bf16[48,1536]{1,0:T(8,128)(2,1)S(1)} %get-tuple-element.69), channel_id=1, source_target_pairs={{0,3},{1,2},{2,1},{3,0},{4,7},{5,6},{6,5},{7,4},{8,11},{9,10},{10,... | collective-permute-start | bytes 442376 | tf_op jit(solution)/shard_map/ppermute | solution.py:374
  126.3 3.8 %weight_grads.7 = (f32[1536,3072]{1,0:T(8,128)}, f32[3072,1536]{1,0:T(8,128)}, f32[8,128]{1,0:T(8,128)}) custom-call(s32[1]{0:T(128)} %bitcast.refs_0_, bf16[1536,384]{1,0:T(8,128)(2,1)S(1)} %get-tuple-element.42.refs_7_.refs_1_, bf16[384,1536]{1,0:T(8,128)(2,1)S(1)} %get-tuple-element.45.refs_2_, ...), custom_call_target="tpu_custom_call", output_to_operand_aliasing={{0}: (6, {}), {1}: (7, {})} | custom-call | flops 1207959552 | bytes 6291456 | tf_op jit(solution)/shard_map/weight_grads/pallas_call | solution.py:67
  130.2 5.5 %collective-permute-done.28 = bf16[48,1536]{1,0:T(8,128)(2,1)S(1)} collective-permute-done((bf16[48,1536]{1,0:T(8,128)(2,1)S(1)}, bf16[48,1536]{1,0:T(8,128)(2,1)S(1)}, u32[]{:S(2)}, u32[]{:S(2)}) %collective-permute-start.28) | collective-permute-done | bytes 147488 | tf_op jit(solution)/shard_map/ppermute | solution.py:374
  135.7 0.8 add_convert_fusion
  (31 shorter events, 0.6 us)
Async XLA Ops:
  1.6 10.1 %collective-permute-start.1 = (bf16[2,48,1536]{2,1,0:T(8,128)(2,1)S(1)}, bf16[2,48,1536]{2,1,0:T(8,128)(2,1)S(1)}, u32[]{:S(2)}, u32[]{:S(2)}) collective-permute-start(bf16[2,48,1536]{2,1,0:T(8,128)(2,1)S(1)} %pad_maximum_fusion.3.refs_1_), channel_id=1, source_target_pairs={{0,1},{1,0},{2,3},{3,2},{4,5},{5,4},{6,7},{7,6},{8,9},{9,8},{10,11... | collective-permute-start | bytes 884744 | tf_op jit(solution)/shard_map/ppermute | solution.py:374
  4.7 7.7 %collective-permute-start.2 = (bf16[2,48,1536]{2,1,0:T(8,128)(2,1)S(1)}, bf16[2,48,1536]{2,1,0:T(8,128)(2,1)S(1)}, u32[]{:S(2)}, u32[]{:S(2)}) collective-permute-start(bf16[2,48,1536]{2,1,0:T(8,128)(2,1)S(1)} %pad_maximum_fusion.3.refs_1_), channel_id=1, source_target_pairs={{1,2},{2,1},{5,6},{6,5},{9,10},{10,9},{13,14},{14,13},{17,18},{18,... | collective-permute-start | bytes 884744 | tf_op jit(solution)/shard_map/ppermute | solution.py:390
  5.4 8.5 %collective-permute-start = (bf16[2,48,1536]{2,1,0:T(8,128)(2,1)S(1)}, bf16[2,48,1536]{2,1,0:T(8,128)(2,1)S(1)}, u32[]{:S(2)}, u32[]{:S(2)}) collective-permute-start(bf16[2,48,1536]{2,1,0:T(8,128)(2,1)S(1)} %pad_maximum_fusion.3.refs_1_), channel_id=1, source_target_pairs={{0,16},{16,0},{1,17},{17,1},{2,18},{18,2},{3,19},{19,3},{4,20},{20... | collective-permute-start | bytes 884744 | tf_op jit(solution)/shard_map/ppermute | solution.py:374
  11.7 18.5 %collective-permute-start.7 = (bf16[2,48,1536]{2,1,0:T(8,128)(2,1)S(1)}, bf16[2,48,1536]{2,1,0:T(8,128)(2,1)S(1)}, u32[]{:S(2)}, u32[]{:S(2)}) collective-permute-start(bf16[2,48,1536]{2,1,0:T(8,128)(2,1)S(1)} %collective-permute-done.1.refs_6_.refs_1_.refs_3_), channel_id=1, source_target_pairs={{1,2},{2,1},{5,6},{6,5},{9,10},{10,9},{13,14},{14,13},{17,18},{18,... | collective-permute-start | bytes 884744 | tf_op jit(solution)/shard_map/ppermute | solution.py:391
  12.4 19.1 %collective-permute-start.6 = (bf16[2,48,1536]{2,1,0:T(8,128)(2,1)S(1)}, bf16[2,48,1536]{2,1,0:T(8,128)(2,1)S(1)}, u32[]{:S(2)}, u32[]{:S(2)}) collective-permute-start(bf16[2,48,1536]{2,1,0:T(8,128)(2,1)S(1)} %collective-permute-done.2.refs_7_), channel_id=1, source_target_pairs={{1,0},{2,3},{5,4},{6,7},{9,8},{10,11},{13,12},{14,15},{17,16},{18,... | collective-permute-start | bytes 884744 | tf_op jit(solution)/shard_map/ppermute | solution.py:392
  21.1 11.2 %collective-permute-start.4 = (bf16[96,1536]{1,0:T(8,128)(2,1)S(1)}, bf16[96,1536]{1,0:T(8,128)(2,1)S(1)}, u32[]{:S(2)}, u32[]{:S(2)}) collective-permute-start(bf16[96,1536]{1,0:T(8,128)(2,1)S(1)} %get-tuple-element.33), channel_id=1, source_target_pairs={{0,4},{4,0},{8,12},{12,8},{1,5},{5,1},{9,13},{13,9},{2,6},{6,2},{1... | collective-permute-start | bytes 884744 | tf_op jit(solution)/shard_map/ppermute | solution.py:374
  21.1 11.1 %collective-permute-start.3 = (bf16[96,1536]{1,0:T(8,128)(2,1)S(1)}, bf16[96,1536]{1,0:T(8,128)(2,1)S(1)}, u32[]{:S(2)}, u32[]{:S(2)}) collective-permute-start(bf16[96,1536]{1,0:T(8,128)(2,1)S(1)} %get-tuple-element.31.refs_5_), channel_id=1, source_target_pairs={{0,4},{4,0},{8,12},{12,8},{1,5},{5,1},{9,13},{13,9},{2,6},{6,2},{1... | collective-permute-start | bytes 884744 | tf_op jit(solution)/shard_map/ppermute | solution.py:374
  21.6 10.6 %collective-permute-start.5 = (bf16[2,48,1536]{2,1,0:T(8,128)(2,1)S(1)}, bf16[2,48,1536]{2,1,0:T(8,128)(2,1)S(1)}, u32[]{:S(2)}, u32[]{:S(2)}) collective-permute-start(bf16[2,48,1536]{2,1,0:T(8,128)(2,1)S(1)} %collective-permute-done.1.refs_6_.refs_1_.refs_3_), channel_id=1, source_target_pairs={{0,16},{16,0},{1,17},{17,1},{2,18},{18,2},{3,19},{19,3},{4,20},{20... | collective-permute-start | bytes 884744 | tf_op jit(solution)/shard_map/ppermute | solution.py:374
  30.3 12.6 %collective-permute-start.9 = (bf16[2,48,1536]{2,1,0:T(8,128)(2,1)S(1)}, bf16[2,48,1536]{2,1,0:T(8,128)(2,1)S(1)}, u32[]{:S(2)}, u32[]{:S(2)}) collective-permute-start(bf16[2,48,1536]{2,1,0:T(8,128)(2,1)S(1)} %collective-permute-done.7.refs_6_), channel_id=1, source_target_pairs={{1,0},{2,3},{5,4},{6,7},{9,8},{10,11},{13,12},{14,15},{17,16},{18,... | collective-permute-start | bytes 884744 | tf_op jit(solution)/shard_map/ppermute | solution.py:393
  31.6 15.5 %collective-permute-start.10 = (bf16[2,48,1536]{2,1,0:T(8,128)(2,1)S(1)}, bf16[2,48,1536]{2,1,0:T(8,128)(2,1)S(1)}, u32[]{:S(2)}, u32[]{:S(2)}) collective-permute-start(bf16[2,48,1536]{2,1,0:T(8,128)(2,1)S(1)} %broadcast_select_fusion.1.refs_1_.refs_5_), channel_id=1, source_target_pairs={{0,16},{16,0},{1,17},{17,1},{2,18},{18,2},{3,19},{19,3},{4,20},{20... | collective-permute-start | bytes 884744 | tf_op jit(solution)/shard_map/ppermute | solution.py:374
  32.6 14.8 %collective-permute-start.8 = (bf16[2,96,1536]{2,1,0:T(8,128)(2,1)S(1)}, bf16[2,96,1536]{2,1,0:T(8,128)(2,1)S(1)}, u32[]{:S(2)}, u32[]{:S(2)}) collective-permute-start(bf16[2,96,1536]{2,1,0:T(8,128)(2,1)S(1)} %combine.2.refs_5_), channel_id=1, source_target_pairs={{0,8},{4,12},{8,0},{12,4},{1,9},{5,13},{9,1},{13,5},{2,10},{6,14},... | collective-permute-start | bytes 1769480 | tf_op jit(solution)/shard_map/ppermute | solution.py:374
  37.7 10.5 %collective-permute-start.12 = (bf16[96,1536]{1,0:T(8,128)(2,1)S(1)}, bf16[96,1536]{1,0:T(8,128)(2,1)S(1)}, u32[]{:S(2)}, u32[]{:S(2)}) collective-permute-start(bf16[96,1536]{1,0:T(8,128)(2,1)S(1)} %get-tuple-element.39), channel_id=1, source_target_pairs={{0,4},{4,0},{8,12},{12,8},{1,5},{5,1},{9,13},{13,9},{2,6},{6,2},{1... | collective-permute-start | bytes 884744 | tf_op jit(solution)/shard_map/ppermute | solution.py:374
  37.8 10.4 %collective-permute-start.11 = (bf16[96,1536]{1,0:T(8,128)(2,1)S(1)}, bf16[96,1536]{1,0:T(8,128)(2,1)S(1)}, u32[]{:S(2)}, u32[]{:S(2)}) collective-permute-start(bf16[96,1536]{1,0:T(8,128)(2,1)S(1)} %get-tuple-element.38.refs_5_), channel_id=1, source_target_pairs={{0,4},{4,0},{8,12},{12,8},{1,5},{5,1},{9,13},{13,9},{2,6},{6,2},{1... | collective-permute-start | bytes 884744 | tf_op jit(solution)/shard_map/ppermute | solution.py:374
  42.9 8.2 %collective-permute-start.14 = (bf16[2,48,1536]{2,1,0:T(8,128)(2,1)S(1)}, bf16[2,48,1536]{2,1,0:T(8,128)(2,1)S(1)}, u32[]{:S(2)}, u32[]{:S(2)}) collective-permute-start(bf16[2,48,1536]{2,1,0:T(8,128)(2,1)S(1)} %broadcast_select_fusion.refs_2_.refs_6_), channel_id=1, source_target_pairs={{0,16},{16,0},{1,17},{17,1},{2,18},{18,2},{3,19},{19,3},{4,20},{20... | collective-permute-start | bytes 884744 | tf_op jit(solution)/shard_map/ppermute | solution.py:374
  48.6 14.0 %collective-permute-start.13 = (bf16[2,96,1536]{2,1,0:T(8,128)(2,1)S(1)}, bf16[2,96,1536]{2,1,0:T(8,128)(2,1)S(1)}, u32[]{:S(2)}, u32[]{:S(2)}) collective-permute-start(bf16[2,96,1536]{2,1,0:T(8,128)(2,1)S(1)} %combine.3.refs_7_), channel_id=1, source_target_pairs={{0,8},{4,12},{8,0},{12,4},{1,9},{5,13},{9,1},{13,5},{2,10},{6,14},... | collective-permute-start | bytes 1769480 | tf_op jit(solution)/shard_map/ppermute | solution.py:374
  55.0 8.5 %collective-permute-start.18 = (bf16[192,1536]{1,0:T(8,128)(2,1)S(1)}, bf16[192,1536]{1,0:T(8,128)(2,1)S(1)}, u32[]{:S(2)}, u32[]{:S(2)}) collective-permute-start(bf16[192,1536]{1,0:T(8,128)(2,1)S(1)} %get-tuple-element.41), channel_id=1, source_target_pairs={{0,4},{4,0},{8,12},{12,8},{1,5},{5,1},{9,13},{13,9},{2,6},{6,2},{1... | collective-permute-start | bytes 1769480 | tf_op jit(solution)/shard_map/ppermute | solution.py:374
  55.1 8.4 %collective-permute-start.17 = (bf16[192,1536]{1,0:T(8,128)(2,1)S(1)}, bf16[192,1536]{1,0:T(8,128)(2,1)S(1)}, u32[]{:S(2)}, u32[]{:S(2)}) collective-permute-start(bf16[192,1536]{1,0:T(8,128)(2,1)S(1)} %get-tuple-element.40.refs_7_), channel_id=1, source_target_pairs={{0,4},{4,0},{8,12},{12,8},{1,5},{5,1},{9,13},{13,9},{2,6},{6,2},{1... | collective-permute-start | bytes 1769480 | tf_op jit(solution)/shard_map/ppermute | solution.py:374
  55.6 10.5 %collective-permute-start.15 = (bf16[2,96,1536]{2,1,0:T(8,128)(2,1)S(1)}, bf16[2,96,1536]{2,1,0:T(8,128)(2,1)S(1)}, u32[]{:S(2)}, u32[]{:S(2)}) collective-permute-start(bf16[2,96,1536]{2,1,0:T(8,128)(2,1)S(1)} %activations.5.refs_4_.refs_1_.refs_3_), channel_id=1, source_target_pairs={{0,4},{4,0},{8,12},{12,8},{1,5},{5,1},{9,13},{13,9},{2,6},{6,2},{1... | collective-permute-start | bytes 1769480 | tf_op jit(solution)/shard_map/ppermute | solution.py:374
  63.4 2.7 %collective-permute-start.16 = (bf16[2,96,1536]{2,1,0:T(8,128)(2,1)S(1)}, bf16[2,96,1536]{2,1,0:T(8,128)(2,1)S(1)}, u32[]{:S(2)}, u32[]{:S(2)}) collective-permute-start(bf16[2,96,1536]{2,1,0:T(8,128)(2,1)S(1)} %activations.6.refs_12_.refs_2_.refs_4_), channel_id=1, source_target_pairs={{0,4},{4,0},{8,12},{12,8},{1,5},{5,1},{9,13},{13,9},{2,6},{6,2},{1... | collective-permute-start | bytes 1769480 | tf_op jit(solution)/shard_map/ppermute | solution.py:374
  64.0 11.6 %collective-permute-start.20 = (bf16[2,192,512]{2,1,0:T(8,128)(2,1)S(1)}, bf16[2,192,512]{2,1,0:T(8,128)(2,1)S(1)}, u32[]{:S(2)}, u32[]{:S(2)}) collective-permute-start(bf16[2,192,512]{2,1,0:T(8,128)(2,1)S(1)} %pad_maximum_fusion.2.refs_11_), channel_id=1, source_target_pairs={{0,8},{4,12},{8,0},{12,4},{1,9},{5,13},{9,1},{13,5},{2,10},{6,14},... | collective-permute-start | bytes 1179656 | tf_op jit(solution)/shard_map/ppermute | solution.py:374
  76.1 9.6 %collective-permute-start.24 = (bf16[2,192,512]{2,1,0:T(8,128)(2,1)S(1)}, bf16[2,192,512]{2,1,0:T(8,128)(2,1)S(1)}, u32[]{:S(2)}, u32[]{:S(2)}) collective-permute-start(bf16[2,192,512]{2,1,0:T(8,128)(2,1)S(1)} %activations.7.refs_3_.refs_1_.refs_5_), channel_id=1, source_target_pairs={{0,4},{4,0},{8,12},{12,8},{1,5},{5,1},{9,13},{13,9},{2,6},{6,2},{1... | collective-permute-start | bytes 1179656 | tf_op jit(solution)/shard_map/ppermute | solution.py:374
  76.1 9.4 %collective-permute-start.19 = (bf16[96,1536]{1,0:T(8,128)(2,1)S(1)}, bf16[96,1536]{1,0:T(8,128)(2,1)S(1)}, u32[]{:S(2)}, u32[]{:S(2)}) collective-permute-start(bf16[96,1536]{1,0:T(8,128)(2,1)S(1)} %get-tuple-element.44), channel_id=1, source_target_pairs={{0,16},{16,0},{1,17},{17,1},{2,18},{18,2},{3,19},{19,3},{4,20},{20... | collective-permute-start | bytes 884744 | tf_op jit(solution)/shard_map/ppermute | solution.py:374
  77.7 16.4 %collective-permute-start.23 = (bf16[2,192,512]{2,1,0:T(8,128)(2,1)S(1)}, bf16[2,192,512]{2,1,0:T(8,128)(2,1)S(1)}, u32[]{:S(2)}, u32[]{:S(2)}) collective-permute-start(bf16[2,192,512]{2,1,0:T(8,128)(2,1)S(1)} %pad_maximum_fusion.1.refs_10_), channel_id=1, source_target_pairs={{0,8},{4,12},{8,0},{12,4},{1,9},{5,13},{9,1},{13,5},{2,10},{6,14},... | collective-permute-start | bytes 1179656 | tf_op jit(solution)/shard_map/ppermute | solution.py:374
  94.6 1.8 %collective-permute-start.25 = (bf16[2,192,512]{2,1,0:T(8,128)(2,1)S(1)}, bf16[2,192,512]{2,1,0:T(8,128)(2,1)S(1)}, u32[]{:S(2)}, u32[]{:S(2)}) collective-permute-start(bf16[2,192,512]{2,1,0:T(8,128)(2,1)S(1)} %activations.8.refs_1_.refs_6_.refs_5_), channel_id=1, source_target_pairs={{0,4},{4,0},{8,12},{12,8},{1,5},{5,1},{9,13},{13,9},{2,6},{6,2},{1... | collective-permute-start | bytes 1179656 | tf_op jit(solution)/shard_map/ppermute | solution.py:374
  94.7 11.5 %collective-permute-start.22 = (bf16[2,192,512]{2,1,0:T(8,128)(2,1)S(1)}, bf16[2,192,512]{2,1,0:T(8,128)(2,1)S(1)}, u32[]{:S(2)}, u32[]{:S(2)}) collective-permute-start(bf16[2,192,512]{2,1,0:T(8,128)(2,1)S(1)} %pad_maximum_fusion.refs_9_), channel_id=1, source_target_pairs={{0,8},{4,12},{8,0},{12,4},{1,9},{5,13},{9,1},{13,5},{2,10},{6,14},... | collective-permute-start | bytes 1179656 | tf_op jit(solution)/shard_map/ppermute | solution.py:374
  106.7 1.8 %collective-permute-start.26 = (bf16[2,192,512]{2,1,0:T(8,128)(2,1)S(1)}, bf16[2,192,512]{2,1,0:T(8,128)(2,1)S(1)}, u32[]{:S(2)}, u32[]{:S(2)}) collective-permute-start(bf16[2,192,512]{2,1,0:T(8,128)(2,1)S(1)} %activations.9.refs_1_.refs_6_.refs_5_), channel_id=1, source_target_pairs={{0,4},{4,0},{8,12},{12,8},{1,5},{5,1},{9,13},{13,9},{2,6},{6,2},{1... | collective-permute-start | bytes 1179656 | tf_op jit(solution)/shard_map/ppermute | solution.py:374
  110.4 9.7 %collective-permute-start.27 = (bf16[96,1536]{1,0:T(8,128)(2,1)S(1)}, bf16[96,1536]{1,0:T(8,128)(2,1)S(1)}, u32[]{:S(2)}, u32[]{:S(2)}) collective-permute-start(bf16[96,1536]{1,0:T(8,128)(2,1)S(1)} %get-tuple-element.51), channel_id=1, source_target_pairs={{0,16},{16,0},{1,17},{17,1},{2,18},{18,2},{3,19},{19,3},{4,20},{20... | collective-permute-start | bytes 884744 | tf_op jit(solution)/shard_map/ppermute | solution.py:374
  111.9 18.2 %collective-permute-start.21 = (bf16[48,1536]{1,0:T(8,128)(2,1)S(1)}, bf16[48,1536]{1,0:T(8,128)(2,1)S(1)}, u32[]{:S(2)}, u32[]{:S(2)}) collective-permute-start(bf16[48,1536]{1,0:T(8,128)(2,1)S(1)} %fold.2.refs_5_), channel_id=1, source_target_pairs={{0,1},{1,0},{2,3},{3,2},{4,5},{5,4},{6,7},{7,6},{8,9},{9,8},{10,11... | collective-permute-start | bytes 442376 | tf_op jit(solution)/shard_map/ppermute | solution.py:374
  120.2 15.5 %collective-permute-start.28 = (bf16[48,1536]{1,0:T(8,128)(2,1)S(1)}, bf16[48,1536]{1,0:T(8,128)(2,1)S(1)}, u32[]{:S(2)}, u32[]{:S(2)}) collective-permute-start(bf16[48,1536]{1,0:T(8,128)(2,1)S(1)} %get-tuple-element.68), channel_id=1, source_target_pairs={{0,2},{1,3},{2,0},{3,1},{4,6},{5,7},{6,4},{7,5},{8,10},{9,11},{10,... | collective-permute-start | bytes 442376 | tf_op jit(solution)/shard_map/ppermute | solution.py:374
  124.6 11.1 %collective-permute-start.29 = (bf16[48,1536]{1,0:T(8,128)(2,1)S(1)}, bf16[48,1536]{1,0:T(8,128)(2,1)S(1)}, u32[]{:S(2)}, u32[]{:S(2)}) collective-permute-start(bf16[48,1536]{1,0:T(8,128)(2,1)S(1)} %get-tuple-element.69), channel_id=1, source_target_pairs={{0,3},{1,2},{2,1},{3,0},{4,7},{5,6},{6,5},{7,4},{8,11},{9,10},{10,... | collective-permute-start | bytes 442376 | tf_op jit(solution)/shard_map/ppermute | solution.py:374

commit v5 on v4

--- a/solution.py
+++ b/solution.py
@@ -91,10 +91,53 @@
     return core_ref[0] if side == 0 else 1 - core_ref[0]
 
 
-def partial_sums(core, units, up, down, side, apart, load, after=()):
+def bring(core, up, down):
+    depth, full = up.shape
+    half = full // 2
+    parts = 2
+
+    def body(core_ref, up_ref, down_ref, *refs):
+        *outs, sems = refs
+        copies = []
+        for side in range(2):
+            begin = pl.multiple_of(side_of(core_ref, side) * half, half)
+            up_out, down_out = outs[2 * side : 2 * side + 2]
+            for part in range(parts):
+                rows = pl.ds(part * (depth // parts), depth // parts)
+                copies.append((up_ref.at[rows, pl.ds(begin, half)], up_out.at[rows]))
+                size = half // parts
+                rows = pl.ds(pl.multiple_of(begin + part * size, size), size)
+                copies.append((down_ref.at[rows], down_out.at[pl.ds(part * size, size)]))
+        copies = [
+            pltpu.make_async_copy(source, target, sems.at[n])
+            for n, (source, target) in enumerate(copies)
+        ]
+        for copy in copies:
+            copy.start()
+        for copy in copies:
+            copy.wait()
+
+    up, down = (pltpu.with_memory_space_constraint(array, pltpu.HBM) for array in (up, down))
+    shapes = [(depth, half), (half, depth)] * 2
+    return call(
+        body,
+        core,
+        [up, down],
+        [pl.BlockSpec(memory_space=pltpu.HBM)] * 2,
+        [jax.ShapeDtypeStruct(shape, BF16) for shape in shapes],
+        [pl.BlockSpec(memory_space=pl.ANY)] * 4,
+        (1,),
+        (0, 4 * depth * full),
+        "bring",
+        (),
+        [pltpu.SemaphoreType.DMA((4 * parts,))],
+    )
+
+
+def partial_sums(core, units, up, down, side, apart, after=()):
     _, rows, depth = units[0].shape
     tokens = rows * len(units)
-    width = up.shape[1] // 2 if load else up.shape[1]
+    width = up.shape[1]
     tile = tile_of(width, 256)
     dtype = BF16 if side else F32
 
@@ -107,9 +150,6 @@
             for n, ref in enumerate(unit_refs):
                 acts[:, n * rows : (n + 1) * rows, :] = ref[...]
 
-        if load:
-            out_refs[-2][...] = up_ref[...]
-            out_refs[-1][...] = down_ref[...]
         preact = contract(acts[0], up_ref[...], 1, 0)
         grad_hidden = contract(acts[1], down_ref[...], 1, 1)
         if apart:
@@ -119,31 +159,20 @@
             out_refs[0][0] = preact.astype(dtype)
             out_refs[0][1] = grad_hidden.astype(dtype)
 
-    def place(i, c):
-        return side_of(c, side) * (width // tile) + i if load else i
-
     if apart:
         outs = [jax.ShapeDtypeStruct((tokens, width), dtype)] * 2
         specs = [pl.BlockSpec((tokens, tile), lambda i, c: (0, i))] * 2
     else:
         outs = [jax.ShapeDtypeStruct((2, tokens, width), dtype)]
         specs = [pl.BlockSpec((2, tokens, tile), lambda i, c: (0, 0, i))]
-    if load:
-        outs += [jax.ShapeDtypeStruct((depth, width), BF16), jax.ShapeDtypeStruct((width, depth), BF16)]
-        specs += [
-            pl.BlockSpec((depth, tile), lambda i, c: (0, i)),
-            pl.BlockSpec((tile, depth), lambda i, c: (i, 0)),
-        ]
-        up, down = (pltpu.with_memory_space_constraint(array, pltpu.HBM) for array in (up, down))
-
     return call(
         body,
         core,
         [*units, up, down],
         [whole(units[0].shape)] * len(units)
         + [
-            pl.BlockSpec((depth, tile), lambda i, c: (0, place(i, c))),
-            pl.BlockSpec((tile, depth), lambda i, c: (place(i, c), 0)),
+            pl.BlockSpec((depth, tile), lambda i, c: (0, i)),
+            pl.BlockSpec((tile, depth), lambda i, c: (i, 0)),
         ],
         outs,
         specs,
@@ -261,18 +290,18 @@
     )
 
 
-def fold(core, stay, near, after=()):
+def fold(core, stay, near, dtype, after=()):
     rows, depth = stay.shape
 
     def body(core_ref, stay_ref, near_ref, out_ref):
-        out_ref[...] = (stay_ref[...] + near_ref[...].astype(F32)).astype(BF16)
+        out_ref[...] = (stay_ref[...] + near_ref[...].astype(F32)).astype(dtype)
 
     return call(
         body,
         core,
         [stay, near],
         [whole(stay.shape)] * 2,
-        jax.ShapeDtypeStruct(stay.shape, BF16),
+        jax.ShapeDtypeStruct(stay.shape, dtype),
         whole(stay.shape),
         (1,),
         (rows * depth, 8 * rows * depth),
@@ -402,17 +431,12 @@
     ]
 
     pieces = [(0, 0, half), (1, 0, half)] + [(2, j * width, width) for j in range(chunks)]
-    near, keep, far, act, act_near, ups, downs = {}, {}, {}, {}, {}, {}, {}
+    near, keep, far, act, act_near = {}, {}, {}, {}, {}
+    *weights, = bring(core, up, down)
+    ups, downs = weights[0::2], weights[1::2]
 
     def sums(group, side, after):
-        if group:
-            return partial_sums(
-                core, groups[group], ups[side], downs[side], side, side == 1, False, after
-            )
-        *out, ups[side], downs[side] = partial_sums(
-            core, groups[group], up, down, side, side == 1, True, after
-        )
-        return out
+        return partial_sums(core, groups[group], ups[side], downs[side], side, side == 1, after)
 
     def product(group, after, between=()):
         out = sums(group, 1, after)
@@ -455,11 +479,11 @@
             core, inputs_t, cotan, sides, acts, j * width, width, up.shape, outputs, after
         )
 
-    last = product(0, (), [unit[1, 0], first])
+    last = product(0, (), ())
     last = cross(0, [unit[1, 1], first_on, second])
     last = product(1, last, [second_on])
-    last = ready(0, last + [unit[2, 1]])
-    last = cross(1, last + [])
+    last = ready(0, [*last, unit[2, 1]])
+    last = cross(1, last)
     last = product(2, last)
     last = ready(1, last)
     for j in range(chunks):
@@ -470,26 +494,36 @@
 
     part, last = None, [stay1]
     for j in range(chunks):
-        n = 2 + j
+        n, final = 2 + j, j + 1 == chunks
         last = ready(n, last)
+        if j:
+            last = part, = inward((n - 1,), (j - 1) * width, part, None, None, last)
+        if final:
+            stay2, go2 = inward((n,), j * width, part, (0, 1, 2, 3), 2, last)
+            near2 = swap(go2, "gx", 2, 1)
+            last = [stay2]
+        if j:
+            *outputs, done = gradients(j - 1, (1,), last)
+            last = [done]
+        if final:
+            back2 = fold(core, stay2, near2, BF16, last)
+            far2 = swap(back2[:rows], "gz", 4, 2)
+            far3 = swap(back2[rows:], "gz", 4, 3)
+            last = [back2]
+        *outputs, done = gradients(j, (0,), last)
+        last = [done]
         if j == 0:
-            total = stay1[:rows] + near1[:rows].astype(F32)
-            back1 = fold(core, stay1[rows:], near1[rows:], last)
+            total = fold(core, stay1[:rows], near1[:rows], F32, last)
+            back1 = fold(core, stay1[rows:], near1[rows:], BF16, [total])
             far1 = swap(back1, "gz", 4, 1)
             last = [back1]
-        if j + 1 < chunks:
-            last = part, = inward((n,), j * width, part, None, None, last)
-            *outputs, done = gradients(j, (0, 1), last)
-            last = [done]
-        else:
-            stay2, go2 = inward((n,), j * width, part, (0, 1, 2, 3), 2, last)
-            near2 = swap(go2, "gx", 2, 1)
-            *outputs, done = gradients(j, (0,), [stay2])
-            back2 = fold(core, stay2, near2, [done])
-            far2 = swap(back2[:rows], "gz", 4, 2)
-            far3 = swap(back2[rows:], "gz", 4, 3)
-            *outputs, done = gradients(j, (1,), [back2])
-    total = total + far1.astype(F32) + far2.astype(F32) + far3.astype(F32)
+        elif j == 1 and not final:
+            total = fold(core, total, far1, F32, last)
+            last = [total]
+    if chunks < 3:
+        total = total + far1.astype(F32)
+    *outputs, done = gradients(chunks - 1, (1,), last)
+    total = total + far2.astype(F32) + far3.astype(F32)
     return (total.astype(BF16), *outputs)
 
 

time: 137 us -> 129 us (0.942)
  waiting for transfers between devices: 34.7 us -> 22.7 us
  local copies, waits for them, and re-layouts: 0.05 us -> 9.14 us
  starting transfers between devices: 34.7 us -> 28.5 us
  Pallas kernels: 63.6 us -> 65.1 us
    ppermute x26, waiting for transfers between devices: 30.1 us -> 16.3 us  [swap(): return lax.ppermute(value, axis, [(i, i ^ bits) for i in range(size)])]
    unnamed x0 -> x22, local copies, waits for them, and re-layouts: none -> 9.06 us
    ppermute x26, starting transfers between devices: 30.8 us -> 23.8 us  [swap(): return lax.ppermute(value, axis, [(i, i ^ bits) for i in range(size)])]
    ppermute x1, waiting for transfers between devices: 0.01 us -> 3.73 us  [cube_body(): first_on = lax.ppermute(first, 'gz', outward)]
    ppermute x1, waiting for transfers between devices: 4.58 us -> 2.67 us  [cube_body(): second_on = lax.ppermute(second, 'gz', outward)]
    pallas_call x24 -> x29, Pallas kernels: 63.6 us -> 65.1 us  [call(): pl.pallas_call(kernel, grid_spec=pltpu.PrefetchScalarGridSpec(num_scalar_...]
  transfers between devices with their start and end apart: 30 -> 30, of which waited for: 12 -> 7; matrix products, arithmetic and copies ran while one was open for 0% -> 1% of each run, Pallas kernels for 44% -> 49%
where the time goes in v5:
time: 129 us
  Pallas kernels  65.1 us (50%)
  starting transfers between devices  28.5 us (22%)
  waiting for transfers between devices  22.7 us (18%)
  local copies, waits for them, and re-layouts  9.14 us (7%)
  other arithmetic  2.36 us (2%)
    pallas_call x29, Pallas kernels, call(): pl.pallas_call(kernel, grid_spec=pltpu.PrefetchScalarGridSpec(num_scalar_...  65.1 us
    ppermute x26, starting transfers between devices, swap(): return lax.ppermute(value, axis, [(i, i ^ bits) for i in range(size)])  23.8 us
    ppermute x26, waiting for transfers between devices, swap(): return lax.ppermute(value, axis, [(i, i ^ bits) for i in range(size)])  16.3 us
    unnamed x22, local copies, waits for them, and re-layouts  9.06 us
    ppermute x1, waiting for transfers between devices, cube_body(): first_on = lax.ppermute(first, 'gz', outward)  3.73 us
    ppermute x1, waiting for transfers between devices, cube_body(): second_on = lax.ppermute(second, 'gz', outward)  2.67 us
  transfers between devices with their start and end apart: 30, of which 7 were waited for; matrix products, arithmetic and copies ran while one was open for 1% of the time, Pallas kernels for 49%

profile of v5, /device:TPU:0, one launch (start us, length us, event | category | flops | bytes accessed | tf_op | source)
XLA Modules:
  0.0 128.9 jit_solution(18097483749009031742)
XLA Ops:
  0.6 1.0 pad_maximum_fusion.3.refs_1_
  1.6 3.0 %collective-permute-start = (bf16[2,48,1536]{2,1,0:T(8,128)(2,1)S(1)}, bf16[2,48,1536]{2,1,0:T(8,128)(2,1)S(1)}, u32[]{:S(2)}, u32[]{:S(2)}) collective-permute-start(bf16[2,48,1536]{2,1,0:T(8,128)(2,1)S(1)} %pad_maximum_fusion.3.refs_1_), channel_id=1, source_target_pairs={{0,16},{16,0},{1,17},{17,1},{2,18},{18,2},{3,19},{19,3},{4,20},{20... | collective-permute-start | bytes 884744 | tf_op jit(solution)/shard_map/ppermute | solution.py:403
  4.6 1.6 %collective-permute-start.3 = (bf16[2,48,1536]{2,1,0:T(8,128)(2,1)S(1)}, bf16[2,48,1536]{2,1,0:T(8,128)(2,1)S(1)}, u32[]{:S(2)}, u32[]{:S(2)}) collective-permute-start(bf16[2,48,1536]{2,1,0:T(8,128)(2,1)S(1)} %pad_maximum_fusion.3.refs_1_), channel_id=1, source_target_pairs={{0,1},{1,0},{2,3},{3,2},{4,5},{5,4},{6,7},{7,6},{8,9},{9,8},{10,11... | collective-permute-start | bytes 884744 | tf_op jit(solution)/shard_map/ppermute | solution.py:403
  6.2 1.4 %collective-permute-start.5 = (bf16[2,48,1536]{2,1,0:T(8,128)(2,1)S(1)}, bf16[2,48,1536]{2,1,0:T(8,128)(2,1)}, u32[]{:S(2)}, u32[]{:S(2)}) collective-permute-start(bf16[2,48,1536]{2,1,0:T(8,128)(2,1)S(1)} %pad_maximum_fusion.3.refs_1_), channel_id=1, source_target_pairs={{1,2},{2,1},{5,6},{6,5},{9,10},{10,9},{13,14},{14,13},{17,18},{18,... | collective-permute-start | bytes 884744 | tf_op jit(solution)/shard_map/ppermute | solution.py:419
  7.6 6.5 %bring.1 = (bf16[1536,1536]{1,0:T(8,128)(2,1)S(1)}, bf16[1536,1536]{1,0:T(8,128)(2,1)S(1)}, bf16[1536,1536]{1,0:T(8,128)(2,1)S(1)}, bf16[1536,1536]{1,0:T(8,128)(2,1)S(1)}) custom-call(s32[1]{0:T(128)} %bitcast.refs_0_, bf16[1536,3072]{1,0:T(8,128)(2,1)} %refs_1_.1, bf16[3072,1536]{1,0:T(8,128)(2,1)} %refs_2_.1), custom_call_target="tpu_custom_call" | custom-call | bytes 18874368 | tf_op jit(solution)/shard_map/bring/pallas_call | solution.py:67
  14.2 2.2 %copy-done.5 = bf16[1536,1536]{1,0:T(8,128)(2,1)} copy-done((bf16[1536,1536]{1,0:T(8,128)(2,1)}, bf16[1536,1536]{1,0:T(8,128)(2,1)S(1)}, u32[]{:S(2)}) %copy-start.5) | copy-done | bytes 4718616
  16.3 3.6 %sums_send.3 = (bf16[96,1536]{1,0:T(8,128)(2,1)S(1)}, bf16[96,1536]{1,0:T(8,128)(2,1)S(1)}) custom-call(s32[1]{0:T(128)} %bitcast.refs_0_, bf16[2,48,1536]{2,1,0:T(8,128)(2,1)S(1)} %pad_maximum_fusion.3.refs_1_, bf16[2,48,1536]{2,1,0:T(8,128)(2,1)S(1)} %collective-permute-done.refs_2_, ...), custom_call_target="tpu_custom_call" | custom-call | flops 905969664 | bytes 9437184 | tf_op jit(solution)/shard_map/sums_send/pallas_call | solution.py:67
  19.9 2.2 %copy-done = bf16[1536,1536]{1,0:T(8,128)(2,1)} copy-done((bf16[1536,1536]{1,0:T(8,128)(2,1)}, bf16[1536,1536]{1,0:T(8,128)(2,1)S(1)}, u32[]{:S(2)}) %copy-start) | copy-done | bytes 4718616
  22.1 0.5 collective-permute-start.2
  22.6 0.5 collective-permute-start.4
  23.2 0.7 collective-permute-start.7
  23.8 1.3 %collective-permute-start.6 = (bf16[2,48,1536]{2,1,0:T(8,128)(2,1)}, bf16[2,48,1536]{2,1,0:T(8,128)(2,1)S(1)}, u32[]{:S(2)}, u32[]{:S(2)}) collective-permute-start(bf16[2,48,1536]{2,1,0:T(8,128)(2,1)} %collective-permute-done.5), channel_id=1, source_target_pairs={{1,0},{2,3},{5,4},{6,7},{9,8},{10,11},{13,12},{14,15},{17,16},{18,... | collective-permute-start | bytes 884744 | tf_op jit(solution)/shard_map/ppermute | solution.py:421
  25.2 2.3 %copy-done.2 = bf16[1536,1536]{1,0:T(8,128)(2,1)S(1)} copy-done((bf16[1536,1536]{1,0:T(8,128)(2,1)S(1)}, bf16[1536,1536]{1,0:T(8,128)(2,1)}, u32[]{:S(2)}) %copy-start.2) | copy-done | bytes 4718616
  27.5 2.3 %copy-done.6 = bf16[1536,1536]{1,0:T(8,128)(2,1)S(1)} copy-done((bf16[1536,1536]{1,0:T(8,128)(2,1)S(1)}, bf16[1536,1536]{1,0:T(8,128)(2,1)}, u32[]{:S(2)}) %copy-start.6) | copy-done | bytes 4718616
  29.8 3.6 %sums_keep.3.refs_1_ = f32[2,96,1536]{2,1,0:T(8,128)S(1)} custom-call(s32[1]{0:T(128)} %bitcast.refs_0_, bf16[2,48,1536]{2,1,0:T(8,128)(2,1)S(1)} %pad_maximum_fusion.3.refs_1_, bf16[2,48,1536]{2,1,0:T(8,128)(2,1)S(1)} %collective-permute-done.refs_2_, bf16[1536,1536]{1,0:T(8,128)(2,1)S(1)} %copy-done.2, bf16[1536,1536]{1,0:T(8,128)(2,1)S(1)} %copy-done.6, ...), custom_call_target="tpu_custom_call" | custom-call | flops 905969664 | bytes 9437184 | tf_op jit(solution)/shard_map/sums_keep/pallas_call | solution.py:67
  33.5 3.7 %collective-permute-done.6.refs_5_ = bf16[2,48,1536]{2,1,0:T(8,128)(2,1)S(1)} collective-permute-done((bf16[2,48,1536]{2,1,0:T(8,128)(2,1)}, bf16[2,48,1536]{2,1,0:T(8,128)(2,1)S(1)}, u32[]{:S(2)}, u32[]{:S(2)}) %collective-permute-start.6) | collective-permute-done | bytes 294944 | tf_op jit(solution)/shard_map/ppermute | solution.py:421
  37.2 0.3 combine.2.refs_5_
  37.6 1.6 %collective-permute-start.8 = (bf16[2,96,1536]{2,1,0:T(8,128)(2,1)S(1)}, bf16[2,96,1536]{2,1,0:T(8,128)(2,1)S(1)}, u32[]{:S(2)}, u32[]{:S(2)}) collective-permute-start(bf16[2,96,1536]{2,1,0:T(8,128)(2,1)S(1)} %combine.2.refs_5_), channel_id=1, source_target_pairs={{0,8},{4,12},{8,0},{12,4},{1,9},{5,13},{9,1},{13,5},{2,10},{6,14},... | collective-permute-start | bytes 1769480 | tf_op jit(solution)/shard_map/ppermute | solution.py:403
  39.1 1.3 collective-permute-start.9
  40.5 1.6 %collective-permute-start.10 = (bf16[2,48,1536]{2,1,0:T(8,128)(2,1)S(1)}, bf16[2,48,1536]{2,1,0:T(8,128)(2,1)S(1)}, u32[]{:S(2)}, u32[]{:S(2)}) collective-permute-start(bf16[2,48,1536]{2,1,0:T(8,128)(2,1)S(1)} %broadcast_select_fusion.1.refs_1_.refs_5_), channel_id=1, source_target_pairs={{0,16},{16,0},{1,17},{17,1},{2,18},{18,2},{3,19},{19,3},{4,20},{20... | collective-permute-start | bytes 884744 | tf_op jit(solution)/shard_map/ppermute | solution.py:403
  42.1 3.6 %sums_send.4 = (bf16[96,1536]{1,0:T(8,128)(2,1)S(1)}, bf16[96,1536]{1,0:T(8,128)(2,1)S(1)}) custom-call(s32[1]{0:T(128)} %bitcast.refs_0_, bf16[2,48,1536]{2,1,0:T(8,128)(2,1)S(1)} %collective-permute-done.3.refs_1_.refs_3_, bf16[2,48,1536]{2,1,0:T(8,128)(2,1)S(1)} %collective-permute-done.4.refs_4_.refs_2_, bf16[1536,1536]{1,0:T(8,128)(2,1)S(1)} %bitcast.64, ...), custom_call_target="tpu_custom_call" | custom-call | flops 905969664 | bytes 9437184 | tf_op jit(solution)/shard_map/sums_send/pallas_call | solution.py:67
  45.6 0.1 collective-permute-start.11
  45.7 0.5 collective-permute-start.12
  46.2 2.7 %collective-permute-done.9.refs_6_ = bf16[2,48,1536]{2,1,0:T(8,128)(2,1)S(1)} collective-permute-done((bf16[2,48,1536]{2,1,0:T(8,128)(2,1)S(1)}, bf16[2,48,1536]{2,1,0:T(8,128)(2,1)S(1)}, u32[]{:S(2)}, u32[]{:S(2)}) %collective-permute-start.9) | collective-permute-done | bytes 294944 | tf_op jit(solution)/shard_map/ppermute | solution.py:422
  48.9 1.6 %collective-permute-start.14 = (bf16[2,48,1536]{2,1,0:T(8,128)(2,1)S(1)}, bf16[2,48,1536]{2,1,0:T(8,128)(2,1)S(1)}, u32[]{:S(2)}, u32[]{:S(2)}) collective-permute-start(bf16[2,48,1536]{2,1,0:T(8,128)(2,1)S(1)} %broadcast_select_fusion.refs_2_.refs_6_), channel_id=1, source_target_pairs={{0,16},{16,0},{1,17},{17,1},{2,18},{18,2},{3,19},{19,3},{4,20},{20... | collective-permute-start | bytes 884744 | tf_op jit(solution)/shard_map/ppermute | solution.py:403
  50.5 3.6 %sums_keep.4.refs_5_.refs_1_ = f32[2,96,1536]{2,1,0:T(8,128)S(1)} custom-call(s32[1]{0:T(128)} %bitcast.refs_0_, bf16[2,48,1536]{2,1,0:T(8,128)(2,1)S(1)} %collective-permute-done.3.refs_1_.refs_3_, bf16[2,48,1536]{2,1,0:T(8,128)(2,1)S(1)} %collective-permute-done.4.refs_4_.refs_2_, bf16[1536,1536]{1,0:T(8,128)(2,1)S(1)} %bitcast.66, ...), custom_call_target="tpu_custom_call" | custom-call | flops 905969664 | bytes 9437184 | tf_op jit(solution)/shard_map/sums_keep/pallas_call | solution.py:67
  54.1 0.8 activations.5.refs_4_.refs_1_.refs_3_
  55.0 0.4 combine.3.refs_7_
  55.3 0.6 collective-permute-start.13
  55.9 3.8 %sums_send.5 = (bf16[192,1536]{1,0:T(8,128)(2,1)S(1)}, bf16[192,1536]{1,0:T(8,128)(2,1)S(1)}) custom-call(s32[1]{0:T(128)} %bitcast.refs_0_, bf16[2,48,1536]{2,1,0:T(8,128)(2,1)S(1)} %broadcast_select_fusion.1.refs_1_.refs_5_, bf16[2,48,1536]{2,1,0:T(8,128)(2,1)S(1)} %broadcast_select_fusion.refs_2_.refs_6_, ...), custom_call_target="tpu_custom_call" | custom-call | flops 1811939328 | bytes 9437184 | tf_op jit(solution)/shard_map/sums_send/pallas_call | solution.py:67
  59.9 0.5 collective-permute-start.18
  60.4 0.1 collective-permute-start.15
  60.4 3.9 %sums_keep.5.refs_5_.refs_1_ = f32[2,192,1536]{2,1,0:T(8,128)S(1)} custom-call(s32[1]{0:T(128)} %bitcast.refs_0_, bf16[2,48,1536]{2,1,0:T(8,128)(2,1)S(1)} %broadcast_select_fusion.1.refs_1_.refs_5_, bf16[2,48,1536]{2,1,0:T(8,128)(2,1)S(1)} %broadcast_select_fusion.refs_2_.refs_6_, bf16[2,48,1536]{2,1,0:T(8,128)(2,1)S(1)} %collective-permute-done.10.refs_6_.refs_3_.refs_7_, ...), custom_call_target="tpu_custom_call" | custom-call | flops 1811939328 | bytes 9437184 | tf_op jit(solution)/shard_map/sums_keep/pallas_call | solution.py:67
  64.3 4.1 %collective-permute-done.13.refs_4_ = bf16[2,96,1536]{2,1,0:T(8,128)(2,1)S(1)} collective-permute-done((bf16[2,96,1536]{2,1,0:T(8,128)(2,1)S(1)}, bf16[2,96,1536]{2,1,0:T(8,128)(2,1)S(1)}, u32[]{:S(2)}, u32[]{:S(2)}) %collective-permute-start.13) | collective-permute-done | bytes 589856 | tf_op jit(solution)/shard_map/ppermute | solution.py:403
  68.4 0.8 activations.6.refs_12_.refs_2_.refs_4_
  69.3 0.4 fusion.16
  69.8 0.6 collective-permute-start.20
  70.4 1.6 %collective-permute-start.22 = (bf16[2,192,512]{2,1,0:T(8,128)(2,1)S(1)}, bf16[2,192,512]{2,1,0:T(8,128)(2,1)S(1)}, u32[]{:S(2)}, u32[]{:S(2)}) collective-permute-start(bf16[2,192,512]{2,1,0:T(8,128)(2,1)S(1)} %pad_maximum_fusion.1.refs_10_), channel_id=1, source_target_pairs={{0,8},{4,12},{8,0},{12,4},{1,9},{5,13},{9,1},{13,5},{2,10},{6,14},... | collective-permute-start | bytes 1179656 | tf_op jit(solution)/shard_map/ppermute | solution.py:403
  72.0 0.6 collective-permute-start.24
  72.6 0.4 arrange.1
  73.0 3.6 %back.4 = (f32[96,1536]{1,0:T(8,128)S(1)}, bf16[96,1536]{1,0:T(8,128)(2,1)S(1)}) custom-call(s32[1]{0:T(128)} %bitcast.refs_0_, bf16[2,96,1536]{2,1,0:T(8,128)(2,1)S(1)} %activations.5.refs_4_.refs_1_.refs_3_, bf16[2,96,1536]{2,1,0:T(8,128)(2,1)S(1)} %activations.6.refs_12_.refs_2_.refs_4_, bf16[2,96,1536]{2,1,0:T(8,128)(2,1)S(1)} %collective-permute-done.15.refs_3_, ...), custom_call_target="tpu_custom_call" | custom-call | flops 1811939328 | bytes 10616832 | tf_op jit(solution)/shard_map/back/pallas_call | solution.py:67
  76.6 1.1 collective-permute-start.19
  77.7 4.0 %collective-permute-done.20.refs_4_ = bf16[2,192,512]{2,1,0:T(8,128)(2,1)S(1)} collective-permute-done((bf16[2,192,512]{2,1,0:T(8,128)(2,1)S(1)}, bf16[2,192,512]{2,1,0:T(8,128)(2,1)S(1)}, u32[]{:S(2)}, u32[]{:S(2)}) %collective-permute-start.20) | collective-permute-done | bytes 393248 | tf_op jit(solution)/shard_map/ppermute | solution.py:403
  81.7 0.5 activations.7.refs_5_.refs_6_.refs_1_
  82.3 3.9 %weight_grads.6 = (f32[1536,3072]{1,0:T(8,128)}, f32[3072,1536]{1,0:T(8,128)}, f32[8,128]{1,0:T(8,128)S(1)}) custom-call(s32[1]{0:T(128)} %bitcast.refs_0_, bf16[1536,384]{1,0:T(8,128)(2,1)S(1)} %get-tuple-element.46.refs_7_.refs_1_, bf16[384,1536]{1,0:T(8,128)(2,1)S(1)} %get-tuple-element.49.refs_2_, ...), custom_call_target="tpu_custom_call" | custom-call | flops 1207959552 | bytes 6291456 | tf_op jit(solution)/shard_map/weight_grads/pallas_call | solution.py:67
  86.3 2.1 %collective-permute-start.21 = (bf16[48,1536]{1,0:T(8,128)(2,1)S(1)}, bf16[48,1536]{1,0:T(8,128)(2,1)S(1)}, u32[]{:S(2)}, u32[]{:S(2)}) collective-permute-start(bf16[48,1536]{1,0:T(8,128)(2,1)S(1)} %fold.5.refs_5_), channel_id=1, source_target_pairs={{0,1},{1,0},{2,3},{3,2},{4,5},{5,4},{6,7},{7,6},{8,9},{9,8},{10,11... | collective-permute-start | bytes 442376 | tf_op jit(solution)/shard_map/ppermute | solution.py:403
  88.4 1.8 %collective-permute-done.22.refs_4_ = bf16[2,192,512]{2,1,0:T(8,128)(2,1)S(1)} collective-permute-done((bf16[2,192,512]{2,1,0:T(8,128)(2,1)S(1)}, bf16[2,192,512]{2,1,0:T(8,128)(2,1)S(1)}, u32[]{:S(2)}, u32[]{:S(2)}) %collective-permute-start.22) | collective-permute-done | bytes 393248 | tf_op jit(solution)/shard_map/ppermute | solution.py:403
  90.2 0.5 activations.8.refs_5_.refs_1_
  90.7 1.8 %back.5.refs_8_.refs_5_ = f32[192,1536]{1,0:T(8,128)S(1)} custom-call(s32[1]{0:T(128)} %bitcast.refs_0_, bf16[2,192,512]{2,1,0:T(8,128)(2,1)S(1)} %activations.7.refs_5_.refs_6_.refs_1_, bf16[2,192,512]{2,1,0:T(8,128)(2,1)S(1)} %collective-permute-done.23.refs_2_.refs_5_, bf16[1536,1536]{1,0:T(8,128)(2,1)S(1)} %bitcast.66, bf16[1536,1536]{1,0:T(8,128)(2,1)S(1)} %bitcast.64, ...), custom_call_target="tpu_custom_call" | custom-call | flops 603979776 | bytes 4325376 | tf_op jit(solution)/shard_map/back/pallas_call | solution.py:67
  92.6 3.9 %weight_grads.7 = (f32[1536,3072]{1,0:T(8,128)}, f32[3072,1536]{1,0:T(8,128)}, f32[8,128]{1,0:T(8,128)S(1)}) custom-call(s32[1]{0:T(128)} %bitcast.refs_0_, bf16[1536,384]{1,0:T(8,128)(2,1)S(1)} %get-tuple-element.46.refs_7_.refs_1_, bf16[384,1536]{1,0:T(8,128)(2,1)S(1)} %get-tuple-element.49.refs_2_, ...), custom_call_target="tpu_custom_call", output_to_operand_aliasing={{0}: (6, {}), {1}: (7, {})} | custom-call | flops 1207959552 | bytes 6291456 | tf_op jit(solution)/shard_map/weight_grads/pallas_call | solution.py:67
  96.4 3.8 %weight_grads.8 = (f32[1536,3072]{1,0:T(8,128)}, f32[3072,1536]{1,0:T(8,128)}, f32[8,128]{1,0:T(8,128)S(1)}) custom-call(s32[1]{0:T(128)} %bitcast.refs_0_, bf16[1536,384]{1,0:T(8,128)(2,1)S(1)} %get-tuple-element.46.refs_7_.refs_1_, bf16[384,1536]{1,0:T(8,128)(2,1)S(1)} %get-tuple-element.49.refs_2_, ...), custom_call_target="tpu_custom_call", output_to_operand_aliasing={{0}: (6, {}), {1}: (7, {})} | custom-call | flops 1207959552 | bytes 6291456 | tf_op jit(solution)/shard_map/weight_grads/pallas_call | solution.py:67
  100.3 0.5 activations.9.refs_6_.refs_1_.refs_5_
  100.8 0.5 collective-permute-start.25
  101.4 1.9 %back.6.refs_5_.refs_6_ = f32[192,1536]{1,0:T(8,128)S(1)} custom-call(s32[1]{0:T(128)} %bitcast.refs_0_, bf16[2,192,512]{2,1,0:T(8,128)(2,1)S(1)} %activations.8.refs_5_.refs_1_, bf16[2,192,512]{2,1,0:T(8,128)(2,1)S(1)} %collective-permute-done.26.refs_2_.refs_5_, bf16[1536,1536]{1,0:T(8,128)(2,1)S(1)} %bitcast.66, bf16[1536,1536]{1,0:T(8,128)(2,1)S(1)} %bitcast.64, ...), custom_call_target="tpu_custom_call" | custom-call | flops 603979776 | bytes 4325376 | tf_op jit(solution)/shard_map/back/pallas_call | solution.py:67
  103.3 1.9 %back.7 = (f32[96,1536]{1,0:T(8,128)S(1)}, bf16[96,1536]{1,0:T(8,128)(2,1)S(1)}) custom-call(s32[1]{0:T(128)} %bitcast.refs_0_, bf16[2,192,512]{2,1,0:T(8,128)(2,1)S(1)} %activations.9.refs_6_.refs_1_.refs_5_, bf16[2,192,512]{2,1,0:T(8,128)(2,1)S(1)} %collective-permute-done.25.refs_2_.refs_5_, bf16[1536,1536]{1,0:T(8,128)(2,1)S(1)} %bitcast.66, ...), custom_call_target="tpu_custom_call" | custom-call | flops 603979776 | bytes 4325376 | tf_op jit(solution)/shard_map/back/pallas_call | solution.py:67
  105.2 0.6 collective-permute-start.27
  105.8 3.8 %weight_grads.9 = (f32[1536,3072]{1,0:T(8,128)}, f32[3072,1536]{1,0:T(8,128)}, f32[8,128]{1,0:T(8,128)S(1)}) custom-call(s32[1]{0:T(128)} %bitcast.refs_0_, bf16[1536,384]{1,0:T(8,128)(2,1)S(1)} %get-tuple-element.46.refs_7_.refs_1_, bf16[384,1536]{1,0:T(8,128)(2,1)S(1)} %get-tuple-element.49.refs_2_, ...), custom_call_target="tpu_custom_call", output_to_operand_aliasing={{0}: (6, {}), {1}: (7, {})} | custom-call | flops 1207959552 | bytes 6291456 | tf_op jit(solution)/shard_map/weight_grads/pallas_call | solution.py:67
  109.6 4.6 %collective-permute-done.27.refs_2_ = bf16[96,1536]{1,0:T(8,128)(2,1)S(1)} collective-permute-done((bf16[96,1536]{1,0:T(8,128)(2,1)S(1)}, bf16[96,1536]{1,0:T(8,128)(2,1)S(1)}, u32[]{:S(2)}, u32[]{:S(2)}) %collective-permute-start.27) | collective-permute-done | bytes 294944 | tf_op jit(solution)/shard_map/ppermute | solution.py:403
  114.3 3.3 %collective-permute-start.28 = (bf16[48,1536]{1,0:T(8,128)(2,1)S(1)}, bf16[48,1536]{1,0:T(8,128)(2,1)S(1)}, u32[]{:S(2)}, u32[]{:S(2)}) collective-permute-start(bf16[48,1536]{1,0:T(8,128)(2,1)S(1)} %get-tuple-element.80), channel_id=1, source_target_pairs={{0,2},{1,3},{2,0},{3,1},{4,6},{5,7},{6,4},{7,5},{8,10},{9,11},{10,... | collective-permute-start | bytes 442376 | tf_op jit(solution)/shard_map/ppermute | solution.py:403
  117.6 1.2 collective-permute-start.29
  118.8 3.8 %weight_grads.10 = (f32[1536,3072]{1,0:T(8,128)}, f32[3072,1536]{1,0:T(8,128)}, f32[8,128]{1,0:T(8,128)S(1)}) custom-call(s32[1]{0:T(128)} %bitcast.refs_0_, bf16[1536,384]{1,0:T(8,128)(2,1)S(1)} %get-tuple-element.46.refs_7_.refs_1_, bf16[384,1536]{1,0:T(8,128)(2,1)S(1)} %get-tuple-element.49.refs_2_, ...), custom_call_target="tpu_custom_call", output_to_operand_aliasing={{0}: (6, {}), {1}: (7, {})} | custom-call | flops 1207959552 | bytes 6291456 | tf_op jit(solution)/shard_map/weight_grads/pallas_call | solution.py:67
  122.6 3.8 %weight_grads.11 = (f32[1536,3072]{1,0:T(8,128)}, f32[3072,1536]{1,0:T(8,128)}, f32[8,128]{1,0:T(8,128)}) custom-call(s32[1]{0:T(128)} %bitcast.refs_0_, bf16[1536,384]{1,0:T(8,128)(2,1)S(1)} %get-tuple-element.46.refs_7_.refs_1_, bf16[384,1536]{1,0:T(8,128)(2,1)S(1)} %get-tuple-element.49.refs_2_, ...), custom_call_target="tpu_custom_call", output_to_operand_aliasing={{0}: (6, {}), {1}: (7, {})} | custom-call | flops 1207959552 | bytes 6291456 | tf_op jit(solution)/shard_map/weight_grads/pallas_call | solution.py:67
  126.5 1.7 %collective-permute-done.28 = bf16[48,1536]{1,0:T(8,128)(2,1)S(1)} collective-permute-done((bf16[48,1536]{1,0:T(8,128)(2,1)S(1)}, bf16[48,1536]{1,0:T(8,128)(2,1)S(1)}, u32[]{:S(2)}, u32[]{:S(2)}) %collective-permute-start.28) | collective-permute-done | bytes 147488 | tf_op jit(solution)/shard_map/ppermute | solution.py:403
  128.2 0.7 add_convert_fusion
  (60 shorter events, 0.8 us)
Async XLA Ops:
  1.6 14.7 %collective-permute-start = (bf16[2,48,1536]{2,1,0:T(8,128)(2,1)S(1)}, bf16[2,48,1536]{2,1,0:T(8,128)(2,1)S(1)}, u32[]{:S(2)}, u32[]{:S(2)}) collective-permute-start(bf16[2,48,1536]{2,1,0:T(8,128)(2,1)S(1)} %pad_maximum_fusion.3.refs_1_), channel_id=1, source_target_pairs={{0,16},{16,0},{1,17},{17,1},{2,18},{18,2},{3,19},{19,3},{4,20},{20... | collective-permute-start | bytes 884744 | tf_op jit(solution)/shard_map/ppermute | solution.py:403
  4.6 18.0 %collective-permute-start.3 = (bf16[2,48,1536]{2,1,0:T(8,128)(2,1)S(1)}, bf16[2,48,1536]{2,1,0:T(8,128)(2,1)S(1)}, u32[]{:S(2)}, u32[]{:S(2)}) collective-permute-start(bf16[2,48,1536]{2,1,0:T(8,128)(2,1)S(1)} %pad_maximum_fusion.3.refs_1_), channel_id=1, source_target_pairs={{0,1},{1,0},{2,3},{3,2},{4,5},{5,4},{6,7},{7,6},{8,9},{9,8},{10,11... | collective-permute-start | bytes 884744 | tf_op jit(solution)/shard_map/ppermute | solution.py:403
  6.2 17.6 %collective-permute-start.5 = (bf16[2,48,1536]{2,1,0:T(8,128)(2,1)S(1)}, bf16[2,48,1536]{2,1,0:T(8,128)(2,1)}, u32[]{:S(2)}, u32[]{:S(2)}) collective-permute-start(bf16[2,48,1536]{2,1,0:T(8,128)(2,1)S(1)} %pad_maximum_fusion.3.refs_1_), channel_id=1, source_target_pairs={{1,2},{2,1},{5,6},{6,5},{9,10},{10,9},{13,14},{14,13},{17,18},{18,... | collective-permute-start | bytes 884744 | tf_op jit(solution)/shard_map/ppermute | solution.py:419
  14.1 2.2 %copy-start.5 = (bf16[1536,1536]{1,0:T(8,128)(2,1)}, bf16[1536,1536]{1,0:T(8,128)(2,1)S(1)}, u32[]{:S(2)}) copy-start(bf16[1536,1536]{1,0:T(8,128)(2,1)S(1)} %get-tuple-element.37.refs_4_.refs_6_) | copy-start | bytes 14155780
  16.3 3.6 %copy-start.1 = (bf16[1536,1536]{1,0:T(8,128)(2,1)}, bf16[1536,1536]{1,0:T(8,128)(2,1)S(1)}, u32[]{:S(2)}) copy-start(bf16[1536,1536]{1,0:T(8,128)(2,1)S(1)} %get-tuple-element.36.refs_3_.refs_5_) | copy-start | bytes 14155780
  16.3 5.8 %copy-start.3 = (bf16[1536,1536]{1,0:T(8,128)(2,1)}, bf16[1536,1536]{1,0:T(8,128)(2,1)S(1)}, u32[]{:S(2)}) copy-start(bf16[1536,1536]{1,0:T(8,128)(2,1)S(1)} %get-tuple-element.39.refs_4_.refs_6_) | copy-start | bytes 14155780
  19.9 2.2 %copy-start = (bf16[1536,1536]{1,0:T(8,128)(2,1)}, bf16[1536,1536]{1,0:T(8,128)(2,1)S(1)}, u32[]{:S(2)}) copy-start(bf16[1536,1536]{1,0:T(8,128)(2,1)S(1)} %get-tuple-element.38.refs_3_.refs_5_.refs_6_.refs_4_) | copy-start | bytes 14155780
  22.1 19.9 %slice-start = ((s8[4718592]{0:T(1024)(128)(4,1)}), s8[524288]{0:T(1024)(128)(4,1)S(1)}, s32[]{:S(2)}) async-start(s8[4718592]{0:T(1024)(128)(4,1)} %bitcast.63), calls=%async_computation | async-start | bytes 1048576
  22.1 11.3 %collective-permute-start.1 = (bf16[96,1536]{1,0:T(8,128)(2,1)S(1)}, bf16[96,1536]{1,0:T(8,128)(2,1)S(1)}, u32[]{:S(2)}, u32[]{:S(2)}) collective-permute-start(bf16[96,1536]{1,0:T(8,128)(2,1)S(1)} %get-tuple-element.40.refs_5_), channel_id=1, source_target_pairs={{0,4},{4,0},{8,12},{12,8},{1,5},{5,1},{9,13},{13,9},{2,6},{6,2},{1... | collective-permute-start | bytes 884744 | tf_op jit(solution)/shard_map/ppermute | solution.py:403
  22.1 11.3 %collective-permute-start.2 = (bf16[96,1536]{1,0:T(8,128)(2,1)S(1)}, bf16[96,1536]{1,0:T(8,128)(2,1)S(1)}, u32[]{:S(2)}, u32[]{:S(2)}) collective-permute-start(bf16[96,1536]{1,0:T(8,128)(2,1)S(1)} %get-tuple-element.41), channel_id=1, source_target_pairs={{0,4},{4,0},{8,12},{12,8},{1,5},{5,1},{9,13},{13,9},{2,6},{6,2},{1... | collective-permute-start | bytes 884744 | tf_op jit(solution)/shard_map/ppermute | solution.py:403
  22.6 10.8 %collective-permute-start.4 = (bf16[2,48,1536]{2,1,0:T(8,128)(2,1)S(1)}, bf16[2,48,1536]{2,1,0:T(8,128)(2,1)S(1)}, u32[]{:S(2)}, u32[]{:S(2)}) collective-permute-start(bf16[2,48,1536]{2,1,0:T(8,128)(2,1)S(1)} %collective-permute-done.3.refs_1_.refs_3_), channel_id=1, source_target_pairs={{0,16},{16,0},{1,17},{17,1},{2,18},{18,2},{3,19},{19,3},{4,20},{20... | collective-permute-start | bytes 884744 | tf_op jit(solution)/shard_map/ppermute | solution.py:403
  23.2 10.3 %collective-permute-start.7 = (bf16[2,48,1536]{2,1,0:T(8,128)(2,1)S(1)}, bf16[2,48,1536]{2,1,0:T(8,128)(2,1)S(1)}, u32[]{:S(2)}, u32[]{:S(2)}) collective-permute-start(bf16[2,48,1536]{2,1,0:T(8,128)(2,1)S(1)} %collective-permute-done.3.refs_1_.refs_3_), channel_id=1, source_target_pairs={{1,2},{2,1},{5,6},{6,5},{9,10},{10,9},{13,14},{14,13},{17,18},{18,... | collective-permute-start | bytes 884744 | tf_op jit(solution)/shard_map/ppermute | solution.py:420
  23.8 13.4 %collective-permute-start.6 = (bf16[2,48,1536]{2,1,0:T(8,128)(2,1)}, bf16[2,48,1536]{2,1,0:T(8,128)(2,1)S(1)}, u32[]{:S(2)}, u32[]{:S(2)}) collective-permute-start(bf16[2,48,1536]{2,1,0:T(8,128)(2,1)} %collective-permute-done.5), channel_id=1, source_target_pairs={{1,0},{2,3},{5,4},{6,7},{9,8},{10,11},{13,12},{14,15},{17,16},{18,... | collective-permute-start | bytes 884744 | tf_op jit(solution)/shard_map/ppermute | solution.py:421
  25.2 2.3 %copy-start.2 = (bf16[1536,1536]{1,0:T(8,128)(2,1)S(1)}, bf16[1536,1536]{1,0:T(8,128)(2,1)}, u32[]{:S(2)}) copy-start(bf16[1536,1536]{1,0:T(8,128)(2,1)} %copy-done.1) | copy-start | bytes 14155780
  27.5 2.3 %copy-start.6 = (bf16[1536,1536]{1,0:T(8,128)(2,1)S(1)}, bf16[1536,1536]{1,0:T(8,128)(2,1)}, u32[]{:S(2)}) copy-start(bf16[1536,1536]{1,0:T(8,128)(2,1)} %copy-done.5) | copy-start | bytes 14155780
  29.8 12.2 %slice-start.1 = ((s8[4718592]{0:T(1024)(128)(4,1)}), s8[4194304]{0:T(1024)(128)(4,1)S(1)}, s32[]{:S(2)}) async-start(s8[4718592]{0:T(1024)(128)(4,1)} %bitcast.63), calls=%async_computation.1 | async-start | bytes 8388608
  29.8 12.2 %copy-start.4 = (bf16[1536,1536]{1,0:T(8,128)(2,1)S(1)}, bf16[1536,1536]{1,0:T(8,128)(2,1)}, u32[]{:S(2)}) copy-start(bf16[1536,1536]{1,0:T(8,128)(2,1)} %copy-done.3) | copy-start | bytes 14155780
  33.4 17.1 %slice-start.2 = ((s8[4718592]{0:T(1024)(128)(4,1)}), s8[4194304]{0:T(1024)(128)(4,1)S(1)}, s32[]{:S(2)}) async-start(s8[4718592]{0:T(1024)(128)(4,1)} %bitcast.65), calls=%async_computation.2 | async-start | bytes 8388608
  37.6 16.5 %collective-permute-start.8 = (bf16[2,96,1536]{2,1,0:T(8,128)(2,1)S(1)}, bf16[2,96,1536]{2,1,0:T(8,128)(2,1)S(1)}, u32[]{:S(2)}, u32[]{:S(2)}) collective-permute-start(bf16[2,96,1536]{2,1,0:T(8,128)(2,1)S(1)} %combine.2.refs_5_), channel_id=1, source_target_pairs={{0,8},{4,12},{8,0},{12,4},{1,9},{5,13},{9,1},{13,5},{2,10},{6,14},... | collective-permute-start | bytes 1769480 | tf_op jit(solution)/shard_map/ppermute | solution.py:403
  39.1 9.7 %collective-permute-start.9 = (bf16[2,48,1536]{2,1,0:T(8,128)(2,1)S(1)}, bf16[2,48,1536]{2,1,0:T(8,128)(2,1)S(1)}, u32[]{:S(2)}, u32[]{:S(2)}) collective-permute-start(bf16[2,48,1536]{2,1,0:T(8,128)(2,1)S(1)} %collective-permute-done.7.refs_6_), channel_id=1, source_target_pairs={{1,0},{2,3},{5,4},{6,7},{9,8},{10,11},{13,12},{14,15},{17,16},{18,... | collective-permute-start | bytes 884744 | tf_op jit(solution)/shard_map/ppermute | solution.py:422
  40.5 10.0 %slice-start.3 = ((s8[4718592]{0:T(1024)(128)(4,1)}), s8[524288]{0:T(1024)(128)(4,1)S(1)}, s32[]{:S(2)}) async-start(s8[4718592]{0:T(1024)(128)(4,1)} %bitcast.65), calls=%async_computation.3 | async-start | bytes 1048576
  40.5 13.6 %collective-permute-start.10 = (bf16[2,48,1536]{2,1,0:T(8,128)(2,1)S(1)}, bf16[2,48,1536]{2,1,0:T(8,128)(2,1)S(1)}, u32[]{:S(2)}, u32[]{:S(2)}) collective-permute-start(bf16[2,48,1536]{2,1,0:T(8,128)(2,1)S(1)} %broadcast_select_fusion.1.refs_1_.refs_5_), channel_id=1, source_target_pairs={{0,16},{16,0},{1,17},{17,1},{2,18},{18,2},{3,19},{19,3},{4,20},{20... | collective-permute-start | bytes 884744 | tf_op jit(solution)/shard_map/ppermute | solution.py:403
  45.6 9.3 %collective-permute-start.11 = (bf16[96,1536]{1,0:T(8,128)(2,1)S(1)}, bf16[96,1536]{1,0:T(8,128)(2,1)S(1)}, u32[]{:S(2)}, u32[]{:S(2)}) collective-permute-start(bf16[96,1536]{1,0:T(8,128)(2,1)S(1)} %get-tuple-element.42.refs_5_), channel_id=1, source_target_pairs={{0,4},{4,0},{8,12},{12,8},{1,5},{5,1},{9,13},{13,9},{2,6},{6,2},{1... | collective-permute-start | bytes 884744 | tf_op jit(solution)/shard_map/ppermute | solution.py:403
  45.7 9.2 %collective-permute-start.12 = (bf16[96,1536]{1,0:T(8,128)(2,1)S(1)}, bf16[96,1536]{1,0:T(8,128)(2,1)S(1)}, u32[]{:S(2)}, u32[]{:S(2)}) collective-permute-start(bf16[96,1536]{1,0:T(8,128)(2,1)S(1)} %get-tuple-element.43), channel_id=1, source_target_pairs={{0,4},{4,0},{8,12},{12,8},{1,5},{5,1},{9,13},{13,9},{2,6},{6,2},{1... | collective-permute-start | bytes 884744 | tf_op jit(solution)/shard_map/ppermute | solution.py:403
  48.9 7.0 %collective-permute-start.14 = (bf16[2,48,1536]{2,1,0:T(8,128)(2,1)S(1)}, bf16[2,48,1536]{2,1,0:T(8,128)(2,1)S(1)}, u32[]{:S(2)}, u32[]{:S(2)}) collective-permute-start(bf16[2,48,1536]{2,1,0:T(8,128)(2,1)S(1)} %broadcast_select_fusion.refs_2_.refs_6_), channel_id=1, source_target_pairs={{0,16},{16,0},{1,17},{17,1},{2,18},{18,2},{3,19},{19,3},{4,20},{20... | collective-permute-start | bytes 884744 | tf_op jit(solution)/shard_map/ppermute | solution.py:403
  55.3 13.0 %collective-permute-start.13 = (bf16[2,96,1536]{2,1,0:T(8,128)(2,1)S(1)}, bf16[2,96,1536]{2,1,0:T(8,128)(2,1)S(1)}, u32[]{:S(2)}, u32[]{:S(2)}) collective-permute-start(bf16[2,96,1536]{2,1,0:T(8,128)(2,1)S(1)} %combine.3.refs_7_), channel_id=1, source_target_pairs={{0,8},{4,12},{8,0},{12,4},{1,9},{5,13},{9,1},{13,5},{2,10},{6,14},... | collective-permute-start | bytes 1769480 | tf_op jit(solution)/shard_map/ppermute | solution.py:403
  59.8 9.5 %collective-permute-start.17 = (bf16[192,1536]{1,0:T(8,128)(2,1)S(1)}, bf16[192,1536]{1,0:T(8,128)(2,1)S(1)}, u32[]{:S(2)}, u32[]{:S(2)}) collective-permute-start(bf16[192,1536]{1,0:T(8,128)(2,1)S(1)} %get-tuple-element.44.refs_7_), channel_id=1, source_target_pairs={{0,4},{4,0},{8,12},{12,8},{1,5},{5,1},{9,13},{13,9},{2,6},{6,2},{1... | collective-permute-start | bytes 1769480 | tf_op jit(solution)/shard_map/ppermute | solution.py:403
  59.9 9.4 %collective-permute-start.18 = (bf16[192,1536]{1,0:T(8,128)(2,1)S(1)}, bf16[192,1536]{1,0:T(8,128)(2,1)S(1)}, u32[]{:S(2)}, u32[]{:S(2)}) collective-permute-start(bf16[192,1536]{1,0:T(8,128)(2,1)S(1)} %get-tuple-element.45), channel_id=1, source_target_pairs={{0,4},{4,0},{8,12},{12,8},{1,5},{5,1},{9,13},{13,9},{2,6},{6,2},{1... | collective-permute-start | bytes 1769480 | tf_op jit(solution)/shard_map/ppermute | solution.py:403
  60.4 12.6 %collective-permute-start.15 = (bf16[2,96,1536]{2,1,0:T(8,128)(2,1)S(1)}, bf16[2,96,1536]{2,1,0:T(8,128)(2,1)S(1)}, u32[]{:S(2)}, u32[]{:S(2)}) collective-permute-start(bf16[2,96,1536]{2,1,0:T(8,128)(2,1)S(1)} %activations.5.refs_4_.refs_1_.refs_3_), channel_id=1, source_target_pairs={{0,4},{4,0},{8,12},{12,8},{1,5},{5,1},{9,13},{13,9},{2,6},{6,2},{1... | collective-permute-start | bytes 1769480 | tf_op jit(solution)/shard_map/ppermute | solution.py:403
  69.2 3.8 %collective-permute-start.16 = (bf16[2,96,1536]{2,1,0:T(8,128)(2,1)S(1)}, bf16[2,96,1536]{2,1,0:T(8,128)(2,1)S(1)}, u32[]{:S(2)}, u32[]{:S(2)}) collective-permute-start(bf16[2,96,1536]{2,1,0:T(8,128)(2,1)S(1)} %activations.6.refs_12_.refs_2_.refs_4_), channel_id=1, source_target_pairs={{0,4},{4,0},{8,12},{12,8},{1,5},{5,1},{9,13},{13,9},{2,6},{6,2},{1... | collective-permute-start | bytes 1769480 | tf_op jit(solution)/shard_map/ppermute | solution.py:403
  69.8 12.0 %collective-permute-start.20 = (bf16[2,192,512]{2,1,0:T(8,128)(2,1)S(1)}, bf16[2,192,512]{2,1,0:T(8,128)(2,1)S(1)}, u32[]{:S(2)}, u32[]{:S(2)}) collective-permute-start(bf16[2,192,512]{2,1,0:T(8,128)(2,1)S(1)} %pad_maximum_fusion.2.refs_11_), channel_id=1, source_target_pairs={{0,8},{4,12},{8,0},{12,4},{1,9},{5,13},{9,1},{13,5},{2,10},{6,14},... | collective-permute-start | bytes 1179656 | tf_op jit(solution)/shard_map/ppermute | solution.py:403
  70.4 19.8 %collective-permute-start.22 = (bf16[2,192,512]{2,1,0:T(8,128)(2,1)S(1)}, bf16[2,192,512]{2,1,0:T(8,128)(2,1)S(1)}, u32[]{:S(2)}, u32[]{:S(2)}) collective-permute-start(bf16[2,192,512]{2,1,0:T(8,128)(2,1)S(1)} %pad_maximum_fusion.1.refs_10_), channel_id=1, source_target_pairs={{0,8},{4,12},{8,0},{12,4},{1,9},{5,13},{9,1},{13,5},{2,10},{6,14},... | collective-permute-start | bytes 1179656 | tf_op jit(solution)/shard_map/ppermute | solution.py:403
  72.0 28.3 %collective-permute-start.24 = (bf16[2,192,512]{2,1,0:T(8,128)(2,1)S(1)}, bf16[2,192,512]{2,1,0:T(8,128)(2,1)S(1)}, u32[]{:S(2)}, u32[]{:S(2)}) collective-permute-start(bf16[2,192,512]{2,1,0:T(8,128)(2,1)S(1)} %pad_maximum_fusion.refs_9_), channel_id=1, source_target_pairs={{0,8},{4,12},{8,0},{12,4},{1,9},{5,13},{9,1},{13,5},{2,10},{6,14},... | collective-permute-start | bytes 1179656 | tf_op jit(solution)/shard_map/ppermute | solution.py:403
  76.6 9.6 %collective-permute-start.19 = (bf16[96,1536]{1,0:T(8,128)(2,1)S(1)}, bf16[96,1536]{1,0:T(8,128)(2,1)S(1)}, u32[]{:S(2)}, u32[]{:S(2)}) collective-permute-start(bf16[96,1536]{1,0:T(8,128)(2,1)S(1)} %get-tuple-element.48), channel_id=1, source_target_pairs={{0,16},{16,0},{1,17},{17,1},{2,18},{18,2},{3,19},{19,3},{4,20},{20... | collective-permute-start | bytes 884744 | tf_op jit(solution)/shard_map/ppermute | solution.py:403
  82.2 8.5 %collective-permute-start.23 = (bf16[2,192,512]{2,1,0:T(8,128)(2,1)S(1)}, bf16[2,192,512]{2,1,0:T(8,128)(2,1)S(1)}, u32[]{:S(2)}, u32[]{:S(2)}) collective-permute-start(bf16[2,192,512]{2,1,0:T(8,128)(2,1)S(1)} %activations.7.refs_5_.refs_6_.refs_1_), channel_id=1, source_target_pairs={{0,4},{4,0},{8,12},{12,8},{1,5},{5,1},{9,13},{13,9},{2,6},{6,2},{1... | collective-permute-start | bytes 1179656 | tf_op jit(solution)/shard_map/ppermute | solution.py:403
  86.3 14.0 %collective-permute-start.21 = (bf16[48,1536]{1,0:T(8,128)(2,1)S(1)}, bf16[48,1536]{1,0:T(8,128)(2,1)S(1)}, u32[]{:S(2)}, u32[]{:S(2)}) collective-permute-start(bf16[48,1536]{1,0:T(8,128)(2,1)S(1)} %fold.5.refs_5_), channel_id=1, source_target_pairs={{0,1},{1,0},{2,3},{3,2},{4,5},{5,4},{6,7},{7,6},{8,9},{9,8},{10,11... | collective-permute-start | bytes 442376 | tf_op jit(solution)/shard_map/ppermute | solution.py:403
  90.7 10.7 %collective-permute-start.26 = (bf16[2,192,512]{2,1,0:T(8,128)(2,1)S(1)}, bf16[2,192,512]{2,1,0:T(8,128)(2,1)S(1)}, u32[]{:S(2)}, u32[]{:S(2)}) collective-permute-start(bf16[2,192,512]{2,1,0:T(8,128)(2,1)S(1)} %activations.8.refs_5_.refs_1_), channel_id=1, source_target_pairs={{0,4},{4,0},{8,12},{12,8},{1,5},{5,1},{9,13},{13,9},{2,6},{6,2},{1... | collective-permute-start | bytes 1179656 | tf_op jit(solution)/shard_map/ppermute | solution.py:403
  100.8 2.5 %collective-permute-start.25 = (bf16[2,192,512]{2,1,0:T(8,128)(2,1)S(1)}, bf16[2,192,512]{2,1,0:T(8,128)(2,1)S(1)}, u32[]{:S(2)}, u32[]{:S(2)}) collective-permute-start(bf16[2,192,512]{2,1,0:T(8,128)(2,1)S(1)} %activations.9.refs_6_.refs_1_.refs_5_), channel_id=1, source_target_pairs={{0,4},{4,0},{8,12},{12,8},{1,5},{5,1},{9,13},{13,9},{2,6},{6,2},{1... | collective-permute-start | bytes 1179656 | tf_op jit(solution)/shard_map/ppermute | solution.py:403
  105.2 9.0 %collective-permute-start.27 = (bf16[96,1536]{1,0:T(8,128)(2,1)S(1)}, bf16[96,1536]{1,0:T(8,128)(2,1)S(1)}, u32[]{:S(2)}, u32[]{:S(2)}) collective-permute-start(bf16[96,1536]{1,0:T(8,128)(2,1)S(1)} %get-tuple-element.58), channel_id=1, source_target_pairs={{0,16},{16,0},{1,17},{17,1},{2,18},{18,2},{3,19},{19,3},{4,20},{20... | collective-permute-start | bytes 884744 | tf_op jit(solution)/shard_map/ppermute | solution.py:403
  114.3 13.9 %collective-permute-start.28 = (bf16[48,1536]{1,0:T(8,128)(2,1)S(1)}, bf16[48,1536]{1,0:T(8,128)(2,1)S(1)}, u32[]{:S(2)}, u32[]{:S(2)}) collective-permute-start(bf16[48,1536]{1,0:T(8,128)(2,1)S(1)} %get-tuple-element.80), channel_id=1, source_target_pairs={{0,2},{1,3},{2,0},{3,1},{4,6},{5,7},{6,4},{7,5},{8,10},{9,11},{10,... | collective-permute-start | bytes 442376 | tf_op jit(solution)/shard_map/ppermute | solution.py:403
  117.6 10.6 %collective-permute-start.29 = (bf16[48,1536]{1,0:T(8,128)(2,1)S(1)}, bf16[48,1536]{1,0:T(8,128)(2,1)S(1)}, u32[]{:S(2)}, u32[]{:S(2)}) collective-permute-start(bf16[48,1536]{1,0:T(8,128)(2,1)S(1)} %get-tuple-element.81), channel_id=1, source_target_pairs={{0,3},{1,2},{2,1},{3,0},{4,7},{5,6},{6,5},{7,4},{8,11},{9,10},{10,... | collective-permute-start | bytes 442376 | tf_op jit(solution)/shard_map/ppermute | solution.py:403

commit v6 on v5

--- a/solution.py
+++ b/solution.py
@@ -124,8 +124,8 @@
         core,
         [up, down],
         [pl.BlockSpec(memory_space=pltpu.HBM)] * 2,
-        [jax.ShapeDtypeStruct(shape, BF16) for shape in shapes],
-        [pl.BlockSpec(memory_space=pl.ANY)] * 4,
+        [pltpu.VMEM(shape, BF16) for shape in shapes],
+        [pl.BlockSpec(memory_space=pltpu.VMEM)] * 4,
         (1,),
         (0, 4 * depth * full),
         "bring",
@@ -134,11 +134,11 @@
     )
 
 
-def partial_sums(core, units, up, down, side, apart, after=()):
+def partial_sums(core, units, up, down, side, apart, start, width, after=()):
     _, rows, depth = units[0].shape
     tokens = rows * len(units)
-    width = up.shape[1]
     tile = tile_of(width, 256)
+    first = start // tile
     dtype = BF16 if side else F32
 
     def body(core_ref, *refs):
@@ -171,8 +171,8 @@
         [*units, up, down],
         [whole(units[0].shape)] * len(units)
         + [
-            pl.BlockSpec((depth, tile), lambda i, c: (0, i)),
-            pl.BlockSpec((tile, depth), lambda i, c: (i, 0)),
+            pl.BlockSpec((depth, tile), lambda i, c: (0, first + i)),
+            pl.BlockSpec((tile, depth), lambda i, c: (first + i, 0)),
         ],
         outs,
         specs,
@@ -184,11 +184,11 @@
     )
 
 
-def combine(core, keep, near, after):
+def combine(core, keep, near, start, after):
     _, tokens, width = keep.shape
-    tile = tile_of(width, 512)
+    tile = tile_of(width, 256)
     both = pl.BlockSpec((2, tokens, tile), lambda i, c: (0, 0, i))
-    one = pl.BlockSpec((tokens, tile), lambda i, c: (0, i))
+    one = pl.BlockSpec((tokens, tile), lambda i, c: (0, start // tile + i))
 
     def body(core_ref, keep_ref, preact_ref, grad_ref, chip_ref):
         chip_ref[0] = (keep_ref[0] + preact_ref[...].astype(F32)).astype(BF16)
@@ -208,20 +208,20 @@
     )
 
 
-def activations(core, keep, near, far, start, after=()):
+def activations(core, keep, near, far, row, start, near_start, after=()):
     _, tokens, width = far.shape
     tile = tile_of(width, 256)
-    first = start // tile
-    both = pl.BlockSpec((2, tokens, tile), lambda i, c: (0, 0, first + i))
+    first, near_first, block = start // tile, near_start // tile, row // tokens
+    both = pl.BlockSpec((2, tokens, tile), lambda i, c: (0, block, first + i))
     both_here = pl.BlockSpec((2, tokens, tile), lambda i, c: (0, 0, i))
-    one = pl.BlockSpec((tokens, tile), lambda i, c: (0, first + i))
+    one = pl.BlockSpec((tokens, tile), lambda i, c: (block, near_first + i))
 
     def body(core_ref, keep_ref, *refs):
         *near_refs, far_ref, act_ref = refs
 
         def total(which):
-            part = near_refs[which][...] if len(near) > 1 else near_refs[0][which]
-            return keep_ref[which] + part.astype(F32) + far_ref[which].astype(F32)
+            part = near_refs[which][...].astype(F32)
+            return keep_ref[which] + part + far_ref[which].astype(F32)
 
         preact = total(0)
         cdf = 0.5 + 0.5 * lax.erf(preact * (0.5**0.5))
@@ -233,7 +233,7 @@
         body,
         core,
         [keep, *near, far],
-        [both] + [one if len(near) > 1 else both] * len(near) + [both_here],
+        [both, one, one, both_here],
         jax.ShapeDtypeStruct(far.shape, BF16),
         both_here,
         (width // tile,),
@@ -243,9 +243,8 @@
     )
 
 
-def back(core, acts, ups, start, before, order, leave, after=()):
-    width = acts[0][0].shape[2]
-    tokens = sum(keep.shape[1] for keep, _ in acts)
+def back(core, acts, ups, start, width, before, order, leave, after=()):
+    tokens = sum(which[0].shape[1] for which in acts)
     depth = ups[0].shape[0]
     tile = tile_of(depth, 512)
     groups = len(acts)
@@ -274,11 +273,15 @@
         rows = tokens // len(order)
         kinds = [(leave * rows, F32), (tokens - leave * rows, BF16)]
     operands = [which[side] for side in range(2) for which in acts]
+    firsts = [which[2] // width for side in range(2) for which in acts]
     return call(
         body,
         core,
         [*operands, *ups] + ([] if before is None else [before]),
-        [pl.BlockSpec((1, array.shape[1], width), lambda i, c: (1, 0, 0)) for array in operands]
+        [
+            pl.BlockSpec((1, array.shape[1], width), lambda i, c, first=first: (1, 0, first))
+            for array, first in zip(operands, firsts)
+        ]
         + [pl.BlockSpec((tile, width), lambda i, c: (i, start // width))] * 2
         + ([] if before is None else [pl.BlockSpec((tokens, tile), lambda i, c: (0, i))]),
         [jax.ShapeDtypeStruct((rows, depth), dtype) for rows, dtype in kinds],
@@ -406,8 +409,7 @@
 def cube_body(inputs, cotangent, up, down):
     rows = inputs.shape[0]
     half = up.shape[1] // 2
-    width = half // 3 if half % 384 == 0 else half
-    chunks = half // width
+    width = half // 2
     core = (lax.axis_index("gy") % 2).astype(jnp.int32).reshape(1)
 
     unit = {(0, 0): jnp.stack([inputs, cotangent])}
@@ -427,51 +429,71 @@
     groups = [
         [unit[0, 0], unit[0, 1]],
         [unit[1, 0], unit[1, 1]],
-        [unit[2, 0], unit[3, 0], unit[2, 1], unit[3, 1]],
+        [unit[2, 0], unit[2, 1], unit[3, 0], unit[3, 1]],
     ]
 
-    pieces = [(0, 0, half), (1, 0, half)] + [(2, j * width, width) for j in range(chunks)]
+    pair = 2 * rows
+    pieces = [
+        (0, 0, 0, width),
+        (0, 0, width, width),
+        (1, 0, 0, half),
+        (2, 0, 0, half),
+        (2, pair, 0, width),
+        (2, pair, width, width),
+    ]
     near, keep, far, act, act_near = {}, {}, {}, {}, {}
     *weights, = bring(core, up, down)
     ups, downs = weights[0::2], weights[1::2]
 
-    def sums(group, side, after):
-        return partial_sums(core, groups[group], ups[side], downs[side], side, side == 1, after)
-
-    def product(group, after, between=()):
-        out = sums(group, 1, after)
+    def send(group, after=()):
+        out = partial_sums(
+            core, groups[group], ups[1], downs[1], 1, True, 0, half, after
+        )
         near[group] = [swap(array, "gy", 4, 1) for array in out]
-        keep[group], = sums(group, 0, [out[0], *between])
-        return [keep[group]]
+        return [out[0]]
+
+    def hold(group, start, size, after):
+        out, = partial_sums(
+            core, groups[group], ups[0], downs[0], 0, False, start, size, after
+        )
+        keep[group, start] = out
+        return [out]
+
+    def kept(group, start):
+        return (keep[group, start], 0) if (group, start) in keep else (keep[group, 0], start)
 
     def cross(n, after=()):
-        group, start, size = pieces[n]
-        span = slice(start, start + size)
+        group, row, start, size = pieces[n]
+        array, column = kept(group, start)
         if after:
-            chip = combine(core, keep[group], near[group], after)
+            chip = combine(core, array, near[group], start, after)
         else:
             chip = jnp.stack([
-                (keep[group][which, :, span] + near[group][which][:, span].astype(F32)).astype(BF16)
+                (
+                    array[which, row : row + pair, column : column + size]
+                    + near[group][which][row : row + pair, start : start + size].astype(F32)
+                ).astype(BF16)
                 for which in range(2)
             ])
         far[n] = swap(chip, "gy", 4, 2)
         return [chip]
 
     def ready(n, after):
-        group, start, _ = pieces[n]
-        act[n] = activations(core, keep[group], near[group], far[n], start, after)
+        group, row, start, _ = pieces[n]
+        array, column = kept(group, start)
+        act[n] = activations(core, array, near[group], far[n], row, column, start, after)
         act_near[n] = swap(act[n], "gy", 4, 1)
         return [act[n]]
 
-    def inward(many, start, part, order, leave, after):
-        which = [(act[n], act_near[n]) for n in many]
-        return back(core, which, (ups[0], ups[1]), start, part, order, leave, after)
+    def inward(which, start, size, part, order, leave, after):
+        acts = [(act[n], act_near[n], offset) for n, offset in which]
+        return back(core, acts, ups, start, size, part, order, leave, after)
 
     outputs = None
 
     def gradients(j, sides, after):
         acts = [
-            [(array[n], j * width) for n in range(2)] + [(array[2 + j], 0)]
+            [(array[j], 0), (array[2], j * width), (array[3], j * width), (array[4 + j], 0)]
             for array in (act, act_near)
         ]
         acts = [acts[side] for side in sides]
@@ -479,50 +501,50 @@
             core, inputs_t, cotan, sides, acts, j * width, width, up.shape, outputs, after
         )
 
-    last = product(0, (), ())
-    last = cross(0, [unit[1, 1], first_on, second])
-    last = product(1, last, [second_on])
-    last = ready(0, [*last, unit[2, 1]])
-    last = cross(1, last)
-    last = product(2, last)
-    last = ready(1, last)
-    for j in range(chunks):
-        last = cross(2 + j) + last
+    def finish(j, sides, after):
+        nonlocal outputs
+        *outputs, done = gradients(j, sides, after)
+        return [done]
+
+    last = send(0)
+    last = hold(0, 0, width, last)
+    last = cross(0) + last
+    last = hold(0, width, width, last + [])
+    last = cross(1, last + [])
+    last = send(1, last + [unit[1, 1], second, first_on])
+    last = hold(1, 0, half, [*last, second_on])
+    last = ready(0, last)
+    last = ready(1, [*last, unit[2, 1]])
+    last = cross(2, last)
+    last = send(2, last)
+    last = hold(2, 0, half, last)
+    last = ready(2, last)
+    last = cross(3) + cross(4) + cross(5) + last
     inputs_t, cotan = arrange(core, [u for group in groups for u in group], last)
-    stay1, go1 = inward((0, 1), 0, None, (0, 2, 1, 3), 2, [inputs_t])
+    part, = inward(((0, 0), (2, 0)), 0, width, None, None, None, [inputs_t])
+    stay1, go1 = inward(((1, 0), (2, width)), width, width, part, (0, 2, 1, 3), 2, [part])
     near1 = swap(go1, "gx", 2, 1)
 
-    part, last = None, [stay1]
-    for j in range(chunks):
-        n, final = 2 + j, j + 1 == chunks
-        last = ready(n, last)
-        if j:
-            last = part, = inward((n - 1,), (j - 1) * width, part, None, None, last)
-        if final:
-            stay2, go2 = inward((n,), j * width, part, (0, 1, 2, 3), 2, last)
-            near2 = swap(go2, "gx", 2, 1)
-            last = [stay2]
-        if j:
-            *outputs, done = gradients(j - 1, (1,), last)
-            last = [done]
-        if final:
-            back2 = fold(core, stay2, near2, BF16, last)
-            far2 = swap(back2[:rows], "gz", 4, 2)
-            far3 = swap(back2[rows:], "gz", 4, 3)
-            last = [back2]
-        *outputs, done = gradients(j, (0,), last)
-        last = [done]
-        if j == 0:
-            total = fold(core, stay1[:rows], near1[:rows], F32, last)
-            back1 = fold(core, stay1[rows:], near1[rows:], BF16, [total])
-            far1 = swap(back1, "gz", 4, 1)
-            last = [back1]
-        elif j == 1 and not final:
-            total = fold(core, total, far1, F32, last)
-            last = [total]
-    if chunks < 3:
-        total = total + far1.astype(F32)
-    *outputs, done = gradients(chunks - 1, (1,), last)
+    last = ready(3, [stay1])
+    total = fold(core, stay1[:rows], near1[:rows], F32, last)
+    back1 = fold(core, stay1[rows:], near1[rows:], BF16, [total])
+    far1 = swap(back1, "gz", 4, 1)
+    stay2, go2 = inward(((3, 0),), 0, half, None, (0, 1), 1, [back1])
+    near2 = swap(go2, "gx", 2, 1)
+
+    last = ready(4, [stay2])
+    last = finish(0, (0,), last)
+    back2 = fold(core, stay2, near2, BF16, last)
+    far2 = swap(back2, "gz", 4, 2)
+    total = fold(core, total, far1, F32, [back2])
+    last = ready(5, [total])
+    part, = inward(((4, 0),), 0, width, None, None, None, last)
+    stay3, go3 = inward(((5, 0),), width, width, part, (0, 1), 1, [part])
+    near3 = swap(go3, "gx", 2, 1)
+    last = finish(0, (1,), [stay3])
+    back3 = fold(core, stay3, near3, BF16, last)
+    far3 = swap(back3, "gz", 4, 3)
+    finish(1, (0, 1), [back3])
     total = total + far2.astype(F32) + far3.astype(F32)
     return (total.astype(BF16), *outputs)
 

time: 129 us -> 130 us (level)
    ppermute x1, waiting for transfers between devices: 2.67 us -> 0.22 us  [cube_body(): second_on = lax.ppermute(second, 'gz', outward)]
    ppermute x26 -> x29, waiting for transfers between devices: 16.3 us -> 18.6 us  [swap(): return lax.ppermute(value, axis, [(i, i ^ bits) for i in range(size)])]
    ppermute x26 -> x29, starting transfers between devices: 23.8 us -> 25 us  [swap(): return lax.ppermute(value, axis, [(i, i ^ bits) for i in range(size)])]
    pallas_call x29 -> x30, Pallas kernels: 65.1 us -> 66.1 us  [call(): pl.pallas_call(kernel, grid_spec=pltpu.PrefetchScalarGridSpec(num_scalar_...]
    unnamed x22 -> x28, local copies, waits for them, and re-layouts: 9.06 us -> 9.15 us
  transfers between devices with their start and end apart: 30 -> 33, of which waited for: 7 -> 7; matrix products, arithmetic and copies ran while one was open for 1% -> 0% of each run, Pallas kernels for 49% -> 51%
where the time goes in v6:
time: 130 us
  Pallas kernels  66.1 us (51%)
  starting transfers between devices  28.9 us (22%)
  waiting for transfers between devices  21.9 us (17%)
  local copies, waits for them, and re-layouts  9.21 us (7%)
  other arithmetic  2.26 us (2%)
    pallas_call x30, Pallas kernels, call(): pl.pallas_call(kernel, grid_spec=pltpu.PrefetchScalarGridSpec(num_scalar_...  66.1 us
    ppermute x29, starting transfers between devices, swap(): return lax.ppermute(value, axis, [(i, i ^ bits) for i in range(size)])  25 us
    ppermute x29, waiting for transfers between devices, swap(): return lax.ppermute(value, axis, [(i, i ^ bits) for i in range(size)])  18.6 us
    unnamed x28, local copies, waits for them, and re-layouts  9.15 us
    ppermute x1, waiting for transfers between devices, cube_body(): first_on = lax.ppermute(first, 'gz', outward)  3.05 us
  transfers between devices with their start and end apart: 33, of which 7 were waited for; matrix products, arithmetic and copies ran while one was open for 0% of the time, Pallas kernels for 51%

profile of v6, /device:TPU:0, one launch (start us, length us, event | category | flops | bytes accessed | tf_op | source)
XLA Modules:
  0.0 129.6 jit_solution(3924605483400489361)
XLA Ops:
  0.6 1.0 pad_maximum_fusion.1.refs_1_
  1.6 3.0 %collective-permute-start = (bf16[2,48,1536]{2,1,0:T(8,128)(2,1)S(1)}, bf16[2,48,1536]{2,1,0:T(8,128)(2,1)S(1)}, u32[]{:S(2)}, u32[]{:S(2)}) collective-permute-start(bf16[2,48,1536]{2,1,0:T(8,128)(2,1)S(1)} %pad_maximum_fusion.1.refs_1_), channel_id=1, source_target_pairs={{0,16},{16,0},{1,17},{17,1},{2,18},{18,2},{3,19},{19,3},{4,20},{20... | collective-permute-start | bytes 884744 | tf_op jit(solution)/shard_map/ppermute | solution.py:406
  4.6 1.6 %collective-permute-start.5 = (bf16[2,48,1536]{2,1,0:T(8,128)(2,1)S(1)}, bf16[2,48,1536]{2,1,0:T(8,128)(2,1)S(1)}, u32[]{:S(2)}, u32[]{:S(2)}) collective-permute-start(bf16[2,48,1536]{2,1,0:T(8,128)(2,1)S(1)} %pad_maximum_fusion.1.refs_1_), channel_id=1, source_target_pairs={{0,1},{1,0},{2,3},{3,2},{4,5},{5,4},{6,7},{7,6},{8,9},{9,8},{10,11... | collective-permute-start | bytes 884744 | tf_op jit(solution)/shard_map/ppermute | solution.py:406
  6.2 0.7 collective-permute-start.8
  6.9 6.5 %bring.1 = (bf16[1536,1536]{1,0:T(8,128)(2,1)S(1)}, bf16[1536,1536]{1,0:T(8,128)(2,1)S(1)}, bf16[1536,1536]{1,0:T(8,128)(2,1)S(1)}, bf16[1536,1536]{1,0:T(8,128)(2,1)S(1)}) custom-call(s32[1]{0:T(128)} %bitcast.refs_0_, bf16[1536,3072]{1,0:T(8,128)(2,1)} %refs_1_.1, bf16[3072,1536]{1,0:T(8,128)(2,1)} %refs_2_.1), custom_call_target="tpu_custom_call" | custom-call | bytes 18874368 | tf_op jit(solution)/shard_map/bring/pallas_call | solution.py:67
  13.5 2.2 %copy-done = bf16[1536,1536]{1,0:T(8,128)(2,1)} copy-done((bf16[1536,1536]{1,0:T(8,128)(2,1)}, bf16[1536,1536]{1,0:T(8,128)(2,1)S(1)}, u32[]{:S(2)}) %copy-start) | copy-done | bytes 4718616
  15.6 2.2 %copy-done.3 = bf16[1536,1536]{1,0:T(8,128)(2,1)} copy-done((bf16[1536,1536]{1,0:T(8,128)(2,1)}, bf16[1536,1536]{1,0:T(8,128)(2,1)S(1)}, u32[]{:S(2)}) %copy-start.3) | copy-done | bytes 4718616
  17.8 3.6 %sums_send.3 = (bf16[96,1536]{1,0:T(8,128)(2,1)S(1)}, bf16[96,1536]{1,0:T(8,128)(2,1)S(1)}) custom-call(s32[1]{0:T(128)} %bitcast.refs_0_, bf16[2,48,1536]{2,1,0:T(8,128)(2,1)S(1)} %pad_maximum_fusion.1.refs_1_, bf16[2,48,1536]{2,1,0:T(8,128)(2,1)S(1)} %collective-permute-done.refs_2_, ...), custom_call_target="tpu_custom_call" | custom-call | flops 905969664 | bytes 9437184 | tf_op jit(solution)/shard_map/sums_send/pallas_call | solution.py:67
  21.5 0.5 collective-permute-start.2
  22.0 0.7 collective-permute-start.7
  22.7 0.6 collective-permute-start.6
  23.3 1.3 collective-permute-start.9
  24.6 2.3 %copy-done.1 = bf16[1536,1536]{1,0:T(8,128)(2,1)S(1)} copy-done((bf16[1536,1536]{1,0:T(8,128)(2,1)S(1)}, bf16[1536,1536]{1,0:T(8,128)(2,1)}, u32[]{:S(2)}) %copy-start.1) | copy-done | bytes 4718616
  26.9 2.3 %copy-done.4 = bf16[1536,1536]{1,0:T(8,128)(2,1)S(1)} copy-done((bf16[1536,1536]{1,0:T(8,128)(2,1)S(1)}, bf16[1536,1536]{1,0:T(8,128)(2,1)}, u32[]{:S(2)}) %copy-start.4) | copy-done | bytes 4718616
  29.2 1.8 %sums_keep.4.refs_6_.refs_1_ = f32[2,96,768]{2,1,0:T(8,128)S(1)} custom-call(s32[1]{0:T(128)} %bitcast.refs_0_, bf16[2,48,1536]{2,1,0:T(8,128)(2,1)S(1)} %pad_maximum_fusion.1.refs_1_, bf16[2,48,1536]{2,1,0:T(8,128)(2,1)S(1)} %collective-permute-done.refs_2_, bf16[1536,1536]{1,0:T(8,128)(2,1)S(1)} %copy-done.1, bf16[1536,1536]{1,0:T(8,128)(2,1)S(1)} %copy-done.4, ...), custom_call_target="tpu_custom_call" | custom-call | flops 452984832 | bytes 4718592 | tf_op jit(solution)/shard_map/sums_keep/pallas_call | solution.py:67
  31.2 1.6 %collective-permute-start.4 = (bf16[2,96,768]{2,1,0:T(8,128)(2,1)S(1)}, bf16[2,96,768]{2,1,0:T(8,128)(2,1)S(1)}, u32[]{:S(2)}, u32[]{:S(2)}) collective-permute-start(bf16[2,96,768]{2,1,0:T(8,128)(2,1)S(1)} %pad_maximum_fusion.2.refs_5_), channel_id=1, source_target_pairs={{0,8},{4,12},{8,0},{12,4},{1,9},{5,13},{9,1},{13,5},{2,10},{6,14},... | collective-permute-start | bytes 884744 | tf_op jit(solution)/shard_map/ppermute | solution.py:406
  32.8 1.3 collective-permute-start.10
  34.1 3.1 %collective-permute-done.9.refs_8_ = bf16[2,48,1536]{2,1,0:T(8,128)(2,1)S(1)} collective-permute-done((bf16[2,48,1536]{2,1,0:T(8,128)(2,1)S(1)}, bf16[2,48,1536]{2,1,0:T(8,128)(2,1)S(1)}, u32[]{:S(2)}, u32[]{:S(2)}) %collective-permute-start.9) | collective-permute-done | bytes 294944 | tf_op jit(solution)/shard_map/ppermute | solution.py:423
  37.2 1.9 %sums_keep.5.refs_1_.refs_4_ = f32[2,96,768]{2,1,0:T(8,128)S(1)} custom-call(s32[1]{0:T(128)} %bitcast.refs_0_, bf16[2,48,1536]{2,1,0:T(8,128)(2,1)S(1)} %pad_maximum_fusion.1.refs_1_, bf16[2,48,1536]{2,1,0:T(8,128)(2,1)S(1)} %collective-permute-done.refs_2_, bf16[1536,1536]{1,0:T(8,128)(2,1)S(1)} %copy-done.1, bf16[1536,1536]{1,0:T(8,128)(2,1)S(1)} %copy-done.4, ...), custom_call_target="tpu_custom_call" | custom-call | flops 452984832 | bytes 4718592 | tf_op jit(solution)/shard_map/sums_keep/pallas_call | solution.py:67
  39.1 1.6 %collective-permute-start.11 = (bf16[2,48,1536]{2,1,0:T(8,128)(2,1)S(1)}, bf16[2,48,1536]{2,1,0:T(8,128)(2,1)S(1)}, u32[]{:S(2)}, u32[]{:S(2)}) collective-permute-start(bf16[2,48,1536]{2,1,0:T(8,128)(2,1)S(1)} %broadcast_select_fusion.1.refs_1_.refs_5_), channel_id=1, source_target_pairs={{0,16},{16,0},{1,17},{17,1},{2,18},{18,2},{3,19},{19,3},{4,20},{20... | collective-permute-start | bytes 884744 | tf_op jit(solution)/shard_map/ppermute | solution.py:406
  40.6 0.2 combine.2.refs_5_
  40.9 1.6 %collective-permute-start.3 = (bf16[2,96,768]{2,1,0:T(8,128)(2,1)S(1)}, bf16[2,96,768]{2,1,0:T(8,128)(2,1)S(1)}, u32[]{:S(2)}, u32[]{:S(2)}) collective-permute-start(bf16[2,96,768]{2,1,0:T(8,128)(2,1)S(1)} %combine.2.refs_5_), channel_id=1, source_target_pairs={{0,8},{4,12},{8,0},{12,4},{1,9},{5,13},{9,1},{13,5},{2,10},{6,14},... | collective-permute-start | bytes 884744 | tf_op jit(solution)/shard_map/ppermute | solution.py:406
  42.5 3.6 %sums_send.4 = (bf16[96,1536]{1,0:T(8,128)(2,1)S(1)}, bf16[96,1536]{1,0:T(8,128)(2,1)S(1)}) custom-call(s32[1]{0:T(128)} %bitcast.refs_0_, bf16[2,48,1536]{2,1,0:T(8,128)(2,1)S(1)} %collective-permute-done.5.refs_1_.refs_3_, bf16[2,48,1536]{2,1,0:T(8,128)(2,1)S(1)} %collective-permute-done.6.refs_2_.refs_6_.refs_4_, bf16[1536,1536]{1,0:T(8,128)(2,1)S(1)} %bitcast.86, ...), custom_call_target="tpu_custom_call" | custom-call | flops 905969664 | bytes 9437184 | tf_op jit(solution)/shard_map/sums_send/pallas_call | solution.py:67
  46.2 0.2 collective-permute-done.10.refs_6_
  46.4 0.3 collective-permute-start.13
  46.7 1.3 collective-permute-start.15
  48.0 3.6 %sums_keep.6.refs_5_.refs_1_ = f32[2,96,1536]{2,1,0:T(8,128)S(1)} custom-call(s32[1]{0:T(128)} %bitcast.refs_0_, bf16[2,48,1536]{2,1,0:T(8,128)(2,1)S(1)} %collective-permute-done.5.refs_1_.refs_3_, bf16[2,48,1536]{2,1,0:T(8,128)(2,1)S(1)} %collective-permute-done.6.refs_2_.refs_6_.refs_4_, bf16[1536,1536]{1,0:T(8,128)(2,1)S(1)} %bitcast.84, ...), custom_call_target="tpu_custom_call" | custom-call | flops 905969664 | bytes 9437184 | tf_op jit(solution)/shard_map/sums_keep/pallas_call | solution.py:67
  51.6 0.4 activations.6.refs_5_.refs_1_.refs_3_
  52.1 0.4 activations.7.refs_4_.refs_1_.refs_3_
  52.6 0.4 combine.3.refs_7_
  53.0 0.6 collective-permute-start.14
  53.6 2.4 %collective-permute-done.15.refs_4_.refs_8_ = bf16[2,48,1536]{2,1,0:T(8,128)(2,1)S(1)} collective-permute-done((bf16[2,48,1536]{2,1,0:T(8,128)(2,1)S(1)}, bf16[2,48,1536]{2,1,0:T(8,128)(2,1)S(1)}, u32[]{:S(2)}, u32[]{:S(2)}) %collective-permute-start.15) | collective-permute-done | bytes 294944 | tf_op jit(solution)/shard_map/ppermute | solution.py:406
  55.9 3.8 %sums_send.5 = (bf16[192,1536]{1,0:T(8,128)(2,1)S(1)}, bf16[192,1536]{1,0:T(8,128)(2,1)S(1)}) custom-call(s32[1]{0:T(128)} %bitcast.refs_0_, bf16[2,48,1536]{2,1,0:T(8,128)(2,1)S(1)} %broadcast_select_fusion.1.refs_1_.refs_5_, bf16[2,48,1536]{2,1,0:T(8,128)(2,1)S(1)} %collective-permute-done.11.refs_6_.refs_2_, ...), custom_call_target="tpu_custom_call" | custom-call | flops 1811939328 | bytes 9437184 | tf_op jit(solution)/shard_map/sums_send/pallas_call | solution.py:67
  59.9 0.5 collective-permute-start.20
  60.4 0.4 collective-permute-start.18
  60.9 3.9 %sums_keep.7.refs_5_.refs_1_ = f32[2,192,1536]{2,1,0:T(8,128)S(1)} custom-call(s32[1]{0:T(128)} %bitcast.refs_0_, bf16[2,48,1536]{2,1,0:T(8,128)(2,1)S(1)} %broadcast_select_fusion.1.refs_1_.refs_5_, bf16[2,48,1536]{2,1,0:T(8,128)(2,1)S(1)} %collective-permute-done.11.refs_6_.refs_2_, bf16[2,48,1536]{2,1,0:T(8,128)(2,1)S(1)} %broadcast_select_fusion.refs_3_.refs_7_, ...), custom_call_target="tpu_custom_call" | custom-call | flops 1811939328 | bytes 9437184 | tf_op jit(solution)/shard_map/sums_keep/pallas_call | solution.py:67
  64.7 3.8 %collective-permute-done.14.refs_4_ = bf16[2,96,1536]{2,1,0:T(8,128)(2,1)S(1)} collective-permute-done((bf16[2,96,1536]{2,1,0:T(8,128)(2,1)S(1)}, bf16[2,96,1536]{2,1,0:T(8,128)(2,1)S(1)}, u32[]{:S(2)}, u32[]{:S(2)}) %collective-permute-start.14) | collective-permute-done | bytes 589856 | tf_op jit(solution)/shard_map/ppermute | solution.py:406
  68.5 0.8 activations.8.refs_12_.refs_2_.refs_4_
  69.6 0.6 collective-permute-start.22
  70.4 1.6 %collective-permute-start.28 = (bf16[2,96,768]{2,1,0:T(8,128)(2,1)S(1)}, bf16[2,96,768]{2,1,0:T(8,128)(2,1)S(1)}, u32[]{:S(2)}, u32[]{:S(2)}) collective-permute-start(bf16[2,96,768]{2,1,0:T(8,128)(2,1)S(1)} %pad_maximum_fusion.4.refs_11_), channel_id=1, source_target_pairs={{0,8},{4,12},{8,0},{12,4},{1,9},{5,13},{9,1},{13,5},{2,10},{6,14},... | collective-permute-start | bytes 884744 | tf_op jit(solution)/shard_map/ppermute | solution.py:406
  72.0 0.4 arrange.1
  72.4 0.6 collective-permute-start.26
  73.0 2.5 %back.5.refs_7_.refs_8_ = f32[192,1536]{1,0:T(8,128)S(1)} custom-call(s32[1]{0:T(128)} %bitcast.refs_0_, bf16[2,96,768]{2,1,0:T(8,128)(2,1)S(1)} %activations.6.refs_5_.refs_1_.refs_3_, bf16[2,96,1536]{2,1,0:T(8,128)(2,1)S(1)} %activations.8.refs_12_.refs_2_.refs_4_, bf16[2,96,768]{2,1,0:T(8,128)(2,1)S(1)} %collective-permute-done.18.refs_3_, ...), custom_call_target="tpu_custom_call" | custom-call | flops 905969664 | bytes 5898240 | tf_op jit(solution)/shard_map/back/pallas_call | solution.py:67
  75.5 2.6 %back.6 = (f32[96,1536]{1,0:T(8,128)S(1)}, bf16[96,1536]{1,0:T(8,128)(2,1)S(1)}) custom-call(s32[1]{0:T(128)} %bitcast.refs_0_, bf16[2,96,768]{2,1,0:T(8,128)(2,1)S(1)} %activations.7.refs_4_.refs_1_.refs_3_, bf16[2,96,1536]{2,1,0:T(8,128)(2,1)S(1)} %activations.8.refs_12_.refs_2_.refs_4_, bf16[2,96,768]{2,1,0:T(8,128)(2,1)S(1)} %collective-permute-done.16.refs_3_.refs_7_, ...), custom_call_target="tpu_custom_call" | custom-call | flops 905969664 | bytes 5898240 | tf_op jit(solution)/shard_map/back/pallas_call | solution.py:67
  78.0 0.6 collective-permute-start.21
  78.6 7.2 %collective-permute-done.22.refs_4_ = bf16[2,96,1536]{2,1,0:T(8,128)(2,1)S(1)} collective-permute-done((bf16[2,96,1536]{2,1,0:T(8,128)(2,1)S(1)}, bf16[2,96,1536]{2,1,0:T(8,128)(2,1)S(1)}, u32[]{:S(2)}, u32[]{:S(2)}) %collective-permute-start.22) | collective-permute-done | bytes 589856 | tf_op jit(solution)/shard_map/ppermute | solution.py:406
  85.8 0.8 activations.9.refs_3_.refs_1_.refs_5_
  86.9 1.5 %collective-permute-start.23 = (bf16[48,1536]{1,0:T(8,128)(2,1)S(1)}, bf16[48,1536]{1,0:T(8,128)(2,1)S(1)}, u32[]{:S(2)}, u32[]{:S(2)}) collective-permute-start(bf16[48,1536]{1,0:T(8,128)(2,1)S(1)} %fold.6.refs_5_), channel_id=1, source_target_pairs={{0,1},{1,0},{2,3},{3,2},{4,5},{5,4},{6,7},{7,6},{8,9},{9,8},{10,11... | collective-permute-start | bytes 442376 | tf_op jit(solution)/shard_map/ppermute | solution.py:406
  88.3 0.3 collective-permute-done.24.refs_2_.refs_5_.refs_9_
  88.7 3.3 %back.7 = (f32[48,1536]{1,0:T(8,128)S(1)}, bf16[48,1536]{1,0:T(8,128)(2,1)S(1)}) custom-call(s32[1]{0:T(128)} %bitcast.refs_0_, bf16[2,96,1536]{2,1,0:T(8,128)(2,1)S(1)} %activations.9.refs_3_.refs_1_.refs_5_, bf16[2,96,1536]{2,1,0:T(8,128)(2,1)S(1)} %collective-permute-done.24.refs_2_.refs_5_.refs_9_, bf16[1536,1536]{1,0:T(8,128)(2,1)S(1)} %bitcast.84, ...), custom_call_target="tpu_custom_call" | custom-call | flops 905969664 | bytes 10027008 | tf_op jit(solution)/shard_map/back/pallas_call | solution.py:67
  92.0 1.2 collective-permute-start.25
  93.2 4.9 %collective-permute-done.26.refs_4_ = bf16[2,96,768]{2,1,0:T(8,128)(2,1)S(1)} collective-permute-done((bf16[2,96,768]{2,1,0:T(8,128)(2,1)S(1)}, bf16[2,96,768]{2,1,0:T(8,128)(2,1)S(1)}, u32[]{:S(2)}, u32[]{:S(2)}) %collective-permute-start.26) | collective-permute-done | bytes 294944 | tf_op jit(solution)/shard_map/ppermute | solution.py:406
  98.0 0.4 activations.10.refs_6_.refs_7_.refs_1_
  98.5 5.5 %weight_grads.3 = (f32[1536,3072]{1,0:T(8,128)}, f32[3072,1536]{1,0:T(8,128)}, f32[8,128]{1,0:T(8,128)S(1)}) custom-call(s32[1]{0:T(128)} %bitcast.refs_0_, bf16[1536,384]{1,0:T(8,128)(2,1)S(1)} %get-tuple-element.39.refs_7_.refs_1_, bf16[384,1536]{1,0:T(8,128)(2,1)S(1)} %get-tuple-element.44.refs_2_, ...), custom_call_target="tpu_custom_call" | custom-call | flops 1811939328 | bytes 9437184 | tf_op jit(solution)/shard_map/weight_grads/pallas_call | solution.py:67
  104.1 0.4 activations.11.refs_5_.refs_1_.refs_6_
  104.5 0.5 collective-permute-start.29
  105.1 2.2 %collective-permute-start.27 = (bf16[48,1536]{1,0:T(8,128)(2,1)S(1)}, bf16[48,1536]{1,0:T(8,128)(2,1)S(1)}, u32[]{:S(2)}, u32[]{:S(2)}) collective-permute-start(bf16[48,1536]{1,0:T(8,128)(2,1)S(1)} %fold.7.refs_3_), channel_id=1, source_target_pairs={{0,2},{1,3},{2,0},{3,1},{4,6},{5,7},{6,4},{7,5},{8,10},{9,11},{10,... | collective-permute-start | bytes 442376 | tf_op jit(solution)/shard_map/ppermute | solution.py:406
  107.3 2.2 %back.8.refs_5_.refs_6_ = f32[96,1536]{1,0:T(8,128)S(1)} custom-call(s32[1]{0:T(128)} %bitcast.refs_0_, bf16[2,96,768]{2,1,0:T(8,128)(2,1)S(1)} %activations.10.refs_6_.refs_7_.refs_1_, bf16[2,96,768]{2,1,0:T(8,128)(2,1)S(1)} %collective-permute-done.30.refs_2_.refs_6_, bf16[1536,1536]{1,0:T(8,128)(2,1)S(1)} %bitcast.84, bf16[1536,1536]{1,0:T(8,128)(2,1)S(1)} %bitcast.86, ...), custom_call_target="tpu_custom_call" | custom-call | flops 452984832 | bytes 5308416 | tf_op jit(solution)/shard_map/back/pallas_call | solution.py:67
  109.5 2.3 %back.9 = (f32[48,1536]{1,0:T(8,128)S(1)}, bf16[48,1536]{1,0:T(8,128)(2,1)S(1)}) custom-call(s32[1]{0:T(128)} %bitcast.refs_0_, bf16[2,96,768]{2,1,0:T(8,128)(2,1)S(1)} %activations.11.refs_5_.refs_1_.refs_6_, bf16[2,96,768]{2,1,0:T(8,128)(2,1)S(1)} %collective-permute-done.29.refs_2_.refs_10_, bf16[1536,1536]{1,0:T(8,128)(2,1)S(1)} %bitcast.84, ...), custom_call_target="tpu_custom_call" | custom-call | flops 452984832 | bytes 5308416 | tf_op jit(solution)/shard_map/back/pallas_call | solution.py:67
  111.8 1.3 %collective-permute-start.31 = (bf16[48,1536]{1,0:T(8,128)(2,1)S(1)}, bf16[48,1536]{1,0:T(8,128)(2,1)S(1)}, u32[]{:S(2)}, u32[]{:S(2)}) collective-permute-start(bf16[48,1536]{1,0:T(8,128)(2,1)S(1)} %get-tuple-element.47), channel_id=1, source_target_pairs={{0,16},{16,0},{1,17},{17,1},{2,18},{18,2},{3,19},{19,3},{4,20},{20... | collective-permute-start | bytes 442376 | tf_op jit(solution)/shard_map/ppermute | solution.py:406
  113.1 5.4 %weight_grads.4 = (f32[1536,3072]{1,0:T(8,128)}, f32[3072,1536]{1,0:T(8,128)}, f32[8,128]{1,0:T(8,128)S(1)}) custom-call(s32[1]{0:T(128)} %bitcast.refs_0_, bf16[1536,384]{1,0:T(8,128)(2,1)S(1)} %get-tuple-element.39.refs_7_.refs_1_, bf16[384,1536]{1,0:T(8,128)(2,1)S(1)} %get-tuple-element.44.refs_2_, ...), custom_call_target="tpu_custom_call", output_to_operand_aliasing={{0}: (7, {}), {1}: (8, {})} | custom-call | flops 1811939328 | bytes 9437184 | tf_op jit(solution)/shard_map/weight_grads/pallas_call | solution.py:67
  118.6 1.0 collective-permute-start.32
  119.5 9.3 %weight_grads.5 = (f32[1536,3072]{1,0:T(8,128)}, f32[3072,1536]{1,0:T(8,128)}, f32[8,128]{1,0:T(8,128)}) custom-call(s32[1]{0:T(128)} %bitcast.refs_0_, bf16[1536,384]{1,0:T(8,128)(2,1)S(1)} %get-tuple-element.39.refs_7_.refs_1_, bf16[384,1536]{1,0:T(8,128)(2,1)S(1)} %get-tuple-element.44.refs_2_, ...), custom_call_target="tpu_custom_call", output_to_operand_aliasing={{0}: (11, {}), {1}: (12, {})} | custom-call | flops 3623878656 | bytes 18874368 | tf_op jit(solution)/shard_map/weight_grads/pallas_call | solution.py:67
  128.8 0.7 add_convert_fusion
  (77 shorter events, 1.4 us)
Async XLA Ops:
  1.6 16.2 %collective-permute-start = (bf16[2,48,1536]{2,1,0:T(8,128)(2,1)S(1)}, bf16[2,48,1536]{2,1,0:T(8,128)(2,1)S(1)}, u32[]{:S(2)}, u32[]{:S(2)}) collective-permute-start(bf16[2,48,1536]{2,1,0:T(8,128)(2,1)S(1)} %pad_maximum_fusion.1.refs_1_), channel_id=1, source_target_pairs={{0,16},{16,0},{1,17},{17,1},{2,18},{18,2},{3,19},{19,3},{4,20},{20... | collective-permute-start | bytes 884744 | tf_op jit(solution)/shard_map/ppermute | solution.py:406
  4.6 17.3 %collective-permute-start.5 = (bf16[2,48,1536]{2,1,0:T(8,128)(2,1)S(1)}, bf16[2,48,1536]{2,1,0:T(8,128)(2,1)S(1)}, u32[]{:S(2)}, u32[]{:S(2)}) collective-permute-start(bf16[2,48,1536]{2,1,0:T(8,128)(2,1)S(1)} %pad_maximum_fusion.1.refs_1_), channel_id=1, source_target_pairs={{0,1},{1,0},{2,3},{3,2},{4,5},{5,4},{6,7},{7,6},{8,9},{9,8},{10,11... | collective-permute-start | bytes 884744 | tf_op jit(solution)/shard_map/ppermute | solution.py:406
  6.2 17.1 %collective-permute-start.8 = (bf16[2,48,1536]{2,1,0:T(8,128)(2,1)S(1)}, bf16[2,48,1536]{2,1,0:T(8,128)(2,1)S(1)}, u32[]{:S(2)}, u32[]{:S(2)}) collective-permute-start(bf16[2,48,1536]{2,1,0:T(8,128)(2,1)S(1)} %pad_maximum_fusion.1.refs_1_), channel_id=1, source_target_pairs={{1,2},{2,1},{5,6},{6,5},{9,10},{10,9},{13,14},{14,13},{17,18},{18,... | collective-permute-start | bytes 884744 | tf_op jit(solution)/shard_map/ppermute | solution.py:421
  13.4 2.2 %copy-start = (bf16[1536,1536]{1,0:T(8,128)(2,1)}, bf16[1536,1536]{1,0:T(8,128)(2,1)S(1)}, u32[]{:S(2)}) copy-start(bf16[1536,1536]{1,0:T(8,128)(2,1)S(1)} %get-tuple-element.29.refs_3_.refs_5_) | copy-start | bytes 14155780
  15.6 2.2 %copy-start.3 = (bf16[1536,1536]{1,0:T(8,128)(2,1)}, bf16[1536,1536]{1,0:T(8,128)(2,1)S(1)}, u32[]{:S(2)}) copy-start(bf16[1536,1536]{1,0:T(8,128)(2,1)S(1)} %get-tuple-element.30.refs_4_.refs_6_) | copy-start | bytes 14155780
  17.8 3.6 %copy-start.2 = (bf16[1536,1536]{1,0:T(8,128)(2,1)}, bf16[1536,1536]{1,0:T(8,128)(2,1)S(1)}, u32[]{:S(2)}) copy-start(bf16[1536,1536]{1,0:T(8,128)(2,1)S(1)} %get-tuple-element.31.refs_3_.refs_5_.refs_6_.refs_4_) | copy-start | bytes 14155780
  17.8 3.7 %copy-start.5 = (bf16[1536,1536]{1,0:T(8,128)(2,1)}, bf16[1536,1536]{1,0:T(8,128)(2,1)S(1)}, u32[]{:S(2)}) copy-start(bf16[1536,1536]{1,0:T(8,128)(2,1)S(1)} %get-tuple-element.32.refs_4_.refs_6_) | copy-start | bytes 14155780
  21.5 9.6 %collective-permute-start.1 = (bf16[96,1536]{1,0:T(8,128)(2,1)S(1)}, bf16[96,1536]{1,0:T(8,128)(2,1)S(1)}, u32[]{:S(2)}, u32[]{:S(2)}) collective-permute-start(bf16[96,1536]{1,0:T(8,128)(2,1)S(1)} %get-tuple-element.33.refs_5_), channel_id=1, source_target_pairs={{0,4},{4,0},{8,12},{12,8},{1,5},{5,1},{9,13},{13,9},{2,6},{6,2},{1... | collective-permute-start | bytes 884744 | tf_op jit(solution)/shard_map/ppermute | solution.py:406
  21.5 9.6 %collective-permute-start.2 = (bf16[96,1536]{1,0:T(8,128)(2,1)S(1)}, bf16[96,1536]{1,0:T(8,128)(2,1)S(1)}, u32[]{:S(2)}, u32[]{:S(2)}) collective-permute-start(bf16[96,1536]{1,0:T(8,128)(2,1)S(1)} %get-tuple-element.34), channel_id=1, source_target_pairs={{0,4},{4,0},{8,12},{12,8},{1,5},{5,1},{9,13},{13,9},{2,6},{6,2},{1... | collective-permute-start | bytes 884744 | tf_op jit(solution)/shard_map/ppermute | solution.py:406
  22.0 10.8 %collective-permute-start.7 = (bf16[2,48,1536]{2,1,0:T(8,128)(2,1)S(1)}, bf16[2,48,1536]{2,1,0:T(8,128)(2,1)S(1)}, u32[]{:S(2)}, u32[]{:S(2)}) collective-permute-start(bf16[2,48,1536]{2,1,0:T(8,128)(2,1)S(1)} %collective-permute-done.5.refs_1_.refs_3_), channel_id=1, source_target_pairs={{1,2},{2,1},{5,6},{6,5},{9,10},{10,9},{13,14},{14,13},{17,18},{18,... | collective-permute-start | bytes 884744 | tf_op jit(solution)/shard_map/ppermute | solution.py:422
  22.7 19.8 %collective-permute-start.6 = (bf16[2,48,1536]{2,1,0:T(8,128)(2,1)S(1)}, bf16[2,48,1536]{2,1,0:T(8,128)(2,1)S(1)}, u32[]{:S(2)}, u32[]{:S(2)}) collective-permute-start(bf16[2,48,1536]{2,1,0:T(8,128)(2,1)S(1)} %collective-permute-done.5.refs_1_.refs_3_), channel_id=1, source_target_pairs={{0,16},{16,0},{1,17},{17,1},{2,18},{18,2},{3,19},{19,3},{4,20},{20... | collective-permute-start | bytes 884744 | tf_op jit(solution)/shard_map/ppermute | solution.py:406
  23.3 13.9 %collective-permute-start.9 = (bf16[2,48,1536]{2,1,0:T(8,128)(2,1)S(1)}, bf16[2,48,1536]{2,1,0:T(8,128)(2,1)S(1)}, u32[]{:S(2)}, u32[]{:S(2)}) collective-permute-start(bf16[2,48,1536]{2,1,0:T(8,128)(2,1)S(1)} %collective-permute-done.8), channel_id=1, source_target_pairs={{1,0},{2,3},{5,4},{6,7},{9,8},{10,11},{13,12},{14,15},{17,16},{18,... | collective-permute-start | bytes 884744 | tf_op jit(solution)/shard_map/ppermute | solution.py:423
  24.6 2.3 %copy-start.1 = (bf16[1536,1536]{1,0:T(8,128)(2,1)S(1)}, bf16[1536,1536]{1,0:T(8,128)(2,1)}, u32[]{:S(2)}) copy-start(bf16[1536,1536]{1,0:T(8,128)(2,1)} %copy-done) | copy-start | bytes 14155780
  26.9 2.3 %copy-start.4 = (bf16[1536,1536]{1,0:T(8,128)(2,1)S(1)}, bf16[1536,1536]{1,0:T(8,128)(2,1)}, u32[]{:S(2)}) copy-start(bf16[1536,1536]{1,0:T(8,128)(2,1)} %copy-done.3) | copy-start | bytes 14155780
  31.2 15.5 %collective-permute-start.4 = (bf16[2,96,768]{2,1,0:T(8,128)(2,1)S(1)}, bf16[2,96,768]{2,1,0:T(8,128)(2,1)S(1)}, u32[]{:S(2)}, u32[]{:S(2)}) collective-permute-start(bf16[2,96,768]{2,1,0:T(8,128)(2,1)S(1)} %pad_maximum_fusion.2.refs_5_), channel_id=1, source_target_pairs={{0,8},{4,12},{8,0},{12,4},{1,9},{5,13},{9,1},{13,5},{2,10},{6,14},... | collective-permute-start | bytes 884744 | tf_op jit(solution)/shard_map/ppermute | solution.py:406
  32.8 13.6 %collective-permute-start.10 = (bf16[2,48,1536]{2,1,0:T(8,128)(2,1)S(1)}, bf16[2,48,1536]{2,1,0:T(8,128)(2,1)S(1)}, u32[]{:S(2)}, u32[]{:S(2)}) collective-permute-start(bf16[2,48,1536]{2,1,0:T(8,128)(2,1)S(1)} %collective-permute-done.7.refs_7_), channel_id=1, source_target_pairs={{1,0},{2,3},{5,4},{6,7},{9,8},{10,11},{13,12},{14,15},{17,16},{18,... | collective-permute-start | bytes 884744 | tf_op jit(solution)/shard_map/ppermute | solution.py:424
  37.1 5.3 %slice-start.2 = ((s8[4718592]{0:T(1024)(128)(4,1)}), s8[4194304]{0:T(1024)(128)(4,1)S(1)}, s32[]{:S(2)}) async-start(s8[4718592]{0:T(1024)(128)(4,1)} %bitcast.85), calls=%async_computation.2 | async-start | bytes 8388608
  37.1 5.3 %slice-start.6 = ((s8[4718592]{0:T(1024)(128)(4,1)}), s8[4194304]{0:T(1024)(128)(4,1)S(1)}, s32[]{:S(2)}) async-start(s8[4718592]{0:T(1024)(128)(4,1)} %bitcast.89), calls=%async_computation.6 | async-start | bytes 8388608
  37.2 5.3 %slice-start.3 = ((s8[4718592]{0:T(1024)(128)(4,1)}), s8[524288]{0:T(1024)(128)(4,1)S(1)}, s32[]{:S(2)}) async-start(s8[4718592]{0:T(1024)(128)(4,1)} %bitcast.85), calls=%async_computation.3 | async-start | bytes 1048576
  37.2 5.3 %slice-start.7 = ((s8[4718592]{0:T(1024)(128)(4,1)}), s8[524288]{0:T(1024)(128)(4,1)S(1)}, s32[]{:S(2)}) async-start(s8[4718592]{0:T(1024)(128)(4,1)} %bitcast.89), calls=%async_computation.7 | async-start | bytes 1048576
  39.1 13.0 %collective-permute-start.11 = (bf16[2,48,1536]{2,1,0:T(8,128)(2,1)S(1)}, bf16[2,48,1536]{2,1,0:T(8,128)(2,1)S(1)}, u32[]{:S(2)}, u32[]{:S(2)}) collective-permute-start(bf16[2,48,1536]{2,1,0:T(8,128)(2,1)S(1)} %broadcast_select_fusion.1.refs_1_.refs_5_), channel_id=1, source_target_pairs={{0,16},{16,0},{1,17},{17,1},{2,18},{18,2},{3,19},{19,3},{4,20},{20... | collective-permute-start | bytes 884744 | tf_op jit(solution)/shard_map/ppermute | solution.py:406
  40.6 7.4 %slice-start = ((s8[4718592]{0:T(1024)(128)(4,1)}), s8[4194304]{0:T(1024)(128)(4,1)S(1)}, s32[]{:S(2)}) async-start(s8[4718592]{0:T(1024)(128)(4,1)} %bitcast.83), calls=%async_computation | async-start | bytes 8388608
  40.6 7.4 %slice-start.4 = ((s8[4718592]{0:T(1024)(128)(4,1)}), s8[4194304]{0:T(1024)(128)(4,1)S(1)}, s32[]{:S(2)}) async-start(s8[4718592]{0:T(1024)(128)(4,1)} %bitcast.87), calls=%async_computation.4 | async-start | bytes 8388608
  40.8 7.2 %slice-start.1 = ((s8[4718592]{0:T(1024)(128)(4,1)}), s8[524288]{0:T(1024)(128)(4,1)S(1)}, s32[]{:S(2)}) async-start(s8[4718592]{0:T(1024)(128)(4,1)} %bitcast.83), calls=%async_computation.1 | async-start | bytes 1048576
  40.9 7.2 %slice-start.5 = ((s8[4718592]{0:T(1024)(128)(4,1)}), s8[524288]{0:T(1024)(128)(4,1)S(1)}, s32[]{:S(2)}) async-start(s8[4718592]{0:T(1024)(128)(4,1)} %bitcast.87), calls=%async_computation.5 | async-start | bytes 1048576
  40.9 11.2 %collective-permute-start.3 = (bf16[2,96,768]{2,1,0:T(8,128)(2,1)S(1)}, bf16[2,96,768]{2,1,0:T(8,128)(2,1)S(1)}, u32[]{:S(2)}, u32[]{:S(2)}) collective-permute-start(bf16[2,96,768]{2,1,0:T(8,128)(2,1)S(1)} %combine.2.refs_5_), channel_id=1, source_target_pairs={{0,8},{4,12},{8,0},{12,4},{1,9},{5,13},{9,1},{13,5},{2,10},{6,14},... | collective-permute-start | bytes 884744 | tf_op jit(solution)/shard_map/ppermute | solution.py:406
  46.1 6.5 %collective-permute-start.12 = (bf16[96,1536]{1,0:T(8,128)(2,1)S(1)}, bf16[96,1536]{1,0:T(8,128)(2,1)S(1)}, u32[]{:S(2)}, u32[]{:S(2)}) collective-permute-start(bf16[96,1536]{1,0:T(8,128)(2,1)S(1)} %get-tuple-element.35.refs_5_), channel_id=1, source_target_pairs={{0,4},{4,0},{8,12},{12,8},{1,5},{5,1},{9,13},{13,9},{2,6},{6,2},{1... | collective-permute-start | bytes 884744 | tf_op jit(solution)/shard_map/ppermute | solution.py:406
  46.4 6.2 %collective-permute-start.13 = (bf16[96,1536]{1,0:T(8,128)(2,1)S(1)}, bf16[96,1536]{1,0:T(8,128)(2,1)S(1)}, u32[]{:S(2)}, u32[]{:S(2)}) collective-permute-start(bf16[96,1536]{1,0:T(8,128)(2,1)S(1)} %get-tuple-element.36), channel_id=1, source_target_pairs={{0,4},{4,0},{8,12},{12,8},{1,5},{5,1},{9,13},{13,9},{2,6},{6,2},{1... | collective-permute-start | bytes 884744 | tf_op jit(solution)/shard_map/ppermute | solution.py:406
  46.7 9.2 %collective-permute-start.15 = (bf16[2,48,1536]{2,1,0:T(8,128)(2,1)S(1)}, bf16[2,48,1536]{2,1,0:T(8,128)(2,1)S(1)}, u32[]{:S(2)}, u32[]{:S(2)}) collective-permute-start(bf16[2,48,1536]{2,1,0:T(8,128)(2,1)S(1)} %broadcast_select_fusion.refs_3_.refs_7_), channel_id=1, source_target_pairs={{0,16},{16,0},{1,17},{17,1},{2,18},{18,2},{3,19},{19,3},{4,20},{20... | collective-permute-start | bytes 884744 | tf_op jit(solution)/shard_map/ppermute | solution.py:406
  53.0 15.5 %collective-permute-start.14 = (bf16[2,96,1536]{2,1,0:T(8,128)(2,1)S(1)}, bf16[2,96,1536]{2,1,0:T(8,128)(2,1)S(1)}, u32[]{:S(2)}, u32[]{:S(2)}) collective-permute-start(bf16[2,96,1536]{2,1,0:T(8,128)(2,1)S(1)} %combine.3.refs_7_), channel_id=1, source_target_pairs={{0,8},{4,12},{8,0},{12,4},{1,9},{5,13},{9,1},{13,5},{2,10},{6,14},... | collective-permute-start | bytes 1769480 | tf_op jit(solution)/shard_map/ppermute | solution.py:406
  59.8 9.6 %collective-permute-start.19 = (bf16[192,1536]{1,0:T(8,128)(2,1)S(1)}, bf16[192,1536]{1,0:T(8,128)(2,1)S(1)}, u32[]{:S(2)}, u32[]{:S(2)}) collective-permute-start(bf16[192,1536]{1,0:T(8,128)(2,1)S(1)} %get-tuple-element.37.refs_7_), channel_id=1, source_target_pairs={{0,4},{4,0},{8,12},{12,8},{1,5},{5,1},{9,13},{13,9},{2,6},{6,2},{1... | collective-permute-start | bytes 1769480 | tf_op jit(solution)/shard_map/ppermute | solution.py:406
  59.9 9.6 %collective-permute-start.20 = (bf16[192,1536]{1,0:T(8,128)(2,1)S(1)}, bf16[192,1536]{1,0:T(8,128)(2,1)S(1)}, u32[]{:S(2)}, u32[]{:S(2)}) collective-permute-start(bf16[192,1536]{1,0:T(8,128)(2,1)S(1)} %get-tuple-element.38), channel_id=1, source_target_pairs={{0,4},{4,0},{8,12},{12,8},{1,5},{5,1},{9,13},{13,9},{2,6},{6,2},{1... | collective-permute-start | bytes 1769480 | tf_op jit(solution)/shard_map/ppermute | solution.py:406
  60.3 15.1 %collective-permute-start.16 = (bf16[2,96,768]{2,1,0:T(8,128)(2,1)S(1)}, bf16[2,96,768]{2,1,0:T(8,128)(2,1)S(1)}, u32[]{:S(2)}, u32[]{:S(2)}) collective-permute-start(bf16[2,96,768]{2,1,0:T(8,128)(2,1)S(1)} %activations.7.refs_4_.refs_1_.refs_3_), channel_id=1, source_target_pairs={{0,4},{4,0},{8,12},{12,8},{1,5},{5,1},{9,13},{13,9},{2,6},{6,2},{1... | collective-permute-start | bytes 884744 | tf_op jit(solution)/shard_map/ppermute | solution.py:406
  60.4 12.0 %collective-permute-start.18 = (bf16[2,96,768]{2,1,0:T(8,128)(2,1)S(1)}, bf16[2,96,768]{2,1,0:T(8,128)(2,1)S(1)}, u32[]{:S(2)}, u32[]{:S(2)}) collective-permute-start(bf16[2,96,768]{2,1,0:T(8,128)(2,1)S(1)} %activations.6.refs_5_.refs_1_.refs_3_), channel_id=1, source_target_pairs={{0,4},{4,0},{8,12},{12,8},{1,5},{5,1},{9,13},{13,9},{2,6},{6,2},{1... | collective-permute-start | bytes 884744 | tf_op jit(solution)/shard_map/ppermute | solution.py:406
  69.3 3.7 %collective-permute-start.17 = (bf16[2,96,1536]{2,1,0:T(8,128)(2,1)S(1)}, bf16[2,96,1536]{2,1,0:T(8,128)(2,1)S(1)}, u32[]{:S(2)}, u32[]{:S(2)}) collective-permute-start(bf16[2,96,1536]{2,1,0:T(8,128)(2,1)S(1)} %activations.8.refs_12_.refs_2_.refs_4_), channel_id=1, source_target_pairs={{0,4},{4,0},{8,12},{12,8},{1,5},{5,1},{9,13},{13,9},{2,6},{6,2},{1... | collective-permute-start | bytes 1769480 | tf_op jit(solution)/shard_map/ppermute | solution.py:406
  69.6 16.2 %collective-permute-start.22 = (bf16[2,96,1536]{2,1,0:T(8,128)(2,1)S(1)}, bf16[2,96,1536]{2,1,0:T(8,128)(2,1)S(1)}, u32[]{:S(2)}, u32[]{:S(2)}) collective-permute-start(bf16[2,96,1536]{2,1,0:T(8,128)(2,1)S(1)} %pad_maximum_fusion.refs_9_), channel_id=1, source_target_pairs={{0,8},{4,12},{8,0},{12,4},{1,9},{5,13},{9,1},{13,5},{2,10},{6,14},... | collective-permute-start | bytes 1769480 | tf_op jit(solution)/shard_map/ppermute | solution.py:406
  70.4 33.7 %collective-permute-start.28 = (bf16[2,96,768]{2,1,0:T(8,128)(2,1)S(1)}, bf16[2,96,768]{2,1,0:T(8,128)(2,1)S(1)}, u32[]{:S(2)}, u32[]{:S(2)}) collective-permute-start(bf16[2,96,768]{2,1,0:T(8,128)(2,1)S(1)} %pad_maximum_fusion.4.refs_11_), channel_id=1, source_target_pairs={{0,8},{4,12},{8,0},{12,4},{1,9},{5,13},{9,1},{13,5},{2,10},{6,14},... | collective-permute-start | bytes 884744 | tf_op jit(solution)/shard_map/ppermute | solution.py:406
  72.4 25.6 %collective-permute-start.26 = (bf16[2,96,768]{2,1,0:T(8,128)(2,1)S(1)}, bf16[2,96,768]{2,1,0:T(8,128)(2,1)S(1)}, u32[]{:S(2)}, u32[]{:S(2)}) collective-permute-start(bf16[2,96,768]{2,1,0:T(8,128)(2,1)S(1)} %pad_maximum_fusion.3.refs_10_), channel_id=1, source_target_pairs={{0,8},{4,12},{8,0},{12,4},{1,9},{5,13},{9,1},{13,5},{2,10},{6,14},... | collective-permute-start | bytes 884744 | tf_op jit(solution)/shard_map/ppermute | solution.py:406
  78.0 8.7 %collective-permute-start.21 = (bf16[96,1536]{1,0:T(8,128)(2,1)S(1)}, bf16[96,1536]{1,0:T(8,128)(2,1)S(1)}, u32[]{:S(2)}, u32[]{:S(2)}) collective-permute-start(bf16[96,1536]{1,0:T(8,128)(2,1)S(1)} %get-tuple-element.41), channel_id=1, source_target_pairs={{0,16},{16,0},{1,17},{17,1},{2,18},{18,2},{3,19},{19,3},{4,20},{20... | collective-permute-start | bytes 884744 | tf_op jit(solution)/shard_map/ppermute | solution.py:406
  86.6 2.1 %collective-permute-start.24 = (bf16[2,96,1536]{2,1,0:T(8,128)(2,1)S(1)}, bf16[2,96,1536]{2,1,0:T(8,128)(2,1)S(1)}, u32[]{:S(2)}, u32[]{:S(2)}) collective-permute-start(bf16[2,96,1536]{2,1,0:T(8,128)(2,1)S(1)} %activations.9.refs_3_.refs_1_.refs_5_), channel_id=1, source_target_pairs={{0,4},{4,0},{8,12},{12,8},{1,5},{5,1},{9,13},{13,9},{2,6},{6,2},{1... | collective-permute-start | bytes 1769480 | tf_op jit(solution)/shard_map/ppermute | solution.py:406
  86.9 17.2 %collective-permute-start.23 = (bf16[48,1536]{1,0:T(8,128)(2,1)S(1)}, bf16[48,1536]{1,0:T(8,128)(2,1)S(1)}, u32[]{:S(2)}, u32[]{:S(2)}) collective-permute-start(bf16[48,1536]{1,0:T(8,128)(2,1)S(1)} %fold.6.refs_5_), channel_id=1, source_target_pairs={{0,1},{1,0},{2,3},{3,2},{4,5},{5,4},{6,7},{7,6},{8,9},{9,8},{10,11... | collective-permute-start | bytes 442376 | tf_op jit(solution)/shard_map/ppermute | solution.py:406
  92.0 12.0 %collective-permute-start.25 = (bf16[48,1536]{1,0:T(8,128)(2,1)S(1)}, bf16[48,1536]{1,0:T(8,128)(2,1)S(1)}, u32[]{:S(2)}, u32[]{:S(2)}) collective-permute-start(bf16[48,1536]{1,0:T(8,128)(2,1)S(1)} %get-tuple-element.43), channel_id=1, source_target_pairs={{0,16},{16,0},{1,17},{17,1},{2,18},{18,2},{3,19},{19,3},{4,20},{20... | collective-permute-start | bytes 442376 | tf_op jit(solution)/shard_map/ppermute | solution.py:406
  98.5 8.8 %collective-permute-start.30 = (bf16[2,96,768]{2,1,0:T(8,128)(2,1)S(1)}, bf16[2,96,768]{2,1,0:T(8,128)(2,1)S(1)}, u32[]{:S(2)}, u32[]{:S(2)}) collective-permute-start(bf16[2,96,768]{2,1,0:T(8,128)(2,1)S(1)} %activations.10.refs_6_.refs_7_.refs_1_), channel_id=1, source_target_pairs={{0,4},{4,0},{8,12},{12,8},{1,5},{5,1},{9,13},{13,9},{2,6},{6,2},{1... | collective-permute-start | bytes 884744 | tf_op jit(solution)/shard_map/ppermute | solution.py:406
  104.5 4.9 %collective-permute-start.29 = (bf16[2,96,768]{2,1,0:T(8,128)(2,1)S(1)}, bf16[2,96,768]{2,1,0:T(8,128)(2,1)S(1)}, u32[]{:S(2)}, u32[]{:S(2)}) collective-permute-start(bf16[2,96,768]{2,1,0:T(8,128)(2,1)S(1)} %activations.11.refs_5_.refs_1_.refs_6_), channel_id=1, source_target_pairs={{0,4},{4,0},{8,12},{12,8},{1,5},{5,1},{9,13},{13,9},{2,6},{6,2},{1... | collective-permute-start | bytes 884744 | tf_op jit(solution)/shard_map/ppermute | solution.py:406
  105.1 23.8 %collective-permute-start.27 = (bf16[48,1536]{1,0:T(8,128)(2,1)S(1)}, bf16[48,1536]{1,0:T(8,128)(2,1)S(1)}, u32[]{:S(2)}, u32[]{:S(2)}) collective-permute-start(bf16[48,1536]{1,0:T(8,128)(2,1)S(1)} %fold.7.refs_3_), channel_id=1, source_target_pairs={{0,2},{1,3},{2,0},{3,1},{4,6},{5,7},{6,4},{7,5},{8,10},{9,11},{10,... | collective-permute-start | bytes 442376 | tf_op jit(solution)/shard_map/ppermute | solution.py:406
  111.8 6.7 %collective-permute-start.31 = (bf16[48,1536]{1,0:T(8,128)(2,1)S(1)}, bf16[48,1536]{1,0:T(8,128)(2,1)S(1)}, u32[]{:S(2)}, u32[]{:S(2)}) collective-permute-start(bf16[48,1536]{1,0:T(8,128)(2,1)S(1)} %get-tuple-element.47), channel_id=1, source_target_pairs={{0,16},{16,0},{1,17},{17,1},{2,18},{18,2},{3,19},{19,3},{4,20},{20... | collective-permute-start | bytes 442376 | tf_op jit(solution)/shard_map/ppermute | solution.py:406
  118.6 10.3 %collective-permute-start.32 = (bf16[48,1536]{1,0:T(8,128)(2,1)S(1)}, bf16[48,1536]{1,0:T(8,128)(2,1)S(1)}, u32[]{:S(2)}, u32[]{:S(2)}) collective-permute-start(bf16[48,1536]{1,0:T(8,128)(2,1)S(1)} %fold.9.refs_13_), channel_id=1, source_target_pairs={{0,3},{1,2},{2,1},{3,0},{4,7},{5,6},{6,5},{7,4},{8,11},{9,10},{10,... | collective-permute-start | bytes 442376 | tf_op jit(solution)/shard_map/ppermute | solution.py:406

commit v7 on v6

--- a/solution.py
+++ b/solution.py
@@ -9,7 +9,8 @@
 
 F32 = jnp.float32
 BF16 = jnp.bfloat16
-VMEM_LIMIT = 24 * 1024 * 1024
+VMEM_LIMIT = 10 * 1024 * 1024
+GRADS_VMEM_LIMIT = 18 * 1024 * 1024
 COST_PART = 1
 
 
@@ -56,7 +57,7 @@
     return tile
 
 
-def call(body, core, operands, in_specs, outs, out_specs, grid, cost, name, after=(), scratch=(), aliases=None):
+def call(body, core, operands, in_specs, outs, out_specs, grid, cost, name, after=(), scratch=(), aliases=None, limit=VMEM_LIMIT):
     after = list(after)
     inner = len(operands) + 1
 
@@ -75,7 +76,7 @@
         ),
         out_shape=outs,
         input_output_aliases=aliases or {},
-        compiler_params=pltpu.CompilerParams(vmem_limit_bytes=VMEM_LIMIT),
+        compiler_params=pltpu.CompilerParams(vmem_limit_bytes=limit),
         cost_estimate=pl.CostEstimate(
             flops=flops // COST_PART, bytes_accessed=moved // COST_PART, transcendentals=0
         ),
@@ -184,11 +185,10 @@
     )
 
 
-def combine(core, keep, near, start, after):
-    _, tokens, width = keep.shape
+def combine(core, keep, near, row, tokens, column, start, width, after):
     tile = tile_of(width, 256)
-    both = pl.BlockSpec((2, tokens, tile), lambda i, c: (0, 0, i))
-    one = pl.BlockSpec((tokens, tile), lambda i, c: (0, start // tile + i))
+    both = pl.BlockSpec((2, tokens, tile), lambda i, c: (0, row // tokens, column // tile + i))
+    one = pl.BlockSpec((tokens, tile), lambda i, c: (row // tokens, start // tile + i))
 
     def body(core_ref, keep_ref, preact_ref, grad_ref, chip_ref):
         chip_ref[0] = (keep_ref[0] + preact_ref[...].astype(F32)).astype(BF16)
@@ -199,8 +199,8 @@
         core,
         [keep, *near],
         [both, one, one],
-        jax.ShapeDtypeStruct(keep.shape, BF16),
-        both,
+        jax.ShapeDtypeStruct((2, tokens, width), BF16),
+        pl.BlockSpec((2, tokens, tile), lambda i, c: (0, 0, i)),
         (width // tile,),
         (4 * tokens * width, 16 * tokens * width),
         "combine",
@@ -399,6 +399,7 @@
         "weight_grads",
         after,
         aliases=aliases,
+        limit=GRADS_VMEM_LIMIT,
     )
 
 
@@ -466,7 +467,7 @@
         group, row, start, size = pieces[n]
         array, column = kept(group, start)
         if after:
-            chip = combine(core, array, near[group], start, after)
+            chip = combine(core, array, near[group], row, pair, column, start, size, after)
         else:
             chip = jnp.stack([
                 (
@@ -519,13 +520,14 @@
     last = send(2, last)
     last = hold(2, 0, half, last)
     last = ready(2, last)
-    last = cross(3) + cross(4) + cross(5) + last
+    last = cross(3) + last
     inputs_t, cotan = arrange(core, [u for group in groups for u in group], last)
     part, = inward(((0, 0), (2, 0)), 0, width, None, None, None, [inputs_t])
     stay1, go1 = inward(((1, 0), (2, width)), width, width, part, (0, 2, 1, 3), 2, [part])
     near1 = swap(go1, "gx", 2, 1)
 
     last = ready(3, [stay1])
+    last = cross(4, last)
     total = fold(core, stay1[:rows], near1[:rows], F32, last)
     back1 = fold(core, stay1[rows:], near1[rows:], BF16, [total])
     far1 = swap(back1, "gz", 4, 1)
@@ -533,18 +535,20 @@
     near2 = swap(go2, "gx", 2, 1)
 
     last = ready(4, [stay2])
+    last = cross(5, last)
     last = finish(0, (0,), last)
     back2 = fold(core, stay2, near2, BF16, last)
     far2 = swap(back2, "gz", 4, 2)
-    total = fold(core, total, far1, F32, [back2])
+    part, = inward(((4, 0),), 0, width, None, None, None, [back2])
+    last = finish(0, (1,), [part])
+    total = fold(core, total, far1, F32, last)
     last = ready(5, [total])
-    part, = inward(((4, 0),), 0, width, None, None, None, last)
-    stay3, go3 = inward(((5, 0),), width, width, part, (0, 1), 1, [part])
+    stay3, go3 = inward(((5, 0),), width, width, part, (0, 1), 1, last)
     near3 = swap(go3, "gx", 2, 1)
-    last = finish(0, (1,), [stay3])
+    last = finish(1, (0,), [stay3])
     back3 = fold(core, stay3, near3, BF16, last)
     far3 = swap(back3, "gz", 4, 3)
-    finish(1, (0, 1), [back3])
+    finish(1, (1,), [back3])
     total = total + far2.astype(F32) + far3.astype(F32)
     return (total.astype(BF16), *outputs)
 

time: 130 us -> 135 us (1.038)
  local copies, waits for them, and re-layouts: 9.21 us -> 11.3 us
  Pallas kernels: 66.1 us -> 68.1 us
  waiting for transfers between devices: 21.9 us -> 23.4 us
    ppermute x29, waiting for transfers between devices: 18.6 us -> 22.8 us  [swap(): return lax.ppermute(value, axis, [(i, i ^ bits) for i in range(size)])]
    ppermute x1, waiting for transfers between devices: 3.05 us -> 0.01 us  [cube_body(): first_on = lax.ppermute(first, 'gz', outward)]
    unnamed x28, local copies, waits for them, and re-layouts: 9.15 us -> 11.2 us
    pallas_call x30 -> x33, Pallas kernels: 66.1 us -> 68.1 us  [call(): pl.pallas_call(kernel, grid_spec=pltpu.PrefetchScalarGridSpec(num_scalar_...]
  transfers between devices with their start and end apart: 33 -> 33, of which waited for: 7 -> 9; matrix products, arithmetic and copies ran while one was open for 0% -> 0% of each run, Pallas kernels for 51% -> 50%
where the time goes in v7:
time: 135 us; the launch traced here: 134 us
  Pallas kernels  68.1 us (50%)
  starting transfers between devices  28.4 us (21%)
  waiting for transfers between devices  23.4 us (17%)
  local copies, waits for them, and re-layouts  11.3 us (8%)
  other arithmetic  2.06 us (2%)
    pallas_call x33, Pallas kernels, call(): pl.pallas_call(kernel, grid_spec=pltpu.PrefetchScalarGridSpec(num_scalar_...  68.1 us
    ppermute x29, starting transfers between devices, swap(): return lax.ppermute(value, axis, [(i, i ^ bits) for i in range(size)])  24.3 us
    ppermute x29, waiting for transfers between devices, swap(): return lax.ppermute(value, axis, [(i, i ^ bits) for i in range(size)])  22.8 us
    unnamed x28, local copies, waits for them, and re-layouts  11.2 us
  transfers between devices with their start and end apart: 33, of which 9 were waited for; matrix products, arithmetic and copies ran while one was open for 0% of the time, Pallas kernels for 50%

profile of v7, /device:TPU:0, one launch (start us, length us, event | category | flops | bytes accessed | tf_op | source)
XLA Modules:
  0.0 134.4 jit_solution(2505351355548234041)
XLA Ops:
  0.6 1.0 pad_maximum_fusion.1.refs_1_
  1.6 3.0 %collective-permute-start = (bf16[2,48,1536]{2,1,0:T(8,128)(2,1)S(1)}, bf16[2,48,1536]{2,1,0:T(8,128)(2,1)S(1)}, u32[]{:S(2)}, u32[]{:S(2)}) collective-permute-start(bf16[2,48,1536]{2,1,0:T(8,128)(2,1)S(1)} %pad_maximum_fusion.1.refs_1_), channel_id=1, source_target_pairs={{0,16},{16,0},{1,17},{17,1},{2,18},{18,2},{3,19},{19,3},{4,20},{20... | collective-permute-start | bytes 884744 | tf_op jit(solution)/shard_map/ppermute | solution.py:407
  4.6 0.7 collective-permute-start.8
  5.3 4.4 %collective-permute-start.5 = (bf16[2,48,1536]{2,1,0:T(8,128)(2,1)S(1)}, bf16[2,48,1536]{2,1,0:T(8,128)(2,1)S(1)}, u32[]{:S(2)}, u32[]{:S(2)}) collective-permute-start(bf16[2,48,1536]{2,1,0:T(8,128)(2,1)S(1)} %pad_maximum_fusion.1.refs_1_), channel_id=1, source_target_pairs={{0,1},{1,0},{2,3},{3,2},{4,5},{5,4},{6,7},{7,6},{8,9},{9,8},{10,11... | collective-permute-start | bytes 884744 | tf_op jit(solution)/shard_map/ppermute | solution.py:407
  9.8 6.5 %bring.1 = (bf16[1536,1536]{1,0:T(8,128)(2,1)S(1)}, bf16[1536,1536]{1,0:T(8,128)(2,1)S(1)}, bf16[1536,1536]{1,0:T(8,128)(2,1)S(1)}, bf16[1536,1536]{1,0:T(8,128)(2,1)S(1)}) custom-call(s32[1]{0:T(128)} %bitcast.refs_0_, bf16[1536,3072]{1,0:T(8,128)(2,1)} %refs_1_.1, bf16[3072,1536]{1,0:T(8,128)(2,1)} %refs_2_.1), custom_call_target="tpu_custom_call" | custom-call | bytes 18874368 | tf_op jit(solution)/shard_map/bring/pallas_call | solution.py:68
  16.3 2.2 %copy-done = bf16[1536,1536]{1,0:T(8,128)(2,1)} copy-done((bf16[1536,1536]{1,0:T(8,128)(2,1)}, bf16[1536,1536]{1,0:T(8,128)(2,1)S(1)}, u32[]{:S(2)}) %copy-start) | copy-done | bytes 4718616
  18.5 2.2 %copy-done.3 = bf16[1536,1536]{1,0:T(8,128)(2,1)} copy-done((bf16[1536,1536]{1,0:T(8,128)(2,1)}, bf16[1536,1536]{1,0:T(8,128)(2,1)S(1)}, u32[]{:S(2)}) %copy-start.3) | copy-done | bytes 4718616
  20.7 3.6 %sums_send.3 = (bf16[96,1536]{1,0:T(8,128)(2,1)S(1)}, bf16[96,1536]{1,0:T(8,128)(2,1)S(1)}) custom-call(s32[1]{0:T(128)} %bitcast.refs_0_, bf16[2,48,1536]{2,1,0:T(8,128)(2,1)S(1)} %pad_maximum_fusion.1.refs_1_, bf16[2,48,1536]{2,1,0:T(8,128)(2,1)S(1)} %collective-permute-done.refs_2_, ...), custom_call_target="tpu_custom_call" | custom-call | flops 905969664 | bytes 9437184 | tf_op jit(solution)/shard_map/sums_send/pallas_call | solution.py:68
  24.3 2.2 %copy-done.2 = bf16[1536,1536]{1,0:T(8,128)(2,1)} copy-done((bf16[1536,1536]{1,0:T(8,128)(2,1)}, bf16[1536,1536]{1,0:T(8,128)(2,1)S(1)}, u32[]{:S(2)}) %copy-start.2) | copy-done | bytes 4718616
  26.4 0.5 collective-permute-start.1
  26.9 0.7 collective-permute-start.7
  27.6 0.6 collective-permute-start.6
  28.2 1.3 collective-permute-start.9
  29.5 2.3 %copy-done.1 = bf16[1536,1536]{1,0:T(8,128)(2,1)S(1)} copy-done((bf16[1536,1536]{1,0:T(8,128)(2,1)S(1)}, bf16[1536,1536]{1,0:T(8,128)(2,1)}, u32[]{:S(2)}) %copy-start.1) | copy-done | bytes 4718616
  31.9 2.3 %copy-done.4 = bf16[1536,1536]{1,0:T(8,128)(2,1)S(1)} copy-done((bf16[1536,1536]{1,0:T(8,128)(2,1)S(1)}, bf16[1536,1536]{1,0:T(8,128)(2,1)}, u32[]{:S(2)}) %copy-start.4) | copy-done | bytes 4718616
  34.2 1.8 %sums_keep.4.refs_6_.refs_1_ = f32[2,96,768]{2,1,0:T(8,128)S(1)} custom-call(s32[1]{0:T(128)} %bitcast.refs_0_, bf16[2,48,1536]{2,1,0:T(8,128)(2,1)S(1)} %pad_maximum_fusion.1.refs_1_, bf16[2,48,1536]{2,1,0:T(8,128)(2,1)S(1)} %collective-permute-done.refs_2_, bf16[1536,1536]{1,0:T(8,128)(2,1)S(1)} %copy-done.1, bf16[1536,1536]{1,0:T(8,128)(2,1)S(1)} %copy-done.4, ...), custom_call_target="tpu_custom_call" | custom-call | flops 452984832 | bytes 4718592 | tf_op jit(solution)/shard_map/sums_keep/pallas_call | solution.py:68
  36.2 1.6 %collective-permute-start.4 = (bf16[2,96,768]{2,1,0:T(8,128)(2,1)S(1)}, bf16[2,96,768]{2,1,0:T(8,128)(2,1)S(1)}, u32[]{:S(2)}, u32[]{:S(2)}) collective-permute-start(bf16[2,96,768]{2,1,0:T(8,128)(2,1)S(1)} %pad_maximum_fusion.2.refs_5_), channel_id=1, source_target_pairs={{0,8},{4,12},{8,0},{12,4},{1,9},{5,13},{9,1},{13,5},{2,10},{6,14},... | collective-permute-start | bytes 884744 | tf_op jit(solution)/shard_map/ppermute | solution.py:407
  37.8 1.4 %collective-permute-start.10 = (bf16[2,48,1536]{2,1,0:T(8,128)(2,1)S(1)}, bf16[2,48,1536]{2,1,0:T(8,128)(2,1)S(1)}, u32[]{:S(2)}, u32[]{:S(2)}) collective-permute-start(bf16[2,48,1536]{2,1,0:T(8,128)(2,1)S(1)} %collective-permute-done.7.refs_7_), channel_id=1, source_target_pairs={{1,0},{2,3},{5,4},{6,7},{9,8},{10,11},{13,12},{14,15},{17,16},{18,... | collective-permute-start | bytes 884744 | tf_op jit(solution)/shard_map/ppermute | solution.py:425
  39.3 1.8 %sums_keep.5.refs_1_.refs_4_ = f32[2,96,768]{2,1,0:T(8,128)S(1)} custom-call(s32[1]{0:T(128)} %bitcast.refs_0_, bf16[2,48,1536]{2,1,0:T(8,128)(2,1)S(1)} %pad_maximum_fusion.1.refs_1_, bf16[2,48,1536]{2,1,0:T(8,128)(2,1)S(1)} %collective-permute-done.refs_2_, bf16[1536,1536]{1,0:T(8,128)(2,1)S(1)} %bitcast.44, bf16[1536,1536]{1,0:T(8,128)(2,1)S(1)} %copy-done.4, ...), custom_call_target="tpu_custom_call" | custom-call | flops 452984832 | bytes 4718592 | tf_op jit(solution)/shard_map/sums_keep/pallas_call | solution.py:68
  41.2 1.6 %collective-permute-start.11 = (bf16[2,48,1536]{2,1,0:T(8,128)(2,1)S(1)}, bf16[2,48,1536]{2,1,0:T(8,128)(2,1)S(1)}, u32[]{:S(2)}, u32[]{:S(2)}) collective-permute-start(bf16[2,48,1536]{2,1,0:T(8,128)(2,1)S(1)} %broadcast_select_fusion.1.refs_1_.refs_5_), channel_id=1, source_target_pairs={{0,16},{16,0},{1,17},{17,1},{2,18},{18,2},{3,19},{19,3},{4,20},{20... | collective-permute-start | bytes 884744 | tf_op jit(solution)/shard_map/ppermute | solution.py:407
  43.0 1.1 collective-permute-start.3
  44.1 3.6 %sums_send.4 = (bf16[96,1536]{1,0:T(8,128)(2,1)S(1)}, bf16[96,1536]{1,0:T(8,128)(2,1)S(1)}) custom-call(s32[1]{0:T(128)} %bitcast.refs_0_, bf16[2,48,1536]{2,1,0:T(8,128)(2,1)S(1)} %collective-permute-done.5.refs_1_.refs_3_, bf16[2,48,1536]{2,1,0:T(8,128)(2,1)S(1)} %collective-permute-done.6.refs_2_.refs_6_.refs_4_, bf16[1536,1536]{1,0:T(8,128)(2,1)S(1)} %bitcast.46, ...), custom_call_target="tpu_custom_call" | custom-call | flops 905969664 | bytes 9437184 | tf_op jit(solution)/shard_map/sums_send/pallas_call | solution.py:68
  47.8 0.6 collective-permute-done.10.refs_6_
  48.5 1.6 %collective-permute-start.15 = (bf16[2,48,1536]{2,1,0:T(8,128)(2,1)S(1)}, bf16[2,48,1536]{2,1,0:T(8,128)(2,1)S(1)}, u32[]{:S(2)}, u32[]{:S(2)}) collective-permute-start(bf16[2,48,1536]{2,1,0:T(8,128)(2,1)S(1)} %broadcast_select_fusion.refs_3_.refs_7_), channel_id=1, source_target_pairs={{0,16},{16,0},{1,17},{17,1},{2,18},{18,2},{3,19},{19,3},{4,20},{20... | collective-permute-start | bytes 884744 | tf_op jit(solution)/shard_map/ppermute | solution.py:407
  50.0 3.6 %sums_keep.6.refs_5_.refs_1_ = f32[2,96,1536]{2,1,0:T(8,128)S(1)} custom-call(s32[1]{0:T(128)} %bitcast.refs_0_, bf16[2,48,1536]{2,1,0:T(8,128)(2,1)S(1)} %collective-permute-done.5.refs_1_.refs_3_, bf16[2,48,1536]{2,1,0:T(8,128)(2,1)S(1)} %collective-permute-done.6.refs_2_.refs_6_.refs_4_, bf16[1536,1536]{1,0:T(8,128)(2,1)S(1)} %bitcast.44, ...), custom_call_target="tpu_custom_call" | custom-call | flops 905969664 | bytes 9437184 | tf_op jit(solution)/shard_map/sums_keep/pallas_call | solution.py:68
  53.6 0.4 activations.6.refs_5_.refs_1_.refs_3_
  54.1 0.4 activations.7.refs_4_.refs_1_.refs_3_
  54.6 0.4 combine.5.refs_7_
  55.0 0.6 collective-permute-start.14
  55.6 2.4 %collective-permute-done.15.refs_4_.refs_8_ = bf16[2,48,1536]{2,1,0:T(8,128)(2,1)S(1)} collective-permute-done((bf16[2,48,1536]{2,1,0:T(8,128)(2,1)S(1)}, bf16[2,48,1536]{2,1,0:T(8,128)(2,1)S(1)}, u32[]{:S(2)}, u32[]{:S(2)}) %collective-permute-start.15) | collective-permute-done | bytes 294944 | tf_op jit(solution)/shard_map/ppermute | solution.py:407
  57.9 3.8 %sums_send.5 = (bf16[192,1536]{1,0:T(8,128)(2,1)S(1)}, bf16[192,1536]{1,0:T(8,128)(2,1)S(1)}) custom-call(s32[1]{0:T(128)} %bitcast.refs_0_, bf16[2,48,1536]{2,1,0:T(8,128)(2,1)S(1)} %broadcast_select_fusion.1.refs_1_.refs_5_, bf16[2,48,1536]{2,1,0:T(8,128)(2,1)S(1)} %collective-permute-done.11.refs_6_.refs_2_, ...), custom_call_target="tpu_custom_call" | custom-call | flops 1811939328 | bytes 9437184 | tf_op jit(solution)/shard_map/sums_send/pallas_call | solution.py:68
  61.9 0.5 collective-permute-start.19
  62.4 3.9 %sums_keep.7.refs_5_.refs_1_ = f32[2,192,1536]{2,1,0:T(8,128)S(1)} custom-call(s32[1]{0:T(128)} %bitcast.refs_0_, bf16[2,48,1536]{2,1,0:T(8,128)(2,1)S(1)} %broadcast_select_fusion.1.refs_1_.refs_5_, bf16[2,48,1536]{2,1,0:T(8,128)(2,1)S(1)} %collective-permute-done.11.refs_6_.refs_2_, bf16[2,48,1536]{2,1,0:T(8,128)(2,1)S(1)} %broadcast_select_fusion.refs_3_.refs_7_, ...), custom_call_target="tpu_custom_call" | custom-call | flops 1811939328 | bytes 9437184 | tf_op jit(solution)/shard_map/sums_keep/pallas_call | solution.py:68
  66.2 4.3 %collective-permute-done.14.refs_4_ = bf16[2,96,1536]{2,1,0:T(8,128)(2,1)S(1)} collective-permute-done((bf16[2,96,1536]{2,1,0:T(8,128)(2,1)S(1)}, bf16[2,96,1536]{2,1,0:T(8,128)(2,1)S(1)}, u32[]{:S(2)}, u32[]{:S(2)}) %collective-permute-start.14) | collective-permute-done | bytes 589856 | tf_op jit(solution)/shard_map/ppermute | solution.py:407
  70.5 0.8 activations.8.refs_10_.refs_2_.refs_4_
  71.6 0.6 collective-permute-start.22
  72.4 0.3 collective-permute-start.16
  72.7 0.4 arrange.1
  73.1 0.7 collective-permute-done.18.refs_3_
  73.8 2.5 %back.5.refs_7_.refs_8_ = f32[192,1536]{1,0:T(8,128)S(1)} custom-call(s32[1]{0:T(128)} %bitcast.refs_0_, bf16[2,96,768]{2,1,0:T(8,128)(2,1)S(1)} %activations.6.refs_5_.refs_1_.refs_3_, bf16[2,96,1536]{2,1,0:T(8,128)(2,1)S(1)} %activations.8.refs_10_.refs_2_.refs_4_, bf16[2,96,768]{2,1,0:T(8,128)(2,1)S(1)} %collective-permute-done.18.refs_3_, ...), custom_call_target="tpu_custom_call" | custom-call | flops 905969664 | bytes 5898240 | tf_op jit(solution)/shard_map/back/pallas_call | solution.py:68
  76.3 2.6 %back.6 = (f32[96,1536]{1,0:T(8,128)S(1)}, bf16[96,1536]{1,0:T(8,128)(2,1)S(1)}) custom-call(s32[1]{0:T(128)} %bitcast.refs_0_, bf16[2,96,768]{2,1,0:T(8,128)(2,1)S(1)} %activations.7.refs_4_.refs_1_.refs_3_, bf16[2,96,1536]{2,1,0:T(8,128)(2,1)S(1)} %activations.8.refs_10_.refs_2_.refs_4_, bf16[2,96,768]{2,1,0:T(8,128)(2,1)S(1)} %collective-permute-done.16.refs_3_, ...), custom_call_target="tpu_custom_call" | custom-call | flops 905969664 | bytes 5898240 | tf_op jit(solution)/shard_map/back/pallas_call | solution.py:68
  78.9 0.6 collective-permute-start.21
  79.5 7.9 %collective-permute-done.22.refs_4_ = bf16[2,96,1536]{2,1,0:T(8,128)(2,1)S(1)} collective-permute-done((bf16[2,96,1536]{2,1,0:T(8,128)(2,1)S(1)}, bf16[2,96,1536]{2,1,0:T(8,128)(2,1)S(1)}, u32[]{:S(2)}, u32[]{:S(2)}) %collective-permute-start.22) | collective-permute-done | bytes 589856 | tf_op jit(solution)/shard_map/ppermute | solution.py:407
  87.4 0.8 activations.9.refs_4_.refs_1_.refs_5_
  88.6 0.6 collective-permute-start.25
  89.2 1.0 collective-permute-done.24.refs_2_.refs_5_
  90.3 3.3 %back.7 = (f32[48,1536]{1,0:T(8,128)S(1)}, bf16[48,1536]{1,0:T(8,128)(2,1)S(1)}) custom-call(s32[1]{0:T(128)} %bitcast.refs_0_, bf16[2,96,1536]{2,1,0:T(8,128)(2,1)S(1)} %activations.9.refs_4_.refs_1_.refs_5_, bf16[2,96,1536]{2,1,0:T(8,128)(2,1)S(1)} %collective-permute-done.24.refs_2_.refs_5_, bf16[1536,1536]{1,0:T(8,128)(2,1)S(1)} %bitcast.44, ...), custom_call_target="tpu_custom_call" | custom-call | flops 905969664 | bytes 10027008 | tf_op jit(solution)/shard_map/back/pallas_call | solution.py:68
  93.5 4.5 %collective-permute-done.25.refs_4_ = bf16[2,96,768]{2,1,0:T(8,128)(2,1)S(1)} collective-permute-done((bf16[2,96,768]{2,1,0:T(8,128)(2,1)S(1)}, bf16[2,96,768]{2,1,0:T(8,128)(2,1)S(1)}, u32[]{:S(2)}, u32[]{:S(2)}) %collective-permute-start.25) | collective-permute-done | bytes 294944 | tf_op jit(solution)/shard_map/ppermute | solution.py:407
  98.0 0.4 activations.10.refs_4_.refs_6_.refs_1_
  98.5 1.0 collective-permute-start.23
  99.5 1.5 %collective-permute-start.27 = (bf16[48,1536]{1,0:T(8,128)(2,1)S(1)}, bf16[48,1536]{1,0:T(8,128)(2,1)S(1)}, u32[]{:S(2)}, u32[]{:S(2)}) collective-permute-start(bf16[48,1536]{1,0:T(8,128)(2,1)S(1)} %get-tuple-element.49), channel_id=1, source_target_pairs={{0,16},{16,0},{1,17},{17,1},{2,18},{18,2},{3,19},{19,3},{4,20},{20... | collective-permute-start | bytes 442376 | tf_op jit(solution)/shard_map/ppermute | solution.py:407
  101.2 1.3 collective-permute-start.29
  102.5 5.4 %weight_grads.4 = (f32[1536,3072]{1,0:T(8,128)}, f32[3072,1536]{1,0:T(8,128)}, f32[8,128]{1,0:T(8,128)S(1)}) custom-call(s32[1]{0:T(128)} %bitcast.refs_0_, bf16[1536,384]{1,0:T(8,128)(2,1)S(1)} %get-tuple-element.42.refs_7_.refs_1_, bf16[384,1536]{1,0:T(8,128)(2,1)S(1)} %get-tuple-element.45.refs_2_, ...), custom_call_target="tpu_custom_call" | custom-call | flops 1811939328 | bytes 9437184 | tf_op jit(solution)/shard_map/weight_grads/pallas_call | solution.py:68
  108.0 2.2 %back.8.refs_9_.refs_5_ = f32[96,1536]{1,0:T(8,128)S(1)} custom-call(s32[1]{0:T(128)} %bitcast.refs_0_, bf16[2,96,768]{2,1,0:T(8,128)(2,1)S(1)} %activations.10.refs_4_.refs_6_.refs_1_, bf16[2,96,768]{2,1,0:T(8,128)(2,1)S(1)} %collective-permute-done.26.refs_2_.refs_6_, bf16[1536,1536]{1,0:T(8,128)(2,1)S(1)} %bitcast.44, bf16[1536,1536]{1,0:T(8,128)(2,1)S(1)} %bitcast.46, ...), custom_call_target="tpu_custom_call" | custom-call | flops 452984832 | bytes 5308416 | tf_op jit(solution)/shard_map/back/pallas_call | solution.py:68
  110.2 5.5 %weight_grads.5 = (f32[1536,3072]{1,0:T(8,128)}, f32[3072,1536]{1,0:T(8,128)}, f32[8,128]{1,0:T(8,128)S(1)}) custom-call(s32[1]{0:T(128)} %bitcast.refs_0_, bf16[1536,384]{1,0:T(8,128)(2,1)S(1)} %get-tuple-element.42.refs_7_.refs_1_, bf16[384,1536]{1,0:T(8,128)(2,1)S(1)} %get-tuple-element.45.refs_2_, ...), custom_call_target="tpu_custom_call", output_to_operand_aliasing={{0}: (7, {}), {1}: (8, {})} | custom-call | flops 1811939328 | bytes 9437184 | tf_op jit(solution)/shard_map/weight_grads/pallas_call | solution.py:68
  115.7 0.4 activations.11.refs_1_.refs_6_
  116.5 1.3 %collective-permute-done.30.refs_2_.refs_6_ = bf16[2,96,768]{2,1,0:T(8,128)(2,1)S(1)} collective-permute-done((bf16[2,96,768]{2,1,0:T(8,128)(2,1)S(1)}, bf16[2,96,768]{2,1,0:T(8,128)(2,1)S(1)}, u32[]{:S(2)}, u32[]{:S(2)}) %collective-permute-start.30) | collective-permute-done | bytes 294944 | tf_op jit(solution)/shard_map/ppermute | solution.py:407
  117.8 2.3 %back.9 = (f32[48,1536]{1,0:T(8,128)S(1)}, bf16[48,1536]{1,0:T(8,128)(2,1)S(1)}) custom-call(s32[1]{0:T(128)} %bitcast.refs_0_, bf16[2,96,768]{2,1,0:T(8,128)(2,1)S(1)} %activations.11.refs_1_.refs_6_, bf16[2,96,768]{2,1,0:T(8,128)(2,1)S(1)} %collective-permute-done.30.refs_2_.refs_6_, bf16[1536,1536]{1,0:T(8,128)(2,1)S(1)} %bitcast.44, ...), custom_call_target="tpu_custom_call" | custom-call | flops 452984832 | bytes 5308416 | tf_op jit(solution)/shard_map/back/pallas_call | solution.py:68
  120.1 0.6 collective-permute-start.31
  120.7 5.4 %weight_grads.6 = (f32[1536,3072]{1,0:T(8,128)}, f32[3072,1536]{1,0:T(8,128)}, f32[8,128]{1,0:T(8,128)S(1)}) custom-call(s32[1]{0:T(128)} %bitcast.refs_0_, bf16[1536,384]{1,0:T(8,128)(2,1)S(1)} %get-tuple-element.42.refs_7_.refs_1_, bf16[384,1536]{1,0:T(8,128)(2,1)S(1)} %get-tuple-element.45.refs_2_, ...), custom_call_target="tpu_custom_call", output_to_operand_aliasing={{0}: (7, {}), {1}: (8, {})} | custom-call | flops 1811939328 | bytes 9437184 | tf_op jit(solution)/shard_map/weight_grads/pallas_call | solution.py:68
  126.1 1.6 %collective-permute-start.32 = (bf16[48,1536]{1,0:T(8,128)(2,1)S(1)}, bf16[48,1536]{1,0:T(8,128)(2,1)S(1)}, u32[]{:S(2)}, u32[]{:S(2)}) collective-permute-start(bf16[48,1536]{1,0:T(8,128)(2,1)S(1)} %fold.9.refs_9_), channel_id=1, source_target_pairs={{0,3},{1,2},{2,1},{3,0},{4,7},{5,6},{6,5},{7,4},{8,11},{9,10},{10,... | collective-permute-start | bytes 442376 | tf_op jit(solution)/shard_map/ppermute | solution.py:407
  127.8 5.4 %weight_grads.7 = (f32[1536,3072]{1,0:T(8,128)}, f32[3072,1536]{1,0:T(8,128)}, f32[8,128]{1,0:T(8,128)}) custom-call(s32[1]{0:T(128)} %bitcast.refs_0_, bf16[1536,384]{1,0:T(8,128)(2,1)S(1)} %get-tuple-element.42.refs_7_.refs_1_, bf16[384,1536]{1,0:T(8,128)(2,1)S(1)} %get-tuple-element.45.refs_2_, ...), custom_call_target="tpu_custom_call", output_to_operand_aliasing={{0}: (7, {}), {1}: (8, {})} | custom-call | flops 1811939328 | bytes 9437184 | tf_op jit(solution)/shard_map/weight_grads/pallas_call | solution.py:68
  133.2 0.5 collective-permute-done.32
  133.7 0.7 add_convert_fusion
  (77 shorter events, 2.2 us)
Async XLA Ops:
  1.6 19.0 %collective-permute-start = (bf16[2,48,1536]{2,1,0:T(8,128)(2,1)S(1)}, bf16[2,48,1536]{2,1,0:T(8,128)(2,1)S(1)}, u32[]{:S(2)}, u32[]{:S(2)}) collective-permute-start(bf16[2,48,1536]{2,1,0:T(8,128)(2,1)S(1)} %pad_maximum_fusion.1.refs_1_), channel_id=1, source_target_pairs={{0,16},{16,0},{1,17},{17,1},{2,18},{18,2},{3,19},{19,3},{4,20},{20... | collective-permute-start | bytes 884744 | tf_op jit(solution)/shard_map/ppermute | solution.py:407
  4.6 23.6 %collective-permute-start.8 = (bf16[2,48,1536]{2,1,0:T(8,128)(2,1)S(1)}, bf16[2,48,1536]{2,1,0:T(8,128)(2,1)S(1)}, u32[]{:S(2)}, u32[]{:S(2)}) collective-permute-start(bf16[2,48,1536]{2,1,0:T(8,128)(2,1)S(1)} %pad_maximum_fusion.1.refs_1_), channel_id=1, source_target_pairs={{1,2},{2,1},{5,6},{6,5},{9,10},{10,9},{13,14},{14,13},{17,18},{18,... | collective-permute-start | bytes 884744 | tf_op jit(solution)/shard_map/ppermute | solution.py:422
  5.3 21.6 %collective-permute-start.5 = (bf16[2,48,1536]{2,1,0:T(8,128)(2,1)S(1)}, bf16[2,48,1536]{2,1,0:T(8,128)(2,1)S(1)}, u32[]{:S(2)}, u32[]{:S(2)}) collective-permute-start(bf16[2,48,1536]{2,1,0:T(8,128)(2,1)S(1)} %pad_maximum_fusion.1.refs_1_), channel_id=1, source_target_pairs={{0,1},{1,0},{2,3},{3,2},{4,5},{5,4},{6,7},{7,6},{8,9},{9,8},{10,11... | collective-permute-start | bytes 884744 | tf_op jit(solution)/shard_map/ppermute | solution.py:407
  16.3 2.2 %copy-start = (bf16[1536,1536]{1,0:T(8,128)(2,1)}, bf16[1536,1536]{1,0:T(8,128)(2,1)S(1)}, u32[]{:S(2)}) copy-start(bf16[1536,1536]{1,0:T(8,128)(2,1)S(1)} %get-tuple-element.32.refs_3_.refs_5_) | copy-start | bytes 14155780
  18.5 2.2 %copy-start.3 = (bf16[1536,1536]{1,0:T(8,128)(2,1)}, bf16[1536,1536]{1,0:T(8,128)(2,1)S(1)}, u32[]{:S(2)}) copy-start(bf16[1536,1536]{1,0:T(8,128)(2,1)S(1)} %get-tuple-element.33.refs_4_.refs_6_) | copy-start | bytes 14155780
  20.7 3.6 %copy-start.5 = (bf16[1536,1536]{1,0:T(8,128)(2,1)}, bf16[1536,1536]{1,0:T(8,128)(2,1)S(1)}, u32[]{:S(2)}) copy-start(bf16[1536,1536]{1,0:T(8,128)(2,1)S(1)} %get-tuple-element.35.refs_4_.refs_6_) | copy-start | bytes 14155780
  20.7 18.6 %slice-start = ((s8[4718592]{0:T(1024)(128)(4,1)}), s8[524288]{0:T(1024)(128)(4,1)S(1)}, s32[]{:S(2)}) async-start(s8[4718592]{0:T(1024)(128)(4,1)} %bitcast.43), calls=%async_computation | async-start | bytes 1048576
  24.3 2.2 %copy-start.2 = (bf16[1536,1536]{1,0:T(8,128)(2,1)}, bf16[1536,1536]{1,0:T(8,128)(2,1)S(1)}, u32[]{:S(2)}) copy-start(bf16[1536,1536]{1,0:T(8,128)(2,1)S(1)} %get-tuple-element.34.refs_3_.refs_5_.refs_6_.refs_4_) | copy-start | bytes 14155780
  26.4 9.6 %collective-permute-start.2 = (bf16[96,1536]{1,0:T(8,128)(2,1)S(1)}, bf16[96,1536]{1,0:T(8,128)(2,1)S(1)}, u32[]{:S(2)}, u32[]{:S(2)}) collective-permute-start(bf16[96,1536]{1,0:T(8,128)(2,1)S(1)} %get-tuple-element.37), channel_id=1, source_target_pairs={{0,4},{4,0},{8,12},{12,8},{1,5},{5,1},{9,13},{13,9},{2,6},{6,2},{1... | collective-permute-start | bytes 884744 | tf_op jit(solution)/shard_map/ppermute | solution.py:407
  26.4 9.6 %collective-permute-start.1 = (bf16[96,1536]{1,0:T(8,128)(2,1)S(1)}, bf16[96,1536]{1,0:T(8,128)(2,1)S(1)}, u32[]{:S(2)}, u32[]{:S(2)}) collective-permute-start(bf16[96,1536]{1,0:T(8,128)(2,1)S(1)} %get-tuple-element.36.refs_5_), channel_id=1, source_target_pairs={{0,4},{4,0},{8,12},{12,8},{1,5},{5,1},{9,13},{13,9},{2,6},{6,2},{1... | collective-permute-start | bytes 884744 | tf_op jit(solution)/shard_map/ppermute | solution.py:407
  26.9 10.8 %collective-permute-start.7 = (bf16[2,48,1536]{2,1,0:T(8,128)(2,1)S(1)}, bf16[2,48,1536]{2,1,0:T(8,128)(2,1)S(1)}, u32[]{:S(2)}, u32[]{:S(2)}) collective-permute-start(bf16[2,48,1536]{2,1,0:T(8,128)(2,1)S(1)} %collective-permute-done.5.refs_1_.refs_3_), channel_id=1, source_target_pairs={{1,2},{2,1},{5,6},{6,5},{9,10},{10,9},{13,14},{14,13},{17,18},{18,... | collective-permute-start | bytes 884744 | tf_op jit(solution)/shard_map/ppermute | solution.py:423
  27.6 16.5 %collective-permute-start.6 = (bf16[2,48,1536]{2,1,0:T(8,128)(2,1)S(1)}, bf16[2,48,1536]{2,1,0:T(8,128)(2,1)S(1)}, u32[]{:S(2)}, u32[]{:S(2)}) collective-permute-start(bf16[2,48,1536]{2,1,0:T(8,128)(2,1)S(1)} %collective-permute-done.5.refs_1_.refs_3_), channel_id=1, source_target_pairs={{0,16},{16,0},{1,17},{17,1},{2,18},{18,2},{3,19},{19,3},{4,20},{20... | collective-permute-start | bytes 884744 | tf_op jit(solution)/shard_map/ppermute | solution.py:407
  28.2 11.0 %collective-permute-start.9 = (bf16[2,48,1536]{2,1,0:T(8,128)(2,1)S(1)}, bf16[2,48,1536]{2,1,0:T(8,128)(2,1)S(1)}, u32[]{:S(2)}, u32[]{:S(2)}) collective-permute-start(bf16[2,48,1536]{2,1,0:T(8,128)(2,1)S(1)} %collective-permute-done.8), channel_id=1, source_target_pairs={{1,0},{2,3},{5,4},{6,7},{9,8},{10,11},{13,12},{14,15},{17,16},{18,... | collective-permute-start | bytes 884744 | tf_op jit(solution)/shard_map/ppermute | solution.py:424
  29.5 2.3 %copy-start.1 = (bf16[1536,1536]{1,0:T(8,128)(2,1)S(1)}, bf16[1536,1536]{1,0:T(8,128)(2,1)}, u32[]{:S(2)}) copy-start(bf16[1536,1536]{1,0:T(8,128)(2,1)} %copy-done) | copy-start | bytes 14155780
  31.9 2.3 %copy-start.4 = (bf16[1536,1536]{1,0:T(8,128)(2,1)S(1)}, bf16[1536,1536]{1,0:T(8,128)(2,1)}, u32[]{:S(2)}) copy-start(bf16[1536,1536]{1,0:T(8,128)(2,1)} %copy-done.3) | copy-start | bytes 14155780
  34.2 5.1 %slice-start.1 = ((s8[4718592]{0:T(1024)(128)(4,1)}), s8[4194304]{0:T(1024)(128)(4,1)S(1)}, s32[]{:S(2)}) async-start(s8[4718592]{0:T(1024)(128)(4,1)} %bitcast.43), calls=%async_computation.1 | async-start | bytes 8388608
  36.0 8.1 %slice-start.2 = ((s8[4718592]{0:T(1024)(128)(4,1)}), s8[4194304]{0:T(1024)(128)(4,1)S(1)}, s32[]{:S(2)}) async-start(s8[4718592]{0:T(1024)(128)(4,1)} %bitcast.45), calls=%async_computation.2 | async-start | bytes 8388608
  36.0 8.1 %slice-start.6 = ((s8[4718592]{0:T(1024)(128)(4,1)}), s8[4194304]{0:T(1024)(128)(4,1)S(1)}, s32[]{:S(2)}) async-start(s8[4718592]{0:T(1024)(128)(4,1)} %bitcast.49), calls=%async_computation.6 | async-start | bytes 8388608
  36.2 12.3 %collective-permute-start.4 = (bf16[2,96,768]{2,1,0:T(8,128)(2,1)S(1)}, bf16[2,96,768]{2,1,0:T(8,128)(2,1)S(1)}, u32[]{:S(2)}, u32[]{:S(2)}) collective-permute-start(bf16[2,96,768]{2,1,0:T(8,128)(2,1)S(1)} %pad_maximum_fusion.2.refs_5_), channel_id=1, source_target_pairs={{0,8},{4,12},{8,0},{12,4},{1,9},{5,13},{9,1},{13,5},{2,10},{6,14},... | collective-permute-start | bytes 884744 | tf_op jit(solution)/shard_map/ppermute | solution.py:407
  37.8 10.6 %collective-permute-start.10 = (bf16[2,48,1536]{2,1,0:T(8,128)(2,1)S(1)}, bf16[2,48,1536]{2,1,0:T(8,128)(2,1)S(1)}, u32[]{:S(2)}, u32[]{:S(2)}) collective-permute-start(bf16[2,48,1536]{2,1,0:T(8,128)(2,1)S(1)} %collective-permute-done.7.refs_7_), channel_id=1, source_target_pairs={{1,0},{2,3},{5,4},{6,7},{9,8},{10,11},{13,12},{14,15},{17,16},{18,... | collective-permute-start | bytes 884744 | tf_op jit(solution)/shard_map/ppermute | solution.py:425
  39.3 4.8 %slice-start.3 = ((s8[4718592]{0:T(1024)(128)(4,1)}), s8[524288]{0:T(1024)(128)(4,1)S(1)}, s32[]{:S(2)}) async-start(s8[4718592]{0:T(1024)(128)(4,1)} %bitcast.45), calls=%async_computation.3 | async-start | bytes 1048576
  39.3 4.8 %slice-start.7 = ((s8[4718592]{0:T(1024)(128)(4,1)}), s8[524288]{0:T(1024)(128)(4,1)S(1)}, s32[]{:S(2)}) async-start(s8[4718592]{0:T(1024)(128)(4,1)} %bitcast.49), calls=%async_computation.7 | async-start | bytes 1048576
  41.1 8.9 %slice-start.4 = ((s8[4718592]{0:T(1024)(128)(4,1)}), s8[4194304]{0:T(1024)(128)(4,1)S(1)}, s32[]{:S(2)}) async-start(s8[4718592]{0:T(1024)(128)(4,1)} %bitcast.47), calls=%async_computation.4 | async-start | bytes 8388608
  41.2 12.9 %collective-permute-start.11 = (bf16[2,48,1536]{2,1,0:T(8,128)(2,1)S(1)}, bf16[2,48,1536]{2,1,0:T(8,128)(2,1)S(1)}, u32[]{:S(2)}, u32[]{:S(2)}) collective-permute-start(bf16[2,48,1536]{2,1,0:T(8,128)(2,1)S(1)} %broadcast_select_fusion.1.refs_1_.refs_5_), channel_id=1, source_target_pairs={{0,16},{16,0},{1,17},{17,1},{2,18},{18,2},{3,19},{19,3},{4,20},{20... | collective-permute-start | bytes 884744 | tf_op jit(solution)/shard_map/ppermute | solution.py:407
  43.0 7.1 %slice-start.5 = ((s8[4718592]{0:T(1024)(128)(4,1)}), s8[524288]{0:T(1024)(128)(4,1)S(1)}, s32[]{:S(2)}) async-start(s8[4718592]{0:T(1024)(128)(4,1)} %bitcast.47), calls=%async_computation.5 | async-start | bytes 1048576
  43.0 11.1 %collective-permute-start.3 = (bf16[2,96,768]{2,1,0:T(8,128)(2,1)S(1)}, bf16[2,96,768]{2,1,0:T(8,128)(2,1)S(1)}, u32[]{:S(2)}, u32[]{:S(2)}) collective-permute-start(bf16[2,96,768]{2,1,0:T(8,128)(2,1)S(1)} %combine.4.refs_5_), channel_id=1, source_target_pairs={{0,8},{4,12},{8,0},{12,4},{1,9},{5,13},{9,1},{13,5},{2,10},{6,14},... | collective-permute-start | bytes 884744 | tf_op jit(solution)/shard_map/ppermute | solution.py:407
  47.7 6.8 %collective-permute-start.13 = (bf16[96,1536]{1,0:T(8,128)(2,1)S(1)}, bf16[96,1536]{1,0:T(8,128)(2,1)S(1)}, u32[]{:S(2)}, u32[]{:S(2)}) collective-permute-start(bf16[96,1536]{1,0:T(8,128)(2,1)S(1)} %get-tuple-element.39), channel_id=1, source_target_pairs={{0,4},{4,0},{8,12},{12,8},{1,5},{5,1},{9,13},{13,9},{2,6},{6,2},{1... | collective-permute-start | bytes 884744 | tf_op jit(solution)/shard_map/ppermute | solution.py:407
  48.4 6.1 %collective-permute-start.12 = (bf16[96,1536]{1,0:T(8,128)(2,1)S(1)}, bf16[96,1536]{1,0:T(8,128)(2,1)S(1)}, u32[]{:S(2)}, u32[]{:S(2)}) collective-permute-start(bf16[96,1536]{1,0:T(8,128)(2,1)S(1)} %get-tuple-element.38.refs_5_), channel_id=1, source_target_pairs={{0,4},{4,0},{8,12},{12,8},{1,5},{5,1},{9,13},{13,9},{2,6},{6,2},{1... | collective-permute-start | bytes 884744 | tf_op jit(solution)/shard_map/ppermute | solution.py:407
  48.5 9.5 %collective-permute-start.15 = (bf16[2,48,1536]{2,1,0:T(8,128)(2,1)S(1)}, bf16[2,48,1536]{2,1,0:T(8,128)(2,1)S(1)}, u32[]{:S(2)}, u32[]{:S(2)}) collective-permute-start(bf16[2,48,1536]{2,1,0:T(8,128)(2,1)S(1)} %broadcast_select_fusion.refs_3_.refs_7_), channel_id=1, source_target_pairs={{0,16},{16,0},{1,17},{17,1},{2,18},{18,2},{3,19},{19,3},{4,20},{20... | collective-permute-start | bytes 884744 | tf_op jit(solution)/shard_map/ppermute | solution.py:407
  55.0 15.5 %collective-permute-start.14 = (bf16[2,96,1536]{2,1,0:T(8,128)(2,1)S(1)}, bf16[2,96,1536]{2,1,0:T(8,128)(2,1)S(1)}, u32[]{:S(2)}, u32[]{:S(2)}) collective-permute-start(bf16[2,96,1536]{2,1,0:T(8,128)(2,1)S(1)} %combine.5.refs_7_), channel_id=1, source_target_pairs={{0,8},{4,12},{8,0},{12,4},{1,9},{5,13},{9,1},{13,5},{2,10},{6,14},... | collective-permute-start | bytes 1769480 | tf_op jit(solution)/shard_map/ppermute | solution.py:407
  61.8 9.6 %collective-permute-start.20 = (bf16[192,1536]{1,0:T(8,128)(2,1)S(1)}, bf16[192,1536]{1,0:T(8,128)(2,1)S(1)}, u32[]{:S(2)}, u32[]{:S(2)}) collective-permute-start(bf16[192,1536]{1,0:T(8,128)(2,1)S(1)} %get-tuple-element.41), channel_id=1, source_target_pairs={{0,4},{4,0},{8,12},{12,8},{1,5},{5,1},{9,13},{13,9},{2,6},{6,2},{1... | collective-permute-start | bytes 1769480 | tf_op jit(solution)/shard_map/ppermute | solution.py:407
  61.9 9.5 %collective-permute-start.19 = (bf16[192,1536]{1,0:T(8,128)(2,1)S(1)}, bf16[192,1536]{1,0:T(8,128)(2,1)S(1)}, u32[]{:S(2)}, u32[]{:S(2)}) collective-permute-start(bf16[192,1536]{1,0:T(8,128)(2,1)S(1)} %get-tuple-element.40.refs_7_), channel_id=1, source_target_pairs={{0,4},{4,0},{8,12},{12,8},{1,5},{5,1},{9,13},{13,9},{2,6},{6,2},{1... | collective-permute-start | bytes 1769480 | tf_op jit(solution)/shard_map/ppermute | solution.py:407
  71.3 2.5 %collective-permute-start.17 = (bf16[2,96,1536]{2,1,0:T(8,128)(2,1)S(1)}, bf16[2,96,1536]{2,1,0:T(8,128)(2,1)S(1)}, u32[]{:S(2)}, u32[]{:S(2)}) collective-permute-start(bf16[2,96,1536]{2,1,0:T(8,128)(2,1)S(1)} %activations.8.refs_10_.refs_2_.refs_4_), channel_id=1, source_target_pairs={{0,4},{4,0},{8,12},{12,8},{1,5},{5,1},{9,13},{13,9},{2,6},{6,2},{1... | collective-permute-start | bytes 1769480 | tf_op jit(solution)/shard_map/ppermute | solution.py:407
  71.6 15.8 %collective-permute-start.22 = (bf16[2,96,1536]{2,1,0:T(8,128)(2,1)S(1)}, bf16[2,96,1536]{2,1,0:T(8,128)(2,1)S(1)}, u32[]{:S(2)}, u32[]{:S(2)}) collective-permute-start(bf16[2,96,1536]{2,1,0:T(8,128)(2,1)S(1)} %pad_maximum_fusion.refs_9_), channel_id=1, source_target_pairs={{0,8},{4,12},{8,0},{12,4},{1,9},{5,13},{9,1},{13,5},{2,10},{6,14},... | collective-permute-start | bytes 1769480 | tf_op jit(solution)/shard_map/ppermute | solution.py:407
  72.2 1.6 %collective-permute-start.18 = (bf16[2,96,768]{2,1,0:T(8,128)(2,1)S(1)}, bf16[2,96,768]{2,1,0:T(8,128)(2,1)S(1)}, u32[]{:S(2)}, u32[]{:S(2)}) collective-permute-start(bf16[2,96,768]{2,1,0:T(8,128)(2,1)S(1)} %activations.6.refs_5_.refs_1_.refs_3_), channel_id=1, source_target_pairs={{0,4},{4,0},{8,12},{12,8},{1,5},{5,1},{9,13},{13,9},{2,6},{6,2},{1... | collective-permute-start | bytes 884744 | tf_op jit(solution)/shard_map/ppermute | solution.py:407
  72.4 3.9 %collective-permute-start.16 = (bf16[2,96,768]{2,1,0:T(8,128)(2,1)S(1)}, bf16[2,96,768]{2,1,0:T(8,128)(2,1)S(1)}, u32[]{:S(2)}, u32[]{:S(2)}) collective-permute-start(bf16[2,96,768]{2,1,0:T(8,128)(2,1)S(1)} %activations.7.refs_4_.refs_1_.refs_3_), channel_id=1, source_target_pairs={{0,4},{4,0},{8,12},{12,8},{1,5},{5,1},{9,13},{13,9},{2,6},{6,2},{1... | collective-permute-start | bytes 884744 | tf_op jit(solution)/shard_map/ppermute | solution.py:407
  78.9 10.3 %collective-permute-start.21 = (bf16[96,1536]{1,0:T(8,128)(2,1)S(1)}, bf16[96,1536]{1,0:T(8,128)(2,1)S(1)}, u32[]{:S(2)}, u32[]{:S(2)}) collective-permute-start(bf16[96,1536]{1,0:T(8,128)(2,1)S(1)} %get-tuple-element.44), channel_id=1, source_target_pairs={{0,16},{16,0},{1,17},{17,1},{2,18},{18,2},{3,19},{19,3},{4,20},{20... | collective-permute-start | bytes 884744 | tf_op jit(solution)/shard_map/ppermute | solution.py:407
  88.2 2.1 %collective-permute-start.24 = (bf16[2,96,1536]{2,1,0:T(8,128)(2,1)S(1)}, bf16[2,96,1536]{2,1,0:T(8,128)(2,1)S(1)}, u32[]{:S(2)}, u32[]{:S(2)}) collective-permute-start(bf16[2,96,1536]{2,1,0:T(8,128)(2,1)S(1)} %activations.9.refs_4_.refs_1_.refs_5_), channel_id=1, source_target_pairs={{0,4},{4,0},{8,12},{12,8},{1,5},{5,1},{9,13},{13,9},{2,6},{6,2},{1... | collective-permute-start | bytes 1769480 | tf_op jit(solution)/shard_map/ppermute | solution.py:407
  88.6 9.5 %collective-permute-start.25 = (bf16[2,96,768]{2,1,0:T(8,128)(2,1)S(1)}, bf16[2,96,768]{2,1,0:T(8,128)(2,1)S(1)}, u32[]{:S(2)}, u32[]{:S(2)}) collective-permute-start(bf16[2,96,768]{2,1,0:T(8,128)(2,1)S(1)} %combine.6.refs_3_), channel_id=1, source_target_pairs={{0,8},{4,12},{8,0},{12,4},{1,9},{5,13},{9,1},{13,5},{2,10},{6,14},... | collective-permute-start | bytes 884744 | tf_op jit(solution)/shard_map/ppermute | solution.py:407
  98.5 9.5 %collective-permute-start.26 = (bf16[2,96,768]{2,1,0:T(8,128)(2,1)S(1)}, bf16[2,96,768]{2,1,0:T(8,128)(2,1)S(1)}, u32[]{:S(2)}, u32[]{:S(2)}) collective-permute-start(bf16[2,96,768]{2,1,0:T(8,128)(2,1)S(1)} %activations.10.refs_4_.refs_6_.refs_1_), channel_id=1, source_target_pairs={{0,4},{4,0},{8,12},{12,8},{1,5},{5,1},{9,13},{13,9},{2,6},{6,2},{1... | collective-permute-start | bytes 884744 | tf_op jit(solution)/shard_map/ppermute | solution.py:407
  98.5 17.2 %collective-permute-start.23 = (bf16[48,1536]{1,0:T(8,128)(2,1)S(1)}, bf16[48,1536]{1,0:T(8,128)(2,1)S(1)}, u32[]{:S(2)}, u32[]{:S(2)}) collective-permute-start(bf16[48,1536]{1,0:T(8,128)(2,1)S(1)} %fold.6.refs_5_), channel_id=1, source_target_pairs={{0,1},{1,0},{2,3},{3,2},{4,5},{5,4},{6,7},{7,6},{8,9},{9,8},{10,11... | collective-permute-start | bytes 442376 | tf_op jit(solution)/shard_map/ppermute | solution.py:407
  99.5 8.5 %collective-permute-start.27 = (bf16[48,1536]{1,0:T(8,128)(2,1)S(1)}, bf16[48,1536]{1,0:T(8,128)(2,1)S(1)}, u32[]{:S(2)}, u32[]{:S(2)}) collective-permute-start(bf16[48,1536]{1,0:T(8,128)(2,1)S(1)} %get-tuple-element.49), channel_id=1, source_target_pairs={{0,16},{16,0},{1,17},{17,1},{2,18},{18,2},{3,19},{19,3},{4,20},{20... | collective-permute-start | bytes 442376 | tf_op jit(solution)/shard_map/ppermute | solution.py:407
  101.2 14.5 %collective-permute-start.29 = (bf16[2,96,768]{2,1,0:T(8,128)(2,1)S(1)}, bf16[2,96,768]{2,1,0:T(8,128)(2,1)S(1)}, u32[]{:S(2)}, u32[]{:S(2)}) collective-permute-start(bf16[2,96,768]{2,1,0:T(8,128)(2,1)S(1)} %combine.7.refs_7_), channel_id=1, source_target_pairs={{0,8},{4,12},{8,0},{12,4},{1,9},{5,13},{9,1},{13,5},{2,10},{6,14},... | collective-permute-start | bytes 884744 | tf_op jit(solution)/shard_map/ppermute | solution.py:407
  116.2 1.6 %collective-permute-start.30 = (bf16[2,96,768]{2,1,0:T(8,128)(2,1)S(1)}, bf16[2,96,768]{2,1,0:T(8,128)(2,1)S(1)}, u32[]{:S(2)}, u32[]{:S(2)}) collective-permute-start(bf16[2,96,768]{2,1,0:T(8,128)(2,1)S(1)} %activations.11.refs_1_.refs_6_), channel_id=1, source_target_pairs={{0,4},{4,0},{8,12},{12,8},{1,5},{5,1},{9,13},{13,9},{2,6},{6,2},{1... | collective-permute-start | bytes 884744 | tf_op jit(solution)/shard_map/ppermute | solution.py:407
  116.3 16.9 %collective-permute-start.28 = (bf16[48,1536]{1,0:T(8,128)(2,1)S(1)}, bf16[48,1536]{1,0:T(8,128)(2,1)S(1)}, u32[]{:S(2)}, u32[]{:S(2)}) collective-permute-start(bf16[48,1536]{1,0:T(8,128)(2,1)S(1)} %fold.7.refs_5_), channel_id=1, source_target_pairs={{0,2},{1,3},{2,0},{3,1},{4,6},{5,7},{6,4},{7,5},{8,10},{9,11},{10,... | collective-permute-start | bytes 442376 | tf_op jit(solution)/shard_map/ppermute | solution.py:407
  120.1 6.0 %collective-permute-start.31 = (bf16[48,1536]{1,0:T(8,128)(2,1)S(1)}, bf16[48,1536]{1,0:T(8,128)(2,1)S(1)}, u32[]{:S(2)}, u32[]{:S(2)}) collective-permute-start(bf16[48,1536]{1,0:T(8,128)(2,1)S(1)} %get-tuple-element.53), channel_id=1, source_target_pairs={{0,16},{16,0},{1,17},{17,1},{2,18},{18,2},{3,19},{19,3},{4,20},{20... | collective-permute-start | bytes 442376 | tf_op jit(solution)/shard_map/ppermute | solution.py:407
  126.1 7.6 %collective-permute-start.32 = (bf16[48,1536]{1,0:T(8,128)(2,1)S(1)}, bf16[48,1536]{1,0:T(8,128)(2,1)S(1)}, u32[]{:S(2)}, u32[]{:S(2)}) collective-permute-start(bf16[48,1536]{1,0:T(8,128)(2,1)S(1)} %fold.9.refs_9_), channel_id=1, source_target_pairs={{0,3},{1,2},{2,1},{3,0},{4,7},{5,6},{6,5},{7,4},{8,11},{9,10},{10,... | collective-permute-start | bytes 442376 | tf_op jit(solution)/shard_map/ppermute | solution.py:407

commit v8 on v7

--- a/solution.py
+++ b/solution.py
@@ -92,46 +92,83 @@
     return core_ref[0] if side == 0 else 1 - core_ref[0]
 
 
-def bring(core, up, down):
-    depth, full = up.shape
-    half = full // 2
-    parts = 2
-
-    def body(core_ref, up_ref, down_ref, *refs):
-        *outs, sems = refs
-        copies = []
-        for side in range(2):
-            begin = pl.multiple_of(side_of(core_ref, side) * half, half)
-            up_out, down_out = outs[2 * side : 2 * side + 2]
-            for part in range(parts):
-                rows = pl.ds(part * (depth // parts), depth // parts)
-                copies.append((up_ref.at[rows, pl.ds(begin, half)], up_out.at[rows]))
-                size = half // parts
-                rows = pl.ds(pl.multiple_of(begin + part * size, size), size)
-                copies.append((down_ref.at[rows], down_out.at[pl.ds(part * size, size)]))
-        copies = [
-            pltpu.make_async_copy(source, target, sems.at[n])
-            for n, (source, target) in enumerate(copies)
-        ]
-        for copy in copies:
+def halves(core_ref, side, up_ref, down_ref, up_out, down_out, sems, parts):
+    half = up_out.shape[1]
+    size = half // parts
+    pairs = []
+    for part in range(parts):
+        begin = pl.multiple_of(side_of(core_ref, side) * half + part * size, size)
+        here = pl.ds(part * size, size)
+        pairs.append((
+            pltpu.make_async_copy(up_ref.at[:, pl.ds(begin, size)], up_out.at[:, here], sems.at[0, part]),
+            pltpu.make_async_copy(down_ref.at[pl.ds(begin, size)], down_out.at[here], sems.at[1, part]),
+        ))
+    return pairs
+
+
+def half_outs(up):
+    depth, half = up.shape[0], up.shape[1] // 2
+    return [pltpu.VMEM((depth, half), BF16), pltpu.VMEM((half, depth), BF16)]
+
+
+def bring(core, side, up, down):
+    def body(core_ref, up_ref, down_ref, up_out, down_out, sems):
+        pairs = halves(core_ref, side, up_ref, down_ref, up_out, down_out, sems, 1)
+        for copy in pairs[0]:
             copy.start()
-        for copy in copies:
+        for copy in pairs[0]:
             copy.wait()
 
-    up, down = (pltpu.with_memory_space_constraint(array, pltpu.HBM) for array in (up, down))
-    shapes = [(depth, half), (half, depth)] * 2
-    return call(
-        body,
-        core,
-        [up, down],
+    return call(
+        body,
+        core,
+        [pltpu.with_memory_space_constraint(array, pltpu.HBM) for array in (up, down)],
         [pl.BlockSpec(memory_space=pltpu.HBM)] * 2,
-        [pltpu.VMEM(shape, BF16) for shape in shapes],
-        [pl.BlockSpec(memory_space=pltpu.VMEM)] * 4,
+        half_outs(up),
+        [pl.BlockSpec(memory_space=pltpu.VMEM)] * 2,
         (1,),
-        (0, 4 * depth * full),
+        (0, 2 * up.size),
         "bring",
         (),
-        [pltpu.SemaphoreType.DMA((4 * parts,))],
+        [pltpu.SemaphoreType.DMA((2, 1))],
+    )
+
+
+def bring_and_sum(core, units, side, up, down, after=()):
+    _, rows, depth = units[0].shape
+    tokens = rows * len(units)
+    half = up.shape[1] // 2
+    parts = 3 if half % 384 == 0 else 1
+    size = half // parts
+
+    def body(core_ref, *refs):
+        unit_refs = refs[: len(units)]
+        up_ref, down_ref, out, up_out, down_out, acts, sems = refs[len(units) :]
+        pairs = halves(core_ref, side, up_ref, down_ref, up_out, down_out, sems, parts)
+        for pair in pairs:
+            for copy in pair:
+                copy.start()
+        for n, ref in enumerate(unit_refs):
+            acts[:, n * rows : (n + 1) * rows, :] = ref[...]
+        for part, pair in enumerate(pairs):
+            for copy in pair:
+                copy.wait()
+            here = slice(part * size, (part + 1) * size)
+            out[0, :, here] = contract(acts[0], up_out[:, here], 1, 0)
+            out[1, :, here] = contract(acts[1], down_out[here, :], 1, 1)
+
+    return call(
+        body,
+        core,
+        [*units] + [pltpu.with_memory_space_constraint(array, pltpu.HBM) for array in (up, down)],
+        [whole(units[0].shape)] * len(units) + [pl.BlockSpec(memory_space=pltpu.HBM)] * 2,
+        [jax.ShapeDtypeStruct((2, tokens, half), F32)] + half_outs(up),
+        [whole((2, tokens, half))] + [pl.BlockSpec(memory_space=pltpu.VMEM)] * 2,
+        (1,),
+        (4 * tokens * depth * half, 2 * up.size),
+        "bring_and_sum",
+        after,
+        [pltpu.VMEM((2, tokens, depth), BF16), pltpu.SemaphoreType.DMA((2, parts))],
     )
 
 
@@ -435,16 +472,15 @@
 
     pair = 2 * rows
     pieces = [
-        (0, 0, 0, width),
-        (0, 0, width, width),
+        (0, 0, 0, half),
         (1, 0, 0, half),
         (2, 0, 0, half),
         (2, pair, 0, width),
         (2, pair, width, width),
     ]
     near, keep, far, act, act_near = {}, {}, {}, {}, {}
-    *weights, = bring(core, up, down)
-    ups, downs = weights[0::2], weights[1::2]
+    ups, downs = {}, {}
+    ups[1], downs[1] = bring(core, 1, up, down)
 
     def send(group, after=()):
         out = partial_sums(
@@ -454,9 +490,12 @@
         return [out[0]]
 
     def hold(group, start, size, after):
-        out, = partial_sums(
-            core, groups[group], ups[0], downs[0], 0, False, start, size, after
-        )
+        if group:
+            out, = partial_sums(
+                core, groups[group], ups[0], downs[0], 0, False, start, size, after
+            )
+        else:
+            out, ups[0], downs[0] = bring_and_sum(core, groups[group], 0, up, down, after)
         keep[group, start] = out
         return [out]
 
@@ -488,13 +527,13 @@
 
     def inward(which, start, size, part, order, leave, after):
         acts = [(act[n], act_near[n], offset) for n, offset in which]
-        return back(core, acts, ups, start, size, part, order, leave, after)
+        return back(core, acts, (ups[0], ups[1]), start, size, part, order, leave, after)
 
     outputs = None
 
     def gradients(j, sides, after):
         acts = [
-            [(array[j], 0), (array[2], j * width), (array[3], j * width), (array[4 + j], 0)]
+            [(array[n], j * width) for n in range(3)] + [(array[3 + j], 0)]
             for array in (act, act_near)
         ]
         acts = [acts[side] for side in sides]
@@ -508,42 +547,38 @@
         return [done]
 
     last = send(0)
-    last = hold(0, 0, width, last)
-    last = cross(0) + last
-    last = hold(0, width, width, last + [])
-    last = cross(1, last + [])
-    last = send(1, last + [unit[1, 1], second, first_on])
+    last = hold(0, 0, half, last)
+    last = cross(0, [*last, unit[1, 1], first_on, second])
+    last = send(1, last)
     last = hold(1, 0, half, [*last, second_on])
-    last = ready(0, last)
-    last = ready(1, [*last, unit[2, 1]])
-    last = cross(2, last)
+    last = ready(0, [*last, unit[2, 1]])
+    last = cross(1, last)
     last = send(2, last)
     last = hold(2, 0, half, last)
-    last = ready(2, last)
-    last = cross(3) + last
+    last = ready(1, last)
+    last = cross(2) + last
     inputs_t, cotan = arrange(core, [u for group in groups for u in group], last)
-    part, = inward(((0, 0), (2, 0)), 0, width, None, None, None, [inputs_t])
-    stay1, go1 = inward(((1, 0), (2, width)), width, width, part, (0, 2, 1, 3), 2, [part])
+    stay1, go1 = inward(((0, 0), (1, 0)), 0, half, None, (0, 2, 1, 3), 2, [inputs_t])
     near1 = swap(go1, "gx", 2, 1)
 
-    last = ready(3, [stay1])
-    last = cross(4, last)
+    last = ready(2, [stay1])
+    last = cross(3, last)
     total = fold(core, stay1[:rows], near1[:rows], F32, last)
     back1 = fold(core, stay1[rows:], near1[rows:], BF16, [total])
     far1 = swap(back1, "gz", 4, 1)
-    stay2, go2 = inward(((3, 0),), 0, half, None, (0, 1), 1, [back1])
+    stay2, go2 = inward(((2, 0),), 0, half, None, (0, 1), 1, [back1])
     near2 = swap(go2, "gx", 2, 1)
 
-    last = ready(4, [stay2])
-    last = cross(5, last)
+    last = ready(3, [stay2])
+    last = cross(4, last)
     last = finish(0, (0,), last)
     back2 = fold(core, stay2, near2, BF16, last)
     far2 = swap(back2, "gz", 4, 2)
-    part, = inward(((4, 0),), 0, width, None, None, None, [back2])
+    part, = inward(((3, 0),), 0, width, None, None, None, [back2])
     last = finish(0, (1,), [part])
     total = fold(core, total, far1, F32, last)
-    last = ready(5, [total])
-    stay3, go3 = inward(((5, 0),), width, width, part, (0, 1), 1, last)
+    last = ready(4, [total])
+    stay3, go3 = inward(((4, 0),), width, width, part, (0, 1), 1, last)
     near3 = swap(go3, "gx", 2, 1)
     last = finish(1, (0,), [stay3])
     back3 = fold(core, stay3, near3, BF16, last)

time: 135 us -> 129 us (0.956)
  local copies, waits for them, and re-layouts: 11.3 us -> 0.06 us
  starting transfers between devices: 28.4 us -> 33.4 us
  waiting for transfers between devices: 23.4 us -> 26.9 us
  Pallas kernels: 68.1 us -> 65.1 us
    unnamed x28 -> x0, local copies, waits for them, and re-layouts: 11.2 us -> none
    ppermute x29 -> x27, starting transfers between devices: 24.3 us -> 29.3 us  [swap(): return lax.ppermute(value, axis, [(i, i ^ bits) for i in range(size)])]
    ppermute x1, waiting for transfers between devices: 0.6 us -> 3.7 us  [cube_body(): second_on = lax.ppermute(second, 'gz', outward)]
    pallas_call x33 -> x30, Pallas kernels: 68.1 us -> 65.1 us  [call(): pl.pallas_call(kernel, grid_spec=pltpu.PrefetchScalarGridSpec(num_scalar_...]
    ppermute x29 -> x27, waiting for transfers between devices: 22.8 us -> 23.1 us  [swap(): return lax.ppermute(value, axis, [(i, i ^ bits) for i in range(size)])]
  transfers between devices with their start and end apart: 33 -> 31, of which waited for: 9 -> 9; matrix products, arithmetic and copies ran while one was open for 0% -> 0% of each run, Pallas kernels for 50% -> 50%
where the time goes in v8:
time: 129 us; the launch traced here: 128 us
  Pallas kernels  65.1 us (50%)
  starting transfers between devices  33.4 us (26%)
  waiting for transfers between devices  26.9 us (21%)
  other arithmetic  1.97 us (2%)
    pallas_call x30, Pallas kernels, call(): pl.pallas_call(kernel, grid_spec=pltpu.PrefetchScalarGridSpec(num_scalar_...  65.1 us
    ppermute x27, starting transfers between devices, swap(): return lax.ppermute(value, axis, [(i, i ^ bits) for i in range(size)])  29.3 us
    ppermute x27, waiting for transfers between devices, swap(): return lax.ppermute(value, axis, [(i, i ^ bits) for i in range(size)])  23.1 us
    ppermute x1, waiting for transfers between devices, cube_body(): second_on = lax.ppermute(second, 'gz', outward)  3.7 us
  transfers between devices with their start and end apart: 31, of which 9 were waited for; matrix products, arithmetic and copies ran while one was open for 0% of the time, Pallas kernels for 50%

profile of v8, /device:TPU:0, one launch (start us, length us, event | category | flops | bytes accessed | tf_op | source)
XLA Modules:
  0.0 128.5 jit_solution(2748970947553265075)
XLA Ops:
  0.6 1.0 pad_maximum_fusion.1.refs_1_
  1.6 3.1 %collective-permute-start.3 = (bf16[2,48,1536]{2,1,0:T(8,128)(2,1)S(1)}, bf16[2,48,1536]{2,1,0:T(8,128)(2,1)S(1)}, u32[]{:S(2)}, u32[]{:S(2)}) collective-permute-start(bf16[2,48,1536]{2,1,0:T(8,128)(2,1)S(1)} %pad_maximum_fusion.1.refs_1_), channel_id=1, source_target_pairs={{0,1},{1,0},{2,3},{3,2},{4,5},{5,4},{6,7},{7,6},{8,9},{9,8},{10,11... | collective-permute-start | bytes 884744 | tf_op jit(solution)/shard_map/ppermute | solution.py:444
  4.7 0.7 collective-permute-start.5
  5.4 1.6 %collective-permute-start = (bf16[2,48,1536]{2,1,0:T(8,128)(2,1)S(1)}, bf16[2,48,1536]{2,1,0:T(8,128)(2,1)S(1)}, u32[]{:S(2)}, u32[]{:S(2)}) collective-permute-start(bf16[2,48,1536]{2,1,0:T(8,128)(2,1)S(1)} %pad_maximum_fusion.1.refs_1_), channel_id=1, source_target_pairs={{0,16},{16,0},{1,17},{17,1},{2,18},{18,2},{3,19},{19,3},{4,20},{20... | collective-permute-start | bytes 884744 | tf_op jit(solution)/shard_map/ppermute | solution.py:444
  7.0 4.8 %collective-permute-done.3.refs_1_.refs_3_ = bf16[2,48,1536]{2,1,0:T(8,128)(2,1)S(1)} collective-permute-done((bf16[2,48,1536]{2,1,0:T(8,128)(2,1)S(1)}, bf16[2,48,1536]{2,1,0:T(8,128)(2,1)S(1)}, u32[]{:S(2)}, u32[]{:S(2)}) %collective-permute-start.3) | collective-permute-done | bytes 294944 | tf_op jit(solution)/shard_map/ppermute | solution.py:444
  11.7 0.7 collective-permute-start.7
  12.4 1.3 %collective-permute-start.6 = (bf16[2,48,1536]{2,1,0:T(8,128)(2,1)S(1)}, bf16[2,48,1536]{2,1,0:T(8,128)(2,1)S(1)}, u32[]{:S(2)}, u32[]{:S(2)}) collective-permute-start(bf16[2,48,1536]{2,1,0:T(8,128)(2,1)S(1)} %collective-permute-done.5), channel_id=1, source_target_pairs={{1,0},{2,3},{5,4},{6,7},{9,8},{10,11},{13,12},{14,15},{17,16},{18,... | collective-permute-start | bytes 884744 | tf_op jit(solution)/shard_map/ppermute | solution.py:461
  13.7 3.8 %bring.1 = (bf16[1536,1536]{1,0:T(8,128)(2,1)S(1)}, bf16[1536,1536]{1,0:T(8,128)(2,1)S(1)}) custom-call(s32[1]{0:T(128)} %bitcast.refs_0_, bf16[1536,3072]{1,0:T(8,128)(2,1)} %refs_3_.1, bf16[3072,1536]{1,0:T(8,128)(2,1)} %refs_4_.1), custom_call_target="tpu_custom_call" | custom-call | bytes 9437184 | tf_op jit(solution)/shard_map/bring/pallas_call | solution.py:68
  17.6 3.6 %sums_send.3 = (bf16[96,1536]{1,0:T(8,128)(2,1)S(1)}, bf16[96,1536]{1,0:T(8,128)(2,1)S(1)}) custom-call(s32[1]{0:T(128)} %bitcast.refs_0_, bf16[2,48,1536]{2,1,0:T(8,128)(2,1)S(1)} %pad_maximum_fusion.1.refs_1_, bf16[2,48,1536]{2,1,0:T(8,128)(2,1)S(1)} %collective-permute-done.refs_2_, ...), custom_call_target="tpu_custom_call" | custom-call | flops 905969664 | bytes 9437184 | tf_op jit(solution)/shard_map/sums_send/pallas_call | solution.py:68
  21.1 0.1 collective-permute-start.2
  21.2 0.5 collective-permute-start.1
  21.7 1.7 %collective-permute-start.4 = (bf16[2,48,1536]{2,1,0:T(8,128)(2,1)S(1)}, bf16[2,48,1536]{2,1,0:T(8,128)(2,1)S(1)}, u32[]{:S(2)}, u32[]{:S(2)}) collective-permute-start(bf16[2,48,1536]{2,1,0:T(8,128)(2,1)S(1)} %collective-permute-done.3.refs_1_.refs_3_), channel_id=1, source_target_pairs={{0,16},{16,0},{1,17},{17,1},{2,18},{18,2},{3,19},{19,3},{4,20},{20... | collective-permute-start | bytes 884744 | tf_op jit(solution)/shard_map/ppermute | solution.py:444
  23.4 4.7 %bring_and_sum.1 = (f32[2,96,1536]{2,1,0:T(8,128)S(1)}, bf16[1536,1536]{1,0:T(8,128)(2,1)S(1)}, bf16[1536,1536]{1,0:T(8,128)(2,1)S(1)}) custom-call(s32[1]{0:T(128)} %bitcast.refs_0_, bf16[2,48,1536]{2,1,0:T(8,128)(2,1)S(1)} %pad_maximum_fusion.1.refs_1_, bf16[2,48,1536]{2,1,0:T(8,128)(2,1)S(1)} %collective-permute-done.refs_2_, bf16[1536,3072]{1,0:T(8,128)(2,1)} %refs_3_.1, ...), custom_call_target="tpu_custom_call" | custom-call | flops 905969664 | bytes 9437184 | tf_op jit(solution)/shard_map/bring_and_sum/pallas_call | solution.py:68
  28.1 1.5 %collective-permute-start.9 = (bf16[2,48,1536]{2,1,0:T(8,128)(2,1)S(1)}, bf16[2,48,1536]{2,1,0:T(8,128)(2,1)S(1)}, u32[]{:S(2)}, u32[]{:S(2)}) collective-permute-start(bf16[2,48,1536]{2,1,0:T(8,128)(2,1)S(1)} %collective-permute-done.7.refs_7_), channel_id=1, source_target_pairs={{1,0},{2,3},{5,4},{6,7},{9,8},{10,11},{13,12},{14,15},{17,16},{18,... | collective-permute-start | bytes 884744 | tf_op jit(solution)/shard_map/ppermute | solution.py:462
  29.6 0.4 collective-permute-start.10
  30.1 0.7 collective-permute-done.4.refs_5_.refs_2_.refs_4_
  30.7 0.4 combine.4.refs_5_
  31.1 1.7 %collective-permute-start.8 = (bf16[2,96,1536]{2,1,0:T(8,128)(2,1)S(1)}, bf16[2,96,1536]{2,1,0:T(8,128)(2,1)S(1)}, u32[]{:S(2)}, u32[]{:S(2)}) collective-permute-start(bf16[2,96,1536]{2,1,0:T(8,128)(2,1)S(1)} %combine.4.refs_5_), channel_id=1, source_target_pairs={{0,8},{4,12},{8,0},{12,4},{1,9},{5,13},{9,1},{13,5},{2,10},{6,14},... | collective-permute-start | bytes 1769480 | tf_op jit(solution)/shard_map/ppermute | solution.py:444
  32.9 3.6 %sums_send.4 = (bf16[96,1536]{1,0:T(8,128)(2,1)S(1)}, bf16[96,1536]{1,0:T(8,128)(2,1)S(1)}) custom-call(s32[1]{0:T(128)} %bitcast.refs_0_, bf16[2,48,1536]{2,1,0:T(8,128)(2,1)S(1)} %collective-permute-done.3.refs_1_.refs_3_, bf16[2,48,1536]{2,1,0:T(8,128)(2,1)S(1)} %collective-permute-done.4.refs_5_.refs_2_.refs_4_, ...), custom_call_target="tpu_custom_call" | custom-call | flops 905969664 | bytes 9437184 | tf_op jit(solution)/shard_map/sums_send/pallas_call | solution.py:68
  36.5 0.5 collective-permute-start.11
  37.0 3.7 %collective-permute-done.9.refs_6_ = bf16[2,48,1536]{2,1,0:T(8,128)(2,1)S(1)} collective-permute-done((bf16[2,48,1536]{2,1,0:T(8,128)(2,1)S(1)}, bf16[2,48,1536]{2,1,0:T(8,128)(2,1)S(1)}, u32[]{:S(2)}, u32[]{:S(2)}) %collective-permute-start.9) | collective-permute-done | bytes 294944 | tf_op jit(solution)/shard_map/ppermute | solution.py:462
  40.8 0.6 collective-permute-start.14
  41.4 3.6 %sums_keep.2.refs_5_.refs_1_ = f32[2,96,1536]{2,1,0:T(8,128)S(1)} custom-call(s32[1]{0:T(128)} %bitcast.refs_0_, bf16[2,48,1536]{2,1,0:T(8,128)(2,1)S(1)} %collective-permute-done.3.refs_1_.refs_3_, bf16[2,48,1536]{2,1,0:T(8,128)(2,1)S(1)} %collective-permute-done.4.refs_5_.refs_2_.refs_4_, bf16[1536,1536]{1,0:T(8,128)(2,1)S(1)} %get-tuple-element.38.refs_3_.refs_5_, ...), custom_call_target="tpu_custom_call" | custom-call | flops 905969664 | bytes 9437184 | tf_op jit(solution)/shard_map/sums_keep/pallas_call | solution.py:68
  45.0 0.7 collective-permute-done.8.refs_4_
  45.7 0.8 activations.5.refs_4_.refs_1_.refs_3_
  46.5 0.4 combine.5.refs_7_
  46.9 1.7 %collective-permute-start.13 = (bf16[2,96,1536]{2,1,0:T(8,128)(2,1)S(1)}, bf16[2,96,1536]{2,1,0:T(8,128)(2,1)S(1)}, u32[]{:S(2)}, u32[]{:S(2)}) collective-permute-start(bf16[2,96,1536]{2,1,0:T(8,128)(2,1)S(1)} %combine.5.refs_7_), channel_id=1, source_target_pairs={{0,8},{4,12},{8,0},{12,4},{1,9},{5,13},{9,1},{13,5},{2,10},{6,14},... | collective-permute-start | bytes 1769480 | tf_op jit(solution)/shard_map/ppermute | solution.py:444
  48.7 0.3 collective-permute-done.14.refs_4_.refs_8_
  49.0 3.8 %sums_send.5 = (bf16[192,1536]{1,0:T(8,128)(2,1)S(1)}, bf16[192,1536]{1,0:T(8,128)(2,1)S(1)}) custom-call(s32[1]{0:T(128)} %bitcast.refs_0_, bf16[2,48,1536]{2,1,0:T(8,128)(2,1)S(1)} %broadcast_select_fusion.1.refs_1_.refs_5_, bf16[2,48,1536]{2,1,0:T(8,128)(2,1)S(1)} %collective-permute-done.10.refs_6_.refs_2_, ...), custom_call_target="tpu_custom_call" | custom-call | flops 1811939328 | bytes 9437184 | tf_op jit(solution)/shard_map/sums_send/pallas_call | solution.py:68
  52.9 0.5 collective-permute-start.17
  53.4 0.1 collective-permute-start.15
  53.5 3.9 %sums_keep.3.refs_5_.refs_1_ = f32[2,192,1536]{2,1,0:T(8,128)S(1)} custom-call(s32[1]{0:T(128)} %bitcast.refs_0_, bf16[2,48,1536]{2,1,0:T(8,128)(2,1)S(1)} %broadcast_select_fusion.1.refs_1_.refs_5_, bf16[2,48,1536]{2,1,0:T(8,128)(2,1)S(1)} %collective-permute-done.10.refs_6_.refs_2_, bf16[2,48,1536]{2,1,0:T(8,128)(2,1)S(1)} %broadcast_select_fusion.refs_3_.refs_7_, ...), custom_call_target="tpu_custom_call" | custom-call | flops 1811939328 | bytes 9437184 | tf_op jit(solution)/shard_map/sums_keep/pallas_call | solution.py:68
  57.4 3.2 %collective-permute-done.13.refs_4_ = bf16[2,96,1536]{2,1,0:T(8,128)(2,1)S(1)} collective-permute-done((bf16[2,96,1536]{2,1,0:T(8,128)(2,1)S(1)}, bf16[2,96,1536]{2,1,0:T(8,128)(2,1)S(1)}, u32[]{:S(2)}, u32[]{:S(2)}) %collective-permute-start.13) | collective-permute-done | bytes 589856 | tf_op jit(solution)/shard_map/ppermute | solution.py:444
  60.5 0.8 activations.6.refs_10_.refs_2_.refs_4_
  61.4 0.1 collective-permute-start.16
  61.5 0.1 fusion.4
  61.6 1.7 %collective-permute-start.20 = (bf16[2,96,1536]{2,1,0:T(8,128)(2,1)S(1)}, bf16[2,96,1536]{2,1,0:T(8,128)(2,1)S(1)}, u32[]{:S(2)}, u32[]{:S(2)}) collective-permute-start(bf16[2,96,1536]{2,1,0:T(8,128)(2,1)S(1)} %pad_maximum_fusion.refs_9_), channel_id=1, source_target_pairs={{0,8},{4,12},{8,0},{12,4},{1,9},{5,13},{9,1},{13,5},{2,10},{6,14},... | collective-permute-start | bytes 1769480 | tf_op jit(solution)/shard_map/ppermute | solution.py:444
  63.4 0.4 arrange.1
  63.8 3.6 %back.4 = (f32[96,1536]{1,0:T(8,128)S(1)}, bf16[96,1536]{1,0:T(8,128)(2,1)S(1)}) custom-call(s32[1]{0:T(128)} %bitcast.refs_0_, bf16[2,96,1536]{2,1,0:T(8,128)(2,1)S(1)} %activations.5.refs_4_.refs_1_.refs_3_, bf16[2,96,1536]{2,1,0:T(8,128)(2,1)S(1)} %activations.6.refs_10_.refs_2_.refs_4_, bf16[2,96,1536]{2,1,0:T(8,128)(2,1)S(1)} %collective-permute-done.15.refs_3_, ...), custom_call_target="tpu_custom_call" | custom-call | flops 1811939328 | bytes 10616832 | tf_op jit(solution)/shard_map/back/pallas_call | solution.py:68
  67.4 1.6 %collective-permute-start.19 = (bf16[96,1536]{1,0:T(8,128)(2,1)S(1)}, bf16[96,1536]{1,0:T(8,128)(2,1)S(1)}, u32[]{:S(2)}, u32[]{:S(2)}) collective-permute-start(bf16[96,1536]{1,0:T(8,128)(2,1)S(1)} %get-tuple-element.46), channel_id=1, source_target_pairs={{0,16},{16,0},{1,17},{17,1},{2,18},{18,2},{3,19},{19,3},{4,20},{20... | collective-permute-start | bytes 884744 | tf_op jit(solution)/shard_map/ppermute | solution.py:444
  69.0 8.4 %collective-permute-done.20.refs_4_ = bf16[2,96,1536]{2,1,0:T(8,128)(2,1)S(1)} collective-permute-done((bf16[2,96,1536]{2,1,0:T(8,128)(2,1)S(1)}, bf16[2,96,1536]{2,1,0:T(8,128)(2,1)S(1)}, u32[]{:S(2)}, u32[]{:S(2)}) %collective-permute-start.20) | collective-permute-done | bytes 589856 | tf_op jit(solution)/shard_map/ppermute | solution.py:444
  77.4 0.8 activations.7.refs_4_.refs_1_.refs_5_
  78.4 0.2 combine.6.refs_3_
  78.6 1.7 %collective-permute-start.23 = (bf16[2,96,768]{2,1,0:T(8,128)(2,1)S(1)}, bf16[2,96,768]{2,1,0:T(8,128)(2,1)S(1)}, u32[]{:S(2)}, u32[]{:S(2)}) collective-permute-start(bf16[2,96,768]{2,1,0:T(8,128)(2,1)S(1)} %combine.6.refs_3_), channel_id=1, source_target_pairs={{0,8},{4,12},{8,0},{12,4},{1,9},{5,13},{9,1},{13,5},{2,10},{6,14},... | collective-permute-start | bytes 884744 | tf_op jit(solution)/shard_map/ppermute | solution.py:444
  80.5 3.3 %back.5 = (f32[48,1536]{1,0:T(8,128)S(1)}, bf16[48,1536]{1,0:T(8,128)(2,1)S(1)}) custom-call(s32[1]{0:T(128)} %bitcast.refs_0_, bf16[2,96,1536]{2,1,0:T(8,128)(2,1)S(1)} %activations.7.refs_4_.refs_1_.refs_5_, bf16[2,96,1536]{2,1,0:T(8,128)(2,1)S(1)} %collective-permute-done.22.refs_2_.refs_5_, bf16[1536,1536]{1,0:T(8,128)(2,1)S(1)} %get-tuple-element.38.refs_3_.refs_5_, ...), custom_call_target="tpu_custom_call" | custom-call | flops 905969664 | bytes 10027008 | tf_op jit(solution)/shard_map/back/pallas_call | solution.py:68
  83.8 4.3 %collective-permute-done.23.refs_4_ = bf16[2,96,768]{2,1,0:T(8,128)(2,1)S(1)} collective-permute-done((bf16[2,96,768]{2,1,0:T(8,128)(2,1)S(1)}, bf16[2,96,768]{2,1,0:T(8,128)(2,1)S(1)}, u32[]{:S(2)}, u32[]{:S(2)}) %collective-permute-start.23) | collective-permute-done | bytes 294944 | tf_op jit(solution)/shard_map/ppermute | solution.py:444
  88.1 0.4 activations.8.refs_4_.refs_6_.refs_1_
  88.6 4.6 %collective-permute-start.21 = (bf16[48,1536]{1,0:T(8,128)(2,1)S(1)}, bf16[48,1536]{1,0:T(8,128)(2,1)S(1)}, u32[]{:S(2)}, u32[]{:S(2)}) collective-permute-start(bf16[48,1536]{1,0:T(8,128)(2,1)S(1)} %fold.6.refs_5_), channel_id=1, source_target_pairs={{0,1},{1,0},{2,3},{3,2},{4,5},{5,4},{6,7},{7,6},{8,9},{9,8},{10,11... | collective-permute-start | bytes 442376 | tf_op jit(solution)/shard_map/ppermute | solution.py:444
  93.2 1.5 %collective-permute-start.25 = (bf16[48,1536]{1,0:T(8,128)(2,1)S(1)}, bf16[48,1536]{1,0:T(8,128)(2,1)S(1)}, u32[]{:S(2)}, u32[]{:S(2)}) collective-permute-start(bf16[48,1536]{1,0:T(8,128)(2,1)S(1)} %get-tuple-element.51), channel_id=1, source_target_pairs={{0,16},{16,0},{1,17},{17,1},{2,18},{18,2},{3,19},{19,3},{4,20},{20... | collective-permute-start | bytes 442376 | tf_op jit(solution)/shard_map/ppermute | solution.py:444
  94.7 0.2 combine.7.refs_7_
  94.9 1.6 %collective-permute-start.27 = (bf16[2,96,768]{2,1,0:T(8,128)(2,1)S(1)}, bf16[2,96,768]{2,1,0:T(8,128)(2,1)S(1)}, u32[]{:S(2)}, u32[]{:S(2)}) collective-permute-start(bf16[2,96,768]{2,1,0:T(8,128)(2,1)S(1)} %combine.7.refs_7_), channel_id=1, source_target_pairs={{0,8},{4,12},{8,0},{12,4},{1,9},{5,13},{9,1},{13,5},{2,10},{6,14},... | collective-permute-start | bytes 884744 | tf_op jit(solution)/shard_map/ppermute | solution.py:444
  96.5 5.4 %weight_grads.4 = (f32[1536,3072]{1,0:T(8,128)}, f32[3072,1536]{1,0:T(8,128)}, f32[8,128]{1,0:T(8,128)S(1)}) custom-call(s32[1]{0:T(128)} %bitcast.refs_0_, bf16[1536,384]{1,0:T(8,128)(2,1)S(1)} %get-tuple-element.44.refs_7_.refs_1_, bf16[384,1536]{1,0:T(8,128)(2,1)S(1)} %get-tuple-element.47.refs_2_, ...), custom_call_target="tpu_custom_call" | custom-call | flops 1811939328 | bytes 9437184 | tf_op jit(solution)/shard_map/weight_grads/pallas_call | solution.py:68
  102.0 2.2 %back.6.refs_9_.refs_5_ = f32[96,1536]{1,0:T(8,128)S(1)} custom-call(s32[1]{0:T(128)} %bitcast.refs_0_, bf16[2,96,768]{2,1,0:T(8,128)(2,1)S(1)} %activations.8.refs_4_.refs_6_.refs_1_, bf16[2,96,768]{2,1,0:T(8,128)(2,1)S(1)} %collective-permute-done.24.refs_2_.refs_6_, bf16[1536,1536]{1,0:T(8,128)(2,1)S(1)} %get-tuple-element.38.refs_3_.refs_5_, ...), custom_call_target="tpu_custom_call" | custom-call | flops 452984832 | bytes 5308416 | tf_op jit(solution)/shard_map/back/pallas_call | solution.py:68
  104.2 5.5 %weight_grads.5 = (f32[1536,3072]{1,0:T(8,128)}, f32[3072,1536]{1,0:T(8,128)}, f32[8,128]{1,0:T(8,128)S(1)}) custom-call(s32[1]{0:T(128)} %bitcast.refs_0_, bf16[1536,384]{1,0:T(8,128)(2,1)S(1)} %get-tuple-element.44.refs_7_.refs_1_, bf16[384,1536]{1,0:T(8,128)(2,1)S(1)} %get-tuple-element.47.refs_2_, ...), custom_call_target="tpu_custom_call", output_to_operand_aliasing={{0}: (7, {}), {1}: (8, {})} | custom-call | flops 1811939328 | bytes 9437184 | tf_op jit(solution)/shard_map/weight_grads/pallas_call | solution.py:68
  109.7 0.4 activations.9.refs_1_.refs_6_
  110.1 0.1 collective-permute-start.28
  110.2 0.8 collective-permute-start.26
  111.0 0.7 collective-permute-done.28.refs_2_.refs_6_
  111.8 2.3 %back.7 = (f32[48,1536]{1,0:T(8,128)S(1)}, bf16[48,1536]{1,0:T(8,128)(2,1)S(1)}) custom-call(s32[1]{0:T(128)} %bitcast.refs_0_, bf16[2,96,768]{2,1,0:T(8,128)(2,1)S(1)} %activations.9.refs_1_.refs_6_, bf16[2,96,768]{2,1,0:T(8,128)(2,1)S(1)} %collective-permute-done.28.refs_2_.refs_6_, bf16[1536,1536]{1,0:T(8,128)(2,1)S(1)} %get-tuple-element.38.refs_3_.refs_5_, ...), custom_call_target="tpu_custom_call" | custom-call | flops 452984832 | bytes 5308416 | tf_op jit(solution)/shard_map/back/pallas_call | solution.py:68
  114.1 0.6 collective-permute-start.29
  114.7 5.4 %weight_grads.6 = (f32[1536,3072]{1,0:T(8,128)}, f32[3072,1536]{1,0:T(8,128)}, f32[8,128]{1,0:T(8,128)S(1)}) custom-call(s32[1]{0:T(128)} %bitcast.refs_0_, bf16[1536,384]{1,0:T(8,128)(2,1)S(1)} %get-tuple-element.44.refs_7_.refs_1_, bf16[384,1536]{1,0:T(8,128)(2,1)S(1)} %get-tuple-element.47.refs_2_, ...), custom_call_target="tpu_custom_call", output_to_operand_aliasing={{0}: (7, {}), {1}: (8, {})} | custom-call | flops 1811939328 | bytes 9437184 | tf_op jit(solution)/shard_map/weight_grads/pallas_call | solution.py:68
  120.1 2.2 %collective-permute-start.30 = (bf16[48,1536]{1,0:T(8,128)(2,1)S(1)}, bf16[48,1536]{1,0:T(8,128)(2,1)S(1)}, u32[]{:S(2)}, u32[]{:S(2)}) collective-permute-start(bf16[48,1536]{1,0:T(8,128)(2,1)S(1)} %fold.9.refs_9_), channel_id=1, source_target_pairs={{0,3},{1,2},{2,1},{3,0},{4,7},{5,6},{6,5},{7,4},{8,11},{9,10},{10,... | collective-permute-start | bytes 442376 | tf_op jit(solution)/shard_map/ppermute | solution.py:444
  122.3 5.4 %weight_grads.7 = (f32[1536,3072]{1,0:T(8,128)}, f32[3072,1536]{1,0:T(8,128)}, f32[8,128]{1,0:T(8,128)}) custom-call(s32[1]{0:T(128)} %bitcast.refs_0_, bf16[1536,384]{1,0:T(8,128)(2,1)S(1)} %get-tuple-element.44.refs_7_.refs_1_, bf16[384,1536]{1,0:T(8,128)(2,1)S(1)} %get-tuple-element.47.refs_2_, ...), custom_call_target="tpu_custom_call", output_to_operand_aliasing={{0}: (7, {}), {1}: (8, {})} | custom-call | flops 1811939328 | bytes 9437184 | tf_op jit(solution)/shard_map/weight_grads/pallas_call | solution.py:68
  127.7 0.7 add_convert_fusion
  (36 shorter events, 0.7 us)
Async XLA Ops:
  1.6 10.1 %collective-permute-start.3 = (bf16[2,48,1536]{2,1,0:T(8,128)(2,1)S(1)}, bf16[2,48,1536]{2,1,0:T(8,128)(2,1)S(1)}, u32[]{:S(2)}, u32[]{:S(2)}) collective-permute-start(bf16[2,48,1536]{2,1,0:T(8,128)(2,1)S(1)} %pad_maximum_fusion.1.refs_1_), channel_id=1, source_target_pairs={{0,1},{1,0},{2,3},{3,2},{4,5},{5,4},{6,7},{7,6},{8,9},{9,8},{10,11... | collective-permute-start | bytes 884744 | tf_op jit(solution)/shard_map/ppermute | solution.py:444
  4.7 7.7 %collective-permute-start.5 = (bf16[2,48,1536]{2,1,0:T(8,128)(2,1)S(1)}, bf16[2,48,1536]{2,1,0:T(8,128)(2,1)S(1)}, u32[]{:S(2)}, u32[]{:S(2)}) collective-permute-start(bf16[2,48,1536]{2,1,0:T(8,128)(2,1)S(1)} %pad_maximum_fusion.1.refs_1_), channel_id=1, source_target_pairs={{1,2},{2,1},{5,6},{6,5},{9,10},{10,9},{13,14},{14,13},{17,18},{18,... | collective-permute-start | bytes 884744 | tf_op jit(solution)/shard_map/ppermute | solution.py:459
  5.4 12.1 %collective-permute-start = (bf16[2,48,1536]{2,1,0:T(8,128)(2,1)S(1)}, bf16[2,48,1536]{2,1,0:T(8,128)(2,1)S(1)}, u32[]{:S(2)}, u32[]{:S(2)}) collective-permute-start(bf16[2,48,1536]{2,1,0:T(8,128)(2,1)S(1)} %pad_maximum_fusion.1.refs_1_), channel_id=1, source_target_pairs={{0,16},{16,0},{1,17},{17,1},{2,18},{18,2},{3,19},{19,3},{4,20},{20... | collective-permute-start | bytes 884744 | tf_op jit(solution)/shard_map/ppermute | solution.py:444
  11.7 16.3 %collective-permute-start.7 = (bf16[2,48,1536]{2,1,0:T(8,128)(2,1)S(1)}, bf16[2,48,1536]{2,1,0:T(8,128)(2,1)S(1)}, u32[]{:S(2)}, u32[]{:S(2)}) collective-permute-start(bf16[2,48,1536]{2,1,0:T(8,128)(2,1)S(1)} %collective-permute-done.3.refs_1_.refs_3_), channel_id=1, source_target_pairs={{1,2},{2,1},{5,6},{6,5},{9,10},{10,9},{13,14},{14,13},{17,18},{18,... | collective-permute-start | bytes 884744 | tf_op jit(solution)/shard_map/ppermute | solution.py:460
  12.4 17.1 %collective-permute-start.6 = (bf16[2,48,1536]{2,1,0:T(8,128)(2,1)S(1)}, bf16[2,48,1536]{2,1,0:T(8,128)(2,1)S(1)}, u32[]{:S(2)}, u32[]{:S(2)}) collective-permute-start(bf16[2,48,1536]{2,1,0:T(8,128)(2,1)S(1)} %collective-permute-done.5), channel_id=1, source_target_pairs={{1,0},{2,3},{5,4},{6,7},{9,8},{10,11},{13,12},{14,15},{17,16},{18,... | collective-permute-start | bytes 884744 | tf_op jit(solution)/shard_map/ppermute | solution.py:461
  21.1 9.6 %collective-permute-start.2 = (bf16[96,1536]{1,0:T(8,128)(2,1)S(1)}, bf16[96,1536]{1,0:T(8,128)(2,1)S(1)}, u32[]{:S(2)}, u32[]{:S(2)}) collective-permute-start(bf16[96,1536]{1,0:T(8,128)(2,1)S(1)} %get-tuple-element.37), channel_id=1, source_target_pairs={{0,4},{4,0},{8,12},{12,8},{1,5},{5,1},{9,13},{13,9},{2,6},{6,2},{1... | collective-permute-start | bytes 884744 | tf_op jit(solution)/shard_map/ppermute | solution.py:444
  21.2 9.5 %collective-permute-start.1 = (bf16[96,1536]{1,0:T(8,128)(2,1)S(1)}, bf16[96,1536]{1,0:T(8,128)(2,1)S(1)}, u32[]{:S(2)}, u32[]{:S(2)}) collective-permute-start(bf16[96,1536]{1,0:T(8,128)(2,1)S(1)} %get-tuple-element.35.refs_5_), channel_id=1, source_target_pairs={{0,4},{4,0},{8,12},{12,8},{1,5},{5,1},{9,13},{13,9},{2,6},{6,2},{1... | collective-permute-start | bytes 884744 | tf_op jit(solution)/shard_map/ppermute | solution.py:444
  21.7 9.0 %collective-permute-start.4 = (bf16[2,48,1536]{2,1,0:T(8,128)(2,1)S(1)}, bf16[2,48,1536]{2,1,0:T(8,128)(2,1)S(1)}, u32[]{:S(2)}, u32[]{:S(2)}) collective-permute-start(bf16[2,48,1536]{2,1,0:T(8,128)(2,1)S(1)} %collective-permute-done.3.refs_1_.refs_3_), channel_id=1, source_target_pairs={{0,16},{16,0},{1,17},{17,1},{2,18},{18,2},{3,19},{19,3},{4,20},{20... | collective-permute-start | bytes 884744 | tf_op jit(solution)/shard_map/ppermute | solution.py:444
  28.1 12.6 %collective-permute-start.9 = (bf16[2,48,1536]{2,1,0:T(8,128)(2,1)S(1)}, bf16[2,48,1536]{2,1,0:T(8,128)(2,1)S(1)}, u32[]{:S(2)}, u32[]{:S(2)}) collective-permute-start(bf16[2,48,1536]{2,1,0:T(8,128)(2,1)S(1)} %collective-permute-done.7.refs_7_), channel_id=1, source_target_pairs={{1,0},{2,3},{5,4},{6,7},{9,8},{10,11},{13,12},{14,15},{17,16},{18,... | collective-permute-start | bytes 884744 | tf_op jit(solution)/shard_map/ppermute | solution.py:462
  29.6 15.3 %collective-permute-start.10 = (bf16[2,48,1536]{2,1,0:T(8,128)(2,1)S(1)}, bf16[2,48,1536]{2,1,0:T(8,128)(2,1)S(1)}, u32[]{:S(2)}, u32[]{:S(2)}) collective-permute-start(bf16[2,48,1536]{2,1,0:T(8,128)(2,1)S(1)} %broadcast_select_fusion.1.refs_1_.refs_5_), channel_id=1, source_target_pairs={{0,16},{16,0},{1,17},{17,1},{2,18},{18,2},{3,19},{19,3},{4,20},{20... | collective-permute-start | bytes 884744 | tf_op jit(solution)/shard_map/ppermute | solution.py:444
  31.1 14.5 %collective-permute-start.8 = (bf16[2,96,1536]{2,1,0:T(8,128)(2,1)S(1)}, bf16[2,96,1536]{2,1,0:T(8,128)(2,1)S(1)}, u32[]{:S(2)}, u32[]{:S(2)}) collective-permute-start(bf16[2,96,1536]{2,1,0:T(8,128)(2,1)S(1)} %combine.4.refs_5_), channel_id=1, source_target_pairs={{0,8},{4,12},{8,0},{12,4},{1,9},{5,13},{9,1},{13,5},{2,10},{6,14},... | collective-permute-start | bytes 1769480 | tf_op jit(solution)/shard_map/ppermute | solution.py:444
  36.5 10.0 %collective-permute-start.12 = (bf16[96,1536]{1,0:T(8,128)(2,1)S(1)}, bf16[96,1536]{1,0:T(8,128)(2,1)S(1)}, u32[]{:S(2)}, u32[]{:S(2)}) collective-permute-start(bf16[96,1536]{1,0:T(8,128)(2,1)S(1)} %get-tuple-element.41), channel_id=1, source_target_pairs={{0,4},{4,0},{8,12},{12,8},{1,5},{5,1},{9,13},{13,9},{2,6},{6,2},{1... | collective-permute-start | bytes 884744 | tf_op jit(solution)/shard_map/ppermute | solution.py:444
  36.5 10.0 %collective-permute-start.11 = (bf16[96,1536]{1,0:T(8,128)(2,1)S(1)}, bf16[96,1536]{1,0:T(8,128)(2,1)S(1)}, u32[]{:S(2)}, u32[]{:S(2)}) collective-permute-start(bf16[96,1536]{1,0:T(8,128)(2,1)S(1)} %get-tuple-element.40.refs_5_), channel_id=1, source_target_pairs={{0,4},{4,0},{8,12},{12,8},{1,5},{5,1},{9,13},{13,9},{2,6},{6,2},{1... | collective-permute-start | bytes 884744 | tf_op jit(solution)/shard_map/ppermute | solution.py:444
  40.8 8.2 %collective-permute-start.14 = (bf16[2,48,1536]{2,1,0:T(8,128)(2,1)S(1)}, bf16[2,48,1536]{2,1,0:T(8,128)(2,1)S(1)}, u32[]{:S(2)}, u32[]{:S(2)}) collective-permute-start(bf16[2,48,1536]{2,1,0:T(8,128)(2,1)S(1)} %broadcast_select_fusion.refs_3_.refs_7_), channel_id=1, source_target_pairs={{0,16},{16,0},{1,17},{17,1},{2,18},{18,2},{3,19},{19,3},{4,20},{20... | collective-permute-start | bytes 884744 | tf_op jit(solution)/shard_map/ppermute | solution.py:444
  46.9 13.6 %collective-permute-start.13 = (bf16[2,96,1536]{2,1,0:T(8,128)(2,1)S(1)}, bf16[2,96,1536]{2,1,0:T(8,128)(2,1)S(1)}, u32[]{:S(2)}, u32[]{:S(2)}) collective-permute-start(bf16[2,96,1536]{2,1,0:T(8,128)(2,1)S(1)} %combine.5.refs_7_), channel_id=1, source_target_pairs={{0,8},{4,12},{8,0},{12,4},{1,9},{5,13},{9,1},{13,5},{2,10},{6,14},... | collective-permute-start | bytes 1769480 | tf_op jit(solution)/shard_map/ppermute | solution.py:444
  52.9 8.6 %collective-permute-start.18 = (bf16[192,1536]{1,0:T(8,128)(2,1)S(1)}, bf16[192,1536]{1,0:T(8,128)(2,1)S(1)}, u32[]{:S(2)}, u32[]{:S(2)}) collective-permute-start(bf16[192,1536]{1,0:T(8,128)(2,1)S(1)} %get-tuple-element.43), channel_id=1, source_target_pairs={{0,4},{4,0},{8,12},{12,8},{1,5},{5,1},{9,13},{13,9},{2,6},{6,2},{1... | collective-permute-start | bytes 1769480 | tf_op jit(solution)/shard_map/ppermute | solution.py:444
  52.9 8.5 %collective-permute-start.17 = (bf16[192,1536]{1,0:T(8,128)(2,1)S(1)}, bf16[192,1536]{1,0:T(8,128)(2,1)S(1)}, u32[]{:S(2)}, u32[]{:S(2)}) collective-permute-start(bf16[192,1536]{1,0:T(8,128)(2,1)S(1)} %get-tuple-element.42.refs_7_), channel_id=1, source_target_pairs={{0,4},{4,0},{8,12},{12,8},{1,5},{5,1},{9,13},{13,9},{2,6},{6,2},{1... | collective-permute-start | bytes 1769480 | tf_op jit(solution)/shard_map/ppermute | solution.py:444
  53.4 10.4 %collective-permute-start.15 = (bf16[2,96,1536]{2,1,0:T(8,128)(2,1)S(1)}, bf16[2,96,1536]{2,1,0:T(8,128)(2,1)S(1)}, u32[]{:S(2)}, u32[]{:S(2)}) collective-permute-start(bf16[2,96,1536]{2,1,0:T(8,128)(2,1)S(1)} %activations.5.refs_4_.refs_1_.refs_3_), channel_id=1, source_target_pairs={{0,4},{4,0},{8,12},{12,8},{1,5},{5,1},{9,13},{13,9},{2,6},{6,2},{1... | collective-permute-start | bytes 1769480 | tf_op jit(solution)/shard_map/ppermute | solution.py:444
  61.4 2.5 %collective-permute-start.16 = (bf16[2,96,1536]{2,1,0:T(8,128)(2,1)S(1)}, bf16[2,96,1536]{2,1,0:T(8,128)(2,1)S(1)}, u32[]{:S(2)}, u32[]{:S(2)}) collective-permute-start(bf16[2,96,1536]{2,1,0:T(8,128)(2,1)S(1)} %activations.6.refs_10_.refs_2_.refs_4_), channel_id=1, source_target_pairs={{0,4},{4,0},{8,12},{12,8},{1,5},{5,1},{9,13},{13,9},{2,6},{6,2},{1... | collective-permute-start | bytes 1769480 | tf_op jit(solution)/shard_map/ppermute | solution.py:444
  61.6 15.8 %collective-permute-start.20 = (bf16[2,96,1536]{2,1,0:T(8,128)(2,1)S(1)}, bf16[2,96,1536]{2,1,0:T(8,128)(2,1)S(1)}, u32[]{:S(2)}, u32[]{:S(2)}) collective-permute-start(bf16[2,96,1536]{2,1,0:T(8,128)(2,1)S(1)} %pad_maximum_fusion.refs_9_), channel_id=1, source_target_pairs={{0,8},{4,12},{8,0},{12,4},{1,9},{5,13},{9,1},{13,5},{2,10},{6,14},... | collective-permute-start | bytes 1769480 | tf_op jit(solution)/shard_map/ppermute | solution.py:444
  67.4 12.9 %collective-permute-start.19 = (bf16[96,1536]{1,0:T(8,128)(2,1)S(1)}, bf16[96,1536]{1,0:T(8,128)(2,1)S(1)}, u32[]{:S(2)}, u32[]{:S(2)}) collective-permute-start(bf16[96,1536]{1,0:T(8,128)(2,1)S(1)} %get-tuple-element.46), channel_id=1, source_target_pairs={{0,16},{16,0},{1,17},{17,1},{2,18},{18,2},{3,19},{19,3},{4,20},{20... | collective-permute-start | bytes 884744 | tf_op jit(solution)/shard_map/ppermute | solution.py:444
  78.2 2.2 %collective-permute-start.22 = (bf16[2,96,1536]{2,1,0:T(8,128)(2,1)S(1)}, bf16[2,96,1536]{2,1,0:T(8,128)(2,1)S(1)}, u32[]{:S(2)}, u32[]{:S(2)}) collective-permute-start(bf16[2,96,1536]{2,1,0:T(8,128)(2,1)S(1)} %activations.7.refs_4_.refs_1_.refs_5_), channel_id=1, source_target_pairs={{0,4},{4,0},{8,12},{12,8},{1,5},{5,1},{9,13},{13,9},{2,6},{6,2},{1... | collective-permute-start | bytes 1769480 | tf_op jit(solution)/shard_map/ppermute | solution.py:444
  78.6 9.5 %collective-permute-start.23 = (bf16[2,96,768]{2,1,0:T(8,128)(2,1)S(1)}, bf16[2,96,768]{2,1,0:T(8,128)(2,1)S(1)}, u32[]{:S(2)}, u32[]{:S(2)}) collective-permute-start(bf16[2,96,768]{2,1,0:T(8,128)(2,1)S(1)} %combine.6.refs_3_), channel_id=1, source_target_pairs={{0,8},{4,12},{8,0},{12,4},{1,9},{5,13},{9,1},{13,5},{2,10},{6,14},... | collective-permute-start | bytes 884744 | tf_op jit(solution)/shard_map/ppermute | solution.py:444
  88.5 13.5 %collective-permute-start.24 = (bf16[2,96,768]{2,1,0:T(8,128)(2,1)S(1)}, bf16[2,96,768]{2,1,0:T(8,128)(2,1)S(1)}, u32[]{:S(2)}, u32[]{:S(2)}) collective-permute-start(bf16[2,96,768]{2,1,0:T(8,128)(2,1)S(1)} %activations.8.refs_4_.refs_6_.refs_1_), channel_id=1, source_target_pairs={{0,4},{4,0},{8,12},{12,8},{1,5},{5,1},{9,13},{13,9},{2,6},{6,2},{1... | collective-permute-start | bytes 884744 | tf_op jit(solution)/shard_map/ppermute | solution.py:444
  88.6 21.1 %collective-permute-start.21 = (bf16[48,1536]{1,0:T(8,128)(2,1)S(1)}, bf16[48,1536]{1,0:T(8,128)(2,1)S(1)}, u32[]{:S(2)}, u32[]{:S(2)}) collective-permute-start(bf16[48,1536]{1,0:T(8,128)(2,1)S(1)} %fold.6.refs_5_), channel_id=1, source_target_pairs={{0,1},{1,0},{2,3},{3,2},{4,5},{5,4},{6,7},{7,6},{8,9},{9,8},{10,11... | collective-permute-start | bytes 442376 | tf_op jit(solution)/shard_map/ppermute | solution.py:444
  93.2 8.7 %collective-permute-start.25 = (bf16[48,1536]{1,0:T(8,128)(2,1)S(1)}, bf16[48,1536]{1,0:T(8,128)(2,1)S(1)}, u32[]{:S(2)}, u32[]{:S(2)}) collective-permute-start(bf16[48,1536]{1,0:T(8,128)(2,1)S(1)} %get-tuple-element.51), channel_id=1, source_target_pairs={{0,16},{16,0},{1,17},{17,1},{2,18},{18,2},{3,19},{19,3},{4,20},{20... | collective-permute-start | bytes 442376 | tf_op jit(solution)/shard_map/ppermute | solution.py:444
  94.9 14.8 %collective-permute-start.27 = (bf16[2,96,768]{2,1,0:T(8,128)(2,1)S(1)}, bf16[2,96,768]{2,1,0:T(8,128)(2,1)S(1)}, u32[]{:S(2)}, u32[]{:S(2)}) collective-permute-start(bf16[2,96,768]{2,1,0:T(8,128)(2,1)S(1)} %combine.7.refs_7_), channel_id=1, source_target_pairs={{0,8},{4,12},{8,0},{12,4},{1,9},{5,13},{9,1},{13,5},{2,10},{6,14},... | collective-permute-start | bytes 884744 | tf_op jit(solution)/shard_map/ppermute | solution.py:444
  110.1 1.6 %collective-permute-start.28 = (bf16[2,96,768]{2,1,0:T(8,128)(2,1)S(1)}, bf16[2,96,768]{2,1,0:T(8,128)(2,1)S(1)}, u32[]{:S(2)}, u32[]{:S(2)}) collective-permute-start(bf16[2,96,768]{2,1,0:T(8,128)(2,1)S(1)} %activations.9.refs_1_.refs_6_), channel_id=1, source_target_pairs={{0,4},{4,0},{8,12},{12,8},{1,5},{5,1},{9,13},{13,9},{2,6},{6,2},{1... | collective-permute-start | bytes 884744 | tf_op jit(solution)/shard_map/ppermute | solution.py:444
  110.2 17.5 %collective-permute-start.26 = (bf16[48,1536]{1,0:T(8,128)(2,1)S(1)}, bf16[48,1536]{1,0:T(8,128)(2,1)S(1)}, u32[]{:S(2)}, u32[]{:S(2)}) collective-permute-start(bf16[48,1536]{1,0:T(8,128)(2,1)S(1)} %fold.7.refs_5_), channel_id=1, source_target_pairs={{0,2},{1,3},{2,0},{3,1},{4,6},{5,7},{6,4},{7,5},{8,10},{9,11},{10,... | collective-permute-start | bytes 442376 | tf_op jit(solution)/shard_map/ppermute | solution.py:444
  114.1 6.0 %collective-permute-start.29 = (bf16[48,1536]{1,0:T(8,128)(2,1)S(1)}, bf16[48,1536]{1,0:T(8,128)(2,1)S(1)}, u32[]{:S(2)}, u32[]{:S(2)}) collective-permute-start(bf16[48,1536]{1,0:T(8,128)(2,1)S(1)} %get-tuple-element.55), channel_id=1, source_target_pairs={{0,16},{16,0},{1,17},{17,1},{2,18},{18,2},{3,19},{19,3},{4,20},{20... | collective-permute-start | bytes 442376 | tf_op jit(solution)/shard_map/ppermute | solution.py:444
  120.1 7.6 %collective-permute-start.30 = (bf16[48,1536]{1,0:T(8,128)(2,1)S(1)}, bf16[48,1536]{1,0:T(8,128)(2,1)S(1)}, u32[]{:S(2)}, u32[]{:S(2)}) collective-permute-start(bf16[48,1536]{1,0:T(8,128)(2,1)S(1)} %fold.9.refs_9_), channel_id=1, source_target_pairs={{0,3},{1,2},{2,1},{3,0},{4,7},{5,6},{6,5},{7,4},{8,11},{9,10},{10,... | collective-permute-start | bytes 442376 | tf_op jit(solution)/shard_map/ppermute | solution.py:444

commit v9 on v8

--- a/solution.py
+++ b/solution.py
@@ -280,7 +280,7 @@
     )
 
 
-def back(core, acts, ups, start, width, before, order, leave, after=()):
+def back(core, acts, ups, start, width, before, row, order, leave, after=()):
     tokens = sum(which[0].shape[1] for which in acts)
     depth = ups[0].shape[0]
     tile = tile_of(depth, 512)
@@ -320,7 +320,7 @@
             for array, first in zip(operands, firsts)
         ]
         + [pl.BlockSpec((tile, width), lambda i, c: (i, start // width))] * 2
-        + ([] if before is None else [pl.BlockSpec((tokens, tile), lambda i, c: (0, i))]),
+        + ([] if before is None else [pl.BlockSpec((tokens, tile), lambda i, c: (row // tokens, i))]),
         [jax.ShapeDtypeStruct((rows, depth), dtype) for rows, dtype in kinds],
         [pl.BlockSpec((rows, tile), lambda i, c: (0, i)) for rows, _ in kinds],
         (depth // tile,),
@@ -457,6 +457,8 @@
     middle = (z == 1) | (z == 2)
     across, outward = [(1, 2), (2, 1)], [(1, 0), (2, 3)]
     first = lax.ppermute(unit[0, 0], "gz", across)
+    ups, downs = {}, {}
+    ups[1], downs[1] = bring(core, 1, up, down)
     second = lax.ppermute(unit[1, 0], "gz", across)
     first_on = lax.ppermute(first, "gz", outward)
     second_on = lax.ppermute(second, "gz", outward)
@@ -472,15 +474,13 @@
 
     pair = 2 * rows
     pieces = [
-        (0, 0, 0, half),
-        (1, 0, 0, half),
-        (2, 0, 0, half),
-        (2, pair, 0, width),
-        (2, pair, width, width),
+        (0, 0, pair, 0, half),
+        (1, 0, pair, 0, half),
+        (2, 0, 2 * pair, 0, width),
+        (2, 0, pair, width, width),
+        (2, pair, pair, width, width),
     ]
     near, keep, far, act, act_near = {}, {}, {}, {}, {}
-    ups, downs = {}, {}
-    ups[1], downs[1] = bring(core, 1, up, down)
 
     def send(group, after=()):
         out = partial_sums(
@@ -503,15 +503,15 @@
         return (keep[group, start], 0) if (group, start) in keep else (keep[group, 0], start)
 
     def cross(n, after=()):
-        group, row, start, size = pieces[n]
+        group, row, count, start, size = pieces[n]
         array, column = kept(group, start)
         if after:
-            chip = combine(core, array, near[group], row, pair, column, start, size, after)
+            chip = combine(core, array, near[group], row, count, column, start, size, after)
         else:
             chip = jnp.stack([
                 (
-                    array[which, row : row + pair, column : column + size]
-                    + near[group][which][row : row + pair, start : start + size].astype(F32)
+                    array[which, row : row + count, column : column + size]
+                    + near[group][which][row : row + count, start : start + size].astype(F32)
                 ).astype(BF16)
                 for which in range(2)
             ])
@@ -519,21 +519,22 @@
         return [chip]
 
     def ready(n, after):
-        group, row, start, _ = pieces[n]
+        group, row, _, start, _ = pieces[n]
         array, column = kept(group, start)
         act[n] = activations(core, array, near[group], far[n], row, column, start, after)
         act_near[n] = swap(act[n], "gy", 4, 1)
         return [act[n]]
 
-    def inward(which, start, size, part, order, leave, after):
+    def inward(which, start, size, part, row, order, leave, after):
         acts = [(act[n], act_near[n], offset) for n, offset in which]
-        return back(core, acts, (ups[0], ups[1]), start, size, part, order, leave, after)
+        return back(core, acts, (ups[0], ups[1]), start, size, part, row, order, leave, after)
 
     outputs = None
 
     def gradients(j, sides, after):
         acts = [
-            [(array[n], j * width) for n in range(3)] + [(array[3 + j], 0)]
+            [(array[n], j * width) for n in range(2)]
+            + ([(array[3], 0), (array[4], 0)] if j else [(array[2], 0)])
             for array in (act, act_near)
         ]
         acts = [acts[side] for side in sides]
@@ -548,8 +549,8 @@
 
     last = send(0)
     last = hold(0, 0, half, last)
-    last = cross(0, [*last, unit[1, 1], first_on, second])
-    last = send(1, last)
+    last = cross(0, [*last, unit[1, 1]])
+    last = send(1, [*last, first_on, second])
     last = hold(1, 0, half, [*last, second_on])
     last = ready(0, [*last, unit[2, 1]])
     last = cross(1, last)
@@ -558,29 +559,28 @@
     last = ready(1, last)
     last = cross(2) + last
     inputs_t, cotan = arrange(core, [u for group in groups for u in group], last)
-    stay1, go1 = inward(((0, 0), (1, 0)), 0, half, None, (0, 2, 1, 3), 2, [inputs_t])
+    stay1, go1 = inward(((0, 0), (1, 0)), 0, half, None, 0, (0, 2, 1, 3), 2, [inputs_t])
     near1 = swap(go1, "gx", 2, 1)
 
     last = ready(2, [stay1])
     last = cross(3, last)
+    last = finish(0, (0,), last)
+    last = ready(3, last)
+    last = cross(4, last)
     total = fold(core, stay1[:rows], near1[:rows], F32, last)
     back1 = fold(core, stay1[rows:], near1[rows:], BF16, [total])
     far1 = swap(back1, "gz", 4, 1)
-    stay2, go2 = inward(((2, 0),), 0, half, None, (0, 1), 1, [back1])
+    part, = inward(((2, 0),), 0, width, None, 0, None, None, [back1])
+    last = finish(0, (1,), [part])
+    stay2, go2 = inward(((3, 0),), width, width, part, 0, (0, 1), 1, last)
     near2 = swap(go2, "gx", 2, 1)
-
-    last = ready(3, [stay2])
-    last = cross(4, last)
-    last = finish(0, (0,), last)
-    back2 = fold(core, stay2, near2, BF16, last)
+    total = fold(core, total, far1, F32, [stay2])
+    last = ready(4, [total])
+    stay3, go3 = inward(((4, 0),), width, width, part, pair, (0, 1), 1, last)
+    near3 = swap(go3, "gx", 2, 1)
+    back2 = fold(core, stay2, near2, BF16, [stay3])
     far2 = swap(back2, "gz", 4, 2)
-    part, = inward(((3, 0),), 0, width, None, None, None, [back2])
-    last = finish(0, (1,), [part])
-    total = fold(core, total, far1, F32, last)
-    last = ready(4, [total])
-    stay3, go3 = inward(((4, 0),), width, width, part, (0, 1), 1, last)
-    near3 = swap(go3, "gx", 2, 1)
-    last = finish(1, (0,), [stay3])
+    last = finish(1, (0,), [back2])
     back3 = fold(core, stay3, near3, BF16, last)
     far3 = swap(back3, "gz", 4, 3)
     finish(1, (1,), [back3])

time: 129 us -> 122 us (0.946)
  waiting for transfers between devices: 26.9 us -> 20 us
  local copies, waits for them, and re-layouts: 0.06 us -> 2.43 us
  starting transfers between devices: 33.4 us -> 32 us
    ppermute x27, waiting for transfers between devices: 23.1 us -> 17.5 us  [swap(): return lax.ppermute(value, axis, [(i, i ^ bits) for i in range(size)])]
    ppermute x1, waiting for transfers between devices: 3.7 us -> 0.24 us  [cube_body(): second_on = lax.ppermute(second, 'gz', outward)]
    unnamed x0 -> x14, local copies, waits for them, and re-layouts: none -> 2.37 us
    ppermute x1, waiting for transfers between devices: 0.01 us -> 2.27 us  [cube_body(): first_on = lax.ppermute(first, 'gz', outward)]
    ppermute x27, starting transfers between devices: 29.3 us -> 27.2 us  [swap(): return lax.ppermute(value, axis, [(i, i ^ bits) for i in range(size)])]
  transfers between devices with their start and end apart: 31 -> 31, of which waited for: 9 -> 10; matrix products, arithmetic and copies ran while one was open for 0% -> 0% of each run, Pallas kernels for 50% -> 52%
where the time goes in v9:
time: 122 us
  Pallas kernels  64.3 us (53%)
  starting transfers between devices  32 us (26%)
  waiting for transfers between devices  20 us (16%)
  local copies, waits for them, and re-layouts  2.43 us (2%)
  other arithmetic  2.04 us (2%)
    pallas_call x30, Pallas kernels, call(): pl.pallas_call(kernel, grid_spec=pltpu.PrefetchScalarGridSpec(num_scalar_...  64.3 us
    ppermute x27, starting transfers between devices, swap(): return lax.ppermute(value, axis, [(i, i ^ bits) for i in range(size)])  27.2 us
    ppermute x27, waiting for transfers between devices, swap(): return lax.ppermute(value, axis, [(i, i ^ bits) for i in range(size)])  17.5 us
  transfers between devices with their start and end apart: 31, of which 10 were waited for; matrix products, arithmetic and copies ran while one was open for 0% of the time, Pallas kernels for 52%

profile of v9, /device:TPU:0, one launch (start us, length us, event | category | flops | bytes accessed | tf_op | source)
XLA Modules:
  0.0 121.9 jit_solution(10930874535916159722)
XLA Ops:
  0.6 1.0 pad_maximum_fusion.1.refs_1_
  1.6 3.0 %collective-permute-start = (bf16[2,48,1536]{2,1,0:T(8,128)(2,1)S(1)}, bf16[2,48,1536]{2,1,0:T(8,128)(2,1)S(1)}, u32[]{:S(2)}, u32[]{:S(2)}) collective-permute-start(bf16[2,48,1536]{2,1,0:T(8,128)(2,1)S(1)} %pad_maximum_fusion.1.refs_1_), channel_id=1, source_target_pairs={{0,16},{16,0},{1,17},{17,1},{2,18},{18,2},{3,19},{19,3},{4,20},{20... | collective-permute-start | bytes 884744 | tf_op jit(solution)/shard_map/ppermute | solution.py:444
  4.6 1.6 %collective-permute-start.3 = (bf16[2,48,1536]{2,1,0:T(8,128)(2,1)S(1)}, bf16[2,48,1536]{2,1,0:T(8,128)(2,1)S(1)}, u32[]{:S(2)}, u32[]{:S(2)}) collective-permute-start(bf16[2,48,1536]{2,1,0:T(8,128)(2,1)S(1)} %pad_maximum_fusion.1.refs_1_), channel_id=1, source_target_pairs={{0,1},{1,0},{2,3},{3,2},{4,5},{5,4},{6,7},{7,6},{8,9},{9,8},{10,11... | collective-permute-start | bytes 884744 | tf_op jit(solution)/shard_map/ppermute | solution.py:444
  6.2 1.4 %collective-permute-start.6 = (bf16[2,48,1536]{2,1,0:T(8,128)(2,1)S(1)}, bf16[2,48,1536]{2,1,0:T(8,128)(2,1)}, u32[]{:S(2)}, u32[]{:S(2)}) collective-permute-start(bf16[2,48,1536]{2,1,0:T(8,128)(2,1)S(1)} %pad_maximum_fusion.1.refs_1_), channel_id=1, source_target_pairs={{1,2},{2,1},{5,6},{6,5},{9,10},{10,9},{13,14},{14,13},{17,18},{18,... | collective-permute-start | bytes 884744 | tf_op jit(solution)/shard_map/ppermute | solution.py:459
  7.6 3.8 %bring.1 = (bf16[1536,1536]{1,0:T(8,128)(2,1)S(1)}, bf16[1536,1536]{1,0:T(8,128)(2,1)S(1)}) custom-call(s32[1]{0:T(128)} %bitcast.refs_0_, bf16[1536,3072]{1,0:T(8,128)(2,1)} %refs_3_.1, bf16[3072,1536]{1,0:T(8,128)(2,1)} %refs_4_.1), custom_call_target="tpu_custom_call" | custom-call | bytes 9437184 | tf_op jit(solution)/shard_map/bring/pallas_call | solution.py:68
  11.4 0.2 collective-permute-done.refs_2_
  11.7 3.6 %sums_send.3 = (bf16[96,1536]{1,0:T(8,128)(2,1)S(1)}, bf16[96,1536]{1,0:T(8,128)(2,1)S(1)}) custom-call(s32[1]{0:T(128)} %bitcast.refs_0_, bf16[2,48,1536]{2,1,0:T(8,128)(2,1)S(1)} %pad_maximum_fusion.1.refs_1_, bf16[2,48,1536]{2,1,0:T(8,128)(2,1)S(1)} %collective-permute-done.refs_2_, ...), custom_call_target="tpu_custom_call" | custom-call | flops 905969664 | bytes 9437184 | tf_op jit(solution)/shard_map/sums_send/pallas_call | solution.py:68
  15.2 0.1 collective-permute-start.1
  15.3 0.5 collective-permute-start.2
  15.8 1.7 %collective-permute-start.4 = (bf16[2,48,1536]{2,1,0:T(8,128)(2,1)S(1)}, bf16[2,48,1536]{2,1,0:T(8,128)(2,1)S(1)}, u32[]{:S(2)}, u32[]{:S(2)}) collective-permute-start(bf16[2,48,1536]{2,1,0:T(8,128)(2,1)S(1)} %collective-permute-done.3.refs_1_.refs_3_), channel_id=1, source_target_pairs={{0,16},{16,0},{1,17},{17,1},{2,18},{18,2},{3,19},{19,3},{4,20},{20... | collective-permute-start | bytes 884744 | tf_op jit(solution)/shard_map/ppermute | solution.py:444
  17.6 0.7 collective-permute-start.8
  18.3 1.3 %collective-permute-start.7 = (bf16[2,48,1536]{2,1,0:T(8,128)(2,1)}, bf16[2,48,1536]{2,1,0:T(8,128)(2,1)S(1)}, u32[]{:S(2)}, u32[]{:S(2)}) collective-permute-start(bf16[2,48,1536]{2,1,0:T(8,128)(2,1)} %collective-permute-done.6), channel_id=1, source_target_pairs={{1,0},{2,3},{5,4},{6,7},{9,8},{10,11},{13,12},{14,15},{17,16},{18,... | collective-permute-start | bytes 884744 | tf_op jit(solution)/shard_map/ppermute | solution.py:463
  19.6 4.8 %bring_and_sum.1 = (f32[2,96,1536]{2,1,0:T(8,128)S(1)}, bf16[1536,1536]{1,0:T(8,128)(2,1)S(1)}, bf16[1536,1536]{1,0:T(8,128)(2,1)S(1)}) custom-call(s32[1]{0:T(128)} %bitcast.refs_0_, bf16[2,48,1536]{2,1,0:T(8,128)(2,1)S(1)} %pad_maximum_fusion.1.refs_1_, bf16[2,48,1536]{2,1,0:T(8,128)(2,1)S(1)} %collective-permute-done.refs_2_, bf16[1536,3072]{1,0:T(8,128)(2,1)} %refs_3_.1, ...), custom_call_target="tpu_custom_call" | custom-call | flops 905969664 | bytes 9437184 | tf_op jit(solution)/shard_map/bring_and_sum/pallas_call | solution.py:68
  24.5 0.4 collective-permute-done.4.refs_5_.refs_2_.refs_4_
  24.8 0.4 combine.4.refs_5_
  25.2 1.8 %collective-permute-start.5 = (bf16[2,96,1536]{2,1,0:T(8,128)(2,1)S(1)}, bf16[2,96,1536]{2,1,0:T(8,128)(2,1)S(1)}, u32[]{:S(2)}, u32[]{:S(2)}) collective-permute-start(bf16[2,96,1536]{2,1,0:T(8,128)(2,1)S(1)} %combine.4.refs_5_), channel_id=1, source_target_pairs={{0,8},{4,12},{8,0},{12,4},{1,9},{5,13},{9,1},{13,5},{2,10},{6,14},... | collective-permute-start | bytes 1769480 | tf_op jit(solution)/shard_map/ppermute | solution.py:444
  27.1 1.5 %collective-permute-start.9 = (bf16[2,48,1536]{2,1,0:T(8,128)(2,1)S(1)}, bf16[2,48,1536]{2,1,0:T(8,128)(2,1)S(1)}, u32[]{:S(2)}, u32[]{:S(2)}) collective-permute-start(bf16[2,48,1536]{2,1,0:T(8,128)(2,1)S(1)} %collective-permute-done.8.refs_7_), channel_id=1, source_target_pairs={{1,0},{2,3},{5,4},{6,7},{9,8},{10,11},{13,12},{14,15},{17,16},{18,... | collective-permute-start | bytes 884744 | tf_op jit(solution)/shard_map/ppermute | solution.py:464
  28.5 2.3 %collective-permute-done.7.refs_6_ = bf16[2,48,1536]{2,1,0:T(8,128)(2,1)S(1)} collective-permute-done((bf16[2,48,1536]{2,1,0:T(8,128)(2,1)}, bf16[2,48,1536]{2,1,0:T(8,128)(2,1)S(1)}, u32[]{:S(2)}, u32[]{:S(2)}) %collective-permute-start.7) | collective-permute-done | bytes 294944 | tf_op jit(solution)/shard_map/ppermute | solution.py:463
  30.8 1.0 collective-permute-start.10
  31.8 2.3 %copy-done.2 = bf16[1536,1536]{1,0:T(8,128)(2,1)S(1)} copy-done((bf16[1536,1536]{1,0:T(8,128)(2,1)S(1)}, bf16[1536,1536]{1,0:T(8,128)(2,1)}, u32[]{:S(2)}) %copy-start.2) | copy-done | bytes 4718616
  34.2 3.6 %sums_send.4 = (bf16[96,1536]{1,0:T(8,128)(2,1)S(1)}, bf16[96,1536]{1,0:T(8,128)(2,1)S(1)}) custom-call(s32[1]{0:T(128)} %bitcast.refs_0_, bf16[2,48,1536]{2,1,0:T(8,128)(2,1)S(1)} %collective-permute-done.3.refs_1_.refs_3_, bf16[2,48,1536]{2,1,0:T(8,128)(2,1)S(1)} %collective-permute-done.4.refs_5_.refs_2_.refs_4_, bf16[1536,1536]{1,0:T(8,128)(2,1)S(1)} %bitcast.24, ...), custom_call_target="tpu_custom_call" | custom-call | flops 905969664 | bytes 9437184 | tf_op jit(solution)/shard_map/sums_send/pallas_call | solution.py:68
  37.8 0.5 collective-permute-start.12
  38.3 0.2 collective-permute-done.9.refs_6_
  38.6 1.0 collective-permute-start.14
  39.6 3.6 %sums_keep.2.refs_5_.refs_1_ = f32[2,96,1536]{2,1,0:T(8,128)S(1)} custom-call(s32[1]{0:T(128)} %bitcast.refs_0_, bf16[2,48,1536]{2,1,0:T(8,128)(2,1)S(1)} %collective-permute-done.3.refs_1_.refs_3_, bf16[2,48,1536]{2,1,0:T(8,128)(2,1)S(1)} %collective-permute-done.4.refs_5_.refs_2_.refs_4_, bf16[1536,1536]{1,0:T(8,128)(2,1)S(1)} %get-tuple-element.38.refs_3_.refs_5_, ...), custom_call_target="tpu_custom_call" | custom-call | flops 905969664 | bytes 9437184 | tf_op jit(solution)/shard_map/sums_keep/pallas_call | solution.py:68
  43.2 0.8 activations.5.refs_4_.refs_1_.refs_3_
  44.1 0.4 combine.5.refs_7_
  44.5 1.5 %collective-permute-start.13 = (bf16[2,96,1536]{2,1,0:T(8,128)(2,1)S(1)}, bf16[2,96,1536]{2,1,0:T(8,128)(2,1)S(1)}, u32[]{:S(2)}, u32[]{:S(2)}) collective-permute-start(bf16[2,96,1536]{2,1,0:T(8,128)(2,1)S(1)} %combine.5.refs_7_), channel_id=1, source_target_pairs={{0,8},{4,12},{8,0},{12,4},{1,9},{5,13},{9,1},{13,5},{2,10},{6,14},... | collective-permute-start | bytes 1769480 | tf_op jit(solution)/shard_map/ppermute | solution.py:444
  46.0 1.4 %collective-permute-done.14.refs_4_.refs_8_ = bf16[2,48,1536]{2,1,0:T(8,128)(2,1)S(1)} collective-permute-done((bf16[2,48,1536]{2,1,0:T(8,128)(2,1)S(1)}, bf16[2,48,1536]{2,1,0:T(8,128)(2,1)S(1)}, u32[]{:S(2)}, u32[]{:S(2)}) %collective-permute-start.14) | collective-permute-done | bytes 294944 | tf_op jit(solution)/shard_map/ppermute | solution.py:444
  47.4 3.8 %sums_send.5 = (bf16[192,1536]{1,0:T(8,128)(2,1)S(1)}, bf16[192,1536]{1,0:T(8,128)(2,1)S(1)}) custom-call(s32[1]{0:T(128)} %bitcast.refs_0_, bf16[2,48,1536]{2,1,0:T(8,128)(2,1)S(1)} %broadcast_select_fusion.1.refs_1_.refs_5_, bf16[2,48,1536]{2,1,0:T(8,128)(2,1)S(1)} %collective-permute-done.10.refs_6_.refs_2_, ...), custom_call_target="tpu_custom_call" | custom-call | flops 1811939328 | bytes 9437184 | tf_op jit(solution)/shard_map/sums_send/pallas_call | solution.py:68
  51.3 0.1 collective-permute-start.17
  51.4 0.5 collective-permute-start.18
  51.9 0.1 collective-permute-start.15
  51.9 3.9 %sums_keep.3.refs_5_.refs_1_ = f32[2,192,1536]{2,1,0:T(8,128)S(1)} custom-call(s32[1]{0:T(128)} %bitcast.refs_0_, bf16[2,48,1536]{2,1,0:T(8,128)(2,1)S(1)} %broadcast_select_fusion.1.refs_1_.refs_5_, bf16[2,48,1536]{2,1,0:T(8,128)(2,1)S(1)} %collective-permute-done.10.refs_6_.refs_2_, bf16[2,48,1536]{2,1,0:T(8,128)(2,1)S(1)} %broadcast_select_fusion.refs_3_.refs_7_, ...), custom_call_target="tpu_custom_call" | custom-call | flops 1811939328 | bytes 9437184 | tf_op jit(solution)/shard_map/sums_keep/pallas_call | solution.py:68
  55.8 3.7 %collective-permute-done.13.refs_4_ = bf16[2,96,1536]{2,1,0:T(8,128)(2,1)S(1)} collective-permute-done((bf16[2,96,1536]{2,1,0:T(8,128)(2,1)S(1)}, bf16[2,96,1536]{2,1,0:T(8,128)(2,1)S(1)}, u32[]{:S(2)}, u32[]{:S(2)}) %collective-permute-start.13) | collective-permute-done | bytes 589856 | tf_op jit(solution)/shard_map/ppermute | solution.py:444
  59.5 0.8 activations.6.refs_10_.refs_2_.refs_4_
  60.4 0.2 fusion.4
  60.7 1.6 %collective-permute-start.20 = (bf16[2,192,768]{2,1,0:T(8,128)(2,1)S(1)}, bf16[2,192,768]{2,1,0:T(8,128)(2,1)S(1)}, u32[]{:S(2)}, u32[]{:S(2)}) collective-permute-start(bf16[2,192,768]{2,1,0:T(8,128)(2,1)S(1)} %pad_maximum_fusion.refs_9_), channel_id=1, source_target_pairs={{0,8},{4,12},{8,0},{12,4},{1,9},{5,13},{9,1},{13,5},{2,10},{6,14},... | collective-permute-start | bytes 1769480 | tf_op jit(solution)/shard_map/ppermute | solution.py:444
  62.3 0.4 arrange.1
  62.7 3.6 %back.4 = (f32[96,1536]{1,0:T(8,128)S(1)}, bf16[96,1536]{1,0:T(8,128)(2,1)S(1)}) custom-call(s32[1]{0:T(128)} %bitcast.refs_0_, bf16[2,96,1536]{2,1,0:T(8,128)(2,1)S(1)} %activations.5.refs_4_.refs_1_.refs_3_, bf16[2,96,1536]{2,1,0:T(8,128)(2,1)S(1)} %activations.6.refs_10_.refs_2_.refs_4_, bf16[2,96,1536]{2,1,0:T(8,128)(2,1)S(1)} %collective-permute-done.15.refs_3_, ...), custom_call_target="tpu_custom_call" | custom-call | flops 1811939328 | bytes 10616832 | tf_op jit(solution)/shard_map/back/pallas_call | solution.py:68
  66.3 10.2 %collective-permute-done.20.refs_4_ = bf16[2,192,768]{2,1,0:T(8,128)(2,1)S(1)} collective-permute-done((bf16[2,192,768]{2,1,0:T(8,128)(2,1)S(1)}, bf16[2,192,768]{2,1,0:T(8,128)(2,1)S(1)}, u32[]{:S(2)}, u32[]{:S(2)}) %collective-permute-start.20) | collective-permute-done | bytes 589856 | tf_op jit(solution)/shard_map/ppermute | solution.py:444
  76.5 0.7 activations.7.refs_4_.refs_5_.refs_1_
  77.2 0.2 combine.6.refs_6_
  77.4 1.6 %collective-permute-start.21 = (bf16[2,96,768]{2,1,0:T(8,128)(2,1)S(1)}, bf16[2,96,768]{2,1,0:T(8,128)(2,1)S(1)}, u32[]{:S(2)}, u32[]{:S(2)}) collective-permute-start(bf16[2,96,768]{2,1,0:T(8,128)(2,1)S(1)} %combine.6.refs_6_), channel_id=1, source_target_pairs={{0,8},{4,12},{8,0},{12,4},{1,9},{5,13},{9,1},{13,5},{2,10},{6,14},... | collective-permute-start | bytes 884744 | tf_op jit(solution)/shard_map/ppermute | solution.py:444
  79.0 0.9 collective-permute-start.19
  80.1 5.4 %weight_grads.4 = (f32[1536,3072]{1,0:T(8,128)}, f32[3072,1536]{1,0:T(8,128)}, f32[8,128]{1,0:T(8,128)S(1)}) custom-call(s32[1]{0:T(128)} %bitcast.refs_0_, bf16[1536,384]{1,0:T(8,128)(2,1)S(1)} %get-tuple-element.44.refs_7_.refs_1_, bf16[384,1536]{1,0:T(8,128)(2,1)S(1)} %get-tuple-element.47.refs_2_, ...), custom_call_target="tpu_custom_call" | custom-call | flops 1811939328 | bytes 9437184 | tf_op jit(solution)/shard_map/weight_grads/pallas_call | solution.py:68
  85.5 0.6 collective-permute-done.21.refs_4_
  86.1 0.4 activations.8.refs_4_.refs_1_.refs_5_
  86.6 0.2 combine.7.refs_3_
  86.9 1.6 %collective-permute-start.26 = (bf16[2,96,768]{2,1,0:T(8,128)(2,1)S(1)}, bf16[2,96,768]{2,1,0:T(8,128)(2,1)S(1)}, u32[]{:S(2)}, u32[]{:S(2)}) collective-permute-start(bf16[2,96,768]{2,1,0:T(8,128)(2,1)S(1)} %combine.7.refs_3_), channel_id=1, source_target_pairs={{0,8},{4,12},{8,0},{12,4},{1,9},{5,13},{9,1},{13,5},{2,10},{6,14},... | collective-permute-start | bytes 884744 | tf_op jit(solution)/shard_map/ppermute | solution.py:444
  88.6 2.2 %collective-permute-start.22 = (bf16[48,1536]{1,0:T(8,128)(2,1)S(1)}, bf16[48,1536]{1,0:T(8,128)(2,1)S(1)}, u32[]{:S(2)}, u32[]{:S(2)}) collective-permute-start(bf16[48,1536]{1,0:T(8,128)(2,1)S(1)} %fold.6.refs_5_), channel_id=1, source_target_pairs={{0,1},{1,0},{2,3},{3,2},{4,5},{5,4},{6,7},{7,6},{8,9},{9,8},{10,11... | collective-permute-start | bytes 442376 | tf_op jit(solution)/shard_map/ppermute | solution.py:444
  90.7 2.4 %back.5.refs_8_.refs_5_ = f32[192,1536]{1,0:T(8,128)S(1)} custom-call(s32[1]{0:T(128)} %bitcast.refs_0_, bf16[2,192,768]{2,1,0:T(8,128)(2,1)S(1)} %activations.7.refs_4_.refs_5_.refs_1_, bf16[2,192,768]{2,1,0:T(8,128)(2,1)S(1)} %collective-permute-done.24.refs_2_.refs_5_, bf16[1536,1536]{1,0:T(8,128)(2,1)S(1)} %get-tuple-element.38.refs_3_.refs_5_, ...), custom_call_target="tpu_custom_call" | custom-call | flops 905969664 | bytes 5898240 | tf_op jit(solution)/shard_map/back/pallas_call | solution.py:68
  93.1 5.4 %weight_grads.5 = (f32[1536,3072]{1,0:T(8,128)}, f32[3072,1536]{1,0:T(8,128)}, f32[8,128]{1,0:T(8,128)S(1)}) custom-call(s32[1]{0:T(128)} %bitcast.refs_0_, bf16[1536,384]{1,0:T(8,128)(2,1)S(1)} %get-tuple-element.44.refs_7_.refs_1_, bf16[384,1536]{1,0:T(8,128)(2,1)S(1)} %get-tuple-element.47.refs_2_, ...), custom_call_target="tpu_custom_call", output_to_operand_aliasing={{0}: (6, {}), {1}: (7, {})} | custom-call | flops 1811939328 | bytes 9437184 | tf_op jit(solution)/shard_map/weight_grads/pallas_call | solution.py:68
  98.6 2.3 %back.6 = (f32[48,1536]{1,0:T(8,128)S(1)}, bf16[48,1536]{1,0:T(8,128)(2,1)S(1)}) custom-call(s32[1]{0:T(128)} %bitcast.refs_0_, bf16[2,96,768]{2,1,0:T(8,128)(2,1)S(1)} %activations.8.refs_4_.refs_1_.refs_5_, bf16[2,96,768]{2,1,0:T(8,128)(2,1)S(1)} %collective-permute-done.23.refs_2_.refs_5_, bf16[1536,1536]{1,0:T(8,128)(2,1)S(1)} %get-tuple-element.38.refs_3_.refs_5_, ...), custom_call_target="tpu_custom_call" | custom-call | flops 452984832 | bytes 5308416 | tf_op jit(solution)/shard_map/back/pallas_call | solution.py:68
  100.9 0.4 activations.9.refs_1_.refs_6_
  101.4 1.6 %collective-permute-start.25 = (bf16[48,1536]{1,0:T(8,128)(2,1)S(1)}, bf16[48,1536]{1,0:T(8,128)(2,1)S(1)}, u32[]{:S(2)}, u32[]{:S(2)}) collective-permute-start(bf16[48,1536]{1,0:T(8,128)(2,1)S(1)} %get-tuple-element.53), channel_id=1, source_target_pairs={{0,16},{16,0},{1,17},{17,1},{2,18},{18,2},{3,19},{19,3},{4,20},{20... | collective-permute-start | bytes 442376 | tf_op jit(solution)/shard_map/ppermute | solution.py:444
  103.0 2.3 %back.7 = (f32[48,1536]{1,0:T(8,128)S(1)}, bf16[48,1536]{1,0:T(8,128)(2,1)S(1)}) custom-call(s32[1]{0:T(128)} %bitcast.refs_0_, bf16[2,96,768]{2,1,0:T(8,128)(2,1)S(1)} %activations.9.refs_1_.refs_6_, bf16[2,96,768]{2,1,0:T(8,128)(2,1)S(1)} %collective-permute-done.27.refs_2_.refs_6_, bf16[1536,1536]{1,0:T(8,128)(2,1)S(1)} %get-tuple-element.38.refs_3_.refs_5_, ...), custom_call_target="tpu_custom_call" | custom-call | flops 452984832 | bytes 5308416 | tf_op jit(solution)/shard_map/back/pallas_call | solution.py:68
  105.3 1.6 %collective-permute-start.29 = (bf16[48,1536]{1,0:T(8,128)(2,1)S(1)}, bf16[48,1536]{1,0:T(8,128)(2,1)S(1)}, u32[]{:S(2)}, u32[]{:S(2)}) collective-permute-start(bf16[48,1536]{1,0:T(8,128)(2,1)S(1)} %get-tuple-element.55), channel_id=1, source_target_pairs={{0,16},{16,0},{1,17},{17,1},{2,18},{18,2},{3,19},{19,3},{4,20},{20... | collective-permute-start | bytes 442376 | tf_op jit(solution)/shard_map/ppermute | solution.py:444
  106.8 0.9 collective-permute-done.25.refs_2_
  107.7 0.9 collective-permute-start.28
  108.6 5.4 %weight_grads.6 = (f32[1536,3072]{1,0:T(8,128)}, f32[3072,1536]{1,0:T(8,128)}, f32[8,128]{1,0:T(8,128)S(1)}) custom-call(s32[1]{0:T(128)} %bitcast.refs_0_, bf16[1536,384]{1,0:T(8,128)(2,1)S(1)} %get-tuple-element.44.refs_7_.refs_1_, bf16[384,1536]{1,0:T(8,128)(2,1)S(1)} %get-tuple-element.47.refs_2_, ...), custom_call_target="tpu_custom_call", output_to_operand_aliasing={{0}: (7, {}), {1}: (8, {})} | custom-call | flops 1811939328 | bytes 9437184 | tf_op jit(solution)/shard_map/weight_grads/pallas_call | solution.py:68
  114.1 1.6 %collective-permute-start.30 = (bf16[48,1536]{1,0:T(8,128)(2,1)S(1)}, bf16[48,1536]{1,0:T(8,128)(2,1)S(1)}, u32[]{:S(2)}, u32[]{:S(2)}) collective-permute-start(bf16[48,1536]{1,0:T(8,128)(2,1)S(1)} %fold.9.refs_9_), channel_id=1, source_target_pairs={{0,3},{1,2},{2,1},{3,0},{4,7},{5,6},{6,5},{7,4},{8,11},{9,10},{10,... | collective-permute-start | bytes 442376 | tf_op jit(solution)/shard_map/ppermute | solution.py:444
  115.7 5.4 %weight_grads.7 = (f32[1536,3072]{1,0:T(8,128)}, f32[3072,1536]{1,0:T(8,128)}, f32[8,128]{1,0:T(8,128)}) custom-call(s32[1]{0:T(128)} %bitcast.refs_0_, bf16[1536,384]{1,0:T(8,128)(2,1)S(1)} %get-tuple-element.44.refs_7_.refs_1_, bf16[384,1536]{1,0:T(8,128)(2,1)S(1)} %get-tuple-element.47.refs_2_, ...), custom_call_target="tpu_custom_call", output_to_operand_aliasing={{0}: (7, {}), {1}: (8, {})} | custom-call | flops 1811939328 | bytes 9437184 | tf_op jit(solution)/shard_map/weight_grads/pallas_call | solution.py:68
  121.2 0.7 add_convert_fusion
  (52 shorter events, 0.9 us)
Async XLA Ops:
  1.6 10.0 %collective-permute-start = (bf16[2,48,1536]{2,1,0:T(8,128)(2,1)S(1)}, bf16[2,48,1536]{2,1,0:T(8,128)(2,1)S(1)}, u32[]{:S(2)}, u32[]{:S(2)}) collective-permute-start(bf16[2,48,1536]{2,1,0:T(8,128)(2,1)S(1)} %pad_maximum_fusion.1.refs_1_), channel_id=1, source_target_pairs={{0,16},{16,0},{1,17},{17,1},{2,18},{18,2},{3,19},{19,3},{4,20},{20... | collective-permute-start | bytes 884744 | tf_op jit(solution)/shard_map/ppermute | solution.py:444
  4.6 11.2 %collective-permute-start.3 = (bf16[2,48,1536]{2,1,0:T(8,128)(2,1)S(1)}, bf16[2,48,1536]{2,1,0:T(8,128)(2,1)S(1)}, u32[]{:S(2)}, u32[]{:S(2)}) collective-permute-start(bf16[2,48,1536]{2,1,0:T(8,128)(2,1)S(1)} %pad_maximum_fusion.1.refs_1_), channel_id=1, source_target_pairs={{0,1},{1,0},{2,3},{3,2},{4,5},{5,4},{6,7},{7,6},{8,9},{9,8},{10,11... | collective-permute-start | bytes 884744 | tf_op jit(solution)/shard_map/ppermute | solution.py:444
  6.2 12.0 %collective-permute-start.6 = (bf16[2,48,1536]{2,1,0:T(8,128)(2,1)S(1)}, bf16[2,48,1536]{2,1,0:T(8,128)(2,1)}, u32[]{:S(2)}, u32[]{:S(2)}) collective-permute-start(bf16[2,48,1536]{2,1,0:T(8,128)(2,1)S(1)} %pad_maximum_fusion.1.refs_1_), channel_id=1, source_target_pairs={{1,2},{2,1},{5,6},{6,5},{9,10},{10,9},{13,14},{14,13},{17,18},{18,... | collective-permute-start | bytes 884744 | tf_op jit(solution)/shard_map/ppermute | solution.py:459
  11.4 3.8 %copy-start = (bf16[1536,1536]{1,0:T(8,128)(2,1)}, bf16[1536,1536]{1,0:T(8,128)(2,1)S(1)}, u32[]{:S(2)}) copy-start(bf16[1536,1536]{1,0:T(8,128)(2,1)S(1)} %get-tuple-element.33.refs_3_.refs_5_.refs_6_.refs_4_) | copy-start | bytes 14155780
  11.4 3.8 %copy-start.1 = (bf16[1536,1536]{1,0:T(8,128)(2,1)}, bf16[1536,1536]{1,0:T(8,128)(2,1)S(1)}, u32[]{:S(2)}) copy-start(bf16[1536,1536]{1,0:T(8,128)(2,1)S(1)} %get-tuple-element.34.refs_4_.refs_6_) | copy-start | bytes 14155780
  15.2 9.2 %collective-permute-start.1 = (bf16[96,1536]{1,0:T(8,128)(2,1)S(1)}, bf16[96,1536]{1,0:T(8,128)(2,1)S(1)}, u32[]{:S(2)}, u32[]{:S(2)}) collective-permute-start(bf16[96,1536]{1,0:T(8,128)(2,1)S(1)} %get-tuple-element.35.refs_5_), channel_id=1, source_target_pairs={{0,4},{4,0},{8,12},{12,8},{1,5},{5,1},{9,13},{13,9},{2,6},{6,2},{1... | collective-permute-start | bytes 884744 | tf_op jit(solution)/shard_map/ppermute | solution.py:444
  15.3 9.1 %collective-permute-start.2 = (bf16[96,1536]{1,0:T(8,128)(2,1)S(1)}, bf16[96,1536]{1,0:T(8,128)(2,1)S(1)}, u32[]{:S(2)}, u32[]{:S(2)}) collective-permute-start(bf16[96,1536]{1,0:T(8,128)(2,1)S(1)} %get-tuple-element.37), channel_id=1, source_target_pairs={{0,4},{4,0},{8,12},{12,8},{1,5},{5,1},{9,13},{13,9},{2,6},{6,2},{1... | collective-permute-start | bytes 884744 | tf_op jit(solution)/shard_map/ppermute | solution.py:444
  15.8 9.0 %collective-permute-start.4 = (bf16[2,48,1536]{2,1,0:T(8,128)(2,1)S(1)}, bf16[2,48,1536]{2,1,0:T(8,128)(2,1)S(1)}, u32[]{:S(2)}, u32[]{:S(2)}) collective-permute-start(bf16[2,48,1536]{2,1,0:T(8,128)(2,1)S(1)} %collective-permute-done.3.refs_1_.refs_3_), channel_id=1, source_target_pairs={{0,16},{16,0},{1,17},{17,1},{2,18},{18,2},{3,19},{19,3},{4,20},{20... | collective-permute-start | bytes 884744 | tf_op jit(solution)/shard_map/ppermute | solution.py:444
  17.6 9.5 %collective-permute-start.8 = (bf16[2,48,1536]{2,1,0:T(8,128)(2,1)S(1)}, bf16[2,48,1536]{2,1,0:T(8,128)(2,1)S(1)}, u32[]{:S(2)}, u32[]{:S(2)}) collective-permute-start(bf16[2,48,1536]{2,1,0:T(8,128)(2,1)S(1)} %collective-permute-done.3.refs_1_.refs_3_), channel_id=1, source_target_pairs={{1,2},{2,1},{5,6},{6,5},{9,10},{10,9},{13,14},{14,13},{17,18},{18,... | collective-permute-start | bytes 884744 | tf_op jit(solution)/shard_map/ppermute | solution.py:462
  18.3 12.6 %collective-permute-start.7 = (bf16[2,48,1536]{2,1,0:T(8,128)(2,1)}, bf16[2,48,1536]{2,1,0:T(8,128)(2,1)S(1)}, u32[]{:S(2)}, u32[]{:S(2)}) collective-permute-start(bf16[2,48,1536]{2,1,0:T(8,128)(2,1)} %collective-permute-done.6), channel_id=1, source_target_pairs={{1,0},{2,3},{5,4},{6,7},{9,8},{10,11},{13,12},{14,15},{17,16},{18,... | collective-permute-start | bytes 884744 | tf_op jit(solution)/shard_map/ppermute | solution.py:463
  19.6 12.3 %slice-start = ((s8[4718592]{0:T(1024)(128)(4,1)}), s8[524288]{0:T(1024)(128)(4,1)S(1)}, s32[]{:S(2)}) async-start(s8[4718592]{0:T(1024)(128)(4,1)} %bitcast.23), calls=%async_computation | async-start | bytes 1048576
  19.6 12.3 %slice-start.1 = ((s8[4718592]{0:T(1024)(128)(4,1)}), s8[4194304]{0:T(1024)(128)(4,1)S(1)}, s32[]{:S(2)}) async-start(s8[4718592]{0:T(1024)(128)(4,1)} %bitcast.23), calls=%async_computation.1 | async-start | bytes 8388608
  25.2 18.0 %collective-permute-start.5 = (bf16[2,96,1536]{2,1,0:T(8,128)(2,1)S(1)}, bf16[2,96,1536]{2,1,0:T(8,128)(2,1)S(1)}, u32[]{:S(2)}, u32[]{:S(2)}) collective-permute-start(bf16[2,96,1536]{2,1,0:T(8,128)(2,1)S(1)} %combine.4.refs_5_), channel_id=1, source_target_pairs={{0,8},{4,12},{8,0},{12,4},{1,9},{5,13},{9,1},{13,5},{2,10},{6,14},... | collective-permute-start | bytes 1769480 | tf_op jit(solution)/shard_map/ppermute | solution.py:444
  27.1 11.5 %collective-permute-start.9 = (bf16[2,48,1536]{2,1,0:T(8,128)(2,1)S(1)}, bf16[2,48,1536]{2,1,0:T(8,128)(2,1)S(1)}, u32[]{:S(2)}, u32[]{:S(2)}) collective-permute-start(bf16[2,48,1536]{2,1,0:T(8,128)(2,1)S(1)} %collective-permute-done.8.refs_7_), channel_id=1, source_target_pairs={{1,0},{2,3},{5,4},{6,7},{9,8},{10,11},{13,12},{14,15},{17,16},{18,... | collective-permute-start | bytes 884744 | tf_op jit(solution)/shard_map/ppermute | solution.py:464
  30.8 12.3 %collective-permute-start.10 = (bf16[2,48,1536]{2,1,0:T(8,128)(2,1)S(1)}, bf16[2,48,1536]{2,1,0:T(8,128)(2,1)S(1)}, u32[]{:S(2)}, u32[]{:S(2)}) collective-permute-start(bf16[2,48,1536]{2,1,0:T(8,128)(2,1)S(1)} %broadcast_select_fusion.1.refs_1_.refs_5_), channel_id=1, source_target_pairs={{0,16},{16,0},{1,17},{17,1},{2,18},{18,2},{3,19},{19,3},{4,20},{20... | collective-permute-start | bytes 884744 | tf_op jit(solution)/shard_map/ppermute | solution.py:444
  31.8 2.3 %copy-start.2 = (bf16[1536,1536]{1,0:T(8,128)(2,1)S(1)}, bf16[1536,1536]{1,0:T(8,128)(2,1)}, u32[]{:S(2)}) copy-start(bf16[1536,1536]{1,0:T(8,128)(2,1)} %copy-done.1) | copy-start | bytes 14155780
  37.7 6.3 %collective-permute-start.11 = (bf16[96,1536]{1,0:T(8,128)(2,1)S(1)}, bf16[96,1536]{1,0:T(8,128)(2,1)S(1)}, u32[]{:S(2)}, u32[]{:S(2)}) collective-permute-start(bf16[96,1536]{1,0:T(8,128)(2,1)S(1)} %get-tuple-element.40.refs_5_), channel_id=1, source_target_pairs={{0,4},{4,0},{8,12},{12,8},{1,5},{5,1},{9,13},{13,9},{2,6},{6,2},{1... | collective-permute-start | bytes 884744 | tf_op jit(solution)/shard_map/ppermute | solution.py:444
  37.8 6.2 %collective-permute-start.12 = (bf16[96,1536]{1,0:T(8,128)(2,1)S(1)}, bf16[96,1536]{1,0:T(8,128)(2,1)S(1)}, u32[]{:S(2)}, u32[]{:S(2)}) collective-permute-start(bf16[96,1536]{1,0:T(8,128)(2,1)S(1)} %get-tuple-element.41), channel_id=1, source_target_pairs={{0,4},{4,0},{8,12},{12,8},{1,5},{5,1},{9,13},{13,9},{2,6},{6,2},{1... | collective-permute-start | bytes 884744 | tf_op jit(solution)/shard_map/ppermute | solution.py:444
  38.6 8.8 %collective-permute-start.14 = (bf16[2,48,1536]{2,1,0:T(8,128)(2,1)S(1)}, bf16[2,48,1536]{2,1,0:T(8,128)(2,1)S(1)}, u32[]{:S(2)}, u32[]{:S(2)}) collective-permute-start(bf16[2,48,1536]{2,1,0:T(8,128)(2,1)S(1)} %broadcast_select_fusion.refs_3_.refs_7_), channel_id=1, source_target_pairs={{0,16},{16,0},{1,17},{17,1},{2,18},{18,2},{3,19},{19,3},{4,20},{20... | collective-permute-start | bytes 884744 | tf_op jit(solution)/shard_map/ppermute | solution.py:444
  39.6 7.8 %slice-start.2 = ((s8[4718592]{0:T(1024)(128)(4,1)}), s8[4194304]{0:T(1024)(128)(4,1)S(1)}, s32[]{:S(2)}) async-start(s8[4718592]{0:T(1024)(128)(4,1)} %bitcast.25), calls=%async_computation.2 | async-start | bytes 8388608
  39.6 7.8 %slice-start.3 = ((s8[4718592]{0:T(1024)(128)(4,1)}), s8[524288]{0:T(1024)(128)(4,1)S(1)}, s32[]{:S(2)}) async-start(s8[4718592]{0:T(1024)(128)(4,1)} %bitcast.25), calls=%async_computation.3 | async-start | bytes 1048576
  44.5 15.0 %collective-permute-start.13 = (bf16[2,96,1536]{2,1,0:T(8,128)(2,1)S(1)}, bf16[2,96,1536]{2,1,0:T(8,128)(2,1)S(1)}, u32[]{:S(2)}, u32[]{:S(2)}) collective-permute-start(bf16[2,96,1536]{2,1,0:T(8,128)(2,1)S(1)} %combine.5.refs_7_), channel_id=1, source_target_pairs={{0,8},{4,12},{8,0},{12,4},{1,9},{5,13},{9,1},{13,5},{2,10},{6,14},... | collective-permute-start | bytes 1769480 | tf_op jit(solution)/shard_map/ppermute | solution.py:444
  51.3 9.1 %collective-permute-start.17 = (bf16[192,1536]{1,0:T(8,128)(2,1)S(1)}, bf16[192,1536]{1,0:T(8,128)(2,1)S(1)}, u32[]{:S(2)}, u32[]{:S(2)}) collective-permute-start(bf16[192,1536]{1,0:T(8,128)(2,1)S(1)} %get-tuple-element.42.refs_7_), channel_id=1, source_target_pairs={{0,4},{4,0},{8,12},{12,8},{1,5},{5,1},{9,13},{13,9},{2,6},{6,2},{1... | collective-permute-start | bytes 1769480 | tf_op jit(solution)/shard_map/ppermute | solution.py:444
  51.4 9.1 %collective-permute-start.18 = (bf16[192,1536]{1,0:T(8,128)(2,1)S(1)}, bf16[192,1536]{1,0:T(8,128)(2,1)S(1)}, u32[]{:S(2)}, u32[]{:S(2)}) collective-permute-start(bf16[192,1536]{1,0:T(8,128)(2,1)S(1)} %get-tuple-element.43), channel_id=1, source_target_pairs={{0,4},{4,0},{8,12},{12,8},{1,5},{5,1},{9,13},{13,9},{2,6},{6,2},{1... | collective-permute-start | bytes 1769480 | tf_op jit(solution)/shard_map/ppermute | solution.py:444
  51.9 10.8 %collective-permute-start.15 = (bf16[2,96,1536]{2,1,0:T(8,128)(2,1)S(1)}, bf16[2,96,1536]{2,1,0:T(8,128)(2,1)S(1)}, u32[]{:S(2)}, u32[]{:S(2)}) collective-permute-start(bf16[2,96,1536]{2,1,0:T(8,128)(2,1)S(1)} %activations.5.refs_4_.refs_1_.refs_3_), channel_id=1, source_target_pairs={{0,4},{4,0},{8,12},{12,8},{1,5},{5,1},{9,13},{13,9},{2,6},{6,2},{1... | collective-permute-start | bytes 1769480 | tf_op jit(solution)/shard_map/ppermute | solution.py:444
  60.3 2.4 %collective-permute-start.16 = (bf16[2,96,1536]{2,1,0:T(8,128)(2,1)S(1)}, bf16[2,96,1536]{2,1,0:T(8,128)(2,1)S(1)}, u32[]{:S(2)}, u32[]{:S(2)}) collective-permute-start(bf16[2,96,1536]{2,1,0:T(8,128)(2,1)S(1)} %activations.6.refs_10_.refs_2_.refs_4_), channel_id=1, source_target_pairs={{0,4},{4,0},{8,12},{12,8},{1,5},{5,1},{9,13},{13,9},{2,6},{6,2},{1... | collective-permute-start | bytes 1769480 | tf_op jit(solution)/shard_map/ppermute | solution.py:444
  60.7 15.8 %collective-permute-start.20 = (bf16[2,192,768]{2,1,0:T(8,128)(2,1)S(1)}, bf16[2,192,768]{2,1,0:T(8,128)(2,1)S(1)}, u32[]{:S(2)}, u32[]{:S(2)}) collective-permute-start(bf16[2,192,768]{2,1,0:T(8,128)(2,1)S(1)} %pad_maximum_fusion.refs_9_), channel_id=1, source_target_pairs={{0,8},{4,12},{8,0},{12,4},{1,9},{5,13},{9,1},{13,5},{2,10},{6,14},... | collective-permute-start | bytes 1769480 | tf_op jit(solution)/shard_map/ppermute | solution.py:444
  77.4 8.7 %collective-permute-start.21 = (bf16[2,96,768]{2,1,0:T(8,128)(2,1)S(1)}, bf16[2,96,768]{2,1,0:T(8,128)(2,1)S(1)}, u32[]{:S(2)}, u32[]{:S(2)}) collective-permute-start(bf16[2,96,768]{2,1,0:T(8,128)(2,1)S(1)} %combine.6.refs_6_), channel_id=1, source_target_pairs={{0,8},{4,12},{8,0},{12,4},{1,9},{5,13},{9,1},{13,5},{2,10},{6,14},... | collective-permute-start | bytes 884744 | tf_op jit(solution)/shard_map/ppermute | solution.py:444
  79.0 9.4 %collective-permute-start.19 = (bf16[96,1536]{1,0:T(8,128)(2,1)S(1)}, bf16[96,1536]{1,0:T(8,128)(2,1)S(1)}, u32[]{:S(2)}, u32[]{:S(2)}) collective-permute-start(bf16[96,1536]{1,0:T(8,128)(2,1)S(1)} %get-tuple-element.46), channel_id=1, source_target_pairs={{0,16},{16,0},{1,17},{17,1},{2,18},{18,2},{3,19},{19,3},{4,20},{20... | collective-permute-start | bytes 884744 | tf_op jit(solution)/shard_map/ppermute | solution.py:444
  80.0 10.7 %collective-permute-start.24 = (bf16[2,192,768]{2,1,0:T(8,128)(2,1)S(1)}, bf16[2,192,768]{2,1,0:T(8,128)(2,1)S(1)}, u32[]{:S(2)}, u32[]{:S(2)}) collective-permute-start(bf16[2,192,768]{2,1,0:T(8,128)(2,1)S(1)} %activations.7.refs_4_.refs_5_.refs_1_), channel_id=1, source_target_pairs={{0,4},{4,0},{8,12},{12,8},{1,5},{5,1},{9,13},{13,9},{2,6},{6,2},{1... | collective-permute-start | bytes 1769480 | tf_op jit(solution)/shard_map/ppermute | solution.py:444
  86.5 12.0 %collective-permute-start.23 = (bf16[2,96,768]{2,1,0:T(8,128)(2,1)S(1)}, bf16[2,96,768]{2,1,0:T(8,128)(2,1)S(1)}, u32[]{:S(2)}, u32[]{:S(2)}) collective-permute-start(bf16[2,96,768]{2,1,0:T(8,128)(2,1)S(1)} %activations.8.refs_4_.refs_1_.refs_5_), channel_id=1, source_target_pairs={{0,4},{4,0},{8,12},{12,8},{1,5},{5,1},{9,13},{13,9},{2,6},{6,2},{1... | collective-permute-start | bytes 884744 | tf_op jit(solution)/shard_map/ppermute | solution.py:444
  86.9 14.0 %collective-permute-start.26 = (bf16[2,96,768]{2,1,0:T(8,128)(2,1)S(1)}, bf16[2,96,768]{2,1,0:T(8,128)(2,1)S(1)}, u32[]{:S(2)}, u32[]{:S(2)}) collective-permute-start(bf16[2,96,768]{2,1,0:T(8,128)(2,1)S(1)} %combine.7.refs_3_), channel_id=1, source_target_pairs={{0,8},{4,12},{8,0},{12,4},{1,9},{5,13},{9,1},{13,5},{2,10},{6,14},... | collective-permute-start | bytes 884744 | tf_op jit(solution)/shard_map/ppermute | solution.py:444
  88.6 12.3 %collective-permute-start.22 = (bf16[48,1536]{1,0:T(8,128)(2,1)S(1)}, bf16[48,1536]{1,0:T(8,128)(2,1)S(1)}, u32[]{:S(2)}, u32[]{:S(2)}) collective-permute-start(bf16[48,1536]{1,0:T(8,128)(2,1)S(1)} %fold.6.refs_5_), channel_id=1, source_target_pairs={{0,1},{1,0},{2,3},{3,2},{4,5},{5,4},{6,7},{7,6},{8,9},{9,8},{10,11... | collective-permute-start | bytes 442376 | tf_op jit(solution)/shard_map/ppermute | solution.py:444
  101.4 1.6 %collective-permute-start.27 = (bf16[2,96,768]{2,1,0:T(8,128)(2,1)S(1)}, bf16[2,96,768]{2,1,0:T(8,128)(2,1)S(1)}, u32[]{:S(2)}, u32[]{:S(2)}) collective-permute-start(bf16[2,96,768]{2,1,0:T(8,128)(2,1)S(1)} %activations.9.refs_1_.refs_6_), channel_id=1, source_target_pairs={{0,4},{4,0},{8,12},{12,8},{1,5},{5,1},{9,13},{13,9},{2,6},{6,2},{1... | collective-permute-start | bytes 884744 | tf_op jit(solution)/shard_map/ppermute | solution.py:444
  101.4 6.3 %collective-permute-start.25 = (bf16[48,1536]{1,0:T(8,128)(2,1)S(1)}, bf16[48,1536]{1,0:T(8,128)(2,1)S(1)}, u32[]{:S(2)}, u32[]{:S(2)}) collective-permute-start(bf16[48,1536]{1,0:T(8,128)(2,1)S(1)} %get-tuple-element.53), channel_id=1, source_target_pairs={{0,16},{16,0},{1,17},{17,1},{2,18},{18,2},{3,19},{19,3},{4,20},{20... | collective-permute-start | bytes 442376 | tf_op jit(solution)/shard_map/ppermute | solution.py:444
  105.3 8.8 %collective-permute-start.29 = (bf16[48,1536]{1,0:T(8,128)(2,1)S(1)}, bf16[48,1536]{1,0:T(8,128)(2,1)S(1)}, u32[]{:S(2)}, u32[]{:S(2)}) collective-permute-start(bf16[48,1536]{1,0:T(8,128)(2,1)S(1)} %get-tuple-element.55), channel_id=1, source_target_pairs={{0,16},{16,0},{1,17},{17,1},{2,18},{18,2},{3,19},{19,3},{4,20},{20... | collective-permute-start | bytes 442376 | tf_op jit(solution)/shard_map/ppermute | solution.py:444
  107.7 13.4 %collective-permute-start.28 = (bf16[48,1536]{1,0:T(8,128)(2,1)S(1)}, bf16[48,1536]{1,0:T(8,128)(2,1)S(1)}, u32[]{:S(2)}, u32[]{:S(2)}) collective-permute-start(bf16[48,1536]{1,0:T(8,128)(2,1)S(1)} %fold.8.refs_9_), channel_id=1, source_target_pairs={{0,2},{1,3},{2,0},{3,1},{4,6},{5,7},{6,4},{7,5},{8,10},{9,11},{10,... | collective-permute-start | bytes 442376 | tf_op jit(solution)/shard_map/ppermute | solution.py:444
  114.1 7.1 %collective-permute-start.30 = (bf16[48,1536]{1,0:T(8,128)(2,1)S(1)}, bf16[48,1536]{1,0:T(8,128)(2,1)S(1)}, u32[]{:S(2)}, u32[]{:S(2)}) collective-permute-start(bf16[48,1536]{1,0:T(8,128)(2,1)S(1)} %fold.9.refs_9_), channel_id=1, source_target_pairs={{0,3},{1,2},{2,1},{3,0},{4,7},{5,6},{6,5},{7,4},{8,11},{9,10},{10,... | collective-permute-start | bytes 442376 | tf_op jit(solution)/shard_map/ppermute | solution.py:444

commit v10 on v9

--- a/solution.py
+++ b/solution.py
@@ -291,7 +291,7 @@
         for side in range(2):
             mine = [ref[0] for ref in refs[side * groups : (side + 1) * groups]]
             mine = mine[0] if groups == 1 else jnp.concatenate(mine, axis=0)
-            term = contract(mine, refs[2 * groups + side][...], 1, 1)
+            term = contract(mine, refs[2 * groups + side][:, start : start + width], 1, 1)
             part = term if part is None else part + term
         refs = refs[2 * groups + 2 :]
         if before is not None:
@@ -319,7 +319,7 @@
             pl.BlockSpec((1, array.shape[1], width), lambda i, c, first=first: (1, 0, first))
             for array, first in zip(operands, firsts)
         ]
-        + [pl.BlockSpec((tile, width), lambda i, c: (i, start // width))] * 2
+        + [pl.BlockSpec((tile, ups[0].shape[1]), lambda i, c: (i, 0))] * 2
         + ([] if before is None else [pl.BlockSpec((tokens, tile), lambda i, c: (row // tokens, i))]),
         [jax.ShapeDtypeStruct((rows, depth), dtype) for rows, dtype in kinds],
         [pl.BlockSpec((rows, tile), lambda i, c: (0, i)) for rows, _ in kinds],
@@ -447,7 +447,8 @@
 def cube_body(inputs, cotangent, up, down):
     rows = inputs.shape[0]
     half = up.shape[1] // 2
-    width = half // 2
+    width = half // 3 if half % 768 == 0 else half // 2
+    spans = [(0, width), (width, half - width)]
     core = (lax.axis_index("gy") % 2).astype(jnp.int32).reshape(1)
 
     unit = {(0, 0): jnp.stack([inputs, cotangent])}
@@ -476,9 +477,9 @@
     pieces = [
         (0, 0, pair, 0, half),
         (1, 0, pair, 0, half),
-        (2, 0, 2 * pair, 0, width),
-        (2, 0, pair, width, width),
-        (2, pair, pair, width, width),
+        (2, 0, 2 * pair, *spans[0]),
+        (2, 0, pair, *spans[1]),
+        (2, pair, pair, *spans[1]),
     ]
     near, keep, far, act, act_near = {}, {}, {}, {}, {}
 
@@ -533,13 +534,13 @@
 
     def gradients(j, sides, after):
         acts = [
-            [(array[n], j * width) for n in range(2)]
+            [(array[n], spans[j][0]) for n in range(2)]
             + ([(array[3], 0), (array[4], 0)] if j else [(array[2], 0)])
             for array in (act, act_near)
         ]
         acts = [acts[side] for side in sides]
         return weight_grads(
-            core, inputs_t, cotan, sides, acts, j * width, width, up.shape, outputs, after
+            core, inputs_t, cotan, sides, acts, *spans[j], up.shape, outputs, after
         )
 
     def finish(j, sides, after):
@@ -565,18 +566,18 @@
     last = ready(2, [stay1])
     last = cross(3, last)
     last = finish(0, (0,), last)
-    last = ready(3, last)
-    last = cross(4, last)
     total = fold(core, stay1[:rows], near1[:rows], F32, last)
     back1 = fold(core, stay1[rows:], near1[rows:], BF16, [total])
     far1 = swap(back1, "gz", 4, 1)
-    part, = inward(((2, 0),), 0, width, None, 0, None, None, [back1])
-    last = finish(0, (1,), [part])
-    stay2, go2 = inward(((3, 0),), width, width, part, 0, (0, 1), 1, last)
+    part, = inward(((2, 0),), *spans[0], None, 0, None, None, [back1])
+    last = ready(3, [part])
+    last = cross(4, last)
+    last = finish(0, (1,), last)
+    stay2, go2 = inward(((3, 0),), *spans[1], part, 0, (0, 1), 1, last)
     near2 = swap(go2, "gx", 2, 1)
     total = fold(core, total, far1, F32, [stay2])
     last = ready(4, [total])
-    stay3, go3 = inward(((4, 0),), width, width, part, pair, (0, 1), 1, last)
+    stay3, go3 = inward(((4, 0),), *spans[1], part, pair, (0, 1), 1, last)
     near3 = swap(go3, "gx", 2, 1)
     back2 = fold(core, stay2, near2, BF16, [stay3])
     far2 = swap(back2, "gz", 4, 2)

time: 122 us -> 126 us (1.033)
  starting transfers between devices: 32 us -> 37.5 us
  waiting for transfers between devices: 20 us -> 22.5 us
  local copies, waits for them, and re-layouts: 2.43 us -> 0.06 us
  Pallas kernels: 64.3 us -> 62.9 us
    ppermute x27, starting transfers between devices: 27.2 us -> 33.4 us  [swap(): return lax.ppermute(value, axis, [(i, i ^ bits) for i in range(size)])]
    ppermute x1, waiting for transfers between devices: 0.24 us -> 3.7 us  [cube_body(): second_on = lax.ppermute(second, 'gz', outward)]
    unnamed x14 -> x0, local copies, waits for them, and re-layouts: 2.37 us -> none
    ppermute x1, waiting for transfers between devices: 2.27 us -> 0.01 us  [cube_body(): first_on = lax.ppermute(first, 'gz', outward)]
    pallas_call x30, Pallas kernels: 64.3 us -> 62.9 us  [call(): pl.pallas_call(kernel, grid_spec=pltpu.PrefetchScalarGridSpec(num_scalar_...]
    ppermute x27, waiting for transfers between devices: 17.5 us -> 18.8 us  [swap(): return lax.ppermute(value, axis, [(i, i ^ bits) for i in range(size)])]
  transfers between devices with their start and end apart: 31 -> 31, of which waited for: 10 -> 10; matrix products, arithmetic and copies ran while one was open for 0% -> 0% of each run, Pallas kernels for 52% -> 49%
where the time goes in v10:
time: 126 us
  Pallas kernels  62.9 us (50%)
  starting transfers between devices  37.5 us (30%)
  waiting for transfers between devices  22.5 us (18%)
  other arithmetic  1.97 us (2%)
    pallas_call x30, Pallas kernels, call(): pl.pallas_call(kernel, grid_spec=pltpu.PrefetchScalarGridSpec(num_scalar_...  62.9 us
    ppermute x27, starting transfers between devices, swap(): return lax.ppermute(value, axis, [(i, i ^ bits) for i in range(size)])  33.4 us
    ppermute x27, waiting for transfers between devices, swap(): return lax.ppermute(value, axis, [(i, i ^ bits) for i in range(size)])  18.8 us
    ppermute x1, waiting for transfers between devices, cube_body(): second_on = lax.ppermute(second, 'gz', outward)  3.7 us
  transfers between devices with their start and end apart: 31, of which 10 were waited for; matrix products, arithmetic and copies ran while one was open for 0% of the time, Pallas kernels for 49%

profile of v10, /device:TPU:0, one launch (start us, length us, event | category | flops | bytes accessed | tf_op | source)
XLA Modules:
  0.0 126.0 jit_solution(11594169017222399363)
XLA Ops:
  0.6 1.0 pad_maximum_fusion.1.refs_1_
  1.6 3.1 %collective-permute-start.3 = (bf16[2,48,1536]{2,1,0:T(8,128)(2,1)S(1)}, bf16[2,48,1536]{2,1,0:T(8,128)(2,1)S(1)}, u32[]{:S(2)}, u32[]{:S(2)}) collective-permute-start(bf16[2,48,1536]{2,1,0:T(8,128)(2,1)S(1)} %pad_maximum_fusion.1.refs_1_), channel_id=1, source_target_pairs={{0,1},{1,0},{2,3},{3,2},{4,5},{5,4},{6,7},{7,6},{8,9},{9,8},{10,11... | collective-permute-start | bytes 884744 | tf_op jit(solution)/shard_map/ppermute | solution.py:444
  4.7 0.7 collective-permute-start.6
  5.4 1.6 %collective-permute-start = (bf16[2,48,1536]{2,1,0:T(8,128)(2,1)S(1)}, bf16[2,48,1536]{2,1,0:T(8,128)(2,1)S(1)}, u32[]{:S(2)}, u32[]{:S(2)}) collective-permute-start(bf16[2,48,1536]{2,1,0:T(8,128)(2,1)S(1)} %pad_maximum_fusion.1.refs_1_), channel_id=1, source_target_pairs={{0,16},{16,0},{1,17},{17,1},{2,18},{18,2},{3,19},{19,3},{4,20},{20... | collective-permute-start | bytes 884744 | tf_op jit(solution)/shard_map/ppermute | solution.py:444
  7.0 4.8 %collective-permute-done.3.refs_1_.refs_3_ = bf16[2,48,1536]{2,1,0:T(8,128)(2,1)S(1)} collective-permute-done((bf16[2,48,1536]{2,1,0:T(8,128)(2,1)S(1)}, bf16[2,48,1536]{2,1,0:T(8,128)(2,1)S(1)}, u32[]{:S(2)}, u32[]{:S(2)}) %collective-permute-start.3) | collective-permute-done | bytes 294944 | tf_op jit(solution)/shard_map/ppermute | solution.py:444
  11.7 0.7 collective-permute-start.8
  12.4 1.3 %collective-permute-start.7 = (bf16[2,48,1536]{2,1,0:T(8,128)(2,1)S(1)}, bf16[2,48,1536]{2,1,0:T(8,128)(2,1)S(1)}, u32[]{:S(2)}, u32[]{:S(2)}) collective-permute-start(bf16[2,48,1536]{2,1,0:T(8,128)(2,1)S(1)} %collective-permute-done.6), channel_id=1, source_target_pairs={{1,0},{2,3},{5,4},{6,7},{9,8},{10,11},{13,12},{14,15},{17,16},{18,... | collective-permute-start | bytes 884744 | tf_op jit(solution)/shard_map/ppermute | solution.py:464
  13.7 3.8 %bring.1 = (bf16[1536,1536]{1,0:T(8,128)(2,1)S(1)}, bf16[1536,1536]{1,0:T(8,128)(2,1)S(1)}) custom-call(s32[1]{0:T(128)} %bitcast.refs_0_, bf16[1536,3072]{1,0:T(8,128)(2,1)} %refs_3_.1, bf16[3072,1536]{1,0:T(8,128)(2,1)} %refs_4_.1), custom_call_target="tpu_custom_call" | custom-call | bytes 9437184 | tf_op jit(solution)/shard_map/bring/pallas_call | solution.py:68
  17.6 3.6 %sums_send.3 = (bf16[96,1536]{1,0:T(8,128)(2,1)S(1)}, bf16[96,1536]{1,0:T(8,128)(2,1)S(1)}) custom-call(s32[1]{0:T(128)} %bitcast.refs_0_, bf16[2,48,1536]{2,1,0:T(8,128)(2,1)S(1)} %pad_maximum_fusion.1.refs_1_, bf16[2,48,1536]{2,1,0:T(8,128)(2,1)S(1)} %collective-permute-done.refs_2_, ...), custom_call_target="tpu_custom_call" | custom-call | flops 905969664 | bytes 9437184 | tf_op jit(solution)/shard_map/sums_send/pallas_call | solution.py:68
  21.1 0.1 collective-permute-start.2
  21.2 0.5 collective-permute-start.1
  21.7 1.7 %collective-permute-start.4 = (bf16[2,48,1536]{2,1,0:T(8,128)(2,1)S(1)}, bf16[2,48,1536]{2,1,0:T(8,128)(2,1)S(1)}, u32[]{:S(2)}, u32[]{:S(2)}) collective-permute-start(bf16[2,48,1536]{2,1,0:T(8,128)(2,1)S(1)} %collective-permute-done.3.refs_1_.refs_3_), channel_id=1, source_target_pairs={{0,16},{16,0},{1,17},{17,1},{2,18},{18,2},{3,19},{19,3},{4,20},{20... | collective-permute-start | bytes 884744 | tf_op jit(solution)/shard_map/ppermute | solution.py:444
  23.4 4.7 %bring_and_sum.1 = (f32[2,96,1536]{2,1,0:T(8,128)S(1)}, bf16[1536,1536]{1,0:T(8,128)(2,1)S(1)}, bf16[1536,1536]{1,0:T(8,128)(2,1)S(1)}) custom-call(s32[1]{0:T(128)} %bitcast.refs_0_, bf16[2,48,1536]{2,1,0:T(8,128)(2,1)S(1)} %pad_maximum_fusion.1.refs_1_, bf16[2,48,1536]{2,1,0:T(8,128)(2,1)S(1)} %collective-permute-done.refs_2_, bf16[1536,3072]{1,0:T(8,128)(2,1)} %refs_3_.1, ...), custom_call_target="tpu_custom_call" | custom-call | flops 905969664 | bytes 9437184 | tf_op jit(solution)/shard_map/bring_and_sum/pallas_call | solution.py:68
  28.1 1.5 %collective-permute-start.9 = (bf16[2,48,1536]{2,1,0:T(8,128)(2,1)S(1)}, bf16[2,48,1536]{2,1,0:T(8,128)(2,1)S(1)}, u32[]{:S(2)}, u32[]{:S(2)}) collective-permute-start(bf16[2,48,1536]{2,1,0:T(8,128)(2,1)S(1)} %collective-permute-done.8.refs_7_), channel_id=1, source_target_pairs={{1,0},{2,3},{5,4},{6,7},{9,8},{10,11},{13,12},{14,15},{17,16},{18,... | collective-permute-start | bytes 884744 | tf_op jit(solution)/shard_map/ppermute | solution.py:465
  29.6 0.4 collective-permute-start.10
  30.1 0.7 collective-permute-done.4.refs_5_.refs_2_.refs_4_
  30.7 0.4 combine.4.refs_5_
  31.1 1.7 %collective-permute-start.5 = (bf16[2,96,1536]{2,1,0:T(8,128)(2,1)S(1)}, bf16[2,96,1536]{2,1,0:T(8,128)(2,1)S(1)}, u32[]{:S(2)}, u32[]{:S(2)}) collective-permute-start(bf16[2,96,1536]{2,1,0:T(8,128)(2,1)S(1)} %combine.4.refs_5_), channel_id=1, source_target_pairs={{0,8},{4,12},{8,0},{12,4},{1,9},{5,13},{9,1},{13,5},{2,10},{6,14},... | collective-permute-start | bytes 1769480 | tf_op jit(solution)/shard_map/ppermute | solution.py:444
  32.9 3.6 %sums_send.4 = (bf16[96,1536]{1,0:T(8,128)(2,1)S(1)}, bf16[96,1536]{1,0:T(8,128)(2,1)S(1)}) custom-call(s32[1]{0:T(128)} %bitcast.refs_0_, bf16[2,48,1536]{2,1,0:T(8,128)(2,1)S(1)} %collective-permute-done.3.refs_1_.refs_3_, bf16[2,48,1536]{2,1,0:T(8,128)(2,1)S(1)} %collective-permute-done.4.refs_5_.refs_2_.refs_4_, ...), custom_call_target="tpu_custom_call" | custom-call | flops 905969664 | bytes 9437184 | tf_op jit(solution)/shard_map/sums_send/pallas_call | solution.py:68
  36.5 0.1 collective-permute-start.12
  36.5 0.5 collective-permute-start.11
  37.0 3.7 %collective-permute-done.9.refs_6_ = bf16[2,48,1536]{2,1,0:T(8,128)(2,1)S(1)} collective-permute-done((bf16[2,48,1536]{2,1,0:T(8,128)(2,1)S(1)}, bf16[2,48,1536]{2,1,0:T(8,128)(2,1)S(1)}, u32[]{:S(2)}, u32[]{:S(2)}) %collective-permute-start.9) | collective-permute-done | bytes 294944 | tf_op jit(solution)/shard_map/ppermute | solution.py:465
  40.8 0.6 collective-permute-start.14
  41.4 3.6 %sums_keep.2.refs_5_.refs_1_ = f32[2,96,1536]{2,1,0:T(8,128)S(1)} custom-call(s32[1]{0:T(128)} %bitcast.refs_0_, bf16[2,48,1536]{2,1,0:T(8,128)(2,1)S(1)} %collective-permute-done.3.refs_1_.refs_3_, bf16[2,48,1536]{2,1,0:T(8,128)(2,1)S(1)} %collective-permute-done.4.refs_5_.refs_2_.refs_4_, bf16[1536,1536]{1,0:T(8,128)(2,1)S(1)} %get-tuple-element.38.refs_3_.refs_5_, ...), custom_call_target="tpu_custom_call" | custom-call | flops 905969664 | bytes 9437184 | tf_op jit(solution)/shard_map/sums_keep/pallas_call | solution.py:68
  45.0 0.7 collective-permute-done.5.refs_4_
  45.7 0.8 activations.5.refs_4_.refs_1_.refs_3_
  46.5 0.4 combine.5.refs_7_
  46.9 1.7 %collective-permute-start.13 = (bf16[2,96,1536]{2,1,0:T(8,128)(2,1)S(1)}, bf16[2,96,1536]{2,1,0:T(8,128)(2,1)S(1)}, u32[]{:S(2)}, u32[]{:S(2)}) collective-permute-start(bf16[2,96,1536]{2,1,0:T(8,128)(2,1)S(1)} %combine.5.refs_7_), channel_id=1, source_target_pairs={{0,8},{4,12},{8,0},{12,4},{1,9},{5,13},{9,1},{13,5},{2,10},{6,14},... | collective-permute-start | bytes 1769480 | tf_op jit(solution)/shard_map/ppermute | solution.py:444
  48.7 0.3 collective-permute-done.14.refs_4_.refs_8_
  49.0 3.8 %sums_send.5 = (bf16[192,1536]{1,0:T(8,128)(2,1)S(1)}, bf16[192,1536]{1,0:T(8,128)(2,1)S(1)}) custom-call(s32[1]{0:T(128)} %bitcast.refs_0_, bf16[2,48,1536]{2,1,0:T(8,128)(2,1)S(1)} %broadcast_select_fusion.1.refs_1_.refs_5_, bf16[2,48,1536]{2,1,0:T(8,128)(2,1)S(1)} %collective-permute-done.10.refs_6_.refs_2_, ...), custom_call_target="tpu_custom_call" | custom-call | flops 1811939328 | bytes 9437184 | tf_op jit(solution)/shard_map/sums_send/pallas_call | solution.py:68
  52.9 0.5 collective-permute-start.17
  53.4 0.1 collective-permute-start.15
  53.5 3.9 %sums_keep.3.refs_5_.refs_1_ = f32[2,192,1536]{2,1,0:T(8,128)S(1)} custom-call(s32[1]{0:T(128)} %bitcast.refs_0_, bf16[2,48,1536]{2,1,0:T(8,128)(2,1)S(1)} %broadcast_select_fusion.1.refs_1_.refs_5_, bf16[2,48,1536]{2,1,0:T(8,128)(2,1)S(1)} %collective-permute-done.10.refs_6_.refs_2_, bf16[2,48,1536]{2,1,0:T(8,128)(2,1)S(1)} %broadcast_select_fusion.refs_3_.refs_7_, ...), custom_call_target="tpu_custom_call" | custom-call | flops 1811939328 | bytes 9437184 | tf_op jit(solution)/shard_map/sums_keep/pallas_call | solution.py:68
  57.4 3.2 %collective-permute-done.13.refs_4_ = bf16[2,96,1536]{2,1,0:T(8,128)(2,1)S(1)} collective-permute-done((bf16[2,96,1536]{2,1,0:T(8,128)(2,1)S(1)}, bf16[2,96,1536]{2,1,0:T(8,128)(2,1)S(1)}, u32[]{:S(2)}, u32[]{:S(2)}) %collective-permute-start.13) | collective-permute-done | bytes 589856 | tf_op jit(solution)/shard_map/ppermute | solution.py:444
  60.5 0.8 activations.6.refs_10_.refs_2_.refs_4_
  61.5 0.1 fusion.4
  61.6 1.7 %collective-permute-start.20 = (bf16[2,192,512]{2,1,0:T(8,128)(2,1)S(1)}, bf16[2,192,512]{2,1,0:T(8,128)(2,1)S(1)}, u32[]{:S(2)}, u32[]{:S(2)}) collective-permute-start(bf16[2,192,512]{2,1,0:T(8,128)(2,1)S(1)} %pad_maximum_fusion.refs_9_), channel_id=1, source_target_pairs={{0,8},{4,12},{8,0},{12,4},{1,9},{5,13},{9,1},{13,5},{2,10},{6,14},... | collective-permute-start | bytes 1179656 | tf_op jit(solution)/shard_map/ppermute | solution.py:444
  63.4 0.4 arrange.1
  63.8 3.6 %back.4 = (f32[96,1536]{1,0:T(8,128)S(1)}, bf16[96,1536]{1,0:T(8,128)(2,1)S(1)}) custom-call(s32[1]{0:T(128)} %bitcast.refs_0_, bf16[2,96,1536]{2,1,0:T(8,128)(2,1)S(1)} %activations.5.refs_4_.refs_1_.refs_3_, bf16[2,96,1536]{2,1,0:T(8,128)(2,1)S(1)} %activations.6.refs_10_.refs_2_.refs_4_, bf16[2,96,1536]{2,1,0:T(8,128)(2,1)S(1)} %collective-permute-done.15.refs_3_, ...), custom_call_target="tpu_custom_call" | custom-call | flops 1811939328 | bytes 10616832 | tf_op jit(solution)/shard_map/back/pallas_call | solution.py:68
  67.4 1.6 %collective-permute-start.19 = (bf16[96,1536]{1,0:T(8,128)(2,1)S(1)}, bf16[96,1536]{1,0:T(8,128)(2,1)S(1)}, u32[]{:S(2)}, u32[]{:S(2)}) collective-permute-start(bf16[96,1536]{1,0:T(8,128)(2,1)S(1)} %get-tuple-element.46), channel_id=1, source_target_pairs={{0,16},{16,0},{1,17},{17,1},{2,18},{18,2},{3,19},{19,3},{4,20},{20... | collective-permute-start | bytes 884744 | tf_op jit(solution)/shard_map/ppermute | solution.py:444
  69.0 4.2 %collective-permute-done.20.refs_4_ = bf16[2,192,512]{2,1,0:T(8,128)(2,1)S(1)} collective-permute-done((bf16[2,192,512]{2,1,0:T(8,128)(2,1)S(1)}, bf16[2,192,512]{2,1,0:T(8,128)(2,1)S(1)}, u32[]{:S(2)}, u32[]{:S(2)}) %collective-permute-start.20) | collective-permute-done | bytes 393248 | tf_op jit(solution)/shard_map/ppermute | solution.py:444
  73.2 0.5 activations.7.refs_4_.refs_5_.refs_1_
  73.8 0.3 combine.6.refs_6_
  74.1 1.7 %collective-permute-start.22 = (bf16[2,96,1024]{2,1,0:T(8,128)(2,1)S(1)}, bf16[2,96,1024]{2,1,0:T(8,128)(2,1)S(1)}, u32[]{:S(2)}, u32[]{:S(2)}) collective-permute-start(bf16[2,96,1024]{2,1,0:T(8,128)(2,1)S(1)} %combine.6.refs_6_), channel_id=1, source_target_pairs={{0,8},{4,12},{8,0},{12,4},{1,9},{5,13},{9,1},{13,5},{2,10},{6,14},... | collective-permute-start | bytes 1179656 | tf_op jit(solution)/shard_map/ppermute | solution.py:444
  75.8 3.8 %weight_grads.4 = (f32[1536,3072]{1,0:T(8,128)}, f32[3072,1536]{1,0:T(8,128)}, f32[8,128]{1,0:T(8,128)S(1)}) custom-call(s32[1]{0:T(128)} %bitcast.refs_0_, bf16[1536,384]{1,0:T(8,128)(2,1)S(1)} %get-tuple-element.44.refs_7_.refs_1_, bf16[384,1536]{1,0:T(8,128)(2,1)S(1)} %get-tuple-element.47.refs_2_, ...), custom_call_target="tpu_custom_call" | custom-call | flops 1207959552 | bytes 6291456 | tf_op jit(solution)/shard_map/weight_grads/pallas_call | solution.py:68
  79.8 1.6 %back.5.refs_5_ = f32[192,1536]{1,0:T(8,128)S(1)} custom-call(s32[1]{0:T(128)} %bitcast.refs_0_, bf16[2,192,512]{2,1,0:T(8,128)(2,1)S(1)} %activations.7.refs_4_.refs_5_.refs_1_, bf16[2,192,512]{2,1,0:T(8,128)(2,1)S(1)} %collective-permute-done.23.refs_2_.refs_5_, bf16[1536,1536]{1,0:T(8,128)(2,1)S(1)} %get-tuple-element.38.refs_3_.refs_5_, ...), custom_call_target="tpu_custom_call" | custom-call | flops 603979776 | bytes 4325376 | tf_op jit(solution)/shard_map/back/pallas_call | solution.py:68
  81.4 4.3 %collective-permute-done.22.refs_4_ = bf16[2,96,1024]{2,1,0:T(8,128)(2,1)S(1)} collective-permute-done((bf16[2,96,1024]{2,1,0:T(8,128)(2,1)S(1)}, bf16[2,96,1024]{2,1,0:T(8,128)(2,1)S(1)}, u32[]{:S(2)}, u32[]{:S(2)}) %collective-permute-start.22) | collective-permute-done | bytes 393248 | tf_op jit(solution)/shard_map/ppermute | solution.py:444
  85.6 0.6 activations.8.refs_4_.refs_1_.refs_5_
  86.3 0.3 combine.7.refs_8_
  86.6 1.7 %collective-permute-start.26 = (bf16[2,96,1024]{2,1,0:T(8,128)(2,1)S(1)}, bf16[2,96,1024]{2,1,0:T(8,128)(2,1)S(1)}, u32[]{:S(2)}, u32[]{:S(2)}) collective-permute-start(bf16[2,96,1024]{2,1,0:T(8,128)(2,1)S(1)} %combine.7.refs_8_), channel_id=1, source_target_pairs={{0,8},{4,12},{8,0},{12,4},{1,9},{5,13},{9,1},{13,5},{2,10},{6,14},... | collective-permute-start | bytes 1179656 | tf_op jit(solution)/shard_map/ppermute | solution.py:444
  88.4 4.4 %collective-permute-start.21 = (bf16[48,1536]{1,0:T(8,128)(2,1)S(1)}, bf16[48,1536]{1,0:T(8,128)(2,1)S(1)}, u32[]{:S(2)}, u32[]{:S(2)}) collective-permute-start(bf16[48,1536]{1,0:T(8,128)(2,1)S(1)} %fold.6.refs_5_), channel_id=1, source_target_pairs={{0,1},{1,0},{2,3},{3,2},{4,5},{5,4},{6,7},{7,6},{8,9},{9,8},{10,11... | collective-permute-start | bytes 442376 | tf_op jit(solution)/shard_map/ppermute | solution.py:444
  92.8 3.8 %weight_grads.5 = (f32[1536,3072]{1,0:T(8,128)}, f32[3072,1536]{1,0:T(8,128)}, f32[8,128]{1,0:T(8,128)S(1)}) custom-call(s32[1]{0:T(128)} %bitcast.refs_0_, bf16[1536,384]{1,0:T(8,128)(2,1)S(1)} %get-tuple-element.44.refs_7_.refs_1_, bf16[384,1536]{1,0:T(8,128)(2,1)S(1)} %get-tuple-element.47.refs_2_, ...), custom_call_target="tpu_custom_call", output_to_operand_aliasing={{0}: (6, {}), {1}: (7, {})} | custom-call | flops 1207959552 | bytes 6291456 | tf_op jit(solution)/shard_map/weight_grads/pallas_call | solution.py:68
  96.6 2.4 %back.6 = (f32[48,1536]{1,0:T(8,128)S(1)}, bf16[48,1536]{1,0:T(8,128)(2,1)S(1)}) custom-call(s32[1]{0:T(128)} %bitcast.refs_0_, bf16[2,96,1024]{2,1,0:T(8,128)(2,1)S(1)} %activations.8.refs_4_.refs_1_.refs_5_, bf16[2,96,1024]{2,1,0:T(8,128)(2,1)S(1)} %collective-permute-done.24.refs_2_.refs_5_, bf16[1536,1536]{1,0:T(8,128)(2,1)S(1)} %get-tuple-element.38.refs_3_.refs_5_, ...), custom_call_target="tpu_custom_call" | custom-call | flops 603979776 | bytes 6881280 | tf_op jit(solution)/shard_map/back/pallas_call | solution.py:68
  99.1 0.6 activations.9.refs_1_.refs_6_
  99.8 1.6 %collective-permute-start.25 = (bf16[48,1536]{1,0:T(8,128)(2,1)S(1)}, bf16[48,1536]{1,0:T(8,128)(2,1)S(1)}, u32[]{:S(2)}, u32[]{:S(2)}) collective-permute-start(bf16[48,1536]{1,0:T(8,128)(2,1)S(1)} %get-tuple-element.53), channel_id=1, source_target_pairs={{0,16},{16,0},{1,17},{17,1},{2,18},{18,2},{3,19},{19,3},{4,20},{20... | collective-permute-start | bytes 442376 | tf_op jit(solution)/shard_map/ppermute | solution.py:444
  101.3 0.1 collective-permute-done.27.refs_2_.refs_6_
  101.5 2.4 %back.7 = (f32[48,1536]{1,0:T(8,128)S(1)}, bf16[48,1536]{1,0:T(8,128)(2,1)S(1)}) custom-call(s32[1]{0:T(128)} %bitcast.refs_0_, bf16[2,96,1024]{2,1,0:T(8,128)(2,1)S(1)} %activations.9.refs_1_.refs_6_, bf16[2,96,1024]{2,1,0:T(8,128)(2,1)S(1)} %collective-permute-done.27.refs_2_.refs_6_, bf16[1536,1536]{1,0:T(8,128)(2,1)S(1)} %get-tuple-element.38.refs_3_.refs_5_, ...), custom_call_target="tpu_custom_call" | custom-call | flops 603979776 | bytes 6881280 | tf_op jit(solution)/shard_map/back/pallas_call | solution.py:68
  103.9 1.6 %collective-permute-start.29 = (bf16[48,1536]{1,0:T(8,128)(2,1)S(1)}, bf16[48,1536]{1,0:T(8,128)(2,1)S(1)}, u32[]{:S(2)}, u32[]{:S(2)}) collective-permute-start(bf16[48,1536]{1,0:T(8,128)(2,1)S(1)} %get-tuple-element.55), channel_id=1, source_target_pairs={{0,16},{16,0},{1,17},{17,1},{2,18},{18,2},{3,19},{19,3},{4,20},{20... | collective-permute-start | bytes 442376 | tf_op jit(solution)/shard_map/ppermute | solution.py:444
  105.5 0.6 collective-permute-done.25.refs_2_
  106.1 4.4 %collective-permute-start.28 = (bf16[48,1536]{1,0:T(8,128)(2,1)S(1)}, bf16[48,1536]{1,0:T(8,128)(2,1)S(1)}, u32[]{:S(2)}, u32[]{:S(2)}) collective-permute-start(bf16[48,1536]{1,0:T(8,128)(2,1)S(1)} %fold.8.refs_9_), channel_id=1, source_target_pairs={{0,2},{1,3},{2,0},{3,1},{4,6},{5,7},{6,4},{7,5},{8,10},{9,11},{10,... | collective-permute-start | bytes 442376 | tf_op jit(solution)/shard_map/ppermute | solution.py:444
  110.5 6.5 %weight_grads.6 = (f32[1536,3072]{1,0:T(8,128)}, f32[3072,1536]{1,0:T(8,128)}, f32[8,128]{1,0:T(8,128)S(1)}) custom-call(s32[1]{0:T(128)} %bitcast.refs_0_, bf16[1536,384]{1,0:T(8,128)(2,1)S(1)} %get-tuple-element.44.refs_7_.refs_1_, bf16[384,1536]{1,0:T(8,128)(2,1)S(1)} %get-tuple-element.47.refs_2_, ...), custom_call_target="tpu_custom_call", output_to_operand_aliasing={{0}: (7, {}), {1}: (8, {})} | custom-call | flops 2415919104 | bytes 12582912 | tf_op jit(solution)/shard_map/weight_grads/pallas_call | solution.py:68
  117.0 1.7 %collective-permute-start.30 = (bf16[48,1536]{1,0:T(8,128)(2,1)S(1)}, bf16[48,1536]{1,0:T(8,128)(2,1)S(1)}, u32[]{:S(2)}, u32[]{:S(2)}) collective-permute-start(bf16[48,1536]{1,0:T(8,128)(2,1)S(1)} %fold.9.refs_9_), channel_id=1, source_target_pairs={{0,3},{1,2},{2,1},{3,0},{4,7},{5,6},{6,5},{7,4},{8,11},{9,10},{10,... | collective-permute-start | bytes 442376 | tf_op jit(solution)/shard_map/ppermute | solution.py:444
  118.8 6.5 %weight_grads.7 = (f32[1536,3072]{1,0:T(8,128)}, f32[3072,1536]{1,0:T(8,128)}, f32[8,128]{1,0:T(8,128)}) custom-call(s32[1]{0:T(128)} %bitcast.refs_0_, bf16[1536,384]{1,0:T(8,128)(2,1)S(1)} %get-tuple-element.44.refs_7_.refs_1_, bf16[384,1536]{1,0:T(8,128)(2,1)S(1)} %get-tuple-element.47.refs_2_, ...), custom_call_target="tpu_custom_call", output_to_operand_aliasing={{0}: (7, {}), {1}: (8, {})} | custom-call | flops 2415919104 | bytes 12582912 | tf_op jit(solution)/shard_map/weight_grads/pallas_call | solution.py:68
  125.3 0.7 add_convert_fusion
  (36 shorter events, 0.7 us)
Async XLA Ops:
  1.6 10.1 %collective-permute-start.3 = (bf16[2,48,1536]{2,1,0:T(8,128)(2,1)S(1)}, bf16[2,48,1536]{2,1,0:T(8,128)(2,1)S(1)}, u32[]{:S(2)}, u32[]{:S(2)}) collective-permute-start(bf16[2,48,1536]{2,1,0:T(8,128)(2,1)S(1)} %pad_maximum_fusion.1.refs_1_), channel_id=1, source_target_pairs={{0,1},{1,0},{2,3},{3,2},{4,5},{5,4},{6,7},{7,6},{8,9},{9,8},{10,11... | collective-permute-start | bytes 884744 | tf_op jit(solution)/shard_map/ppermute | solution.py:444
  4.7 7.7 %collective-permute-start.6 = (bf16[2,48,1536]{2,1,0:T(8,128)(2,1)S(1)}, bf16[2,48,1536]{2,1,0:T(8,128)(2,1)S(1)}, u32[]{:S(2)}, u32[]{:S(2)}) collective-permute-start(bf16[2,48,1536]{2,1,0:T(8,128)(2,1)S(1)} %pad_maximum_fusion.1.refs_1_), channel_id=1, source_target_pairs={{1,2},{2,1},{5,6},{6,5},{9,10},{10,9},{13,14},{14,13},{17,18},{18,... | collective-permute-start | bytes 884744 | tf_op jit(solution)/shard_map/ppermute | solution.py:460
  5.4 12.1 %collective-permute-start = (bf16[2,48,1536]{2,1,0:T(8,128)(2,1)S(1)}, bf16[2,48,1536]{2,1,0:T(8,128)(2,1)S(1)}, u32[]{:S(2)}, u32[]{:S(2)}) collective-permute-start(bf16[2,48,1536]{2,1,0:T(8,128)(2,1)S(1)} %pad_maximum_fusion.1.refs_1_), channel_id=1, source_target_pairs={{0,16},{16,0},{1,17},{17,1},{2,18},{18,2},{3,19},{19,3},{4,20},{20... | collective-permute-start | bytes 884744 | tf_op jit(solution)/shard_map/ppermute | solution.py:444
  11.7 16.3 %collective-permute-start.8 = (bf16[2,48,1536]{2,1,0:T(8,128)(2,1)S(1)}, bf16[2,48,1536]{2,1,0:T(8,128)(2,1)S(1)}, u32[]{:S(2)}, u32[]{:S(2)}) collective-permute-start(bf16[2,48,1536]{2,1,0:T(8,128)(2,1)S(1)} %collective-permute-done.3.refs_1_.refs_3_), channel_id=1, source_target_pairs={{1,2},{2,1},{5,6},{6,5},{9,10},{10,9},{13,14},{14,13},{17,18},{18,... | collective-permute-start | bytes 884744 | tf_op jit(solution)/shard_map/ppermute | solution.py:463
  12.4 17.1 %collective-permute-start.7 = (bf16[2,48,1536]{2,1,0:T(8,128)(2,1)S(1)}, bf16[2,48,1536]{2,1,0:T(8,128)(2,1)S(1)}, u32[]{:S(2)}, u32[]{:S(2)}) collective-permute-start(bf16[2,48,1536]{2,1,0:T(8,128)(2,1)S(1)} %collective-permute-done.6), channel_id=1, source_target_pairs={{1,0},{2,3},{5,4},{6,7},{9,8},{10,11},{13,12},{14,15},{17,16},{18,... | collective-permute-start | bytes 884744 | tf_op jit(solution)/shard_map/ppermute | solution.py:464
  21.1 9.6 %collective-permute-start.2 = (bf16[96,1536]{1,0:T(8,128)(2,1)S(1)}, bf16[96,1536]{1,0:T(8,128)(2,1)S(1)}, u32[]{:S(2)}, u32[]{:S(2)}) collective-permute-start(bf16[96,1536]{1,0:T(8,128)(2,1)S(1)} %get-tuple-element.37), channel_id=1, source_target_pairs={{0,4},{4,0},{8,12},{12,8},{1,5},{5,1},{9,13},{13,9},{2,6},{6,2},{1... | collective-permute-start | bytes 884744 | tf_op jit(solution)/shard_map/ppermute | solution.py:444
  21.2 9.5 %collective-permute-start.1 = (bf16[96,1536]{1,0:T(8,128)(2,1)S(1)}, bf16[96,1536]{1,0:T(8,128)(2,1)S(1)}, u32[]{:S(2)}, u32[]{:S(2)}) collective-permute-start(bf16[96,1536]{1,0:T(8,128)(2,1)S(1)} %get-tuple-element.35.refs_5_), channel_id=1, source_target_pairs={{0,4},{4,0},{8,12},{12,8},{1,5},{5,1},{9,13},{13,9},{2,6},{6,2},{1... | collective-permute-start | bytes 884744 | tf_op jit(solution)/shard_map/ppermute | solution.py:444
  21.7 9.0 %collective-permute-start.4 = (bf16[2,48,1536]{2,1,0:T(8,128)(2,1)S(1)}, bf16[2,48,1536]{2,1,0:T(8,128)(2,1)S(1)}, u32[]{:S(2)}, u32[]{:S(2)}) collective-permute-start(bf16[2,48,1536]{2,1,0:T(8,128)(2,1)S(1)} %collective-permute-done.3.refs_1_.refs_3_), channel_id=1, source_target_pairs={{0,16},{16,0},{1,17},{17,1},{2,18},{18,2},{3,19},{19,3},{4,20},{20... | collective-permute-start | bytes 884744 | tf_op jit(solution)/shard_map/ppermute | solution.py:444
  28.1 12.6 %collective-permute-start.9 = (bf16[2,48,1536]{2,1,0:T(8,128)(2,1)S(1)}, bf16[2,48,1536]{2,1,0:T(8,128)(2,1)S(1)}, u32[]{:S(2)}, u32[]{:S(2)}) collective-permute-start(bf16[2,48,1536]{2,1,0:T(8,128)(2,1)S(1)} %collective-permute-done.8.refs_7_), channel_id=1, source_target_pairs={{1,0},{2,3},{5,4},{6,7},{9,8},{10,11},{13,12},{14,15},{17,16},{18,... | collective-permute-start | bytes 884744 | tf_op jit(solution)/shard_map/ppermute | solution.py:465
  29.6 15.3 %collective-permute-start.10 = (bf16[2,48,1536]{2,1,0:T(8,128)(2,1)S(1)}, bf16[2,48,1536]{2,1,0:T(8,128)(2,1)S(1)}, u32[]{:S(2)}, u32[]{:S(2)}) collective-permute-start(bf16[2,48,1536]{2,1,0:T(8,128)(2,1)S(1)} %broadcast_select_fusion.1.refs_1_.refs_5_), channel_id=1, source_target_pairs={{0,16},{16,0},{1,17},{17,1},{2,18},{18,2},{3,19},{19,3},{4,20},{20... | collective-permute-start | bytes 884744 | tf_op jit(solution)/shard_map/ppermute | solution.py:444
  31.1 14.5 %collective-permute-start.5 = (bf16[2,96,1536]{2,1,0:T(8,128)(2,1)S(1)}, bf16[2,96,1536]{2,1,0:T(8,128)(2,1)S(1)}, u32[]{:S(2)}, u32[]{:S(2)}) collective-permute-start(bf16[2,96,1536]{2,1,0:T(8,128)(2,1)S(1)} %combine.4.refs_5_), channel_id=1, source_target_pairs={{0,8},{4,12},{8,0},{12,4},{1,9},{5,13},{9,1},{13,5},{2,10},{6,14},... | collective-permute-start | bytes 1769480 | tf_op jit(solution)/shard_map/ppermute | solution.py:444
  36.5 10.0 %collective-permute-start.12 = (bf16[96,1536]{1,0:T(8,128)(2,1)S(1)}, bf16[96,1536]{1,0:T(8,128)(2,1)S(1)}, u32[]{:S(2)}, u32[]{:S(2)}) collective-permute-start(bf16[96,1536]{1,0:T(8,128)(2,1)S(1)} %get-tuple-element.41), channel_id=1, source_target_pairs={{0,4},{4,0},{8,12},{12,8},{1,5},{5,1},{9,13},{13,9},{2,6},{6,2},{1... | collective-permute-start | bytes 884744 | tf_op jit(solution)/shard_map/ppermute | solution.py:444
  36.5 10.0 %collective-permute-start.11 = (bf16[96,1536]{1,0:T(8,128)(2,1)S(1)}, bf16[96,1536]{1,0:T(8,128)(2,1)S(1)}, u32[]{:S(2)}, u32[]{:S(2)}) collective-permute-start(bf16[96,1536]{1,0:T(8,128)(2,1)S(1)} %get-tuple-element.40.refs_5_), channel_id=1, source_target_pairs={{0,4},{4,0},{8,12},{12,8},{1,5},{5,1},{9,13},{13,9},{2,6},{6,2},{1... | collective-permute-start | bytes 884744 | tf_op jit(solution)/shard_map/ppermute | solution.py:444
  40.8 8.2 %collective-permute-start.14 = (bf16[2,48,1536]{2,1,0:T(8,128)(2,1)S(1)}, bf16[2,48,1536]{2,1,0:T(8,128)(2,1)S(1)}, u32[]{:S(2)}, u32[]{:S(2)}) collective-permute-start(bf16[2,48,1536]{2,1,0:T(8,128)(2,1)S(1)} %broadcast_select_fusion.refs_3_.refs_7_), channel_id=1, source_target_pairs={{0,16},{16,0},{1,17},{17,1},{2,18},{18,2},{3,19},{19,3},{4,20},{20... | collective-permute-start | bytes 884744 | tf_op jit(solution)/shard_map/ppermute | solution.py:444
  46.9 13.6 %collective-permute-start.13 = (bf16[2,96,1536]{2,1,0:T(8,128)(2,1)S(1)}, bf16[2,96,1536]{2,1,0:T(8,128)(2,1)S(1)}, u32[]{:S(2)}, u32[]{:S(2)}) collective-permute-start(bf16[2,96,1536]{2,1,0:T(8,128)(2,1)S(1)} %combine.5.refs_7_), channel_id=1, source_target_pairs={{0,8},{4,12},{8,0},{12,4},{1,9},{5,13},{9,1},{13,5},{2,10},{6,14},... | collective-permute-start | bytes 1769480 | tf_op jit(solution)/shard_map/ppermute | solution.py:444
  52.8 8.6 %collective-permute-start.18 = (bf16[192,1536]{1,0:T(8,128)(2,1)S(1)}, bf16[192,1536]{1,0:T(8,128)(2,1)S(1)}, u32[]{:S(2)}, u32[]{:S(2)}) collective-permute-start(bf16[192,1536]{1,0:T(8,128)(2,1)S(1)} %get-tuple-element.43), channel_id=1, source_target_pairs={{0,4},{4,0},{8,12},{12,8},{1,5},{5,1},{9,13},{13,9},{2,6},{6,2},{1... | collective-permute-start | bytes 1769480 | tf_op jit(solution)/shard_map/ppermute | solution.py:444
  52.9 8.5 %collective-permute-start.17 = (bf16[192,1536]{1,0:T(8,128)(2,1)S(1)}, bf16[192,1536]{1,0:T(8,128)(2,1)S(1)}, u32[]{:S(2)}, u32[]{:S(2)}) collective-permute-start(bf16[192,1536]{1,0:T(8,128)(2,1)S(1)} %get-tuple-element.42.refs_7_), channel_id=1, source_target_pairs={{0,4},{4,0},{8,12},{12,8},{1,5},{5,1},{9,13},{13,9},{2,6},{6,2},{1... | collective-permute-start | bytes 1769480 | tf_op jit(solution)/shard_map/ppermute | solution.py:444
  53.4 10.4 %collective-permute-start.15 = (bf16[2,96,1536]{2,1,0:T(8,128)(2,1)S(1)}, bf16[2,96,1536]{2,1,0:T(8,128)(2,1)S(1)}, u32[]{:S(2)}, u32[]{:S(2)}) collective-permute-start(bf16[2,96,1536]{2,1,0:T(8,128)(2,1)S(1)} %activations.5.refs_4_.refs_1_.refs_3_), channel_id=1, source_target_pairs={{0,4},{4,0},{8,12},{12,8},{1,5},{5,1},{9,13},{13,9},{2,6},{6,2},{1... | collective-permute-start | bytes 1769480 | tf_op jit(solution)/shard_map/ppermute | solution.py:444
  61.4 2.5 %collective-permute-start.16 = (bf16[2,96,1536]{2,1,0:T(8,128)(2,1)S(1)}, bf16[2,96,1536]{2,1,0:T(8,128)(2,1)S(1)}, u32[]{:S(2)}, u32[]{:S(2)}) collective-permute-start(bf16[2,96,1536]{2,1,0:T(8,128)(2,1)S(1)} %activations.6.refs_10_.refs_2_.refs_4_), channel_id=1, source_target_pairs={{0,4},{4,0},{8,12},{12,8},{1,5},{5,1},{9,13},{13,9},{2,6},{6,2},{1... | collective-permute-start | bytes 1769480 | tf_op jit(solution)/shard_map/ppermute | solution.py:444
  61.6 11.6 %collective-permute-start.20 = (bf16[2,192,512]{2,1,0:T(8,128)(2,1)S(1)}, bf16[2,192,512]{2,1,0:T(8,128)(2,1)S(1)}, u32[]{:S(2)}, u32[]{:S(2)}) collective-permute-start(bf16[2,192,512]{2,1,0:T(8,128)(2,1)S(1)} %pad_maximum_fusion.refs_9_), channel_id=1, source_target_pairs={{0,8},{4,12},{8,0},{12,4},{1,9},{5,13},{9,1},{13,5},{2,10},{6,14},... | collective-permute-start | bytes 1179656 | tf_op jit(solution)/shard_map/ppermute | solution.py:444
  67.4 12.2 %collective-permute-start.19 = (bf16[96,1536]{1,0:T(8,128)(2,1)S(1)}, bf16[96,1536]{1,0:T(8,128)(2,1)S(1)}, u32[]{:S(2)}, u32[]{:S(2)}) collective-permute-start(bf16[96,1536]{1,0:T(8,128)(2,1)S(1)} %get-tuple-element.46), channel_id=1, source_target_pairs={{0,16},{16,0},{1,17},{17,1},{2,18},{18,2},{3,19},{19,3},{4,20},{20... | collective-permute-start | bytes 884744 | tf_op jit(solution)/shard_map/ppermute | solution.py:444
  73.7 6.1 %collective-permute-start.23 = (bf16[2,192,512]{2,1,0:T(8,128)(2,1)S(1)}, bf16[2,192,512]{2,1,0:T(8,128)(2,1)S(1)}, u32[]{:S(2)}, u32[]{:S(2)}) collective-permute-start(bf16[2,192,512]{2,1,0:T(8,128)(2,1)S(1)} %activations.7.refs_4_.refs_5_.refs_1_), channel_id=1, source_target_pairs={{0,4},{4,0},{8,12},{12,8},{1,5},{5,1},{9,13},{13,9},{2,6},{6,2},{1... | collective-permute-start | bytes 1179656 | tf_op jit(solution)/shard_map/ppermute | solution.py:444
  74.1 11.6 %collective-permute-start.22 = (bf16[2,96,1024]{2,1,0:T(8,128)(2,1)S(1)}, bf16[2,96,1024]{2,1,0:T(8,128)(2,1)S(1)}, u32[]{:S(2)}, u32[]{:S(2)}) collective-permute-start(bf16[2,96,1024]{2,1,0:T(8,128)(2,1)S(1)} %combine.6.refs_6_), channel_id=1, source_target_pairs={{0,8},{4,12},{8,0},{12,4},{1,9},{5,13},{9,1},{13,5},{2,10},{6,14},... | collective-permute-start | bytes 1179656 | tf_op jit(solution)/shard_map/ppermute | solution.py:444
  86.2 10.4 %collective-permute-start.24 = (bf16[2,96,1024]{2,1,0:T(8,128)(2,1)S(1)}, bf16[2,96,1024]{2,1,0:T(8,128)(2,1)S(1)}, u32[]{:S(2)}, u32[]{:S(2)}) collective-permute-start(bf16[2,96,1024]{2,1,0:T(8,128)(2,1)S(1)} %activations.8.refs_4_.refs_1_.refs_5_), channel_id=1, source_target_pairs={{0,4},{4,0},{8,12},{12,8},{1,5},{5,1},{9,13},{13,9},{2,6},{6,2},{1... | collective-permute-start | bytes 1179656 | tf_op jit(solution)/shard_map/ppermute | solution.py:444
  86.6 12.5 %collective-permute-start.26 = (bf16[2,96,1024]{2,1,0:T(8,128)(2,1)S(1)}, bf16[2,96,1024]{2,1,0:T(8,128)(2,1)S(1)}, u32[]{:S(2)}, u32[]{:S(2)}) collective-permute-start(bf16[2,96,1024]{2,1,0:T(8,128)(2,1)S(1)} %combine.7.refs_8_), channel_id=1, source_target_pairs={{0,8},{4,12},{8,0},{12,4},{1,9},{5,13},{9,1},{13,5},{2,10},{6,14},... | collective-permute-start | bytes 1179656 | tf_op jit(solution)/shard_map/ppermute | solution.py:444
  88.4 10.7 %collective-permute-start.21 = (bf16[48,1536]{1,0:T(8,128)(2,1)S(1)}, bf16[48,1536]{1,0:T(8,128)(2,1)S(1)}, u32[]{:S(2)}, u32[]{:S(2)}) collective-permute-start(bf16[48,1536]{1,0:T(8,128)(2,1)S(1)} %fold.6.refs_5_), channel_id=1, source_target_pairs={{0,1},{1,0},{2,3},{3,2},{4,5},{5,4},{6,7},{7,6},{8,9},{9,8},{10,11... | collective-permute-start | bytes 442376 | tf_op jit(solution)/shard_map/ppermute | solution.py:444
  99.7 1.8 %collective-permute-start.27 = (bf16[2,96,1024]{2,1,0:T(8,128)(2,1)S(1)}, bf16[2,96,1024]{2,1,0:T(8,128)(2,1)S(1)}, u32[]{:S(2)}, u32[]{:S(2)}) collective-permute-start(bf16[2,96,1024]{2,1,0:T(8,128)(2,1)S(1)} %activations.9.refs_1_.refs_6_), channel_id=1, source_target_pairs={{0,4},{4,0},{8,12},{12,8},{1,5},{5,1},{9,13},{13,9},{2,6},{6,2},{1... | collective-permute-start | bytes 1179656 | tf_op jit(solution)/shard_map/ppermute | solution.py:444
  99.8 6.3 %collective-permute-start.25 = (bf16[48,1536]{1,0:T(8,128)(2,1)S(1)}, bf16[48,1536]{1,0:T(8,128)(2,1)S(1)}, u32[]{:S(2)}, u32[]{:S(2)}) collective-permute-start(bf16[48,1536]{1,0:T(8,128)(2,1)S(1)} %get-tuple-element.53), channel_id=1, source_target_pairs={{0,16},{16,0},{1,17},{17,1},{2,18},{18,2},{3,19},{19,3},{4,20},{20... | collective-permute-start | bytes 442376 | tf_op jit(solution)/shard_map/ppermute | solution.py:444
  103.9 13.1 %collective-permute-start.29 = (bf16[48,1536]{1,0:T(8,128)(2,1)S(1)}, bf16[48,1536]{1,0:T(8,128)(2,1)S(1)}, u32[]{:S(2)}, u32[]{:S(2)}) collective-permute-start(bf16[48,1536]{1,0:T(8,128)(2,1)S(1)} %get-tuple-element.55), channel_id=1, source_target_pairs={{0,16},{16,0},{1,17},{17,1},{2,18},{18,2},{3,19},{19,3},{4,20},{20... | collective-permute-start | bytes 442376 | tf_op jit(solution)/shard_map/ppermute | solution.py:444
  106.1 19.2 %collective-permute-start.28 = (bf16[48,1536]{1,0:T(8,128)(2,1)S(1)}, bf16[48,1536]{1,0:T(8,128)(2,1)S(1)}, u32[]{:S(2)}, u32[]{:S(2)}) collective-permute-start(bf16[48,1536]{1,0:T(8,128)(2,1)S(1)} %fold.8.refs_9_), channel_id=1, source_target_pairs={{0,2},{1,3},{2,0},{3,1},{4,6},{5,7},{6,4},{7,5},{8,10},{9,11},{10,... | collective-permute-start | bytes 442376 | tf_op jit(solution)/shard_map/ppermute | solution.py:444
  117.0 8.3 %collective-permute-start.30 = (bf16[48,1536]{1,0:T(8,128)(2,1)S(1)}, bf16[48,1536]{1,0:T(8,128)(2,1)S(1)}, u32[]{:S(2)}, u32[]{:S(2)}) collective-permute-start(bf16[48,1536]{1,0:T(8,128)(2,1)S(1)} %fold.9.refs_9_), channel_id=1, source_target_pairs={{0,3},{1,2},{2,1},{3,0},{4,7},{5,6},{6,5},{7,4},{8,11},{9,10},{10,... | collective-permute-start | bytes 442376 | tf_op jit(solution)/shard_map/ppermute | solution.py:444

commit v11 on v10

--- a/solution.py
+++ b/solution.py
@@ -570,9 +570,9 @@
     back1 = fold(core, stay1[rows:], near1[rows:], BF16, [total])
     far1 = swap(back1, "gz", 4, 1)
     part, = inward(((2, 0),), *spans[0], None, 0, None, None, [back1])
-    last = ready(3, [part])
-    last = cross(4, last)
+    last = cross(4, [part])
     last = finish(0, (1,), last)
+    last = ready(3, last)
     stay2, go2 = inward(((3, 0),), *spans[1], part, 0, (0, 1), 1, last)
     near2 = swap(go2, "gx", 2, 1)
     total = fold(core, total, far1, F32, [stay2])

time: 126 us -> 126 us (level)
  waiting for transfers between devices: 22.5 us -> 21 us
    ppermute x27, waiting for transfers between devices: 18.8 us -> 17.3 us  [swap(): return lax.ppermute(value, axis, [(i, i ^ bits) for i in range(size)])]
  transfers between devices with their start and end apart: 31 -> 31, of which waited for: 10 -> 11; matrix products, arithmetic and copies ran while one was open for 0% -> 0% of each run, Pallas kernels for 49% -> 49%
where the time goes in v11:
time: 126 us
  Pallas kernels  62.9 us (50%)
  starting transfers between devices  38.7 us (31%)
  waiting for transfers between devices  21 us (17%)
  other arithmetic  1.97 us (2%)
    pallas_call x30, Pallas kernels, call(): pl.pallas_call(kernel, grid_spec=pltpu.PrefetchScalarGridSpec(num_scalar_...  62.9 us
    ppermute x27, starting transfers between devices, swap(): return lax.ppermute(value, axis, [(i, i ^ bits) for i in range(size)])  34.6 us
    ppermute x27, waiting for transfers between devices, swap(): return lax.ppermute(value, axis, [(i, i ^ bits) for i in range(size)])  17.3 us
    ppermute x1, waiting for transfers between devices, cube_body(): second_on = lax.ppermute(second, 'gz', outward)  3.7 us
  transfers between devices with their start and end apart: 31, of which 11 were waited for; matrix products, arithmetic and copies ran while one was open for 0% of the time, Pallas kernels for 49%

profile of v11, /device:TPU:0, one launch (start us, length us, event | category | flops | bytes accessed | tf_op | source)
XLA Modules:
  0.0 125.7 jit_solution(7097382836095110397)
XLA Ops:
  0.6 1.0 pad_maximum_fusion.1.refs_1_
  1.6 3.1 %collective-permute-start.3 = (bf16[2,48,1536]{2,1,0:T(8,128)(2,1)S(1)}, bf16[2,48,1536]{2,1,0:T(8,128)(2,1)S(1)}, u32[]{:S(2)}, u32[]{:S(2)}) collective-permute-start(bf16[2,48,1536]{2,1,0:T(8,128)(2,1)S(1)} %pad_maximum_fusion.1.refs_1_), channel_id=1, source_target_pairs={{0,1},{1,0},{2,3},{3,2},{4,5},{5,4},{6,7},{7,6},{8,9},{9,8},{10,11... | collective-permute-start | bytes 884744 | tf_op jit(solution)/shard_map/ppermute | solution.py:444
  4.7 0.7 collective-permute-start.6
  5.4 1.6 %collective-permute-start = (bf16[2,48,1536]{2,1,0:T(8,128)(2,1)S(1)}, bf16[2,48,1536]{2,1,0:T(8,128)(2,1)S(1)}, u32[]{:S(2)}, u32[]{:S(2)}) collective-permute-start(bf16[2,48,1536]{2,1,0:T(8,128)(2,1)S(1)} %pad_maximum_fusion.1.refs_1_), channel_id=1, source_target_pairs={{0,16},{16,0},{1,17},{17,1},{2,18},{18,2},{3,19},{19,3},{4,20},{20... | collective-permute-start | bytes 884744 | tf_op jit(solution)/shard_map/ppermute | solution.py:444
  7.0 4.8 %collective-permute-done.3.refs_1_.refs_3_ = bf16[2,48,1536]{2,1,0:T(8,128)(2,1)S(1)} collective-permute-done((bf16[2,48,1536]{2,1,0:T(8,128)(2,1)S(1)}, bf16[2,48,1536]{2,1,0:T(8,128)(2,1)S(1)}, u32[]{:S(2)}, u32[]{:S(2)}) %collective-permute-start.3) | collective-permute-done | bytes 294944 | tf_op jit(solution)/shard_map/ppermute | solution.py:444
  11.7 0.7 collective-permute-start.8
  12.4 1.3 %collective-permute-start.7 = (bf16[2,48,1536]{2,1,0:T(8,128)(2,1)S(1)}, bf16[2,48,1536]{2,1,0:T(8,128)(2,1)S(1)}, u32[]{:S(2)}, u32[]{:S(2)}) collective-permute-start(bf16[2,48,1536]{2,1,0:T(8,128)(2,1)S(1)} %collective-permute-done.6), channel_id=1, source_target_pairs={{1,0},{2,3},{5,4},{6,7},{9,8},{10,11},{13,12},{14,15},{17,16},{18,... | collective-permute-start | bytes 884744 | tf_op jit(solution)/shard_map/ppermute | solution.py:464
  13.7 3.8 %bring.1 = (bf16[1536,1536]{1,0:T(8,128)(2,1)S(1)}, bf16[1536,1536]{1,0:T(8,128)(2,1)S(1)}) custom-call(s32[1]{0:T(128)} %bitcast.refs_0_, bf16[1536,3072]{1,0:T(8,128)(2,1)} %refs_3_.1, bf16[3072,1536]{1,0:T(8,128)(2,1)} %refs_4_.1), custom_call_target="tpu_custom_call" | custom-call | bytes 9437184 | tf_op jit(solution)/shard_map/bring/pallas_call | solution.py:68
  17.6 3.6 %sums_send.3 = (bf16[96,1536]{1,0:T(8,128)(2,1)S(1)}, bf16[96,1536]{1,0:T(8,128)(2,1)S(1)}) custom-call(s32[1]{0:T(128)} %bitcast.refs_0_, bf16[2,48,1536]{2,1,0:T(8,128)(2,1)S(1)} %pad_maximum_fusion.1.refs_1_, bf16[2,48,1536]{2,1,0:T(8,128)(2,1)S(1)} %collective-permute-done.refs_2_, ...), custom_call_target="tpu_custom_call" | custom-call | flops 905969664 | bytes 9437184 | tf_op jit(solution)/shard_map/sums_send/pallas_call | solution.py:68
  21.2 0.5 collective-permute-start.1
  21.7 1.7 %collective-permute-start.4 = (bf16[2,48,1536]{2,1,0:T(8,128)(2,1)S(1)}, bf16[2,48,1536]{2,1,0:T(8,128)(2,1)S(1)}, u32[]{:S(2)}, u32[]{:S(2)}) collective-permute-start(bf16[2,48,1536]{2,1,0:T(8,128)(2,1)S(1)} %collective-permute-done.3.refs_1_.refs_3_), channel_id=1, source_target_pairs={{0,16},{16,0},{1,17},{17,1},{2,18},{18,2},{3,19},{19,3},{4,20},{20... | collective-permute-start | bytes 884744 | tf_op jit(solution)/shard_map/ppermute | solution.py:444
  23.4 4.7 %bring_and_sum.1 = (f32[2,96,1536]{2,1,0:T(8,128)S(1)}, bf16[1536,1536]{1,0:T(8,128)(2,1)S(1)}, bf16[1536,1536]{1,0:T(8,128)(2,1)S(1)}) custom-call(s32[1]{0:T(128)} %bitcast.refs_0_, bf16[2,48,1536]{2,1,0:T(8,128)(2,1)S(1)} %pad_maximum_fusion.1.refs_1_, bf16[2,48,1536]{2,1,0:T(8,128)(2,1)S(1)} %collective-permute-done.refs_2_, bf16[1536,3072]{1,0:T(8,128)(2,1)} %refs_3_.1, ...), custom_call_target="tpu_custom_call" | custom-call | flops 905969664 | bytes 9437184 | tf_op jit(solution)/shard_map/bring_and_sum/pallas_call | solution.py:68
  28.1 1.5 %collective-permute-start.9 = (bf16[2,48,1536]{2,1,0:T(8,128)(2,1)S(1)}, bf16[2,48,1536]{2,1,0:T(8,128)(2,1)S(1)}, u32[]{:S(2)}, u32[]{:S(2)}) collective-permute-start(bf16[2,48,1536]{2,1,0:T(8,128)(2,1)S(1)} %collective-permute-done.8.refs_7_), channel_id=1, source_target_pairs={{1,0},{2,3},{5,4},{6,7},{9,8},{10,11},{13,12},{14,15},{17,16},{18,... | collective-permute-start | bytes 884744 | tf_op jit(solution)/shard_map/ppermute | solution.py:465
  29.6 0.4 collective-permute-start.10
  30.1 0.7 collective-permute-done.4.refs_5_.refs_2_.refs_4_
  30.7 0.4 combine.4.refs_5_
  31.1 1.7 %collective-permute-start.5 = (bf16[2,96,1536]{2,1,0:T(8,128)(2,1)S(1)}, bf16[2,96,1536]{2,1,0:T(8,128)(2,1)S(1)}, u32[]{:S(2)}, u32[]{:S(2)}) collective-permute-start(bf16[2,96,1536]{2,1,0:T(8,128)(2,1)S(1)} %combine.4.refs_5_), channel_id=1, source_target_pairs={{0,8},{4,12},{8,0},{12,4},{1,9},{5,13},{9,1},{13,5},{2,10},{6,14},... | collective-permute-start | bytes 1769480 | tf_op jit(solution)/shard_map/ppermute | solution.py:444
  32.9 3.6 %sums_send.4 = (bf16[96,1536]{1,0:T(8,128)(2,1)S(1)}, bf16[96,1536]{1,0:T(8,128)(2,1)S(1)}) custom-call(s32[1]{0:T(128)} %bitcast.refs_0_, bf16[2,48,1536]{2,1,0:T(8,128)(2,1)S(1)} %collective-permute-done.3.refs_1_.refs_3_, bf16[2,48,1536]{2,1,0:T(8,128)(2,1)S(1)} %collective-permute-done.4.refs_5_.refs_2_.refs_4_, ...), custom_call_target="tpu_custom_call" | custom-call | flops 905969664 | bytes 9437184 | tf_op jit(solution)/shard_map/sums_send/pallas_call | solution.py:68
  36.5 0.5 collective-permute-start.11
  37.0 3.7 %collective-permute-done.9.refs_6_ = bf16[2,48,1536]{2,1,0:T(8,128)(2,1)S(1)} collective-permute-done((bf16[2,48,1536]{2,1,0:T(8,128)(2,1)S(1)}, bf16[2,48,1536]{2,1,0:T(8,128)(2,1)S(1)}, u32[]{:S(2)}, u32[]{:S(2)}) %collective-permute-start.9) | collective-permute-done | bytes 294944 | tf_op jit(solution)/shard_map/ppermute | solution.py:465
  40.8 0.6 collective-permute-start.14
  41.4 3.6 %sums_keep.2.refs_5_.refs_1_ = f32[2,96,1536]{2,1,0:T(8,128)S(1)} custom-call(s32[1]{0:T(128)} %bitcast.refs_0_, bf16[2,48,1536]{2,1,0:T(8,128)(2,1)S(1)} %collective-permute-done.3.refs_1_.refs_3_, bf16[2,48,1536]{2,1,0:T(8,128)(2,1)S(1)} %collective-permute-done.4.refs_5_.refs_2_.refs_4_, bf16[1536,1536]{1,0:T(8,128)(2,1)S(1)} %get-tuple-element.38.refs_3_.refs_5_, ...), custom_call_target="tpu_custom_call" | custom-call | flops 905969664 | bytes 9437184 | tf_op jit(solution)/shard_map/sums_keep/pallas_call | solution.py:68
  45.0 0.7 collective-permute-done.5.refs_4_
  45.7 0.8 activations.5.refs_4_.refs_1_.refs_3_
  46.5 0.4 combine.5.refs_7_
  46.9 1.7 %collective-permute-start.13 = (bf16[2,96,1536]{2,1,0:T(8,128)(2,1)S(1)}, bf16[2,96,1536]{2,1,0:T(8,128)(2,1)S(1)}, u32[]{:S(2)}, u32[]{:S(2)}) collective-permute-start(bf16[2,96,1536]{2,1,0:T(8,128)(2,1)S(1)} %combine.5.refs_7_), channel_id=1, source_target_pairs={{0,8},{4,12},{8,0},{12,4},{1,9},{5,13},{9,1},{13,5},{2,10},{6,14},... | collective-permute-start | bytes 1769480 | tf_op jit(solution)/shard_map/ppermute | solution.py:444
  48.7 0.3 collective-permute-done.14.refs_4_.refs_8_
  49.0 3.8 %sums_send.5 = (bf16[192,1536]{1,0:T(8,128)(2,1)S(1)}, bf16[192,1536]{1,0:T(8,128)(2,1)S(1)}) custom-call(s32[1]{0:T(128)} %bitcast.refs_0_, bf16[2,48,1536]{2,1,0:T(8,128)(2,1)S(1)} %broadcast_select_fusion.1.refs_1_.refs_5_, bf16[2,48,1536]{2,1,0:T(8,128)(2,1)S(1)} %collective-permute-done.10.refs_6_.refs_2_, ...), custom_call_target="tpu_custom_call" | custom-call | flops 1811939328 | bytes 9437184 | tf_op jit(solution)/shard_map/sums_send/pallas_call | solution.py:68
  52.9 0.5 collective-permute-start.17
  53.4 0.1 collective-permute-start.15
  53.5 3.9 %sums_keep.3.refs_5_.refs_1_ = f32[2,192,1536]{2,1,0:T(8,128)S(1)} custom-call(s32[1]{0:T(128)} %bitcast.refs_0_, bf16[2,48,1536]{2,1,0:T(8,128)(2,1)S(1)} %broadcast_select_fusion.1.refs_1_.refs_5_, bf16[2,48,1536]{2,1,0:T(8,128)(2,1)S(1)} %collective-permute-done.10.refs_6_.refs_2_, bf16[2,48,1536]{2,1,0:T(8,128)(2,1)S(1)} %broadcast_select_fusion.refs_3_.refs_7_, ...), custom_call_target="tpu_custom_call" | custom-call | flops 1811939328 | bytes 9437184 | tf_op jit(solution)/shard_map/sums_keep/pallas_call | solution.py:68
  57.4 3.2 %collective-permute-done.13.refs_4_ = bf16[2,96,1536]{2,1,0:T(8,128)(2,1)S(1)} collective-permute-done((bf16[2,96,1536]{2,1,0:T(8,128)(2,1)S(1)}, bf16[2,96,1536]{2,1,0:T(8,128)(2,1)S(1)}, u32[]{:S(2)}, u32[]{:S(2)}) %collective-permute-start.13) | collective-permute-done | bytes 589856 | tf_op jit(solution)/shard_map/ppermute | solution.py:444
  60.5 0.8 activations.6.refs_10_.refs_2_.refs_4_
  61.5 0.1 fusion.4
  61.6 1.7 %collective-permute-start.20 = (bf16[2,192,512]{2,1,0:T(8,128)(2,1)S(1)}, bf16[2,192,512]{2,1,0:T(8,128)(2,1)S(1)}, u32[]{:S(2)}, u32[]{:S(2)}) collective-permute-start(bf16[2,192,512]{2,1,0:T(8,128)(2,1)S(1)} %pad_maximum_fusion.refs_9_), channel_id=1, source_target_pairs={{0,8},{4,12},{8,0},{12,4},{1,9},{5,13},{9,1},{13,5},{2,10},{6,14},... | collective-permute-start | bytes 1179656 | tf_op jit(solution)/shard_map/ppermute | solution.py:444
  63.4 0.4 arrange.1
  63.8 3.6 %back.4 = (f32[96,1536]{1,0:T(8,128)S(1)}, bf16[96,1536]{1,0:T(8,128)(2,1)S(1)}) custom-call(s32[1]{0:T(128)} %bitcast.refs_0_, bf16[2,96,1536]{2,1,0:T(8,128)(2,1)S(1)} %activations.5.refs_4_.refs_1_.refs_3_, bf16[2,96,1536]{2,1,0:T(8,128)(2,1)S(1)} %activations.6.refs_10_.refs_2_.refs_4_, bf16[2,96,1536]{2,1,0:T(8,128)(2,1)S(1)} %collective-permute-done.15.refs_3_, ...), custom_call_target="tpu_custom_call" | custom-call | flops 1811939328 | bytes 10616832 | tf_op jit(solution)/shard_map/back/pallas_call | solution.py:68
  67.4 1.6 %collective-permute-start.19 = (bf16[96,1536]{1,0:T(8,128)(2,1)S(1)}, bf16[96,1536]{1,0:T(8,128)(2,1)S(1)}, u32[]{:S(2)}, u32[]{:S(2)}) collective-permute-start(bf16[96,1536]{1,0:T(8,128)(2,1)S(1)} %get-tuple-element.46), channel_id=1, source_target_pairs={{0,16},{16,0},{1,17},{17,1},{2,18},{18,2},{3,19},{19,3},{4,20},{20... | collective-permute-start | bytes 884744 | tf_op jit(solution)/shard_map/ppermute | solution.py:444
  69.0 4.2 %collective-permute-done.20.refs_4_ = bf16[2,192,512]{2,1,0:T(8,128)(2,1)S(1)} collective-permute-done((bf16[2,192,512]{2,1,0:T(8,128)(2,1)S(1)}, bf16[2,192,512]{2,1,0:T(8,128)(2,1)S(1)}, u32[]{:S(2)}, u32[]{:S(2)}) %collective-permute-start.20) | collective-permute-done | bytes 393248 | tf_op jit(solution)/shard_map/ppermute | solution.py:444
  73.2 0.5 activations.7.refs_4_.refs_5_.refs_1_
  73.8 0.3 combine.6.refs_6_
  74.1 1.7 %collective-permute-start.22 = (bf16[2,96,1024]{2,1,0:T(8,128)(2,1)S(1)}, bf16[2,96,1024]{2,1,0:T(8,128)(2,1)S(1)}, u32[]{:S(2)}, u32[]{:S(2)}) collective-permute-start(bf16[2,96,1024]{2,1,0:T(8,128)(2,1)S(1)} %combine.6.refs_6_), channel_id=1, source_target_pairs={{0,8},{4,12},{8,0},{12,4},{1,9},{5,13},{9,1},{13,5},{2,10},{6,14},... | collective-permute-start | bytes 1179656 | tf_op jit(solution)/shard_map/ppermute | solution.py:444
  75.8 3.8 %weight_grads.4 = (f32[1536,3072]{1,0:T(8,128)}, f32[3072,1536]{1,0:T(8,128)}, f32[8,128]{1,0:T(8,128)S(1)}) custom-call(s32[1]{0:T(128)} %bitcast.refs_0_, bf16[1536,384]{1,0:T(8,128)(2,1)S(1)} %get-tuple-element.44.refs_7_.refs_1_, bf16[384,1536]{1,0:T(8,128)(2,1)S(1)} %get-tuple-element.47.refs_2_, ...), custom_call_target="tpu_custom_call" | custom-call | flops 1207959552 | bytes 6291456 | tf_op jit(solution)/shard_map/weight_grads/pallas_call | solution.py:68
  79.8 1.6 %back.5.refs_4_.refs_5_ = f32[192,1536]{1,0:T(8,128)S(1)} custom-call(s32[1]{0:T(128)} %bitcast.refs_0_, bf16[2,192,512]{2,1,0:T(8,128)(2,1)S(1)} %activations.7.refs_4_.refs_5_.refs_1_, bf16[2,192,512]{2,1,0:T(8,128)(2,1)S(1)} %collective-permute-done.23.refs_2_.refs_5_, bf16[1536,1536]{1,0:T(8,128)(2,1)S(1)} %get-tuple-element.38.refs_3_.refs_5_, ...), custom_call_target="tpu_custom_call" | custom-call | flops 603979776 | bytes 4325376 | tf_op jit(solution)/shard_map/back/pallas_call | solution.py:68
  81.4 0.3 combine.7.refs_8_
  81.7 3.9 %weight_grads.5 = (f32[1536,3072]{1,0:T(8,128)}, f32[3072,1536]{1,0:T(8,128)}, f32[8,128]{1,0:T(8,128)S(1)}) custom-call(s32[1]{0:T(128)} %bitcast.refs_0_, bf16[1536,384]{1,0:T(8,128)(2,1)S(1)} %get-tuple-element.44.refs_7_.refs_1_, bf16[384,1536]{1,0:T(8,128)(2,1)S(1)} %get-tuple-element.47.refs_2_, ...), custom_call_target="tpu_custom_call", output_to_operand_aliasing={{0}: (6, {}), {1}: (7, {})} | custom-call | flops 1207959552 | bytes 6291456 | tf_op jit(solution)/shard_map/weight_grads/pallas_call | solution.py:68
  85.5 0.1 collective-permute-done.22.refs_4_
  85.6 0.6 activations.8.refs_1_.refs_6_.refs_5_
  86.2 0.2 collective-permute-start.24
  86.4 1.7 %collective-permute-start.26 = (bf16[2,96,1024]{2,1,0:T(8,128)(2,1)S(1)}, bf16[2,96,1024]{2,1,0:T(8,128)(2,1)S(1)}, u32[]{:S(2)}, u32[]{:S(2)}) collective-permute-start(bf16[2,96,1024]{2,1,0:T(8,128)(2,1)S(1)} %combine.7.refs_8_), channel_id=1, source_target_pairs={{0,8},{4,12},{8,0},{12,4},{1,9},{5,13},{9,1},{13,5},{2,10},{6,14},... | collective-permute-start | bytes 1179656 | tf_op jit(solution)/shard_map/ppermute | solution.py:444
  88.1 4.4 %collective-permute-start.21 = (bf16[48,1536]{1,0:T(8,128)(2,1)S(1)}, bf16[48,1536]{1,0:T(8,128)(2,1)S(1)}, u32[]{:S(2)}, u32[]{:S(2)}) collective-permute-start(bf16[48,1536]{1,0:T(8,128)(2,1)S(1)} %fold.6.refs_5_), channel_id=1, source_target_pairs={{0,1},{1,0},{2,3},{3,2},{4,5},{5,4},{6,7},{7,6},{8,9},{9,8},{10,11... | collective-permute-start | bytes 442376 | tf_op jit(solution)/shard_map/ppermute | solution.py:444
  92.5 2.4 %back.6 = (f32[48,1536]{1,0:T(8,128)S(1)}, bf16[48,1536]{1,0:T(8,128)(2,1)S(1)}) custom-call(s32[1]{0:T(128)} %bitcast.refs_0_, bf16[2,96,1024]{2,1,0:T(8,128)(2,1)S(1)} %activations.8.refs_1_.refs_6_.refs_5_, bf16[2,96,1024]{2,1,0:T(8,128)(2,1)S(1)} %collective-permute-done.24.refs_2_.refs_5_, bf16[1536,1536]{1,0:T(8,128)(2,1)S(1)} %get-tuple-element.38.refs_3_.refs_5_, ...), custom_call_target="tpu_custom_call" | custom-call | flops 603979776 | bytes 6881280 | tf_op jit(solution)/shard_map/back/pallas_call | solution.py:68
  94.9 1.7 %collective-permute-done.21.refs_2_ = bf16[48,1536]{1,0:T(8,128)(2,1)S(1)} collective-permute-done((bf16[48,1536]{1,0:T(8,128)(2,1)S(1)}, bf16[48,1536]{1,0:T(8,128)(2,1)S(1)}, u32[]{:S(2)}, u32[]{:S(2)}) %collective-permute-start.21) | collective-permute-done | bytes 147488 | tf_op jit(solution)/shard_map/ppermute | solution.py:444
  96.7 1.2 collective-permute-done.26.refs_4_
  97.8 0.6 activations.9.refs_1_.refs_6_
  98.5 1.7 %collective-permute-start.25 = (bf16[48,1536]{1,0:T(8,128)(2,1)S(1)}, bf16[48,1536]{1,0:T(8,128)(2,1)S(1)}, u32[]{:S(2)}, u32[]{:S(2)}) collective-permute-start(bf16[48,1536]{1,0:T(8,128)(2,1)S(1)} %get-tuple-element.53), channel_id=1, source_target_pairs={{0,16},{16,0},{1,17},{17,1},{2,18},{18,2},{3,19},{19,3},{4,20},{20... | collective-permute-start | bytes 442376 | tf_op jit(solution)/shard_map/ppermute | solution.py:444
  100.2 2.4 %back.7 = (f32[48,1536]{1,0:T(8,128)S(1)}, bf16[48,1536]{1,0:T(8,128)(2,1)S(1)}) custom-call(s32[1]{0:T(128)} %bitcast.refs_0_, bf16[2,96,1024]{2,1,0:T(8,128)(2,1)S(1)} %activations.9.refs_1_.refs_6_, bf16[2,96,1024]{2,1,0:T(8,128)(2,1)S(1)} %collective-permute-done.27.refs_2_.refs_6_, bf16[1536,1536]{1,0:T(8,128)(2,1)S(1)} %get-tuple-element.38.refs_3_.refs_5_, ...), custom_call_target="tpu_custom_call" | custom-call | flops 603979776 | bytes 6881280 | tf_op jit(solution)/shard_map/back/pallas_call | solution.py:68
  102.7 1.7 %collective-permute-start.29 = (bf16[48,1536]{1,0:T(8,128)(2,1)S(1)}, bf16[48,1536]{1,0:T(8,128)(2,1)S(1)}, u32[]{:S(2)}, u32[]{:S(2)}) collective-permute-start(bf16[48,1536]{1,0:T(8,128)(2,1)S(1)} %get-tuple-element.55), channel_id=1, source_target_pairs={{0,16},{16,0},{1,17},{17,1},{2,18},{18,2},{3,19},{19,3},{4,20},{20... | collective-permute-start | bytes 442376 | tf_op jit(solution)/shard_map/ppermute | solution.py:444
  104.4 0.4 collective-permute-done.25.refs_2_
  104.8 5.3 %collective-permute-start.28 = (bf16[48,1536]{1,0:T(8,128)(2,1)S(1)}, bf16[48,1536]{1,0:T(8,128)(2,1)S(1)}, u32[]{:S(2)}, u32[]{:S(2)}) collective-permute-start(bf16[48,1536]{1,0:T(8,128)(2,1)S(1)} %fold.8.refs_9_), channel_id=1, source_target_pairs={{0,2},{1,3},{2,0},{3,1},{4,6},{5,7},{6,4},{7,5},{8,10},{9,11},{10,... | collective-permute-start | bytes 442376 | tf_op jit(solution)/shard_map/ppermute | solution.py:444
  110.1 6.5 %weight_grads.6 = (f32[1536,3072]{1,0:T(8,128)}, f32[3072,1536]{1,0:T(8,128)}, f32[8,128]{1,0:T(8,128)S(1)}) custom-call(s32[1]{0:T(128)} %bitcast.refs_0_, bf16[1536,384]{1,0:T(8,128)(2,1)S(1)} %get-tuple-element.44.refs_7_.refs_1_, bf16[384,1536]{1,0:T(8,128)(2,1)S(1)} %get-tuple-element.47.refs_2_, ...), custom_call_target="tpu_custom_call", output_to_operand_aliasing={{0}: (7, {}), {1}: (8, {})} | custom-call | flops 2415919104 | bytes 12582912 | tf_op jit(solution)/shard_map/weight_grads/pallas_call | solution.py:68
  116.7 1.7 %collective-permute-start.30 = (bf16[48,1536]{1,0:T(8,128)(2,1)S(1)}, bf16[48,1536]{1,0:T(8,128)(2,1)S(1)}, u32[]{:S(2)}, u32[]{:S(2)}) collective-permute-start(bf16[48,1536]{1,0:T(8,128)(2,1)S(1)} %fold.9.refs_9_), channel_id=1, source_target_pairs={{0,3},{1,2},{2,1},{3,0},{4,7},{5,6},{6,5},{7,4},{8,11},{9,10},{10,... | collective-permute-start | bytes 442376 | tf_op jit(solution)/shard_map/ppermute | solution.py:444
  118.4 6.5 %weight_grads.7 = (f32[1536,3072]{1,0:T(8,128)}, f32[3072,1536]{1,0:T(8,128)}, f32[8,128]{1,0:T(8,128)}) custom-call(s32[1]{0:T(128)} %bitcast.refs_0_, bf16[1536,384]{1,0:T(8,128)(2,1)S(1)} %get-tuple-element.44.refs_7_.refs_1_, bf16[384,1536]{1,0:T(8,128)(2,1)S(1)} %get-tuple-element.47.refs_2_, ...), custom_call_target="tpu_custom_call", output_to_operand_aliasing={{0}: (7, {}), {1}: (8, {})} | custom-call | flops 2415919104 | bytes 12582912 | tf_op jit(solution)/shard_map/weight_grads/pallas_call | solution.py:68
  125.0 0.7 add_convert_fusion
  (36 shorter events, 0.8 us)
Async XLA Ops:
  1.6 10.1 %collective-permute-start.3 = (bf16[2,48,1536]{2,1,0:T(8,128)(2,1)S(1)}, bf16[2,48,1536]{2,1,0:T(8,128)(2,1)S(1)}, u32[]{:S(2)}, u32[]{:S(2)}) collective-permute-start(bf16[2,48,1536]{2,1,0:T(8,128)(2,1)S(1)} %pad_maximum_fusion.1.refs_1_), channel_id=1, source_target_pairs={{0,1},{1,0},{2,3},{3,2},{4,5},{5,4},{6,7},{7,6},{8,9},{9,8},{10,11... | collective-permute-start | bytes 884744 | tf_op jit(solution)/shard_map/ppermute | solution.py:444
  4.7 7.7 %collective-permute-start.6 = (bf16[2,48,1536]{2,1,0:T(8,128)(2,1)S(1)}, bf16[2,48,1536]{2,1,0:T(8,128)(2,1)S(1)}, u32[]{:S(2)}, u32[]{:S(2)}) collective-permute-start(bf16[2,48,1536]{2,1,0:T(8,128)(2,1)S(1)} %pad_maximum_fusion.1.refs_1_), channel_id=1, source_target_pairs={{1,2},{2,1},{5,6},{6,5},{9,10},{10,9},{13,14},{14,13},{17,18},{18,... | collective-permute-start | bytes 884744 | tf_op jit(solution)/shard_map/ppermute | solution.py:460
  5.4 12.1 %collective-permute-start = (bf16[2,48,1536]{2,1,0:T(8,128)(2,1)S(1)}, bf16[2,48,1536]{2,1,0:T(8,128)(2,1)S(1)}, u32[]{:S(2)}, u32[]{:S(2)}) collective-permute-start(bf16[2,48,1536]{2,1,0:T(8,128)(2,1)S(1)} %pad_maximum_fusion.1.refs_1_), channel_id=1, source_target_pairs={{0,16},{16,0},{1,17},{17,1},{2,18},{18,2},{3,19},{19,3},{4,20},{20... | collective-permute-start | bytes 884744 | tf_op jit(solution)/shard_map/ppermute | solution.py:444
  11.7 16.3 %collective-permute-start.8 = (bf16[2,48,1536]{2,1,0:T(8,128)(2,1)S(1)}, bf16[2,48,1536]{2,1,0:T(8,128)(2,1)S(1)}, u32[]{:S(2)}, u32[]{:S(2)}) collective-permute-start(bf16[2,48,1536]{2,1,0:T(8,128)(2,1)S(1)} %collective-permute-done.3.refs_1_.refs_3_), channel_id=1, source_target_pairs={{1,2},{2,1},{5,6},{6,5},{9,10},{10,9},{13,14},{14,13},{17,18},{18,... | collective-permute-start | bytes 884744 | tf_op jit(solution)/shard_map/ppermute | solution.py:463
  12.4 17.1 %collective-permute-start.7 = (bf16[2,48,1536]{2,1,0:T(8,128)(2,1)S(1)}, bf16[2,48,1536]{2,1,0:T(8,128)(2,1)S(1)}, u32[]{:S(2)}, u32[]{:S(2)}) collective-permute-start(bf16[2,48,1536]{2,1,0:T(8,128)(2,1)S(1)} %collective-permute-done.6), channel_id=1, source_target_pairs={{1,0},{2,3},{5,4},{6,7},{9,8},{10,11},{13,12},{14,15},{17,16},{18,... | collective-permute-start | bytes 884744 | tf_op jit(solution)/shard_map/ppermute | solution.py:464
  21.1 9.6 %collective-permute-start.2 = (bf16[96,1536]{1,0:T(8,128)(2,1)S(1)}, bf16[96,1536]{1,0:T(8,128)(2,1)S(1)}, u32[]{:S(2)}, u32[]{:S(2)}) collective-permute-start(bf16[96,1536]{1,0:T(8,128)(2,1)S(1)} %get-tuple-element.37), channel_id=1, source_target_pairs={{0,4},{4,0},{8,12},{12,8},{1,5},{5,1},{9,13},{13,9},{2,6},{6,2},{1... | collective-permute-start | bytes 884744 | tf_op jit(solution)/shard_map/ppermute | solution.py:444
  21.2 9.5 %collective-permute-start.1 = (bf16[96,1536]{1,0:T(8,128)(2,1)S(1)}, bf16[96,1536]{1,0:T(8,128)(2,1)S(1)}, u32[]{:S(2)}, u32[]{:S(2)}) collective-permute-start(bf16[96,1536]{1,0:T(8,128)(2,1)S(1)} %get-tuple-element.35.refs_5_), channel_id=1, source_target_pairs={{0,4},{4,0},{8,12},{12,8},{1,5},{5,1},{9,13},{13,9},{2,6},{6,2},{1... | collective-permute-start | bytes 884744 | tf_op jit(solution)/shard_map/ppermute | solution.py:444
  21.7 9.0 %collective-permute-start.4 = (bf16[2,48,1536]{2,1,0:T(8,128)(2,1)S(1)}, bf16[2,48,1536]{2,1,0:T(8,128)(2,1)S(1)}, u32[]{:S(2)}, u32[]{:S(2)}) collective-permute-start(bf16[2,48,1536]{2,1,0:T(8,128)(2,1)S(1)} %collective-permute-done.3.refs_1_.refs_3_), channel_id=1, source_target_pairs={{0,16},{16,0},{1,17},{17,1},{2,18},{18,2},{3,19},{19,3},{4,20},{20... | collective-permute-start | bytes 884744 | tf_op jit(solution)/shard_map/ppermute | solution.py:444
  28.1 12.6 %collective-permute-start.9 = (bf16[2,48,1536]{2,1,0:T(8,128)(2,1)S(1)}, bf16[2,48,1536]{2,1,0:T(8,128)(2,1)S(1)}, u32[]{:S(2)}, u32[]{:S(2)}) collective-permute-start(bf16[2,48,1536]{2,1,0:T(8,128)(2,1)S(1)} %collective-permute-done.8.refs_7_), channel_id=1, source_target_pairs={{1,0},{2,3},{5,4},{6,7},{9,8},{10,11},{13,12},{14,15},{17,16},{18,... | collective-permute-start | bytes 884744 | tf_op jit(solution)/shard_map/ppermute | solution.py:465
  29.6 15.3 %collective-permute-start.10 = (bf16[2,48,1536]{2,1,0:T(8,128)(2,1)S(1)}, bf16[2,48,1536]{2,1,0:T(8,128)(2,1)S(1)}, u32[]{:S(2)}, u32[]{:S(2)}) collective-permute-start(bf16[2,48,1536]{2,1,0:T(8,128)(2,1)S(1)} %broadcast_select_fusion.1.refs_1_.refs_5_), channel_id=1, source_target_pairs={{0,16},{16,0},{1,17},{17,1},{2,18},{18,2},{3,19},{19,3},{4,20},{20... | collective-permute-start | bytes 884744 | tf_op jit(solution)/shard_map/ppermute | solution.py:444
  31.1 14.5 %collective-permute-start.5 = (bf16[2,96,1536]{2,1,0:T(8,128)(2,1)S(1)}, bf16[2,96,1536]{2,1,0:T(8,128)(2,1)S(1)}, u32[]{:S(2)}, u32[]{:S(2)}) collective-permute-start(bf16[2,96,1536]{2,1,0:T(8,128)(2,1)S(1)} %combine.4.refs_5_), channel_id=1, source_target_pairs={{0,8},{4,12},{8,0},{12,4},{1,9},{5,13},{9,1},{13,5},{2,10},{6,14},... | collective-permute-start | bytes 1769480 | tf_op jit(solution)/shard_map/ppermute | solution.py:444
  36.5 10.0 %collective-permute-start.12 = (bf16[96,1536]{1,0:T(8,128)(2,1)S(1)}, bf16[96,1536]{1,0:T(8,128)(2,1)S(1)}, u32[]{:S(2)}, u32[]{:S(2)}) collective-permute-start(bf16[96,1536]{1,0:T(8,128)(2,1)S(1)} %get-tuple-element.41), channel_id=1, source_target_pairs={{0,4},{4,0},{8,12},{12,8},{1,5},{5,1},{9,13},{13,9},{2,6},{6,2},{1... | collective-permute-start | bytes 884744 | tf_op jit(solution)/shard_map/ppermute | solution.py:444
  36.5 10.0 %collective-permute-start.11 = (bf16[96,1536]{1,0:T(8,128)(2,1)S(1)}, bf16[96,1536]{1,0:T(8,128)(2,1)S(1)}, u32[]{:S(2)}, u32[]{:S(2)}) collective-permute-start(bf16[96,1536]{1,0:T(8,128)(2,1)S(1)} %get-tuple-element.40.refs_5_), channel_id=1, source_target_pairs={{0,4},{4,0},{8,12},{12,8},{1,5},{5,1},{9,13},{13,9},{2,6},{6,2},{1... | collective-permute-start | bytes 884744 | tf_op jit(solution)/shard_map/ppermute | solution.py:444
  40.8 8.2 %collective-permute-start.14 = (bf16[2,48,1536]{2,1,0:T(8,128)(2,1)S(1)}, bf16[2,48,1536]{2,1,0:T(8,128)(2,1)S(1)}, u32[]{:S(2)}, u32[]{:S(2)}) collective-permute-start(bf16[2,48,1536]{2,1,0:T(8,128)(2,1)S(1)} %broadcast_select_fusion.refs_3_.refs_7_), channel_id=1, source_target_pairs={{0,16},{16,0},{1,17},{17,1},{2,18},{18,2},{3,19},{19,3},{4,20},{20... | collective-permute-start | bytes 884744 | tf_op jit(solution)/shard_map/ppermute | solution.py:444
  46.9 13.6 %collective-permute-start.13 = (bf16[2,96,1536]{2,1,0:T(8,128)(2,1)S(1)}, bf16[2,96,1536]{2,1,0:T(8,128)(2,1)S(1)}, u32[]{:S(2)}, u32[]{:S(2)}) collective-permute-start(bf16[2,96,1536]{2,1,0:T(8,128)(2,1)S(1)} %combine.5.refs_7_), channel_id=1, source_target_pairs={{0,8},{4,12},{8,0},{12,4},{1,9},{5,13},{9,1},{13,5},{2,10},{6,14},... | collective-permute-start | bytes 1769480 | tf_op jit(solution)/shard_map/ppermute | solution.py:444
  52.8 8.6 %collective-permute-start.18 = (bf16[192,1536]{1,0:T(8,128)(2,1)S(1)}, bf16[192,1536]{1,0:T(8,128)(2,1)S(1)}, u32[]{:S(2)}, u32[]{:S(2)}) collective-permute-start(bf16[192,1536]{1,0:T(8,128)(2,1)S(1)} %get-tuple-element.43), channel_id=1, source_target_pairs={{0,4},{4,0},{8,12},{12,8},{1,5},{5,1},{9,13},{13,9},{2,6},{6,2},{1... | collective-permute-start | bytes 1769480 | tf_op jit(solution)/shard_map/ppermute | solution.py:444
  52.9 8.5 %collective-permute-start.17 = (bf16[192,1536]{1,0:T(8,128)(2,1)S(1)}, bf16[192,1536]{1,0:T(8,128)(2,1)S(1)}, u32[]{:S(2)}, u32[]{:S(2)}) collective-permute-start(bf16[192,1536]{1,0:T(8,128)(2,1)S(1)} %get-tuple-element.42.refs_7_), channel_id=1, source_target_pairs={{0,4},{4,0},{8,12},{12,8},{1,5},{5,1},{9,13},{13,9},{2,6},{6,2},{1... | collective-permute-start | bytes 1769480 | tf_op jit(solution)/shard_map/ppermute | solution.py:444
  53.4 10.4 %collective-permute-start.15 = (bf16[2,96,1536]{2,1,0:T(8,128)(2,1)S(1)}, bf16[2,96,1536]{2,1,0:T(8,128)(2,1)S(1)}, u32[]{:S(2)}, u32[]{:S(2)}) collective-permute-start(bf16[2,96,1536]{2,1,0:T(8,128)(2,1)S(1)} %activations.5.refs_4_.refs_1_.refs_3_), channel_id=1, source_target_pairs={{0,4},{4,0},{8,12},{12,8},{1,5},{5,1},{9,13},{13,9},{2,6},{6,2},{1... | collective-permute-start | bytes 1769480 | tf_op jit(solution)/shard_map/ppermute | solution.py:444
  61.4 2.5 %collective-permute-start.16 = (bf16[2,96,1536]{2,1,0:T(8,128)(2,1)S(1)}, bf16[2,96,1536]{2,1,0:T(8,128)(2,1)S(1)}, u32[]{:S(2)}, u32[]{:S(2)}) collective-permute-start(bf16[2,96,1536]{2,1,0:T(8,128)(2,1)S(1)} %activations.6.refs_10_.refs_2_.refs_4_), channel_id=1, source_target_pairs={{0,4},{4,0},{8,12},{12,8},{1,5},{5,1},{9,13},{13,9},{2,6},{6,2},{1... | collective-permute-start | bytes 1769480 | tf_op jit(solution)/shard_map/ppermute | solution.py:444
  61.6 11.6 %collective-permute-start.20 = (bf16[2,192,512]{2,1,0:T(8,128)(2,1)S(1)}, bf16[2,192,512]{2,1,0:T(8,128)(2,1)S(1)}, u32[]{:S(2)}, u32[]{:S(2)}) collective-permute-start(bf16[2,192,512]{2,1,0:T(8,128)(2,1)S(1)} %pad_maximum_fusion.refs_9_), channel_id=1, source_target_pairs={{0,8},{4,12},{8,0},{12,4},{1,9},{5,13},{9,1},{13,5},{2,10},{6,14},... | collective-permute-start | bytes 1179656 | tf_op jit(solution)/shard_map/ppermute | solution.py:444
  67.4 12.2 %collective-permute-start.19 = (bf16[96,1536]{1,0:T(8,128)(2,1)S(1)}, bf16[96,1536]{1,0:T(8,128)(2,1)S(1)}, u32[]{:S(2)}, u32[]{:S(2)}) collective-permute-start(bf16[96,1536]{1,0:T(8,128)(2,1)S(1)} %get-tuple-element.46), channel_id=1, source_target_pairs={{0,16},{16,0},{1,17},{17,1},{2,18},{18,2},{3,19},{19,3},{4,20},{20... | collective-permute-start | bytes 884744 | tf_op jit(solution)/shard_map/ppermute | solution.py:444
  73.7 6.1 %collective-permute-start.23 = (bf16[2,192,512]{2,1,0:T(8,128)(2,1)S(1)}, bf16[2,192,512]{2,1,0:T(8,128)(2,1)S(1)}, u32[]{:S(2)}, u32[]{:S(2)}) collective-permute-start(bf16[2,192,512]{2,1,0:T(8,128)(2,1)S(1)} %activations.7.refs_4_.refs_5_.refs_1_), channel_id=1, source_target_pairs={{0,4},{4,0},{8,12},{12,8},{1,5},{5,1},{9,13},{13,9},{2,6},{6,2},{1... | collective-permute-start | bytes 1179656 | tf_op jit(solution)/shard_map/ppermute | solution.py:444
  74.1 11.6 %collective-permute-start.22 = (bf16[2,96,1024]{2,1,0:T(8,128)(2,1)S(1)}, bf16[2,96,1024]{2,1,0:T(8,128)(2,1)S(1)}, u32[]{:S(2)}, u32[]{:S(2)}) collective-permute-start(bf16[2,96,1024]{2,1,0:T(8,128)(2,1)S(1)} %combine.6.refs_6_), channel_id=1, source_target_pairs={{0,8},{4,12},{8,0},{12,4},{1,9},{5,13},{9,1},{13,5},{2,10},{6,14},... | collective-permute-start | bytes 1179656 | tf_op jit(solution)/shard_map/ppermute | solution.py:444
  86.2 6.2 %collective-permute-start.24 = (bf16[2,96,1024]{2,1,0:T(8,128)(2,1)S(1)}, bf16[2,96,1024]{2,1,0:T(8,128)(2,1)S(1)}, u32[]{:S(2)}, u32[]{:S(2)}) collective-permute-start(bf16[2,96,1024]{2,1,0:T(8,128)(2,1)S(1)} %activations.8.refs_1_.refs_6_.refs_5_), channel_id=1, source_target_pairs={{0,4},{4,0},{8,12},{12,8},{1,5},{5,1},{9,13},{13,9},{2,6},{6,2},{1... | collective-permute-start | bytes 1179656 | tf_op jit(solution)/shard_map/ppermute | solution.py:444
  86.4 11.4 %collective-permute-start.26 = (bf16[2,96,1024]{2,1,0:T(8,128)(2,1)S(1)}, bf16[2,96,1024]{2,1,0:T(8,128)(2,1)S(1)}, u32[]{:S(2)}, u32[]{:S(2)}) collective-permute-start(bf16[2,96,1024]{2,1,0:T(8,128)(2,1)S(1)} %combine.7.refs_8_), channel_id=1, source_target_pairs={{0,8},{4,12},{8,0},{12,4},{1,9},{5,13},{9,1},{13,5},{2,10},{6,14},... | collective-permute-start | bytes 1179656 | tf_op jit(solution)/shard_map/ppermute | solution.py:444
  88.1 8.6 %collective-permute-start.21 = (bf16[48,1536]{1,0:T(8,128)(2,1)S(1)}, bf16[48,1536]{1,0:T(8,128)(2,1)S(1)}, u32[]{:S(2)}, u32[]{:S(2)}) collective-permute-start(bf16[48,1536]{1,0:T(8,128)(2,1)S(1)} %fold.6.refs_5_), channel_id=1, source_target_pairs={{0,1},{1,0},{2,3},{3,2},{4,5},{5,4},{6,7},{7,6},{8,9},{9,8},{10,11... | collective-permute-start | bytes 442376 | tf_op jit(solution)/shard_map/ppermute | solution.py:444
  98.4 1.8 %collective-permute-start.27 = (bf16[2,96,1024]{2,1,0:T(8,128)(2,1)S(1)}, bf16[2,96,1024]{2,1,0:T(8,128)(2,1)S(1)}, u32[]{:S(2)}, u32[]{:S(2)}) collective-permute-start(bf16[2,96,1024]{2,1,0:T(8,128)(2,1)S(1)} %activations.9.refs_1_.refs_6_), channel_id=1, source_target_pairs={{0,4},{4,0},{8,12},{12,8},{1,5},{5,1},{9,13},{13,9},{2,6},{6,2},{1... | collective-permute-start | bytes 1179656 | tf_op jit(solution)/shard_map/ppermute | solution.py:444
  98.5 6.3 %collective-permute-start.25 = (bf16[48,1536]{1,0:T(8,128)(2,1)S(1)}, bf16[48,1536]{1,0:T(8,128)(2,1)S(1)}, u32[]{:S(2)}, u32[]{:S(2)}) collective-permute-start(bf16[48,1536]{1,0:T(8,128)(2,1)S(1)} %get-tuple-element.53), channel_id=1, source_target_pairs={{0,16},{16,0},{1,17},{17,1},{2,18},{18,2},{3,19},{19,3},{4,20},{20... | collective-permute-start | bytes 442376 | tf_op jit(solution)/shard_map/ppermute | solution.py:444
  102.7 14.0 %collective-permute-start.29 = (bf16[48,1536]{1,0:T(8,128)(2,1)S(1)}, bf16[48,1536]{1,0:T(8,128)(2,1)S(1)}, u32[]{:S(2)}, u32[]{:S(2)}) collective-permute-start(bf16[48,1536]{1,0:T(8,128)(2,1)S(1)} %get-tuple-element.55), channel_id=1, source_target_pairs={{0,16},{16,0},{1,17},{17,1},{2,18},{18,2},{3,19},{19,3},{4,20},{20... | collective-permute-start | bytes 442376 | tf_op jit(solution)/shard_map/ppermute | solution.py:444
  104.8 20.2 %collective-permute-start.28 = (bf16[48,1536]{1,0:T(8,128)(2,1)S(1)}, bf16[48,1536]{1,0:T(8,128)(2,1)S(1)}, u32[]{:S(2)}, u32[]{:S(2)}) collective-permute-start(bf16[48,1536]{1,0:T(8,128)(2,1)S(1)} %fold.8.refs_9_), channel_id=1, source_target_pairs={{0,2},{1,3},{2,0},{3,1},{4,6},{5,7},{6,4},{7,5},{8,10},{9,11},{10,... | collective-permute-start | bytes 442376 | tf_op jit(solution)/shard_map/ppermute | solution.py:444
  116.7 8.3 %collective-permute-start.30 = (bf16[48,1536]{1,0:T(8,128)(2,1)S(1)}, bf16[48,1536]{1,0:T(8,128)(2,1)S(1)}, u32[]{:S(2)}, u32[]{:S(2)}) collective-permute-start(bf16[48,1536]{1,0:T(8,128)(2,1)S(1)} %fold.9.refs_9_), channel_id=1, source_target_pairs={{0,3},{1,2},{2,1},{3,0},{4,7},{5,6},{6,5},{7,4},{8,11},{9,10},{10,... | collective-permute-start | bytes 442376 | tf_op jit(solution)/shard_map/ppermute | solution.py:444

commit v12 on v9

--- a/solution.py
+++ b/solution.py
@@ -111,39 +111,20 @@
     return [pltpu.VMEM((depth, half), BF16), pltpu.VMEM((half, depth), BF16)]
 
 
-def bring(core, side, up, down):
-    def body(core_ref, up_ref, down_ref, up_out, down_out, sems):
-        pairs = halves(core_ref, side, up_ref, down_ref, up_out, down_out, sems, 1)
-        for copy in pairs[0]:
-            copy.start()
-        for copy in pairs[0]:
-            copy.wait()
-
-    return call(
-        body,
-        core,
-        [pltpu.with_memory_space_constraint(array, pltpu.HBM) for array in (up, down)],
-        [pl.BlockSpec(memory_space=pltpu.HBM)] * 2,
-        half_outs(up),
-        [pl.BlockSpec(memory_space=pltpu.VMEM)] * 2,
-        (1,),
-        (0, 2 * up.size),
-        "bring",
-        (),
-        [pltpu.SemaphoreType.DMA((2, 1))],
-    )
-
-
 def bring_and_sum(core, units, side, up, down, after=()):
     _, rows, depth = units[0].shape
     tokens = rows * len(units)
     half = up.shape[1] // 2
     parts = 3 if half % 384 == 0 else 1
     size = half // parts
+    if side:
+        kinds = [jax.ShapeDtypeStruct((tokens, half), BF16)] * 2
+    else:
+        kinds = [jax.ShapeDtypeStruct((2, tokens, half), F32)]
 
     def body(core_ref, *refs):
         unit_refs = refs[: len(units)]
-        up_ref, down_ref, out, up_out, down_out, acts, sems = refs[len(units) :]
+        up_ref, down_ref, *outs, up_out, down_out, acts, sems = refs[len(units) :]
         pairs = halves(core_ref, side, up_ref, down_ref, up_out, down_out, sems, parts)
         for pair in pairs:
             for copy in pair:
@@ -154,16 +135,22 @@
             for copy in pair:
                 copy.wait()
             here = slice(part * size, (part + 1) * size)
-            out[0, :, here] = contract(acts[0], up_out[:, here], 1, 0)
-            out[1, :, here] = contract(acts[1], down_out[here, :], 1, 1)
+            preact = contract(acts[0], up_out[:, here], 1, 0)
+            grad_hidden = contract(acts[1], down_out[here, :], 1, 1)
+            if side:
+                outs[0][:, here] = preact.astype(BF16)
+                outs[1][:, here] = grad_hidden.astype(BF16)
+            else:
+                outs[0][0, :, here] = preact
+                outs[0][1, :, here] = grad_hidden
 
     return call(
         body,
         core,
         [*units] + [pltpu.with_memory_space_constraint(array, pltpu.HBM) for array in (up, down)],
         [whole(units[0].shape)] * len(units) + [pl.BlockSpec(memory_space=pltpu.HBM)] * 2,
-        [jax.ShapeDtypeStruct((2, tokens, half), F32)] + half_outs(up),
-        [whole((2, tokens, half))] + [pl.BlockSpec(memory_space=pltpu.VMEM)] * 2,
+        kinds + half_outs(up),
+        [whole(kind.shape) for kind in kinds] + [pl.BlockSpec(memory_space=pltpu.VMEM)] * 2,
         (1,),
         (4 * tokens * depth * half, 2 * up.size),
         "bring_and_sum",
@@ -458,7 +445,6 @@
     across, outward = [(1, 2), (2, 1)], [(1, 0), (2, 3)]
     first = lax.ppermute(unit[0, 0], "gz", across)
     ups, downs = {}, {}
-    ups[1], downs[1] = bring(core, 1, up, down)
     second = lax.ppermute(unit[1, 0], "gz", across)
     first_on = lax.ppermute(first, "gz", outward)
     second_on = lax.ppermute(second, "gz", outward)
@@ -483,9 +469,12 @@
     near, keep, far, act, act_near = {}, {}, {}, {}, {}
 
     def send(group, after=()):
-        out = partial_sums(
-            core, groups[group], ups[1], downs[1], 1, True, 0, half, after
-        )
+        if group:
+            out = partial_sums(
+                core, groups[group], ups[1], downs[1], 1, True, 0, half, after
+            )
+        else:
+            *out, ups[1], downs[1] = bring_and_sum(core, groups[group], 1, up, down, after)
         near[group] = [swap(array, "gy", 4, 1) for array in out]
         return [out[0]]
 

time: 122 us -> 128 us (1.049)
  waiting for transfers between devices: 20 us -> 25.7 us
  local copies, waits for them, and re-layouts: 2.43 us -> 6.78 us
  Pallas kernels: 64.3 us -> 61.7 us
  starting transfers between devices: 32 us -> 29.9 us
    ppermute x27, waiting for transfers between devices: 17.5 us -> 22.8 us  [swap(): return lax.ppermute(value, axis, [(i, i ^ bits) for i in range(size)])]
    unnamed x14, local copies, waits for them, and re-layouts: 2.37 us -> 6.72 us
    pallas_call x30 -> x29, Pallas kernels: 64.3 us -> 61.7 us  [call(): pl.pallas_call(kernel, grid_spec=pltpu.PrefetchScalarGridSpec(num_scalar_...]
    ppermute x27, starting transfers between devices: 27.2 us -> 25.2 us  [swap(): return lax.ppermute(value, axis, [(i, i ^ bits) for i in range(size)])]
  transfers between devices with their start and end apart: 31 -> 31, of which waited for: 10 -> 11; matrix products, arithmetic and copies ran while one was open for 0% -> 0% of each run, Pallas kernels for 52% -> 47%
where the time goes in v12:
time: 128 us; the launch traced here: 127 us
  Pallas kernels  61.7 us (48%)
  starting transfers between devices  29.9 us (23%)
  waiting for transfers between devices  25.7 us (20%)
  local copies, waits for them, and re-layouts  6.78 us (5%)
  other arithmetic  2.04 us (2%)
    pallas_call x29, Pallas kernels, call(): pl.pallas_call(kernel, grid_spec=pltpu.PrefetchScalarGridSpec(num_scalar_...  61.7 us
    ppermute x27, starting transfers between devices, swap(): return lax.ppermute(value, axis, [(i, i ^ bits) for i in range(size)])  25.2 us
    ppermute x27, waiting for transfers between devices, swap(): return lax.ppermute(value, axis, [(i, i ^ bits) for i in range(size)])  22.8 us
    unnamed x14, local copies, waits for them, and re-layouts  6.72 us
  transfers between devices with their start and end apart: 31, of which 11 were waited for; matrix products, arithmetic and copies ran while one was open for 0% of the time, Pallas kernels for 47%

profile of v12, /device:TPU:0, one launch (start us, length us, event | category | flops | bytes accessed | tf_op | source)
XLA Modules:
  0.0 127.3 jit_solution(5413247526041870591)
XLA Ops:
  0.6 1.0 pad_maximum_fusion.1.refs_1_
  1.6 3.0 %collective-permute-start = (bf16[2,48,1536]{2,1,0:T(8,128)(2,1)S(1)}, bf16[2,48,1536]{2,1,0:T(8,128)(2,1)S(1)}, u32[]{:S(2)}, u32[]{:S(2)}) collective-permute-start(bf16[2,48,1536]{2,1,0:T(8,128)(2,1)S(1)} %pad_maximum_fusion.1.refs_1_), channel_id=1, source_target_pairs={{0,16},{16,0},{1,17},{17,1},{2,18},{18,2},{3,19},{19,3},{4,20},{20... | collective-permute-start | bytes 884744 | tf_op jit(solution)/shard_map/ppermute | solution.py:431
  4.6 1.6 %collective-permute-start.3 = (bf16[2,48,1536]{2,1,0:T(8,128)(2,1)S(1)}, bf16[2,48,1536]{2,1,0:T(8,128)(2,1)S(1)}, u32[]{:S(2)}, u32[]{:S(2)}) collective-permute-start(bf16[2,48,1536]{2,1,0:T(8,128)(2,1)S(1)} %pad_maximum_fusion.1.refs_1_), channel_id=1, source_target_pairs={{0,1},{1,0},{2,3},{3,2},{4,5},{5,4},{6,7},{7,6},{8,9},{9,8},{10,11... | collective-permute-start | bytes 884744 | tf_op jit(solution)/shard_map/ppermute | solution.py:431
  6.2 1.4 %collective-permute-start.6 = (bf16[2,48,1536]{2,1,0:T(8,128)(2,1)S(1)}, bf16[2,48,1536]{2,1,0:T(8,128)(2,1)}, u32[]{:S(2)}, u32[]{:S(2)}) collective-permute-start(bf16[2,48,1536]{2,1,0:T(8,128)(2,1)S(1)} %pad_maximum_fusion.1.refs_1_), channel_id=1, source_target_pairs={{1,2},{2,1},{5,6},{6,5},{9,10},{10,9},{13,14},{14,13},{17,18},{18,... | collective-permute-start | bytes 884744 | tf_op jit(solution)/shard_map/ppermute | solution.py:446
  7.6 4.1 %collective-permute-done.refs_2_ = bf16[2,48,1536]{2,1,0:T(8,128)(2,1)S(1)} collective-permute-done((bf16[2,48,1536]{2,1,0:T(8,128)(2,1)S(1)}, bf16[2,48,1536]{2,1,0:T(8,128)(2,1)S(1)}, u32[]{:S(2)}, u32[]{:S(2)}) %collective-permute-start) | collective-permute-done | bytes 294944 | tf_op jit(solution)/shard_map/ppermute | solution.py:431
  11.7 4.7 %bring_and_sum.2 = (bf16[96,1536]{1,0:T(8,128)(2,1)S(1)}, bf16[96,1536]{1,0:T(8,128)(2,1)S(1)}, bf16[1536,1536]{1,0:T(8,128)(2,1)S(1)}, bf16[1536,1536]{1,0:T(8,128)(2,1)S(1)}) custom-call(s32[1]{0:T(128)} %bitcast.refs_0_, bf16[2,48,1536]{2,1,0:T(8,128)(2,1)S(1)} %pad_maximum_fusion.1.refs_1_, bf16[2,48,1536]{2,1,0:T(8,128)(2,1)S(1)} %collective-permute-done.refs_2_, ...), custom_call_target="tpu_custom_call" | custom-call | flops 905969664 | bytes 9437184 | tf_op jit(solution)/shard_map/bring_and_sum/pallas_call | solution.py:68
  16.4 2.2 %copy-done = bf16[1536,1536]{1,0:T(8,128)(2,1)} copy-done((bf16[1536,1536]{1,0:T(8,128)(2,1)}, bf16[1536,1536]{1,0:T(8,128)(2,1)S(1)}, u32[]{:S(2)}) %copy-start) | copy-done | bytes 4718616
  18.6 2.2 %copy-done.1 = bf16[1536,1536]{1,0:T(8,128)(2,1)} copy-done((bf16[1536,1536]{1,0:T(8,128)(2,1)}, bf16[1536,1536]{1,0:T(8,128)(2,1)S(1)}, u32[]{:S(2)}) %copy-start.1) | copy-done | bytes 4718616
  20.7 0.5 collective-permute-start.2
  21.3 1.7 %collective-permute-start.4 = (bf16[2,48,1536]{2,1,0:T(8,128)(2,1)S(1)}, bf16[2,48,1536]{2,1,0:T(8,128)(2,1)S(1)}, u32[]{:S(2)}, u32[]{:S(2)}) collective-permute-start(bf16[2,48,1536]{2,1,0:T(8,128)(2,1)S(1)} %collective-permute-done.3.refs_1_.refs_3_), channel_id=1, source_target_pairs={{0,16},{16,0},{1,17},{17,1},{2,18},{18,2},{3,19},{19,3},{4,20},{20... | collective-permute-start | bytes 884744 | tf_op jit(solution)/shard_map/ppermute | solution.py:431
  23.0 0.7 collective-permute-start.8
  23.7 1.3 %collective-permute-start.7 = (bf16[2,48,1536]{2,1,0:T(8,128)(2,1)}, bf16[2,48,1536]{2,1,0:T(8,128)(2,1)S(1)}, u32[]{:S(2)}, u32[]{:S(2)}) collective-permute-start(bf16[2,48,1536]{2,1,0:T(8,128)(2,1)} %collective-permute-done.6), channel_id=1, source_target_pairs={{1,0},{2,3},{5,4},{6,7},{9,8},{10,11},{13,12},{14,15},{17,16},{18,... | collective-permute-start | bytes 884744 | tf_op jit(solution)/shard_map/ppermute | solution.py:449
  25.0 4.8 %bring_and_sum.3 = (f32[2,96,1536]{2,1,0:T(8,128)S(1)}, bf16[1536,1536]{1,0:T(8,128)(2,1)S(1)}, bf16[1536,1536]{1,0:T(8,128)(2,1)S(1)}) custom-call(s32[1]{0:T(128)} %bitcast.refs_0_, bf16[2,48,1536]{2,1,0:T(8,128)(2,1)S(1)} %pad_maximum_fusion.1.refs_1_, bf16[2,48,1536]{2,1,0:T(8,128)(2,1)S(1)} %collective-permute-done.refs_2_, bf16[1536,3072]{1,0:T(8,128)(2,1)} %refs_3_.3, ...), custom_call_target="tpu_custom_call" | custom-call | flops 905969664 | bytes 9437184 | tf_op jit(solution)/shard_map/bring_and_sum/pallas_call | solution.py:68
  29.9 0.3 collective-permute-done.4.refs_5_.refs_2_.refs_4_
  30.2 0.4 combine.4.refs_5_
  30.6 1.8 %collective-permute-start.5 = (bf16[2,96,1536]{2,1,0:T(8,128)(2,1)S(1)}, bf16[2,96,1536]{2,1,0:T(8,128)(2,1)S(1)}, u32[]{:S(2)}, u32[]{:S(2)}) collective-permute-start(bf16[2,96,1536]{2,1,0:T(8,128)(2,1)S(1)} %combine.4.refs_5_), channel_id=1, source_target_pairs={{0,8},{4,12},{8,0},{12,4},{1,9},{5,13},{9,1},{13,5},{2,10},{6,14},... | collective-permute-start | bytes 1769480 | tf_op jit(solution)/shard_map/ppermute | solution.py:431
  32.4 1.5 %collective-permute-start.9 = (bf16[2,48,1536]{2,1,0:T(8,128)(2,1)S(1)}, bf16[2,48,1536]{2,1,0:T(8,128)(2,1)S(1)}, u32[]{:S(2)}, u32[]{:S(2)}) collective-permute-start(bf16[2,48,1536]{2,1,0:T(8,128)(2,1)S(1)} %collective-permute-done.8.refs_7_), channel_id=1, source_target_pairs={{1,0},{2,3},{5,4},{6,7},{9,8},{10,11},{13,12},{14,15},{17,16},{18,... | collective-permute-start | bytes 884744 | tf_op jit(solution)/shard_map/ppermute | solution.py:450
  33.9 2.3 %collective-permute-done.7.refs_6_ = bf16[2,48,1536]{2,1,0:T(8,128)(2,1)S(1)} collective-permute-done((bf16[2,48,1536]{2,1,0:T(8,128)(2,1)}, bf16[2,48,1536]{2,1,0:T(8,128)(2,1)S(1)}, u32[]{:S(2)}, u32[]{:S(2)}) %collective-permute-start.7) | collective-permute-done | bytes 294944 | tf_op jit(solution)/shard_map/ppermute | solution.py:449
  36.2 0.6 collective-permute-start.10
  36.8 2.3 %copy-done.2 = bf16[1536,1536]{1,0:T(8,128)(2,1)S(1)} copy-done((bf16[1536,1536]{1,0:T(8,128)(2,1)S(1)}, bf16[1536,1536]{1,0:T(8,128)(2,1)}, u32[]{:S(2)}) %copy-start.2) | copy-done | bytes 4718616
  39.1 3.6 %sums_send.2 = (bf16[96,1536]{1,0:T(8,128)(2,1)S(1)}, bf16[96,1536]{1,0:T(8,128)(2,1)S(1)}) custom-call(s32[1]{0:T(128)} %bitcast.refs_0_, bf16[2,48,1536]{2,1,0:T(8,128)(2,1)S(1)} %collective-permute-done.3.refs_1_.refs_3_, bf16[2,48,1536]{2,1,0:T(8,128)(2,1)S(1)} %collective-permute-done.4.refs_5_.refs_2_.refs_4_, bf16[1536,1536]{1,0:T(8,128)(2,1)S(1)} %bitcast.24, ...), custom_call_target="tpu_custom_call" | custom-call | flops 905969664 | bytes 9437184 | tf_op jit(solution)/shard_map/sums_send/pallas_call | solution.py:68
  42.8 0.5 collective-permute-start.12
  43.3 0.6 collective-permute-done.9.refs_6_
  44.0 0.9 collective-permute-start.14
  44.9 3.6 %sums_keep.2.refs_5_.refs_1_ = f32[2,96,1536]{2,1,0:T(8,128)S(1)} custom-call(s32[1]{0:T(128)} %bitcast.refs_0_, bf16[2,48,1536]{2,1,0:T(8,128)(2,1)S(1)} %collective-permute-done.3.refs_1_.refs_3_, bf16[2,48,1536]{2,1,0:T(8,128)(2,1)S(1)} %collective-permute-done.4.refs_5_.refs_2_.refs_4_, bf16[1536,1536]{1,0:T(8,128)(2,1)S(1)} %get-tuple-element.36.refs_3_.refs_5_, ...), custom_call_target="tpu_custom_call" | custom-call | flops 905969664 | bytes 9437184 | tf_op jit(solution)/shard_map/sums_keep/pallas_call | solution.py:68
  48.5 0.8 activations.5.refs_4_.refs_1_.refs_3_
  49.4 0.4 combine.5.refs_7_
  49.8 1.6 %collective-permute-start.13 = (bf16[2,96,1536]{2,1,0:T(8,128)(2,1)S(1)}, bf16[2,96,1536]{2,1,0:T(8,128)(2,1)S(1)}, u32[]{:S(2)}, u32[]{:S(2)}) collective-permute-start(bf16[2,96,1536]{2,1,0:T(8,128)(2,1)S(1)} %combine.5.refs_7_), channel_id=1, source_target_pairs={{0,8},{4,12},{8,0},{12,4},{1,9},{5,13},{9,1},{13,5},{2,10},{6,14},... | collective-permute-start | bytes 1769480 | tf_op jit(solution)/shard_map/ppermute | solution.py:431
  51.4 1.0 collective-permute-done.14.refs_4_.refs_8_
  52.4 3.8 %sums_send.3 = (bf16[192,1536]{1,0:T(8,128)(2,1)S(1)}, bf16[192,1536]{1,0:T(8,128)(2,1)S(1)}) custom-call(s32[1]{0:T(128)} %bitcast.refs_0_, bf16[2,48,1536]{2,1,0:T(8,128)(2,1)S(1)} %broadcast_select_fusion.1.refs_1_.refs_5_, bf16[2,48,1536]{2,1,0:T(8,128)(2,1)S(1)} %collective-permute-done.10.refs_6_.refs_2_, ...), custom_call_target="tpu_custom_call" | custom-call | flops 1811939328 | bytes 9437184 | tf_op jit(solution)/shard_map/sums_send/pallas_call | solution.py:68
  56.3 0.5 collective-permute-start.18
  56.9 3.9 %sums_keep.3.refs_5_.refs_1_ = f32[2,192,1536]{2,1,0:T(8,128)S(1)} custom-call(s32[1]{0:T(128)} %bitcast.refs_0_, bf16[2,48,1536]{2,1,0:T(8,128)(2,1)S(1)} %broadcast_select_fusion.1.refs_1_.refs_5_, bf16[2,48,1536]{2,1,0:T(8,128)(2,1)S(1)} %collective-permute-done.10.refs_6_.refs_2_, bf16[2,48,1536]{2,1,0:T(8,128)(2,1)S(1)} %broadcast_select_fusion.refs_3_.refs_7_, ...), custom_call_target="tpu_custom_call" | custom-call | flops 1811939328 | bytes 9437184 | tf_op jit(solution)/shard_map/sums_keep/pallas_call | solution.py:68
  60.8 4.1 %collective-permute-done.13.refs_4_ = bf16[2,96,1536]{2,1,0:T(8,128)(2,1)S(1)} collective-permute-done((bf16[2,96,1536]{2,1,0:T(8,128)(2,1)S(1)}, bf16[2,96,1536]{2,1,0:T(8,128)(2,1)S(1)}, u32[]{:S(2)}, u32[]{:S(2)}) %collective-permute-start.13) | collective-permute-done | bytes 589856 | tf_op jit(solution)/shard_map/ppermute | solution.py:431
  64.9 0.8 activations.6.refs_10_.refs_2_.refs_4_
  65.8 0.2 fusion.4
  66.1 1.6 %collective-permute-start.20 = (bf16[2,192,768]{2,1,0:T(8,128)(2,1)S(1)}, bf16[2,192,768]{2,1,0:T(8,128)(2,1)S(1)}, u32[]{:S(2)}, u32[]{:S(2)}) collective-permute-start(bf16[2,192,768]{2,1,0:T(8,128)(2,1)S(1)} %pad_maximum_fusion.refs_9_), channel_id=1, source_target_pairs={{0,8},{4,12},{8,0},{12,4},{1,9},{5,13},{9,1},{13,5},{2,10},{6,14},... | collective-permute-start | bytes 1769480 | tf_op jit(solution)/shard_map/ppermute | solution.py:431
  67.6 0.4 arrange.1
  68.1 3.6 %back.4 = (f32[96,1536]{1,0:T(8,128)S(1)}, bf16[96,1536]{1,0:T(8,128)(2,1)S(1)}) custom-call(s32[1]{0:T(128)} %bitcast.refs_0_, bf16[2,96,1536]{2,1,0:T(8,128)(2,1)S(1)} %activations.5.refs_4_.refs_1_.refs_3_, bf16[2,96,1536]{2,1,0:T(8,128)(2,1)S(1)} %activations.6.refs_10_.refs_2_.refs_4_, bf16[2,96,1536]{2,1,0:T(8,128)(2,1)S(1)} %collective-permute-done.15.refs_3_, ...), custom_call_target="tpu_custom_call" | custom-call | flops 1811939328 | bytes 10616832 | tf_op jit(solution)/shard_map/back/pallas_call | solution.py:68
  71.7 10.2 %collective-permute-done.20.refs_4_ = bf16[2,192,768]{2,1,0:T(8,128)(2,1)S(1)} collective-permute-done((bf16[2,192,768]{2,1,0:T(8,128)(2,1)S(1)}, bf16[2,192,768]{2,1,0:T(8,128)(2,1)S(1)}, u32[]{:S(2)}, u32[]{:S(2)}) %collective-permute-start.20) | collective-permute-done | bytes 589856 | tf_op jit(solution)/shard_map/ppermute | solution.py:431
  81.8 0.7 activations.7.refs_4_.refs_5_.refs_1_
  82.5 0.2 combine.6.refs_6_
  82.8 1.6 %collective-permute-start.21 = (bf16[2,96,768]{2,1,0:T(8,128)(2,1)S(1)}, bf16[2,96,768]{2,1,0:T(8,128)(2,1)S(1)}, u32[]{:S(2)}, u32[]{:S(2)}) collective-permute-start(bf16[2,96,768]{2,1,0:T(8,128)(2,1)S(1)} %combine.6.refs_6_), channel_id=1, source_target_pairs={{0,8},{4,12},{8,0},{12,4},{1,9},{5,13},{9,1},{13,5},{2,10},{6,14},... | collective-permute-start | bytes 884744 | tf_op jit(solution)/shard_map/ppermute | solution.py:431
  84.4 0.5 collective-permute-start.19
  85.0 5.4 %weight_grads.4 = (f32[1536,3072]{1,0:T(8,128)}, f32[3072,1536]{1,0:T(8,128)}, f32[8,128]{1,0:T(8,128)S(1)}) custom-call(s32[1]{0:T(128)} %bitcast.refs_0_, bf16[1536,384]{1,0:T(8,128)(2,1)S(1)} %get-tuple-element.44.refs_7_.refs_1_, bf16[384,1536]{1,0:T(8,128)(2,1)S(1)} %get-tuple-element.47.refs_2_, ...), custom_call_target="tpu_custom_call" | custom-call | flops 1811939328 | bytes 9437184 | tf_op jit(solution)/shard_map/weight_grads/pallas_call | solution.py:68
  90.5 1.0 collective-permute-done.21.refs_4_
  91.5 0.4 activations.8.refs_4_.refs_1_.refs_5_
  92.0 0.2 combine.7.refs_3_
  92.2 1.6 %collective-permute-start.26 = (bf16[2,96,768]{2,1,0:T(8,128)(2,1)S(1)}, bf16[2,96,768]{2,1,0:T(8,128)(2,1)S(1)}, u32[]{:S(2)}, u32[]{:S(2)}) collective-permute-start(bf16[2,96,768]{2,1,0:T(8,128)(2,1)S(1)} %combine.7.refs_3_), channel_id=1, source_target_pairs={{0,8},{4,12},{8,0},{12,4},{1,9},{5,13},{9,1},{13,5},{2,10},{6,14},... | collective-permute-start | bytes 884744 | tf_op jit(solution)/shard_map/ppermute | solution.py:431
  93.9 1.7 %collective-permute-start.22 = (bf16[48,1536]{1,0:T(8,128)(2,1)S(1)}, bf16[48,1536]{1,0:T(8,128)(2,1)S(1)}, u32[]{:S(2)}, u32[]{:S(2)}) collective-permute-start(bf16[48,1536]{1,0:T(8,128)(2,1)S(1)} %fold.6.refs_5_), channel_id=1, source_target_pairs={{0,1},{1,0},{2,3},{3,2},{4,5},{5,4},{6,7},{7,6},{8,9},{9,8},{10,11... | collective-permute-start | bytes 442376 | tf_op jit(solution)/shard_map/ppermute | solution.py:431
  95.6 2.4 %back.5.refs_8_.refs_5_ = f32[192,1536]{1,0:T(8,128)S(1)} custom-call(s32[1]{0:T(128)} %bitcast.refs_0_, bf16[2,192,768]{2,1,0:T(8,128)(2,1)S(1)} %activations.7.refs_4_.refs_5_.refs_1_, bf16[2,192,768]{2,1,0:T(8,128)(2,1)S(1)} %collective-permute-done.24.refs_2_.refs_5_, bf16[1536,1536]{1,0:T(8,128)(2,1)S(1)} %get-tuple-element.36.refs_3_.refs_5_, ...), custom_call_target="tpu_custom_call" | custom-call | flops 905969664 | bytes 5898240 | tf_op jit(solution)/shard_map/back/pallas_call | solution.py:68
  98.0 5.4 %weight_grads.5 = (f32[1536,3072]{1,0:T(8,128)}, f32[3072,1536]{1,0:T(8,128)}, f32[8,128]{1,0:T(8,128)S(1)}) custom-call(s32[1]{0:T(128)} %bitcast.refs_0_, bf16[1536,384]{1,0:T(8,128)(2,1)S(1)} %get-tuple-element.44.refs_7_.refs_1_, bf16[384,1536]{1,0:T(8,128)(2,1)S(1)} %get-tuple-element.47.refs_2_, ...), custom_call_target="tpu_custom_call", output_to_operand_aliasing={{0}: (6, {}), {1}: (7, {})} | custom-call | flops 1811939328 | bytes 9437184 | tf_op jit(solution)/shard_map/weight_grads/pallas_call | solution.py:68
  103.4 2.3 %back.6 = (f32[48,1536]{1,0:T(8,128)S(1)}, bf16[48,1536]{1,0:T(8,128)(2,1)S(1)}) custom-call(s32[1]{0:T(128)} %bitcast.refs_0_, bf16[2,96,768]{2,1,0:T(8,128)(2,1)S(1)} %activations.8.refs_4_.refs_1_.refs_5_, bf16[2,96,768]{2,1,0:T(8,128)(2,1)S(1)} %collective-permute-done.23.refs_2_.refs_5_, bf16[1536,1536]{1,0:T(8,128)(2,1)S(1)} %get-tuple-element.36.refs_3_.refs_5_, ...), custom_call_target="tpu_custom_call" | custom-call | flops 452984832 | bytes 5308416 | tf_op jit(solution)/shard_map/back/pallas_call | solution.py:68
  105.8 0.4 activations.9.refs_1_.refs_6_
  106.3 1.0 collective-permute-start.25
  107.3 0.6 collective-permute-done.27.refs_2_.refs_6_
  107.9 2.3 %back.7 = (f32[48,1536]{1,0:T(8,128)S(1)}, bf16[48,1536]{1,0:T(8,128)(2,1)S(1)}) custom-call(s32[1]{0:T(128)} %bitcast.refs_0_, bf16[2,96,768]{2,1,0:T(8,128)(2,1)S(1)} %activations.9.refs_1_.refs_6_, bf16[2,96,768]{2,1,0:T(8,128)(2,1)S(1)} %collective-permute-done.27.refs_2_.refs_6_, bf16[1536,1536]{1,0:T(8,128)(2,1)S(1)} %get-tuple-element.36.refs_3_.refs_5_, ...), custom_call_target="tpu_custom_call" | custom-call | flops 452984832 | bytes 5308416 | tf_op jit(solution)/shard_map/back/pallas_call | solution.py:68
  110.1 1.0 collective-permute-start.29
  111.1 1.4 %collective-permute-done.25.refs_2_ = bf16[48,1536]{1,0:T(8,128)(2,1)S(1)} collective-permute-done((bf16[48,1536]{1,0:T(8,128)(2,1)S(1)}, bf16[48,1536]{1,0:T(8,128)(2,1)S(1)}, u32[]{:S(2)}, u32[]{:S(2)}) %collective-permute-start.25) | collective-permute-done | bytes 147488 | tf_op jit(solution)/shard_map/ppermute | solution.py:431
  112.6 1.4 %collective-permute-start.28 = (bf16[48,1536]{1,0:T(8,128)(2,1)S(1)}, bf16[48,1536]{1,0:T(8,128)(2,1)S(1)}, u32[]{:S(2)}, u32[]{:S(2)}) collective-permute-start(bf16[48,1536]{1,0:T(8,128)(2,1)S(1)} %fold.8.refs_9_), channel_id=1, source_target_pairs={{0,2},{1,3},{2,0},{3,1},{4,6},{5,7},{6,4},{7,5},{8,10},{9,11},{10,... | collective-permute-start | bytes 442376 | tf_op jit(solution)/shard_map/ppermute | solution.py:431
  114.0 5.4 %weight_grads.6 = (f32[1536,3072]{1,0:T(8,128)}, f32[3072,1536]{1,0:T(8,128)}, f32[8,128]{1,0:T(8,128)S(1)}) custom-call(s32[1]{0:T(128)} %bitcast.refs_0_, bf16[1536,384]{1,0:T(8,128)(2,1)S(1)} %get-tuple-element.44.refs_7_.refs_1_, bf16[384,1536]{1,0:T(8,128)(2,1)S(1)} %get-tuple-element.47.refs_2_, ...), custom_call_target="tpu_custom_call", output_to_operand_aliasing={{0}: (7, {}), {1}: (8, {})} | custom-call | flops 1811939328 | bytes 9437184 | tf_op jit(solution)/shard_map/weight_grads/pallas_call | solution.py:68
  119.4 1.5 %collective-permute-start.30 = (bf16[48,1536]{1,0:T(8,128)(2,1)S(1)}, bf16[48,1536]{1,0:T(8,128)(2,1)S(1)}, u32[]{:S(2)}, u32[]{:S(2)}) collective-permute-start(bf16[48,1536]{1,0:T(8,128)(2,1)S(1)} %fold.9.refs_9_), channel_id=1, source_target_pairs={{0,3},{1,2},{2,1},{3,0},{4,7},{5,6},{6,5},{7,4},{8,11},{9,10},{10,... | collective-permute-start | bytes 442376 | tf_op jit(solution)/shard_map/ppermute | solution.py:431
  121.0 5.4 %weight_grads.7 = (f32[1536,3072]{1,0:T(8,128)}, f32[3072,1536]{1,0:T(8,128)}, f32[8,128]{1,0:T(8,128)}) custom-call(s32[1]{0:T(128)} %bitcast.refs_0_, bf16[1536,384]{1,0:T(8,128)(2,1)S(1)} %get-tuple-element.44.refs_7_.refs_1_, bf16[384,1536]{1,0:T(8,128)(2,1)S(1)} %get-tuple-element.47.refs_2_, ...), custom_call_target="tpu_custom_call", output_to_operand_aliasing={{0}: (7, {}), {1}: (8, {})} | custom-call | flops 1811939328 | bytes 9437184 | tf_op jit(solution)/shard_map/weight_grads/pallas_call | solution.py:68
  126.4 0.1 collective-permute-done.30
  126.6 0.7 add_convert_fusion
  (51 shorter events, 0.9 us)
Async XLA Ops:
  1.6 10.0 %collective-permute-start = (bf16[2,48,1536]{2,1,0:T(8,128)(2,1)S(1)}, bf16[2,48,1536]{2,1,0:T(8,128)(2,1)S(1)}, u32[]{:S(2)}, u32[]{:S(2)}) collective-permute-start(bf16[2,48,1536]{2,1,0:T(8,128)(2,1)S(1)} %pad_maximum_fusion.1.refs_1_), channel_id=1, source_target_pairs={{0,16},{16,0},{1,17},{17,1},{2,18},{18,2},{3,19},{19,3},{4,20},{20... | collective-permute-start | bytes 884744 | tf_op jit(solution)/shard_map/ppermute | solution.py:431
  4.6 16.6 %collective-permute-start.3 = (bf16[2,48,1536]{2,1,0:T(8,128)(2,1)S(1)}, bf16[2,48,1536]{2,1,0:T(8,128)(2,1)S(1)}, u32[]{:S(2)}, u32[]{:S(2)}) collective-permute-start(bf16[2,48,1536]{2,1,0:T(8,128)(2,1)S(1)} %pad_maximum_fusion.1.refs_1_), channel_id=1, source_target_pairs={{0,1},{1,0},{2,3},{3,2},{4,5},{5,4},{6,7},{7,6},{8,9},{9,8},{10,11... | collective-permute-start | bytes 884744 | tf_op jit(solution)/shard_map/ppermute | solution.py:431
  6.2 17.4 %collective-permute-start.6 = (bf16[2,48,1536]{2,1,0:T(8,128)(2,1)S(1)}, bf16[2,48,1536]{2,1,0:T(8,128)(2,1)}, u32[]{:S(2)}, u32[]{:S(2)}) collective-permute-start(bf16[2,48,1536]{2,1,0:T(8,128)(2,1)S(1)} %pad_maximum_fusion.1.refs_1_), channel_id=1, source_target_pairs={{1,2},{2,1},{5,6},{6,5},{9,10},{10,9},{13,14},{14,13},{17,18},{18,... | collective-permute-start | bytes 884744 | tf_op jit(solution)/shard_map/ppermute | solution.py:446
  16.4 2.2 %copy-start = (bf16[1536,1536]{1,0:T(8,128)(2,1)}, bf16[1536,1536]{1,0:T(8,128)(2,1)S(1)}, u32[]{:S(2)}) copy-start(bf16[1536,1536]{1,0:T(8,128)(2,1)S(1)} %get-tuple-element.38.refs_3_.refs_5_.refs_6_.refs_4_) | copy-start | bytes 14155780
  18.6 2.2 %copy-start.1 = (bf16[1536,1536]{1,0:T(8,128)(2,1)}, bf16[1536,1536]{1,0:T(8,128)(2,1)S(1)}, u32[]{:S(2)}) copy-start(bf16[1536,1536]{1,0:T(8,128)(2,1)S(1)} %get-tuple-element.39.refs_4_.refs_6_) | copy-start | bytes 14155780
  20.7 9.1 %collective-permute-start.1 = (bf16[96,1536]{1,0:T(8,128)(2,1)S(1)}, bf16[96,1536]{1,0:T(8,128)(2,1)S(1)}, u32[]{:S(2)}, u32[]{:S(2)}) collective-permute-start(bf16[96,1536]{1,0:T(8,128)(2,1)S(1)} %get-tuple-element.33.refs_5_), channel_id=1, source_target_pairs={{0,4},{4,0},{8,12},{12,8},{1,5},{5,1},{9,13},{13,9},{2,6},{6,2},{1... | collective-permute-start | bytes 884744 | tf_op jit(solution)/shard_map/ppermute | solution.py:431
  20.7 9.1 %collective-permute-start.2 = (bf16[96,1536]{1,0:T(8,128)(2,1)S(1)}, bf16[96,1536]{1,0:T(8,128)(2,1)S(1)}, u32[]{:S(2)}, u32[]{:S(2)}) collective-permute-start(bf16[96,1536]{1,0:T(8,128)(2,1)S(1)} %get-tuple-element.35), channel_id=1, source_target_pairs={{0,4},{4,0},{8,12},{12,8},{1,5},{5,1},{9,13},{13,9},{2,6},{6,2},{1... | collective-permute-start | bytes 884744 | tf_op jit(solution)/shard_map/ppermute | solution.py:431
  21.3 8.9 %collective-permute-start.4 = (bf16[2,48,1536]{2,1,0:T(8,128)(2,1)S(1)}, bf16[2,48,1536]{2,1,0:T(8,128)(2,1)S(1)}, u32[]{:S(2)}, u32[]{:S(2)}) collective-permute-start(bf16[2,48,1536]{2,1,0:T(8,128)(2,1)S(1)} %collective-permute-done.3.refs_1_.refs_3_), channel_id=1, source_target_pairs={{0,16},{16,0},{1,17},{17,1},{2,18},{18,2},{3,19},{19,3},{4,20},{20... | collective-permute-start | bytes 884744 | tf_op jit(solution)/shard_map/ppermute | solution.py:431
  23.0 9.4 %collective-permute-start.8 = (bf16[2,48,1536]{2,1,0:T(8,128)(2,1)S(1)}, bf16[2,48,1536]{2,1,0:T(8,128)(2,1)S(1)}, u32[]{:S(2)}, u32[]{:S(2)}) collective-permute-start(bf16[2,48,1536]{2,1,0:T(8,128)(2,1)S(1)} %collective-permute-done.3.refs_1_.refs_3_), channel_id=1, source_target_pairs={{1,2},{2,1},{5,6},{6,5},{9,10},{10,9},{13,14},{14,13},{17,18},{18,... | collective-permute-start | bytes 884744 | tf_op jit(solution)/shard_map/ppermute | solution.py:448
  23.7 12.5 %collective-permute-start.7 = (bf16[2,48,1536]{2,1,0:T(8,128)(2,1)}, bf16[2,48,1536]{2,1,0:T(8,128)(2,1)S(1)}, u32[]{:S(2)}, u32[]{:S(2)}) collective-permute-start(bf16[2,48,1536]{2,1,0:T(8,128)(2,1)} %collective-permute-done.6), channel_id=1, source_target_pairs={{1,0},{2,3},{5,4},{6,7},{9,8},{10,11},{13,12},{14,15},{17,16},{18,... | collective-permute-start | bytes 884744 | tf_op jit(solution)/shard_map/ppermute | solution.py:449
  25.0 11.8 %slice-start = ((s8[4718592]{0:T(1024)(128)(4,1)}), s8[524288]{0:T(1024)(128)(4,1)S(1)}, s32[]{:S(2)}) async-start(s8[4718592]{0:T(1024)(128)(4,1)} %bitcast.23), calls=%async_computation | async-start | bytes 1048576
  25.0 11.8 %slice-start.1 = ((s8[4718592]{0:T(1024)(128)(4,1)}), s8[4194304]{0:T(1024)(128)(4,1)S(1)}, s32[]{:S(2)}) async-start(s8[4718592]{0:T(1024)(128)(4,1)} %bitcast.23), calls=%async_computation.1 | async-start | bytes 8388608
  30.6 17.9 %collective-permute-start.5 = (bf16[2,96,1536]{2,1,0:T(8,128)(2,1)S(1)}, bf16[2,96,1536]{2,1,0:T(8,128)(2,1)S(1)}, u32[]{:S(2)}, u32[]{:S(2)}) collective-permute-start(bf16[2,96,1536]{2,1,0:T(8,128)(2,1)S(1)} %combine.4.refs_5_), channel_id=1, source_target_pairs={{0,8},{4,12},{8,0},{12,4},{1,9},{5,13},{9,1},{13,5},{2,10},{6,14},... | collective-permute-start | bytes 1769480 | tf_op jit(solution)/shard_map/ppermute | solution.py:431
  32.4 11.5 %collective-permute-start.9 = (bf16[2,48,1536]{2,1,0:T(8,128)(2,1)S(1)}, bf16[2,48,1536]{2,1,0:T(8,128)(2,1)S(1)}, u32[]{:S(2)}, u32[]{:S(2)}) collective-permute-start(bf16[2,48,1536]{2,1,0:T(8,128)(2,1)S(1)} %collective-permute-done.8.refs_7_), channel_id=1, source_target_pairs={{1,0},{2,3},{5,4},{6,7},{9,8},{10,11},{13,12},{14,15},{17,16},{18,... | collective-permute-start | bytes 884744 | tf_op jit(solution)/shard_map/ppermute | solution.py:450
  36.2 12.3 %collective-permute-start.10 = (bf16[2,48,1536]{2,1,0:T(8,128)(2,1)S(1)}, bf16[2,48,1536]{2,1,0:T(8,128)(2,1)S(1)}, u32[]{:S(2)}, u32[]{:S(2)}) collective-permute-start(bf16[2,48,1536]{2,1,0:T(8,128)(2,1)S(1)} %broadcast_select_fusion.1.refs_1_.refs_5_), channel_id=1, source_target_pairs={{0,16},{16,0},{1,17},{17,1},{2,18},{18,2},{3,19},{19,3},{4,20},{20... | collective-permute-start | bytes 884744 | tf_op jit(solution)/shard_map/ppermute | solution.py:431
  36.8 2.3 %copy-start.2 = (bf16[1536,1536]{1,0:T(8,128)(2,1)S(1)}, bf16[1536,1536]{1,0:T(8,128)(2,1)}, u32[]{:S(2)}) copy-start(bf16[1536,1536]{1,0:T(8,128)(2,1)} %copy-done.1) | copy-start | bytes 14155780
  42.7 6.6 %collective-permute-start.11 = (bf16[96,1536]{1,0:T(8,128)(2,1)S(1)}, bf16[96,1536]{1,0:T(8,128)(2,1)S(1)}, u32[]{:S(2)}, u32[]{:S(2)}) collective-permute-start(bf16[96,1536]{1,0:T(8,128)(2,1)S(1)} %get-tuple-element.40.refs_5_), channel_id=1, source_target_pairs={{0,4},{4,0},{8,12},{12,8},{1,5},{5,1},{9,13},{13,9},{2,6},{6,2},{1... | collective-permute-start | bytes 884744 | tf_op jit(solution)/shard_map/ppermute | solution.py:431
  42.8 6.6 %collective-permute-start.12 = (bf16[96,1536]{1,0:T(8,128)(2,1)S(1)}, bf16[96,1536]{1,0:T(8,128)(2,1)S(1)}, u32[]{:S(2)}, u32[]{:S(2)}) collective-permute-start(bf16[96,1536]{1,0:T(8,128)(2,1)S(1)} %get-tuple-element.41), channel_id=1, source_target_pairs={{0,4},{4,0},{8,12},{12,8},{1,5},{5,1},{9,13},{13,9},{2,6},{6,2},{1... | collective-permute-start | bytes 884744 | tf_op jit(solution)/shard_map/ppermute | solution.py:431
  44.0 8.4 %collective-permute-start.14 = (bf16[2,48,1536]{2,1,0:T(8,128)(2,1)S(1)}, bf16[2,48,1536]{2,1,0:T(8,128)(2,1)S(1)}, u32[]{:S(2)}, u32[]{:S(2)}) collective-permute-start(bf16[2,48,1536]{2,1,0:T(8,128)(2,1)S(1)} %broadcast_select_fusion.refs_3_.refs_7_), channel_id=1, source_target_pairs={{0,16},{16,0},{1,17},{17,1},{2,18},{18,2},{3,19},{19,3},{4,20},{20... | collective-permute-start | bytes 884744 | tf_op jit(solution)/shard_map/ppermute | solution.py:431
  44.9 7.5 %slice-start.2 = ((s8[4718592]{0:T(1024)(128)(4,1)}), s8[4194304]{0:T(1024)(128)(4,1)S(1)}, s32[]{:S(2)}) async-start(s8[4718592]{0:T(1024)(128)(4,1)} %bitcast.25), calls=%async_computation.2 | async-start | bytes 8388608
  44.9 7.5 %slice-start.3 = ((s8[4718592]{0:T(1024)(128)(4,1)}), s8[524288]{0:T(1024)(128)(4,1)S(1)}, s32[]{:S(2)}) async-start(s8[4718592]{0:T(1024)(128)(4,1)} %bitcast.25), calls=%async_computation.3 | async-start | bytes 1048576
  49.8 15.1 %collective-permute-start.13 = (bf16[2,96,1536]{2,1,0:T(8,128)(2,1)S(1)}, bf16[2,96,1536]{2,1,0:T(8,128)(2,1)S(1)}, u32[]{:S(2)}, u32[]{:S(2)}) collective-permute-start(bf16[2,96,1536]{2,1,0:T(8,128)(2,1)S(1)} %combine.5.refs_7_), channel_id=1, source_target_pairs={{0,8},{4,12},{8,0},{12,4},{1,9},{5,13},{9,1},{13,5},{2,10},{6,14},... | collective-permute-start | bytes 1769480 | tf_op jit(solution)/shard_map/ppermute | solution.py:431
  56.2 9.5 %collective-permute-start.17 = (bf16[192,1536]{1,0:T(8,128)(2,1)S(1)}, bf16[192,1536]{1,0:T(8,128)(2,1)S(1)}, u32[]{:S(2)}, u32[]{:S(2)}) collective-permute-start(bf16[192,1536]{1,0:T(8,128)(2,1)S(1)} %get-tuple-element.42.refs_7_), channel_id=1, source_target_pairs={{0,4},{4,0},{8,12},{12,8},{1,5},{5,1},{9,13},{13,9},{2,6},{6,2},{1... | collective-permute-start | bytes 1769480 | tf_op jit(solution)/shard_map/ppermute | solution.py:431
  56.3 9.5 %collective-permute-start.18 = (bf16[192,1536]{1,0:T(8,128)(2,1)S(1)}, bf16[192,1536]{1,0:T(8,128)(2,1)S(1)}, u32[]{:S(2)}, u32[]{:S(2)}) collective-permute-start(bf16[192,1536]{1,0:T(8,128)(2,1)S(1)} %get-tuple-element.43), channel_id=1, source_target_pairs={{0,4},{4,0},{8,12},{12,8},{1,5},{5,1},{9,13},{13,9},{2,6},{6,2},{1... | collective-permute-start | bytes 1769480 | tf_op jit(solution)/shard_map/ppermute | solution.py:431
  56.8 11.2 %collective-permute-start.15 = (bf16[2,96,1536]{2,1,0:T(8,128)(2,1)S(1)}, bf16[2,96,1536]{2,1,0:T(8,128)(2,1)S(1)}, u32[]{:S(2)}, u32[]{:S(2)}) collective-permute-start(bf16[2,96,1536]{2,1,0:T(8,128)(2,1)S(1)} %activations.5.refs_4_.refs_1_.refs_3_), channel_id=1, source_target_pairs={{0,4},{4,0},{8,12},{12,8},{1,5},{5,1},{9,13},{13,9},{2,6},{6,2},{1... | collective-permute-start | bytes 1769480 | tf_op jit(solution)/shard_map/ppermute | solution.py:431
  65.7 2.4 %collective-permute-start.16 = (bf16[2,96,1536]{2,1,0:T(8,128)(2,1)S(1)}, bf16[2,96,1536]{2,1,0:T(8,128)(2,1)S(1)}, u32[]{:S(2)}, u32[]{:S(2)}) collective-permute-start(bf16[2,96,1536]{2,1,0:T(8,128)(2,1)S(1)} %activations.6.refs_10_.refs_2_.refs_4_), channel_id=1, source_target_pairs={{0,4},{4,0},{8,12},{12,8},{1,5},{5,1},{9,13},{13,9},{2,6},{6,2},{1... | collective-permute-start | bytes 1769480 | tf_op jit(solution)/shard_map/ppermute | solution.py:431
  66.1 15.8 %collective-permute-start.20 = (bf16[2,192,768]{2,1,0:T(8,128)(2,1)S(1)}, bf16[2,192,768]{2,1,0:T(8,128)(2,1)S(1)}, u32[]{:S(2)}, u32[]{:S(2)}) collective-permute-start(bf16[2,192,768]{2,1,0:T(8,128)(2,1)S(1)} %pad_maximum_fusion.refs_9_), channel_id=1, source_target_pairs={{0,8},{4,12},{8,0},{12,4},{1,9},{5,13},{9,1},{13,5},{2,10},{6,14},... | collective-permute-start | bytes 1769480 | tf_op jit(solution)/shard_map/ppermute | solution.py:431
  82.8 8.7 %collective-permute-start.21 = (bf16[2,96,768]{2,1,0:T(8,128)(2,1)S(1)}, bf16[2,96,768]{2,1,0:T(8,128)(2,1)S(1)}, u32[]{:S(2)}, u32[]{:S(2)}) collective-permute-start(bf16[2,96,768]{2,1,0:T(8,128)(2,1)S(1)} %combine.6.refs_6_), channel_id=1, source_target_pairs={{0,8},{4,12},{8,0},{12,4},{1,9},{5,13},{9,1},{13,5},{2,10},{6,14},... | collective-permute-start | bytes 884744 | tf_op jit(solution)/shard_map/ppermute | solution.py:431
  84.4 9.4 %collective-permute-start.19 = (bf16[96,1536]{1,0:T(8,128)(2,1)S(1)}, bf16[96,1536]{1,0:T(8,128)(2,1)S(1)}, u32[]{:S(2)}, u32[]{:S(2)}) collective-permute-start(bf16[96,1536]{1,0:T(8,128)(2,1)S(1)} %get-tuple-element.46), channel_id=1, source_target_pairs={{0,16},{16,0},{1,17},{17,1},{2,18},{18,2},{3,19},{19,3},{4,20},{20... | collective-permute-start | bytes 884744 | tf_op jit(solution)/shard_map/ppermute | solution.py:431
  85.0 10.6 %collective-permute-start.24 = (bf16[2,192,768]{2,1,0:T(8,128)(2,1)S(1)}, bf16[2,192,768]{2,1,0:T(8,128)(2,1)S(1)}, u32[]{:S(2)}, u32[]{:S(2)}) collective-permute-start(bf16[2,192,768]{2,1,0:T(8,128)(2,1)S(1)} %activations.7.refs_4_.refs_5_.refs_1_), channel_id=1, source_target_pairs={{0,4},{4,0},{8,12},{12,8},{1,5},{5,1},{9,13},{13,9},{2,6},{6,2},{1... | collective-permute-start | bytes 1769480 | tf_op jit(solution)/shard_map/ppermute | solution.py:431
  91.9 11.5 %collective-permute-start.23 = (bf16[2,96,768]{2,1,0:T(8,128)(2,1)S(1)}, bf16[2,96,768]{2,1,0:T(8,128)(2,1)S(1)}, u32[]{:S(2)}, u32[]{:S(2)}) collective-permute-start(bf16[2,96,768]{2,1,0:T(8,128)(2,1)S(1)} %activations.8.refs_4_.refs_1_.refs_5_), channel_id=1, source_target_pairs={{0,4},{4,0},{8,12},{12,8},{1,5},{5,1},{9,13},{13,9},{2,6},{6,2},{1... | collective-permute-start | bytes 884744 | tf_op jit(solution)/shard_map/ppermute | solution.py:431
  92.2 13.5 %collective-permute-start.26 = (bf16[2,96,768]{2,1,0:T(8,128)(2,1)S(1)}, bf16[2,96,768]{2,1,0:T(8,128)(2,1)S(1)}, u32[]{:S(2)}, u32[]{:S(2)}) collective-permute-start(bf16[2,96,768]{2,1,0:T(8,128)(2,1)S(1)} %combine.7.refs_3_), channel_id=1, source_target_pairs={{0,8},{4,12},{8,0},{12,4},{1,9},{5,13},{9,1},{13,5},{2,10},{6,14},... | collective-permute-start | bytes 884744 | tf_op jit(solution)/shard_map/ppermute | solution.py:431
  93.9 11.8 %collective-permute-start.22 = (bf16[48,1536]{1,0:T(8,128)(2,1)S(1)}, bf16[48,1536]{1,0:T(8,128)(2,1)S(1)}, u32[]{:S(2)}, u32[]{:S(2)}) collective-permute-start(bf16[48,1536]{1,0:T(8,128)(2,1)S(1)} %fold.6.refs_5_), channel_id=1, source_target_pairs={{0,1},{1,0},{2,3},{3,2},{4,5},{5,4},{6,7},{7,6},{8,9},{9,8},{10,11... | collective-permute-start | bytes 442376 | tf_op jit(solution)/shard_map/ppermute | solution.py:431
  106.2 1.6 %collective-permute-start.27 = (bf16[2,96,768]{2,1,0:T(8,128)(2,1)S(1)}, bf16[2,96,768]{2,1,0:T(8,128)(2,1)S(1)}, u32[]{:S(2)}, u32[]{:S(2)}) collective-permute-start(bf16[2,96,768]{2,1,0:T(8,128)(2,1)S(1)} %activations.9.refs_1_.refs_6_), channel_id=1, source_target_pairs={{0,4},{4,0},{8,12},{12,8},{1,5},{5,1},{9,13},{13,9},{2,6},{6,2},{1... | collective-permute-start | bytes 884744 | tf_op jit(solution)/shard_map/ppermute | solution.py:431
  106.3 6.3 %collective-permute-start.25 = (bf16[48,1536]{1,0:T(8,128)(2,1)S(1)}, bf16[48,1536]{1,0:T(8,128)(2,1)S(1)}, u32[]{:S(2)}, u32[]{:S(2)}) collective-permute-start(bf16[48,1536]{1,0:T(8,128)(2,1)S(1)} %get-tuple-element.53), channel_id=1, source_target_pairs={{0,16},{16,0},{1,17},{17,1},{2,18},{18,2},{3,19},{19,3},{4,20},{20... | collective-permute-start | bytes 442376 | tf_op jit(solution)/shard_map/ppermute | solution.py:431
  110.1 9.3 %collective-permute-start.29 = (bf16[48,1536]{1,0:T(8,128)(2,1)S(1)}, bf16[48,1536]{1,0:T(8,128)(2,1)S(1)}, u32[]{:S(2)}, u32[]{:S(2)}) collective-permute-start(bf16[48,1536]{1,0:T(8,128)(2,1)S(1)} %get-tuple-element.55), channel_id=1, source_target_pairs={{0,16},{16,0},{1,17},{17,1},{2,18},{18,2},{3,19},{19,3},{4,20},{20... | collective-permute-start | bytes 442376 | tf_op jit(solution)/shard_map/ppermute | solution.py:431
  112.6 13.8 %collective-permute-start.28 = (bf16[48,1536]{1,0:T(8,128)(2,1)S(1)}, bf16[48,1536]{1,0:T(8,128)(2,1)S(1)}, u32[]{:S(2)}, u32[]{:S(2)}) collective-permute-start(bf16[48,1536]{1,0:T(8,128)(2,1)S(1)} %fold.8.refs_9_), channel_id=1, source_target_pairs={{0,2},{1,3},{2,0},{3,1},{4,6},{5,7},{6,4},{7,5},{8,10},{9,11},{10,... | collective-permute-start | bytes 442376 | tf_op jit(solution)/shard_map/ppermute | solution.py:431
  119.4 7.1 %collective-permute-start.30 = (bf16[48,1536]{1,0:T(8,128)(2,1)S(1)}, bf16[48,1536]{1,0:T(8,128)(2,1)S(1)}, u32[]{:S(2)}, u32[]{:S(2)}) collective-permute-start(bf16[48,1536]{1,0:T(8,128)(2,1)S(1)} %fold.9.refs_9_), channel_id=1, source_target_pairs={{0,3},{1,2},{2,1},{3,0},{4,7},{5,6},{6,5},{7,4},{8,11},{9,10},{10,... | collective-permute-start | bytes 442376 | tf_op jit(solution)/shard_map/ppermute | solution.py:431
